TPU v7x, 32 devices: a whole 2x2x4 slice. The times are simulated.
32 devices in a mesh: rep: 4 (over y, core), fsdp: 8 (over z, x).
Axes of the slice: x: 2, y: 2, z: 4, core: 2. Of those that a mesh axis runs over, the one named last changes fastest.
Arguments:
- activations: bfloat16 [4, 3072, 4096], P('rep', 'fsdp'), may hold values from -6 to 6
- kv_weight: bfloat16 [4, 4096, 1024], P('rep', 'fsdp'), may hold values from -0.09375 to 0.09375
- kv_cotangent: bfloat16 [4, 3072, 1024], P('rep', 'fsdp'), may hold values from -6 to 6
- first_moment: float32 [4, 4096, 1024], P('rep', 'fsdp'), may hold values from -48 to 48
- second_moment: float32 [4, 4096, 1024], P('rep', 'fsdp'), may hold values from 10 to 1000
- partner: int32 [4], replicated, may hold values from 0 to 3, as said below
- mix_numerator: int32 [4], replicated, may hold values from 8 to 56
Outputs:
- kv_out: bfloat16 [4, 3072, 1024], P('rep', 'fsdp')
- x_grad: bfloat16 [4, 3072, 4096], P('rep', 'fsdp')
- new_weight: bfloat16 [4, 4096, 1024], P('rep', 'fsdp')
- new_first: float32 [4, 4096, 1024], P('rep', 'fsdp')
- new_second: float32 [4, 4096, 1024], P('rep', 'fsdp')
Inputs may be any that keep to these rules, and one draw needn't show every extreme that they name: partner[partner[r]] == r and partner[r] != r for every replica r.
All inputs are finite; a program needn't handle non-finite values.
Results may differ from a plain program's by a relative error of at most 0.018.
Values may be sent and summed in bfloat16 or wider, within the bound.
No kernel may reach another device: no remote copies, remote signals or barrier semaphores. Data moves between devices by JAX's collectives and lax.ppermute only.
A program may use at most 128 MiB of HBM per device.

v0:
```python
import jax
import jax.numpy as jnp
from jax import lax
from jax.sharding import PartitionSpec as P

beta_one = 0.9
beta_two = 0.999
learn_rate = 0.02
weight_decay = 0.1
adam_eps = 1e-08
corr_one = 1.0 - beta_one**10
corr_two = 1.0 - beta_two**10
mix_denom = 64.0


def per_device(
    activations, kv_weight, kv_cotangent, first_moment, second_moment, partner, mix_numerator
):
    tokens_in = activations[0]
    cotangent = kv_cotangent[0]
    weights = kv_weight[0]
    piece = lax.all_gather(weights, "fsdp", axis=0, tiled=True)
    block = tokens_in
    forward = jnp.dot(block, piece, preferred_element_type=jnp.float32)
    partial_back = jnp.einsum("tc,rc->tr", cotangent, piece, preferred_element_type=jnp.float32)
    backward = partial_back
    forward, backward = (forward, backward)
    keys_values = forward.astype(jnp.bfloat16)
    input_grad = backward.astype(jnp.bfloat16)
    block = tokens_in
    gradient = lax.psum_scatter(
        jnp.einsum("td,tc->dc", block, cotangent, preferred_element_type=jnp.float32).astype(
            jnp.bfloat16
        ),
        "fsdp",
        scatter_dimension=0,
        tiled=True,
    ).astype(jnp.float32)
    moment_new_a = beta_one * first_moment[0] + (1.0 - beta_one) * gradient
    moment_new_b = beta_two * second_moment[0] + (1.0 - beta_two) * gradient * gradient
    old_weight = weights.astype(jnp.float32)
    update = (
        moment_new_a / corr_one / (jnp.sqrt(moment_new_b / corr_two) + adam_eps)
        + weight_decay * old_weight
    )
    stepped = (old_weight - learn_rate * update).astype(jnp.bfloat16)
    replica = lax.axis_index("rep")
    partner_index = partner[replica]
    mixing = mix_numerator[replica].astype(jnp.float32) / mix_denom
    piece = lax.all_gather(stepped[None], "rep", axis=0, tiled=True)
    count = piece.shape[0]
    matching = jnp.arange(count, dtype=jnp.int32) == partner_index
    chosen = jnp.sum(jnp.where(matching[:, None, None], piece, jnp.zeros_like(piece)), axis=0)
    averaged = (
        (1.0 - mixing) * stepped.astype(jnp.float32) + mixing * chosen.astype(jnp.float32)
    ).astype(jnp.bfloat16)
    return (
        keys_values[None],
        input_grad[None],
        averaged[None],
        moment_new_a[None],
        moment_new_b[None],
    )


def solution(mesh):
    placed = (
        P("rep", "fsdp", None),
        P("rep", "fsdp", None),
        P("rep", "fsdp", None),
        P("rep", "fsdp", None),
        P("rep", "fsdp", None),
        P(),
        P(),
    )
    return jax.shard_map(
        per_device,
        mesh=mesh,
        in_specs=placed,
        out_specs=(
            P("rep", "fsdp", None),
            P("rep", "fsdp", None),
            P("rep", "fsdp", None),
            P("rep", "fsdp", None),
            P("rep", "fsdp", None),
        ),
        check_vma=False,
    )
```

profile of v0, /device:TPU:0, one launch (start us, length us, event | category | flops | bytes accessed | tf_op | source)
XLA Modules:
  0.0 341.7 jit_solution(4006684624052266470)
XLA Ops:
  7.2 0.0 copy-start
  7.2 0.0 reduce-scatter.2.cloned.1.call-start
  7.2 1.8 copy-done
  9.1 7.8 %convolution_convert_fusion = bf16[4096,1024]{1,0:T(8,128)(2,1)} fusion(bf16[1,384,4096]{2,1,0:T(8,128)(2,1)S(1)} %copy-done, bf16[1,384,1024]{2,1,0:T(8,128)(2,1)} %param.9), kind=kOutput, calls=%fused_computation.4 | convolution fusion | flops 3225419776 | bytes 12320768 | tf_op jit(solution)/shard_map/td,tc->dc/dot_general | solution.py:32
  16.9 0.0 reduce-scatter.2.cloned.1.call-update
  16.9 0.0 all-gather.5.cloned.1.call-start
  17.0 0.7 all-gather.5.cloned.1.call-update
  17.7 0.0 copy-start.3
  17.7 0.0 copy-start.4
  17.7 0.2 all-gather.7.cloned.1.call-start
  17.9 150.9 %reduce-scatter.2.cloned.1.call-done = bf16[512,1024]{1,0:T(8,128)(2,1)} async-done(((bf16[4096,1024]{1,0:T(8,128)(2,1)}), bf16[512,1024]{1,0:T(8,128)(2,1)}) %reduce-scatter.2.cloned.1.call-update) | async-done | bytes 1048592 | tf_op jit(solution)/shard_map/reduce_scatter | solution.py:31
  168.8 7.0 %fusion.28 = (f32[1,512,1024]{2,1,0:T(8,128)}, bf16[512,1024]{1,0:T(8,128)(2,1)}, f32[1,512,1024]{2,1,0:T(8,128)}) fusion(bf16[512,1024]{1,0:T(8,128)(2,1)} %reduce-scatter.2.cloned.1.call-done, f32[1,512,1024]{2,1,0:T(8,128)} %param.11, f32[1,512,1024]{2,1,0:T(8,128)} %param.10, bf16[1,512,1024]{2,1,0:T(8,128)(2,1)} %param.8), kind=kLoop, calls=%fused_computation.23 | loop fusion | flops 9437184 | bytes 11534336 | tf_op jit(solution)/shard_map/broadcast_in_dim | solution.py:62
  175.8 0.0 all-gather.7.cloned.1.call-update
  175.8 0.0 copy-done.3
  175.8 0.6 dynamic_slice.7
  176.4 0.0 copy-done.4
  176.4 0.6 dynamic_slice.6
  177.6 0.7 iota_compare_fusion
  178.3 116.8 %all-gather.5.cloned.1.call-done = bf16[1,4096,1024]{2,1,0:T(8,128)(2,1)} async-done(((bf16[1,512,1024]{2,1,0:T(8,128)(2,1)}), bf16[1,4096,1024]{2,1,0:T(8,128)(2,1)}) %all-gather.5.cloned.1.call-update) | async-done | bytes 8388624 | tf_op jit(solution)/shard_map/all_gather | solution.py:22
  295.1 0.0 copy-start.2
  295.1 8.9 %fusion.7 = bf16[1,384,4096]{2,1,0:T(8,128)(2,1)} fusion(bf16[1,4096,1024]{2,1,0:T(8,128)(2,1)} %all-gather.5.cloned.1.call-done, bf16[1,384,1024]{2,1,0:T(8,128)(2,1)} %param.9), kind=kOutput, calls=%fused_computation.6 | convolution fusion | flops 3222798336 | bytes 12320768 | tf_op jit(solution)/shard_map/tc,rc->tr/dot_general | solution.py:25
  304.0 0.0 copy-done.2
  304.0 4.4 %fusion.22 = bf16[1,384,1024]{2,1,0:T(8,128)(2,1)} fusion(bf16[1,4096,1024]{2,1,0:T(8,128)(2,1)S(1)} %copy-done.2, bf16[1,384,4096]{2,1,0:T(8,128)(2,1)S(1)} %copy-done), kind=kOutput, calls=%fused_computation.21 | convolution fusion | flops 3221618688 | bytes 12320768 | tf_op jit(solution)/shard_map/dot_general | solution.py:24
  308.4 21.7 %all-gather.7.cloned.1.call-done = bf16[2048,1024]{1,0:T(8,128)(2,1)} async-done(((bf16[512,1024]{1,0:T(8,128)(2,1)}), bf16[2048,1024]{1,0:T(8,128)(2,1)}) %all-gather.7.cloned.1.call-update) | async-done | bytes 4194320 | tf_op jit(solution)/shard_map/all_gather | solution.py:50
  330.0 0.0 copy-start.1
  330.0 3.7 %select_reduce_fusion = bf16[512,1024]{1,0:T(8,128)(2,1)S(1)} fusion(bf16[4,512,1024]{2,1,0:T(8,128)(2,1)} %bitcast.55, pred[4]{0:T(512)(128)(4,1)S(1)} %iota_compare_fusion), kind=kLoop, calls=%fused_computation.7 | loop fusion | flops 3670016 | bytes 5242884 | tf_op jit(solution)/shard_map/reduce_sum | solution.py:53
  333.7 0.0 copy-done.1
  333.7 1.4 fusion.29
Async XLA Ops:
  7.2 1.9 copy-start
  7.2 161.6 %reduce-scatter.2.cloned.1.call-start = ((), (), s32[]{:S(2)}) async-start(), calls=%async_computation.1 | async-start | bytes 9437184 | tf_op jit(solution)/shard_map/reduce_scatter | solution.py:31
  16.9 278.2 %all-gather.5.cloned.1.call-start = ((), (), s32[]{:S(2)}) async-start(), calls=%async_computation.2 | async-start | bytes 9437184 | tf_op jit(solution)/shard_map/all_gather | solution.py:22
  17.7 158.1 %copy-start.3 = (s32[4]{0:T(128)S(1)}, s32[4]{0:T(128)}, u32[]{:S(2)}) copy-start(s32[4]{0:T(128)} %param.12) | copy-start | bytes 52
  17.7 158.7 %copy-start.4 = (s32[4]{0:T(128)S(1)}, s32[4]{0:T(128)}, u32[]{:S(2)}) copy-start(s32[4]{0:T(128)} %param.13) | copy-start | bytes 52
  17.7 312.3 %all-gather.7.cloned.1.call-start = ((), (), s32[]{:S(2)}) async-start(), calls=%async_computation.3 | async-start | bytes 5242880 | tf_op jit(solution)/shard_map/all_gather | solution.py:50
  295.1 8.9 %copy-start.2 = (bf16[1,4096,1024]{2,1,0:T(8,128)(2,1)S(1)}, bf16[1,4096,1024]{2,1,0:T(8,128)(2,1)}, u32[]{:S(2)}) copy-start(bf16[1,4096,1024]{2,1,0:T(8,128)(2,1)} %all-gather.5.cloned.1.call-done) | copy-start | bytes 25165828
  330.0 3.7 %copy-start.1 = (bf16[512,1024]{1,0:T(8,128)(2,1)S(1)}, bf16[512,1024]{1,0:T(8,128)(2,1)}, u32[]{:S(2)}) copy-start(bf16[512,1024]{1,0:T(8,128)(2,1)} %get-tuple-element.6) | copy-start | bytes 3145732
Sparse Core Ops, SparseCore 0:
  17.0 151.6 reduce-scatter.1
  171.1 123.9 all-gather.4
  297.3 32.6 all-gather.6
where the time goes:
time: 342 us
  waiting for transfers between devices  290 us (85%)
  matrix products  21.1 us (6%)
  between operations  14.5 us (4%)
  other arithmetic  12.7 us (4%)
    reduce_scatter x1, waiting for transfers between devices, per_device(): lax.psum_scatter(jnp.einsum('td,tc->dc', block, cotangent, preferred_elem...  151 us
    all_gather x1, waiting for transfers between devices, per_device(): piece = lax.all_gather(weights, 'fsdp', axis=0, tiled=True)  117 us
    all_gather x1, waiting for transfers between devices, per_device(): piece = lax.all_gather(stepped[None], 'rep', axis=0, tiled=True)  21.7 us
    dot_general x1, matrix products, per_device(): jnp.einsum('tc,rc->tr', cotangent, piece, preferred_element_type=jnp.floa...  8.88 us
    dot_general x1, matrix products, per_device(): jnp.einsum('td,tc->dc', block, cotangent, preferred_element_type=jnp.floa...  7.83 us
    broadcast_in_dim x1, other arithmetic, per_device(): moment_new_b[None]  6.98 us
  transfers between devices with their start and end apart: 3, of which 3 were waited for; matrix products, arithmetic and copies ran while one was open for 6% of the time, Pallas kernels for 0%

commit v1 on v0

v1 whole, which is shorter than its diff:
```python
import functools

import jax
import jax.numpy as jnp
import numpy as np
from jax import lax
from jax.experimental import pallas as pl
from jax.experimental.pallas import tpu as pltpu
from jax.sharding import PartitionSpec as P

beta_one = 0.9
beta_two = 0.999
learn_rate = 0.02
weight_decay = 0.1
adam_eps = 1e-08
corr_one = 1.0 - beta_one**10
corr_two = 1.0 - beta_two**10
mix_denom = 64.0

CHUNKS = 2
MIB = 1 << 20
ANY = pl.BlockSpec(memory_space=pl.ANY)

TN = (((0,), (0,)), ((), ()))
NT = (((1,), (1,)), ((), ()))


def dot(a, b, dims=(((1,), (0,)), ((), ()))):
    return lax.dot_general(a, b, dims, preferred_element_type=jnp.float32)


class Plan:
    def __init__(self, n):
        self.depth = depth = n // 2
        self.columns = {}
        self.rows = [[] for _ in range(n)]
        order = [
            sorted(range(depth), key=lambda q: (-abs(q - z), (q < z) != (2 * z >= depth)))
            for z in range(depth)
        ]
        self.sources = [set() for _ in range(depth)]
        arrivals = []
        for z in range(depth):
            ups = [(z - t, ("up", t)) for t in range(1, z + 1)]
            downs = [(z + t, ("dn", t)) for t in range(1, depth - z)]
            arrivals.append(downs + ups if 2 * z < depth else ups + downs)
            for j, (_, source) in enumerate(arrivals[z], 1):
                self.sources[j].add(source)
        self.sources = [sorted(s) for s in self.sources]
        for i in range(n):
            z, x = divmod(i, 2)
            put = functools.partial(self._put, i)
            put("own", i)
            for k in range(depth):
                put(f"pack{k}", 2 * order[z][k] + 1 - x)
            for s in range(2, depth + 1):
                for way, q in (("up", z + 1 + depth - s), ("dn", z - 1 - depth + s)):
                    add = 0 <= q < depth
                    put(f"add_{way}{s}", int(add))
                    put(f"blk_{way}{s}", 2 * q + x if add else 0)
                    put(f"pos_{way}{s}", order[z].index(q) if add else 0)
            for j in range(depth):
                q, source = (z, None) if j == 0 else arrivals[z][j - 1]
                put(f"mine{j}", 2 * q + x)
                put(f"theirs{j}", 2 * q + 1 - x)
                put(f"piece{j}", order[z].index(q))
                put(f"source{j}", 0 if j == 0 else self.sources[j].index(source))
        self.table = np.asarray(self.rows, np.int32)

    def _put(self, i, name, value):
        column = self.columns.setdefault(name, len(self.columns))
        assert column == len(self.rows[i])
        self.rows[i].append(value)

    def __getitem__(self, name):
        return self.columns[name]


def call(kernel, row, ins, outs, grid=(1,), aliases=None, scratch=(), flops=0, moved=0, vmem=24):
    return pl.pallas_call(
        kernel,
        grid_spec=pltpu.PrefetchScalarGridSpec(
            num_scalar_prefetch=1,
            grid=grid,
            in_specs=[spec for _, spec in ins],
            out_specs=[spec for _, spec in outs],
            scratch_shapes=list(scratch),
        ),
        out_shape=[shape for shape, _ in outs],
        input_output_aliases=aliases or {},
        compiler_params=pltpu.CompilerParams(vmem_limit_bytes=vmem * MIB),
        cost_estimate=pl.CostEstimate(flops=flops, bytes_accessed=moved, transcendentals=0),
    )(row, *[array for array, _ in ins])


def whole(array):
    rank = array.ndim
    return pl.BlockSpec(array.shape, lambda g, row: (0,) * rank)


def block(shape, column, scale=1, offset=0):
    return pl.BlockSpec(shape, lambda g, row: (0, row[column] * scale + offset))


def struct(shape, dtype):
    return jax.ShapeDtypeStruct(shape, dtype)


def pack(plan, row, act, width, k, after):
    def kernel(row_ref, act_ref, *refs):
        refs[-1][...] = act_ref[...]

    tokens = act.shape[0]
    return call(
        kernel,
        row,
        [(act, block((tokens, width), plan[f"pack{k}"]))] + [(a, ANY) for a in after],
        [(struct((tokens, width), act.dtype), pl.BlockSpec((tokens, width), lambda g, row: (0, 0)))],
        moved=4 * tokens * width,
    )[0]


def relay(plan, row, s, h, got, act, pieces, cot_own, cot_oth):
    tokens, columns = cot_own.shape
    rows = got["up"].shape[0]
    count = len(pieces)
    ways = ("up", "dn")

    def kernel(row_ref, *refs):
        got_refs, act_refs = refs[0:2], refs[2:4]
        piece_refs = refs[4 : 4 + count]
        own_ref, oth_ref = refs[4 + count : 6 + count]
        out_refs = refs[6 + count : 8 + count]
        held = refs[8 + count]
        for d, way in enumerate(ways):
            add = row_ref[plan[f"add_{way}{s}"]]
            pos = row_ref[plan[f"pos_{way}{s}"]]

            @pl.when(add == 0)
            def _():
                out_refs[d][...] = got_refs[d][...]

            @pl.when(add == 1)
            def _():
                for j in range(count):

                    @pl.when(pos == j)
                    def _():
                        held[...] = piece_refs[j][...]

                total = dot(act_refs[d][...], own_ref[...], TN)
                total = total + dot(held[...], oth_ref[...], TN)
                out_refs[d][...] = (total + got_refs[d][...].astype(jnp.float32)).astype(jnp.bfloat16)

    ins = [(got[way], whole(got[way])) for way in ways]
    ins += [
        (act, block((tokens, rows), plan[f"blk_{way}{s}"], CHUNKS, h)) for way in ways
    ]
    ins += [(p, pl.BlockSpec((tokens, rows), lambda g, row: (0, h))) for p in pieces]
    ins += [(cot_own, whole(cot_own)), (cot_oth, whole(cot_oth))]
    out = struct((rows, columns), jnp.bfloat16)
    up, dn = call(
        kernel,
        row,
        ins,
        [(out, whole(out)), (out, whole(out))],
        scratch=[pltpu.VMEM((tokens, rows), jnp.bfloat16)],
        flops=8 * tokens * rows * columns,
        moved=8 * rows * columns + 4 * tokens * columns,
    )
    return {"up": up, "dn": dn}


def own_gradient(plan, row, act, piece, cot_own, cot_oth):
    tokens, columns = cot_own.shape
    rows = piece.shape[1]

    def kernel(row_ref, act_ref, piece_ref, own_ref, oth_ref, out_ref):
        total = dot(act_ref[...], own_ref[...], TN)
        out_ref[...] = total + dot(piece_ref[...], oth_ref[...], TN)

    out = struct((rows, columns), jnp.float32)
    return call(
        kernel,
        row,
        [
            (act, block((tokens, rows), plan["own"])),
            (piece, whole(piece)),
            (cot_own, whole(cot_own)),
            (cot_oth, whole(cot_oth)),
        ],
        [(out, whole(out))],
        flops=4 * tokens * rows * columns,
        moved=4 * rows * columns + 4 * tokens * columns,
    )[0]


def project(plan, row, j, candidates, act, pieces, cot_own, cot_oth, kept):
    tokens, columns = cot_own.shape
    rows = pieces[0].shape[1]
    parts = len(candidates[0])
    last = j == plan.depth - 1
    flat = [c for candidate in candidates for c in candidate]
    n_w, n_p = len(flat), len(pieces)

    def kernel(row_ref, *refs):
        w_refs = refs[:n_w]
        piece_refs = refs[n_w : n_w + n_p]
        act_ref, own_ref, oth_ref = refs[n_w + n_p : n_w + n_p + 3]
        rest = refs[n_w + n_p + 3 :]
        if j > 0:
            _, kv_own_in, kv_oth_in = rest[:3]
            rest = rest[3:]
        xg_own, xg_oth, kv_own, kv_oth, w_buf, p_buf, sems = rest
        size = rows // parts
        for c in range(len(candidates)):

            @pl.when(row_ref[plan[f"source{j}"]] == c)
            def _():
                copies = [
                    pltpu.make_async_copy(
                        w_refs[c * parts + p], w_buf.at[pl.ds(p * size, size)], sems.at[p]
                    )
                    for p in range(parts)
                ]
                for copy in copies:
                    copy.start()
                for copy in copies:
                    copy.wait()

        for p in range(n_p):

            @pl.when(row_ref[plan[f"piece{j}"]] == p)
            def _():
                copy = pltpu.make_async_copy(piece_refs[p], p_buf, sems.at[parts])
                copy.start()
                copy.wait()

        xg_oth[...] = dot(oth_ref[...], w_buf[...], NT).astype(jnp.bfloat16)
        xg_own[...] = dot(own_ref[...], w_buf[...], NT).astype(jnp.bfloat16)
        oth = dot(p_buf[...], w_buf[...])
        own = dot(act_ref[...], w_buf[...])
        if j > 0:
            oth = oth + kv_oth_in[...]
            own = own + kv_own_in[...]
        kv_oth[...] = oth.astype(kv_oth.dtype)
        kv_own[...] = own

    ins = [(w, ANY) for w in flat] + [(p, ANY) for p in pieces]
    ins += [
        (act, block((tokens, rows), plan[f"mine{j}"])),
        (cot_own, whole(cot_own)),
        (cot_oth, whole(cot_oth)),
    ]
    xg = struct(act.shape, jnp.bfloat16)
    aliases = {}
    if j > 0:
        xg_before, kv_own_before, kv_oth_before = kept
        first = 1 + len(ins)
        ins += [(xg_before, ANY), (kv_own_before, whole(kv_own_before)), (kv_oth_before, whole(kv_oth_before))]
        aliases = {first: 0, first + 1: 2}
    kv_own = struct((tokens, columns), jnp.float32)
    kv_oth = struct((tokens, columns), jnp.bfloat16 if last else jnp.float32)
    piece_out = struct((tokens, rows), jnp.bfloat16)
    return call(
        kernel,
        row,
        ins,
        [
            (xg, block((tokens, rows), plan[f"mine{j}"])),
            (piece_out, whole(piece_out)),
            (kv_own, whole(kv_own)),
            (kv_oth, whole(kv_oth)),
        ],
        aliases=aliases,
        scratch=[
            pltpu.VMEM((rows, columns), jnp.bfloat16),
            pltpu.VMEM((tokens, rows), jnp.bfloat16),
            pltpu.SemaphoreType.DMA((parts + 1,)),
        ],
        flops=8 * tokens * rows * columns,
        moved=20 * tokens * columns,
        vmem=32,
    )


def place(plan, row, xg, arrived):
    count = len(arrived)
    tokens, width = arrived[0].shape

    def kernel(row_ref, _, *refs):
        out_ref, sems = refs[count:]
        copies = []
        for j in range(count):
            start = pl.multiple_of(row_ref[plan[f"theirs{j}"]] * width, width)
            copies.append(
                pltpu.make_async_copy(refs[j], out_ref.at[:, pl.ds(start, width)], sems.at[j])
            )
        for copy in copies:
            copy.start()
        for copy in copies:
            copy.wait()

    return call(
        kernel,
        row,
        [(xg, ANY)] + [(a, ANY) for a in arrived],
        [(struct(xg.shape, xg.dtype), ANY)],
        aliases={1: 0},
        scratch=[pltpu.SemaphoreType.DMA((count,))],
        moved=4 * count * tokens * width,
    )[0]


def adam(row, h, got, grad, weights, first, second, kept):
    rows, columns = got["up"].shape
    steps = 4 if rows % 64 == 0 else 1
    size = rows // steps

    def kernel(row_ref, up_ref, dn_ref, grad_ref, w_ref, a_ref, b_ref, *refs):
        a_out, b_out, stepped = refs[-3:]
        gradient = grad_ref[...] + up_ref[...].astype(jnp.float32) + dn_ref[...].astype(jnp.float32)
        moment_a = beta_one * a_ref[...] + (1.0 - beta_one) * gradient
        moment_b = beta_two * b_ref[...] + (1.0 - beta_two) * gradient * gradient
        old = w_ref[...].astype(jnp.float32)
        update = moment_a / corr_one / (jnp.sqrt(moment_b / corr_two) + adam_eps) + weight_decay * old
        a_out[...] = moment_a
        b_out[...] = moment_b
        stepped[...] = (old - learn_rate * update).astype(jnp.bfloat16)

    local = pl.BlockSpec((size, columns), lambda g, row: (g, 0))
    part = pl.BlockSpec((size, columns), lambda g, row: (g + h * steps, 0))
    ins = [(got["up"], local), (got["dn"], local)]
    ins += [(a, part) for a in (grad, weights, first, second)]
    aliases = {}
    if kept is not None:
        aliases = {1 + len(ins): 0, 2 + len(ins): 1}
        ins += [(a, ANY) for a in kept]
    return call(
        kernel,
        row,
        ins,
        [
            (struct(first.shape, jnp.float32), part),
            (struct(second.shape, jnp.float32), part),
            (struct((rows, columns), jnp.bfloat16), local),
        ],
        grid=(steps,),
        aliases=aliases,
        flops=16 * rows * columns,
        moved=28 * rows * columns,
    )


def average(mixing, h, stepped, chosen, kept, height):
    rows, columns = stepped.shape
    steps = 2 if rows % 32 == 0 else 1
    size = rows // steps

    def kernel(mix_ref, stepped_ref, chosen_ref, *refs):
        mix = mix_ref[0].astype(jnp.float32) / mix_denom
        refs[-1][...] = (
            (1.0 - mix) * stepped_ref[...].astype(jnp.float32)
            + mix * chosen_ref[...].astype(jnp.float32)
        ).astype(jnp.bfloat16)

    local = pl.BlockSpec((size, columns), lambda g, row: (g, 0))
    part = pl.BlockSpec((size, columns), lambda g, row: (g + h * steps, 0))
    ins = [(stepped, local), (chosen, local)]
    if kept is not None:
        ins.append((kept, ANY))
    return call(
        kernel,
        mixing,
        ins,
        [(struct((height, columns), jnp.bfloat16), part)],
        grid=(steps,),
        aliases={} if kept is None else {3: 0},
        moved=6 * rows * columns,
    )[0]


def partner_rows(stepped, partner, replica, n_rep):
    if n_rep != 4:
        gathered = lax.all_gather(stepped, "rep", axis=0, tiled=False)
        return lax.dynamic_index_in_dim(gathered, partner[replica], 0, keepdims=False)
    mask = partner[0]
    near = lax.ppermute(stepped, "rep", [(r, r ^ 1) for r in range(4)])
    far = lax.ppermute(
        jnp.where(mask == 3, near, stepped), "rep", [(r, r ^ 2) for r in range(4)]
    )
    return jnp.where(mask == 1, near, far)


def per_device(
    n_rep, n, activations, kv_weight, kv_cotangent, first_moment, second_moment, partner, mix_numerator
):
    act, weights, cot = activations[0], kv_weight[0], kv_cotangent[0]
    first, second = first_moment[0], second_moment[0]
    plan = Plan(n)
    depth = plan.depth
    rows = weights.shape[0]
    size = rows // CHUNKS
    row = lax.dynamic_index_in_dim(
        jnp.asarray(plan.table), lax.axis_index("fsdp"), 0, keepdims=False
    )
    climb = [(i, i + 2) for i in range(n - 2)]
    ways = {"up": climb, "dn": [(b, a) for a, b in climb]}
    swap = functools.partial(lax.ppermute, axis_name="fsdp", perm=[(i, i ^ 1) for i in range(n)])

    def shift(bufs):
        return {way: lax.ppermute(bufs[way], "fsdp", ways[way]) for way in ways}

    got = {}
    for h in range(CHUNKS):
        part = weights[h * size : (h + 1) * size]
        got[1, h] = shift({"up": part, "dn": part})

    cot_oth = swap(cot)
    pieces = []
    for k in range(depth):
        after = [cot_oth] if k == 1 else [pieces[k - 2]] if k > 1 else []
        pieces.append(swap(pack(plan, row, act, rows, k, after)))

    for s in range(2, depth + 1):
        for h in range(CHUNKS):
            bufs = relay(plan, row, s, h, got[s - 1, h], act, pieces[: s - 1], cot, cot_oth)
            got[s, h] = shift(bufs)

    kept = None
    arrived = []
    for j in range(depth):
        if j == 0:
            candidates = [[weights]]
        else:
            candidates = [
                [got[slot, h][way] for h in range(CHUNKS)] for way, slot in plan.sources[j]
            ]
        xg, xg_oth, kv_own, kv_oth = project(
            plan, row, j, candidates, act, pieces, cot, cot_oth, kept
        )
        kept = (xg, kv_own, kv_oth)
        arrived.append(swap(xg_oth))
    kv_out = (kept[1] + swap(kept[2]).astype(jnp.float32)).astype(jnp.bfloat16)
    x_grad = place(plan, row, kept[0], arrived)

    grad = own_gradient(plan, row, act, pieces[depth - 1], cot, cot_oth)
    replica = lax.axis_index("rep")
    mixing = lax.dynamic_slice(mix_numerator, (replica,), (1,))
    moments, averaged = None, None
    for h in range(CHUNKS):
        new_a, new_b, stepped = adam(row, h, got[depth, h], grad, weights, first, second, moments)
        moments = (new_a, new_b)
        chosen = partner_rows(stepped, partner, replica, n_rep)
        averaged = average(mixing, h, stepped, chosen, averaged, rows)
    return (
        kv_out[None],
        x_grad[None],
        averaged[None],
        moments[0][None],
        moments[1][None],
    )


def solution(mesh):
    placed = P("rep", "fsdp", None)
    return jax.shard_map(
        functools.partial(per_device, mesh.shape["rep"], mesh.shape["fsdp"]),
        mesh=mesh,
        in_specs=(placed,) * 5 + (P(), P()),
        out_specs=(placed,) * 5,
        check_vma=False,
    )
```

time: 342 us -> 185 us (0.54)
  waiting for transfers between devices: 290 us -> 55.3 us
  starting transfers between devices: 0.3 us -> 61.2 us
  Pallas kernels: 0 us -> 58.6 us
  matrix products: 21.1 us -> 0 us
  between operations: 14.5 us -> 1.12 us
  other arithmetic: 12.7 us -> 4.61 us
    reduce_scatter x1 -> x0, waiting for transfers between devices: 151 us -> none  [per_device(): lax.psum_scatter(jnp.einsum('td,tc->dc', block, cotangent, preferred_elem...]
    all_gather x2 -> x0, waiting for transfers between devices: 138 us -> none  [the longest x1 117 us: per_device(): piece = lax.all_gather(weights, 'fsdp', axis=0, tiled=True)]
    ppermute x0 -> x30, starting transfers between devices: none -> 61.2 us  [the longest x16 45.1 us: shift(): return {way: lax.ppermute(bufs[way], 'fsdp', ways[way]) for way in ways}]
    pallas_call x0 -> x20, Pallas kernels: none -> 58.6 us  [call(): pl.pallas_call(kernel, grid_spec=pltpu.PrefetchScalarGridSpec(num_scalar_...]
    ppermute x0 -> x30, waiting for transfers between devices: none -> 55.3 us  [the longest x2 17.4 us: partner_rows(): lax.ppermute(jnp.where(mask == 3, near, stepped), 'rep', [(r, r ^ 2) for...]
    dot_general x3 -> x0, matrix products: 21.1 us -> none  [the longest x1 8.88 us: per_device(): jnp.einsum('tc,rc->tr', cotangent, piece, preferred_element_type=jnp.floa...]
    broadcast_in_dim x2 -> x1, other arithmetic: 8.41 us -> 2.27 us  [per_device(): kv_out[None]]
    reduce_sum x1 -> x0, other arithmetic: 3.67 us -> none  [per_device(): jnp.sum(jnp.where(matching[:, None, None], piece, jnp.zeros_like(piece)),...]
  transfers between devices with their start and end apart: 3 -> 30, of which waited for: 3 -> 12; matrix products, arithmetic and copies ran while one was open for 6% -> 2% of each run, Pallas kernels for 0% -> 31%
where the time goes in v1:
time: 185 us; the launch traced here: 184 us
  starting transfers between devices  61.2 us (33%)
  Pallas kernels  58.6 us (32%)
  waiting for transfers between devices  55.3 us (30%)
  other arithmetic  4.61 us (2%)
  local copies, waits for them, and re-layouts  3.65 us (2%)
    pallas_call x20, Pallas kernels, call(): pl.pallas_call(kernel, grid_spec=pltpu.PrefetchScalarGridSpec(num_scalar_...  58.6 us
    ppermute x16, starting transfers between devices, shift(): return {way: lax.ppermute(bufs[way], 'fsdp', ways[way]) for way in ways}  45.1 us
    ppermute x2, waiting for transfers between devices, partner_rows(): lax.ppermute(jnp.where(mask == 3, near, stepped), 'rep', [(r, r ^ 2) for...  17.4 us
    ppermute x16, waiting for transfers between devices, shift(): return {way: lax.ppermute(bufs[way], 'fsdp', ways[way]) for way in ways}  13.8 us
    ppermute x4, waiting for transfers between devices, per_device(): arrived.append(swap(xg_oth))  13.7 us
    ppermute x4, starting transfers between devices, per_device(): pieces.append(swap(pack(plan, row, act, rows, k, after)))  7.61 us
    ppermute x1, waiting for transfers between devices, per_device(): cot_oth = swap(cot)  7.18 us
    ppermute x4, starting transfers between devices, per_device(): arrived.append(swap(xg_oth))  4.27 us
  transfers between devices with their start and end apart: 30, of which 12 were waited for; matrix products, arithmetic and copies ran while one was open for 2% of the time, Pallas kernels for 31%

profile of v1, /device:TPU:0, one launch (start us, length us, event | category | flops | bytes accessed | tf_op | source)
XLA Modules:
  0.0 184.4 jit_solution(4383897848613171538)
XLA Ops:
  1.3 1.9 %copy-done = bf16[1,384,4096]{2,1,0:T(8,128)(2,1)S(1)} copy-done((bf16[1,384,4096]{2,1,0:T(8,128)(2,1)S(1)}, bf16[1,384,4096]{2,1,0:T(8,128)(2,1)}, u32[]{:S(2)}) %copy-start) | copy-done | bytes 3145752
  3.8 3.0 %collective-permute-start.3 = (bf16[384,512]{1,0:T(8,128)(2,1)S(1)}, bf16[384,512]{1,0:T(8,128)(2,1)S(1)}, u32[]{:S(2)}, u32[]{:S(2)}) collective-permute-start(bf16[384,512]{1,0:T(8,128)(2,1)S(1)} %shard_map.119), channel_id=1, source_target_pairs={{0,1},{1,0},{2,3},{3,2},{4,5},{5,4},{6,7},{7,6},{8,9},{9,8},{10,11... | collective-permute-start | bytes 1179656 | tf_op jit(solution)/shard_map/ppermute | solution.py:423
  8.7 4.6 %collective-permute-start.2 = (bf16[256,1024]{1,0:T(8,128)(2,1)S(1)}, bf16[256,1024]{1,0:T(8,128)(2,1)S(1)}, u32[]{:S(2)}, u32[]{:S(2)}) collective-permute-start(bf16[256,1024]{1,0:T(8,128)(2,1)S(1)} %get-tuple-element.74), channel_id=1, source_target_pairs={{0,2},{1,3},{2,4},{3,5},{4,6},{5,7},{8,10},{9,11},{10,12},{11,13},... | collective-permute-start | bytes 1572872 | tf_op jit(solution)/shard_map/ppermute | solution.py:412
  14.6 2.2 %collective-permute-done.3.refs_4_.refs_0_.refs_1_.refs_8_ = bf16[384,512]{1,0:T(8,128)(2,1)S(1)} collective-permute-done((bf16[384,512]{1,0:T(8,128)(2,1)S(1)}, bf16[384,512]{1,0:T(8,128)(2,1)S(1)}, u32[]{:S(2)}, u32[]{:S(2)}) %collective-permute-start.3) | collective-permute-done | bytes 393248 | tf_op jit(solution)/shard_map/ppermute | solution.py:423
  16.8 4.1 %collective-permute-start.9 = (bf16[256,1024]{1,0:T(8,128)(2,1)S(1)}, bf16[256,1024]{1,0:T(8,128)(2,1)S(1)}, u32[]{:S(2)}, u32[]{:S(2)}) collective-permute-start(bf16[256,1024]{1,0:T(8,128)(2,1)S(1)} %get-tuple-element.73), channel_id=1, source_target_pairs={{0,2},{1,3},{2,4},{3,5},{4,6},{5,7},{8,10},{9,11},{10,12},{11,13},... | collective-permute-start | bytes 1572872 | tf_op jit(solution)/shard_map/ppermute | solution.py:412
  20.8 3.3 %collective-permute-done.refs_1_.refs_0_ = bf16[256,1024]{1,0:T(8,128)(2,1)S(1)} collective-permute-done((bf16[256,1024]{1,0:T(8,128)(2,1)S(1)}, bf16[256,1024]{1,0:T(8,128)(2,1)S(1)}, u32[]{:S(2)}, u32[]{:S(2)}) %collective-permute-start) | collective-permute-done | bytes 524320 | tf_op jit(solution)/shard_map/ppermute | solution.py:412
  25.6 7.2 %collective-permute-done.4.refs_6_.refs_0_.refs_7_.refs_10_.refs_14_.refs_8_.oth_ref = bf16[384,1024]{1,0:T(8,128)(2,1)S(1)} collective-permute-done((bf16[384,1024]{1,0:T(8,128)(2,1)S(1)}, bf16[384,1024]{1,0:T(8,128)(2,1)S(1)}, u32[]{:S(2)}, u32[]{:S(2)}) %collective-permute-start.4) | collective-permute-done | bytes 786464 | tf_op jit(solution)/shard_map/ppermute | solution.py:419
  34.2 3.0 %collective-permute-start.5 = (bf16[256,1024]{1,0:T(8,128)(2,1)S(1)}, bf16[256,1024]{1,0:T(8,128)(2,1)S(1)}, u32[]{:S(2)}, u32[]{:S(2)}) collective-permute-start(bf16[256,1024]{1,0:T(8,128)(2,1)S(1)} %get-tuple-element.39), channel_id=1, source_target_pairs={{0,2},{1,3},{2,4},{3,5},{4,6},{5,7},{8,10},{9,11},{10,12},{11,13},... | collective-permute-start | bytes 1572872 | tf_op jit(solution)/shard_map/ppermute | solution.py:412
  42.1 3.9 %collective-permute-start.10 = (bf16[256,1024]{1,0:T(8,128)(2,1)S(1)}, bf16[256,1024]{1,0:T(8,128)(2,1)S(1)}, u32[]{:S(2)}, u32[]{:S(2)}) collective-permute-start(bf16[256,1024]{1,0:T(8,128)(2,1)S(1)} %get-tuple-element.42), channel_id=1, source_target_pairs={{0,2},{1,3},{2,4},{3,5},{4,6},{5,7},{8,10},{9,11},{10,12},{11,13},... | collective-permute-start | bytes 1572872 | tf_op jit(solution)/shard_map/ppermute | solution.py:412
  50.4 3.6 %collective-permute-done.6.refs_1_.refs_0_ = bf16[256,1024]{1,0:T(8,128)(2,1)S(1)} collective-permute-done((bf16[256,1024]{1,0:T(8,128)(2,1)S(1)}, bf16[256,1024]{1,0:T(8,128)(2,1)S(1)}, u32[]{:S(2)}, u32[]{:S(2)}) %collective-permute-start.6) | collective-permute-done | bytes 524320 | tf_op jit(solution)/shard_map/ppermute | solution.py:412
  56.7 4.6 %collective-permute-start.13 = (bf16[256,1024]{1,0:T(8,128)(2,1)S(1)}, bf16[256,1024]{1,0:T(8,128)(2,1)S(1)}, u32[]{:S(2)}, u32[]{:S(2)}) collective-permute-start(bf16[256,1024]{1,0:T(8,128)(2,1)S(1)} %get-tuple-element.45), channel_id=1, source_target_pairs={{0,2},{1,3},{2,4},{3,5},{4,6},{5,7},{8,10},{9,11},{10,12},{11,13},... | collective-permute-start | bytes 1572872 | tf_op jit(solution)/shard_map/ppermute | solution.py:412
  61.9 1.6 collective-permute-start.16
  63.4 1.8 collective-permute-done.11.refs_1_
  68.0 4.8 %collective-permute-start.14 = (bf16[256,1024]{1,0:T(8,128)(2,1)S(1)}, bf16[256,1024]{1,0:T(8,128)(2,1)S(1)}, u32[]{:S(2)}, u32[]{:S(2)}) collective-permute-start(bf16[256,1024]{1,0:T(8,128)(2,1)S(1)} %get-tuple-element.46), channel_id=1, source_target_pairs={{0,2},{1,3},{2,4},{3,5},{4,6},{5,7},{8,10},{9,11},{10,12},{11,13},... | collective-permute-start | bytes 1572872 | tf_op jit(solution)/shard_map/ppermute | solution.py:412
  72.8 3.6 %collective-permute-done.8.refs_2_.refs_1_ = bf16[256,1024]{1,0:T(8,128)(2,1)S(1)} collective-permute-done((bf16[256,1024]{1,0:T(8,128)(2,1)S(1)}, bf16[256,1024]{1,0:T(8,128)(2,1)S(1)}, u32[]{:S(2)}, u32[]{:S(2)}) %collective-permute-start.8) | collective-permute-done | bytes 524320 | tf_op jit(solution)/shard_map/ppermute | solution.py:412
  77.9 4.5 %collective-permute-start.24 = (bf16[256,1024]{1,0:T(8,128)(2,1)S(1)}, bf16[256,1024]{1,0:T(8,128)(2,1)S(1)}, u32[]{:S(2)}, u32[]{:S(2)}) collective-permute-start(bf16[256,1024]{1,0:T(8,128)(2,1)S(1)} %get-tuple-element.65), channel_id=1, source_target_pairs={{0,2},{1,3},{2,4},{3,5},{4,6},{5,7},{8,10},{9,11},{10,12},{11,13},... | collective-permute-start | bytes 1572872 | tf_op jit(solution)/shard_map/ppermute | solution.py:412
  83.7 2.7 %shard_map.127 = (bf16[384,4096]{1,0:T(8,128)(2,1)}, bf16[384,512]{1,0:T(8,128)(2,1)S(1)}, f32[384,1024]{1,0:T(8,128)S(1)}, f32[384,1024]{1,0:T(8,128)S(1)}) custom-call(s32[39]{0:T(128)S(1)} %dynamic-slice_bitcast_fusion.row_ref, bf16[512,1024]{1,0:T(8,128)(2,1)S(1)} %bitcast.53, ...), custom_call_target="tpu_custom_call" | custom-call | flops 1610612736 | bytes 7864320 | tf_op jit(solution)/shard_map/pallas_call | solution.py:80
  86.4 1.6 collective-permute-start.18
  89.5 5.3 %collective-permute-start.22 = (bf16[256,1024]{1,0:T(8,128)(2,1)S(1)}, bf16[256,1024]{1,0:T(8,128)(2,1)S(1)}, u32[]{:S(2)}, u32[]{:S(2)}) collective-permute-start(bf16[256,1024]{1,0:T(8,128)(2,1)S(1)} %get-tuple-element.63), channel_id=1, source_target_pairs={{0,2},{1,3},{2,4},{3,5},{4,6},{5,7},{8,10},{9,11},{10,12},{11,13},... | collective-permute-start | bytes 1572872 | tf_op jit(solution)/shard_map/ppermute | solution.py:412
  96.1 3.3 %shard_map.128 = (bf16[384,4096]{1,0:T(8,128)(2,1)}, bf16[384,512]{1,0:T(8,128)(2,1)S(1)}, f32[384,1024]{1,0:T(8,128)S(1)}, f32[384,1024]{1,0:T(8,128)S(1)}) custom-call(s32[39]{0:T(128)S(1)} %dynamic-slice_bitcast_fusion.row_ref, bf16[256,1024]{1,0:T(8,128)(2,1)S(1)} %collective-permute-done.refs_1_.refs_0_, ...), custom_call_target="tpu_custom_call", output_to_operand_aliasing={{0}: (12, {}), {2}: (13, {})} | custom-call | flops 1610612736 | bytes 7864320 | tf_op jit(solution)/shard_map/pallas_call | solution.py:80
  100.0 2.8 %shard_map.129 = (bf16[384,4096]{1,0:T(8,128)(2,1)}, bf16[384,512]{1,0:T(8,128)(2,1)}, f32[384,1024]{1,0:T(8,128)S(1)}, f32[384,1024]{1,0:T(8,128)S(1)}) custom-call(s32[39]{0:T(128)S(1)} %dynamic-slice_bitcast_fusion.row_ref, bf16[256,1024]{1,0:T(8,128)(2,1)S(1)} %collective-permute-done.6.refs_1_.refs_0_, ...), custom_call_target="tpu_custom_call", output_to_operand_aliasing={{0}: (12, {}), {2}: (13, {})} | custom-call | flops 1610612736 | bytes 7864320 | tf_op jit(solution)/shard_map/pallas_call | solution.py:80
  102.8 1.8 shard_map.133.grad_ref
  105.0 2.7 %shard_map.135 = (f32[512,1024]{1,0:T(8,128)}, f32[512,1024]{1,0:T(8,128)}, bf16[256,1024]{1,0:T(8,128)(2,1)S(1)}) custom-call(s32[39]{0:T(128)S(1)} %dynamic-slice_bitcast_fusion.row_ref, bf16[256,1024]{1,0:T(8,128)(2,1)S(1)} %collective-permute-done.24.up_ref, bf16[256,1024]{1,0:T(8,128)(2,1)S(1)} %collective-permute-done.25.dn_ref, ...), custom_call_target="tpu_custom_call" | custom-call | flops 4194304 | bytes 7340032 | tf_op jit(solution)/shard_map/pallas_call | solution.py:80
  107.7 3.3 %shard_map.130 = (bf16[384,4096]{1,0:T(8,128)(2,1)}, bf16[384,512]{1,0:T(8,128)(2,1)}, f32[384,1024]{1,0:T(8,128)S(1)}, bf16[384,1024]{1,0:T(8,128)(2,1)}) custom-call(s32[39]{0:T(128)S(1)} %dynamic-slice_bitcast_fusion.row_ref, bf16[256,1024]{1,0:T(8,128)(2,1)S(1)} %collective-permute-done.refs_1_.refs_0_, ...), custom_call_target="tpu_custom_call", output_to_operand_aliasing={{0}: (16, {}), {2}: (17, {})} | custom-call | flops 1610612736 | bytes 7864320 | tf_op jit(solution)/shard_map/pallas_call | solution.py:80
  113.1 2.7 %shard_map.136 = (f32[512,1024]{1,0:T(8,128)}, f32[512,1024]{1,0:T(8,128)}, bf16[256,1024]{1,0:T(8,128)(2,1)S(1)}) custom-call(s32[39]{0:T(128)S(1)} %dynamic-slice_bitcast_fusion.row_ref, bf16[256,1024]{1,0:T(8,128)(2,1)S(1)} %collective-permute-done.22.up_ref, ...), custom_call_target="tpu_custom_call", output_to_operand_aliasing={{0}: (7, {}), {1}: (8, {})} | custom-call | flops 4194304 | bytes 7340032 | tf_op jit(solution)/shard_map/pallas_call | solution.py:80
  118.0 5.3 %collective-permute-done.20.refs_2_ = bf16[384,512]{1,0:T(8,128)(2,1)} collective-permute-done((bf16[384,512]{1,0:T(8,128)(2,1)}, bf16[384,512]{1,0:T(8,128)(2,1)}, u32[]{:S(2)}, u32[]{:S(2)}) %collective-permute-start.20) | collective-permute-done | bytes 393248 | tf_op jit(solution)/shard_map/ppermute | solution.py:443
  123.3 8.4 %collective-permute-done.21.refs_3_ = bf16[384,512]{1,0:T(8,128)(2,1)} collective-permute-done((bf16[384,512]{1,0:T(8,128)(2,1)}, bf16[384,512]{1,0:T(8,128)(2,1)}, u32[]{:S(2)}, u32[]{:S(2)}) %collective-permute-start.21) | collective-permute-done | bytes 393248 | tf_op jit(solution)/shard_map/ppermute | solution.py:443
  131.7 25.5 %shard_map.131 = bf16[384,4096]{1,0:T(8,128)(2,1)} custom-call(s32[39]{0:T(128)S(1)} %dynamic-slice_bitcast_fusion.row_ref, bf16[384,4096]{1,0:T(8,128)(2,1)} %get-tuple-element.58._, bf16[384,512]{1,0:T(8,128)(2,1)S(1)} %collective-permute-done.18.refs_0_, bf16[384,512]{1,0:T(8,128)(2,1)S(1)} %collective-permute-done.19.refs_1_, ...), custom_call_target="tpu_custom_call", output_to_operand_aliasing={{}: (1, {})} | custom-call | bytes 3145728 | tf_op jit(solution)/shard_map/pallas_call | solution.py:80
  157.3 1.6 collective-permute-start.29
  159.6 2.3 %fusion = bf16[1,384,1024]{2,1,0:T(8,128)(2,1)} fusion(f32[384,1024]{1,0:T(8,128)S(1)} %get-tuple-element.56, bf16[384,1024]{1,0:T(8,128)(2,1)} %collective-permute-done.17), kind=kLoop, calls=%fused_computation.1 | loop fusion | flops 1179648 | bytes 3145728 | tf_op jit(solution)/shard_map/broadcast_in_dim | solution.py:457
  161.8 10.4 %collective-permute-done.29 = bf16[256,1024]{1,0:T(8,128)(2,1)S(1)} collective-permute-done((bf16[256,1024]{1,0:T(8,128)(2,1)S(1)}, bf16[256,1024]{1,0:T(8,128)(2,1)S(1)}, u32[]{:S(2)}, u32[]{:S(2)}) %collective-permute-start.29) | collective-permute-done | bytes 524320 | tf_op jit(solution)/shard_map/ppermute | solution.py:389
  174.9 6.9 %collective-permute-done.27 = bf16[256,1024]{1,0:T(8,128)(2,1)S(1)} collective-permute-done((bf16[256,1024]{1,0:T(8,128)(2,1)S(1)}, bf16[256,1024]{1,0:T(8,128)(2,1)S(1)}, u32[]{:S(2)}, u32[]{:S(2)}) %collective-permute-start.27) | collective-permute-done | bytes 524320 | tf_op jit(solution)/shard_map/ppermute | solution.py:389
  (72 shorter events, 39.2 us)
Async XLA Ops:
  3.8 12.9 %collective-permute-start.3 = (bf16[384,512]{1,0:T(8,128)(2,1)S(1)}, bf16[384,512]{1,0:T(8,128)(2,1)S(1)}, u32[]{:S(2)}, u32[]{:S(2)}) collective-permute-start(bf16[384,512]{1,0:T(8,128)(2,1)S(1)} %shard_map.119), channel_id=1, source_target_pairs={{0,1},{1,0},{2,3},{3,2},{4,5},{5,4},{6,7},{7,6},{8,9},{9,8},{10,11... | collective-permute-start | bytes 1179656 | tf_op jit(solution)/shard_map/ppermute | solution.py:423
  6.8 26.0 %collective-permute-start.4 = (bf16[384,1024]{1,0:T(8,128)(2,1)S(1)}, bf16[384,1024]{1,0:T(8,128)(2,1)S(1)}, u32[]{:S(2)}, u32[]{:S(2)}) collective-permute-start(bf16[384,1024]{1,0:T(8,128)(2,1)S(1)} %bitcast.41), channel_id=1, source_target_pairs={{0,1},{1,0},{2,3},{3,2},{4,5},{5,4},{6,7},{7,6},{8,9},{9,8},{10,11... | collective-permute-start | bytes 2359304 | tf_op jit(solution)/shard_map/ppermute | solution.py:419
  7.4 16.7 %collective-permute-start = (bf16[256,1024]{1,0:T(8,128)(2,1)S(1)}, bf16[256,1024]{1,0:T(8,128)(2,1)S(1)}, u32[]{:S(2)}, u32[]{:S(2)}) collective-permute-start(bf16[256,1024]{1,0:T(8,128)(2,1)S(1)} %get-tuple-element.74), channel_id=1, source_target_pairs={{2,0},{3,1},{4,2},{5,3},{6,4},{7,5},{10,8},{11,9},{12,10},{13,11},... | collective-permute-start | bytes 1572872 | tf_op jit(solution)/shard_map/ppermute | solution.py:412
  8.7 16.9 %collective-permute-start.2 = (bf16[256,1024]{1,0:T(8,128)(2,1)S(1)}, bf16[256,1024]{1,0:T(8,128)(2,1)S(1)}, u32[]{:S(2)}, u32[]{:S(2)}) collective-permute-start(bf16[256,1024]{1,0:T(8,128)(2,1)S(1)} %get-tuple-element.74), channel_id=1, source_target_pairs={{0,2},{1,3},{2,4},{3,5},{4,6},{5,7},{8,10},{9,11},{10,12},{11,13},... | collective-permute-start | bytes 1572872 | tf_op jit(solution)/shard_map/ppermute | solution.py:412
  13.3 27.4 %collective-permute-start.1 = (bf16[256,1024]{1,0:T(8,128)(2,1)S(1)}, bf16[256,1024]{1,0:T(8,128)(2,1)S(1)}, u32[]{:S(2)}, u32[]{:S(2)}) collective-permute-start(bf16[256,1024]{1,0:T(8,128)(2,1)S(1)} %get-tuple-element.73), channel_id=1, source_target_pairs={{2,0},{3,1},{4,2},{5,3},{6,4},{7,5},{10,8},{11,9},{12,10},{13,11},... | collective-permute-start | bytes 1572872 | tf_op jit(solution)/shard_map/ppermute | solution.py:412
  16.8 23.9 %collective-permute-start.9 = (bf16[256,1024]{1,0:T(8,128)(2,1)S(1)}, bf16[256,1024]{1,0:T(8,128)(2,1)S(1)}, u32[]{:S(2)}, u32[]{:S(2)}) collective-permute-start(bf16[256,1024]{1,0:T(8,128)(2,1)S(1)} %get-tuple-element.73), channel_id=1, source_target_pairs={{0,2},{1,3},{2,4},{3,5},{4,6},{5,7},{8,10},{9,11},{10,12},{11,13},... | collective-permute-start | bytes 1572872 | tf_op jit(solution)/shard_map/ppermute | solution.py:412
  34.2 16.2 %collective-permute-start.5 = (bf16[256,1024]{1,0:T(8,128)(2,1)S(1)}, bf16[256,1024]{1,0:T(8,128)(2,1)S(1)}, u32[]{:S(2)}, u32[]{:S(2)}) collective-permute-start(bf16[256,1024]{1,0:T(8,128)(2,1)S(1)} %get-tuple-element.39), channel_id=1, source_target_pairs={{0,2},{1,3},{2,4},{3,5},{4,6},{5,7},{8,10},{9,11},{10,12},{11,13},... | collective-permute-start | bytes 1572872 | tf_op jit(solution)/shard_map/ppermute | solution.py:412
  37.2 16.8 %collective-permute-start.6 = (bf16[256,1024]{1,0:T(8,128)(2,1)S(1)}, bf16[256,1024]{1,0:T(8,128)(2,1)S(1)}, u32[]{:S(2)}, u32[]{:S(2)}) collective-permute-start(bf16[256,1024]{1,0:T(8,128)(2,1)S(1)} %get-tuple-element.40), channel_id=1, source_target_pairs={{2,0},{3,1},{4,2},{5,3},{6,4},{7,5},{10,8},{11,9},{12,10},{13,11},... | collective-permute-start | bytes 1572872 | tf_op jit(solution)/shard_map/ppermute | solution.py:412
  39.1 9.8 %collective-permute-start.7 = (bf16[384,512]{1,0:T(8,128)(2,1)S(1)}, bf16[384,512]{1,0:T(8,128)(2,1)S(1)}, u32[]{:S(2)}, u32[]{:S(2)}) collective-permute-start(bf16[384,512]{1,0:T(8,128)(2,1)S(1)} %shard_map.121), channel_id=1, source_target_pairs={{0,1},{1,0},{2,3},{3,2},{4,5},{5,4},{6,7},{7,6},{8,9},{9,8},{10,11... | collective-permute-start | bytes 1179656 | tf_op jit(solution)/shard_map/ppermute | solution.py:423
  42.1 19.8 %collective-permute-start.10 = (bf16[256,1024]{1,0:T(8,128)(2,1)S(1)}, bf16[256,1024]{1,0:T(8,128)(2,1)S(1)}, u32[]{:S(2)}, u32[]{:S(2)}) collective-permute-start(bf16[256,1024]{1,0:T(8,128)(2,1)S(1)} %get-tuple-element.42), channel_id=1, source_target_pairs={{0,2},{1,3},{2,4},{3,5},{4,6},{5,7},{8,10},{9,11},{10,12},{11,13},... | collective-permute-start | bytes 1572872 | tf_op jit(solution)/shard_map/ppermute | solution.py:412
  45.9 19.3 %collective-permute-start.11 = (bf16[256,1024]{1,0:T(8,128)(2,1)S(1)}, bf16[256,1024]{1,0:T(8,128)(2,1)S(1)}, u32[]{:S(2)}, u32[]{:S(2)}) collective-permute-start(bf16[256,1024]{1,0:T(8,128)(2,1)S(1)} %get-tuple-element.43), channel_id=1, source_target_pairs={{2,0},{3,1},{4,2},{5,3},{6,4},{7,5},{10,8},{11,9},{12,10},{13,11},... | collective-permute-start | bytes 1572872 | tf_op jit(solution)/shard_map/ppermute | solution.py:412
  48.9 19.1 %collective-permute-start.15 = (bf16[384,512]{1,0:T(8,128)(2,1)S(1)}, bf16[384,512]{1,0:T(8,128)(2,1)S(1)}, u32[]{:S(2)}, u32[]{:S(2)}) collective-permute-start(bf16[384,512]{1,0:T(8,128)(2,1)S(1)} %shard_map.125), channel_id=1, source_target_pairs={{0,1},{1,0},{2,3},{3,2},{4,5},{5,4},{6,7},{7,6},{8,9},{9,8},{10,11... | collective-permute-start | bytes 1179656 | tf_op jit(solution)/shard_map/ppermute | solution.py:423
  55.4 21.0 %collective-permute-start.8 = (bf16[256,1024]{1,0:T(8,128)(2,1)S(1)}, bf16[256,1024]{1,0:T(8,128)(2,1)S(1)}, u32[]{:S(2)}, u32[]{:S(2)}) collective-permute-start(bf16[256,1024]{1,0:T(8,128)(2,1)S(1)} %get-tuple-element.41), channel_id=1, source_target_pairs={{2,0},{3,1},{4,2},{5,3},{6,4},{7,5},{10,8},{11,9},{12,10},{13,11},... | collective-permute-start | bytes 1572872 | tf_op jit(solution)/shard_map/ppermute | solution.py:412
  56.7 19.8 %collective-permute-start.13 = (bf16[256,1024]{1,0:T(8,128)(2,1)S(1)}, bf16[256,1024]{1,0:T(8,128)(2,1)S(1)}, u32[]{:S(2)}, u32[]{:S(2)}) collective-permute-start(bf16[256,1024]{1,0:T(8,128)(2,1)S(1)} %get-tuple-element.45), channel_id=1, source_target_pairs={{0,2},{1,3},{2,4},{3,5},{4,6},{5,7},{8,10},{9,11},{10,12},{11,13},... | collective-permute-start | bytes 1572872 | tf_op jit(solution)/shard_map/ppermute | solution.py:412
  61.9 21.8 %collective-permute-start.16 = (bf16[384,512]{1,0:T(8,128)(2,1)S(1)}, bf16[384,512]{1,0:T(8,128)(2,1)S(1)}, u32[]{:S(2)}, u32[]{:S(2)}) collective-permute-start(bf16[384,512]{1,0:T(8,128)(2,1)S(1)} %shard_map.126), channel_id=1, source_target_pairs={{0,1},{1,0},{2,3},{3,2},{4,5},{5,4},{6,7},{7,6},{8,9},{9,8},{10,11... | collective-permute-start | bytes 1179656 | tf_op jit(solution)/shard_map/ppermute | solution.py:423
  66.6 21.4 %collective-permute-start.12 = (bf16[256,1024]{1,0:T(8,128)(2,1)S(1)}, bf16[256,1024]{1,0:T(8,128)(2,1)S(1)}, u32[]{:S(2)}, u32[]{:S(2)}) collective-permute-start(bf16[256,1024]{1,0:T(8,128)(2,1)S(1)} %get-tuple-element.44), channel_id=1, source_target_pairs={{2,0},{3,1},{4,2},{5,3},{6,4},{7,5},{10,8},{11,9},{12,10},{13,11},... | collective-permute-start | bytes 1572872 | tf_op jit(solution)/shard_map/ppermute | solution.py:412
  67.9 15.8 %copy-start.1 = (bf16[1,384,4096]{2,1,0:T(8,128)(2,1)S(1)}, bf16[1,384,4096]{2,1,0:T(8,128)(2,1)}, u32[]{:S(2)}) copy-start(bf16[1,384,4096]{2,1,0:T(8,128)(2,1)} %param.8) | copy-start | bytes 9437188
  68.0 20.1 %collective-permute-start.14 = (bf16[256,1024]{1,0:T(8,128)(2,1)S(1)}, bf16[256,1024]{1,0:T(8,128)(2,1)S(1)}, u32[]{:S(2)}, u32[]{:S(2)}) collective-permute-start(bf16[256,1024]{1,0:T(8,128)(2,1)S(1)} %get-tuple-element.46), channel_id=1, source_target_pairs={{0,2},{1,3},{2,4},{3,5},{4,6},{5,7},{8,10},{9,11},{10,12},{11,13},... | collective-permute-start | bytes 1572872 | tf_op jit(solution)/shard_map/ppermute | solution.py:412
  77.9 21.5 %collective-permute-start.24 = (bf16[256,1024]{1,0:T(8,128)(2,1)S(1)}, bf16[256,1024]{1,0:T(8,128)(2,1)S(1)}, u32[]{:S(2)}, u32[]{:S(2)}) collective-permute-start(bf16[256,1024]{1,0:T(8,128)(2,1)S(1)} %get-tuple-element.65), channel_id=1, source_target_pairs={{0,2},{1,3},{2,4},{3,5},{4,6},{5,7},{8,10},{9,11},{10,12},{11,13},... | collective-permute-start | bytes 1572872 | tf_op jit(solution)/shard_map/ppermute | solution.py:412
  82.4 22.3 %collective-permute-start.25 = (bf16[256,1024]{1,0:T(8,128)(2,1)S(1)}, bf16[256,1024]{1,0:T(8,128)(2,1)S(1)}, u32[]{:S(2)}, u32[]{:S(2)}) collective-permute-start(bf16[256,1024]{1,0:T(8,128)(2,1)S(1)} %get-tuple-element.66), channel_id=1, source_target_pairs={{2,0},{3,1},{4,2},{5,3},{6,4},{7,5},{10,8},{11,9},{12,10},{13,11},... | collective-permute-start | bytes 1572872 | tf_op jit(solution)/shard_map/ppermute | solution.py:412
  86.4 29.3 %collective-permute-start.18 = (bf16[384,512]{1,0:T(8,128)(2,1)S(1)}, bf16[384,512]{1,0:T(8,128)(2,1)S(1)}, u32[]{:S(2)}, u32[]{:S(2)}) collective-permute-start(bf16[384,512]{1,0:T(8,128)(2,1)S(1)} %get-tuple-element.59), channel_id=1, source_target_pairs={{0,1},{1,0},{2,3},{3,2},{4,5},{5,4},{6,7},{7,6},{8,9},{9,8},{10,11... | collective-permute-start | bytes 1179656 | tf_op jit(solution)/shard_map/ppermute | solution.py:443
  89.5 21.5 %collective-permute-start.22 = (bf16[256,1024]{1,0:T(8,128)(2,1)S(1)}, bf16[256,1024]{1,0:T(8,128)(2,1)S(1)}, u32[]{:S(2)}, u32[]{:S(2)}) collective-permute-start(bf16[256,1024]{1,0:T(8,128)(2,1)S(1)} %get-tuple-element.63), channel_id=1, source_target_pairs={{0,2},{1,3},{2,4},{3,5},{4,6},{5,7},{8,10},{9,11},{10,12},{11,13},... | collective-permute-start | bytes 1572872 | tf_op jit(solution)/shard_map/ppermute | solution.py:412
  94.8 17.8 %collective-permute-start.23 = (bf16[256,1024]{1,0:T(8,128)(2,1)S(1)}, bf16[256,1024]{1,0:T(8,128)(2,1)S(1)}, u32[]{:S(2)}, u32[]{:S(2)}) collective-permute-start(bf16[256,1024]{1,0:T(8,128)(2,1)S(1)} %get-tuple-element.64), channel_id=1, source_target_pairs={{2,0},{3,1},{4,2},{5,3},{6,4},{7,5},{10,8},{11,9},{12,10},{13,11},... | collective-permute-start | bytes 1572872 | tf_op jit(solution)/shard_map/ppermute | solution.py:412
  99.4 16.4 %collective-permute-start.19 = (bf16[384,512]{1,0:T(8,128)(2,1)S(1)}, bf16[384,512]{1,0:T(8,128)(2,1)S(1)}, u32[]{:S(2)}, u32[]{:S(2)}) collective-permute-start(bf16[384,512]{1,0:T(8,128)(2,1)S(1)} %get-tuple-element.60), channel_id=1, source_target_pairs={{0,1},{1,0},{2,3},{3,2},{4,5},{5,4},{6,7},{7,6},{8,9},{9,8},{10,11... | collective-permute-start | bytes 1179656 | tf_op jit(solution)/shard_map/ppermute | solution.py:443
  107.7 49.5 %collective-permute-start.28 = (bf16[256,1024]{1,0:T(8,128)(2,1)S(1)}, bf16[256,1024]{1,0:T(8,128)(2,1)}, u32[]{:S(2)}, u32[]{:S(2)}) collective-permute-start(bf16[256,1024]{1,0:T(8,128)(2,1)S(1)} %get-tuple-element.70.stepped_ref), channel_id=1, source_target_pairs={{0,8},{8,0},{16,24},{24,16},{1,9},{9,1},{17,25},{25,17},{2,10},{10... | collective-permute-start | bytes 1572872 | tf_op jit(solution)/shard_map/ppermute | solution.py:388
  111.0 12.3 %collective-permute-start.20 = (bf16[384,512]{1,0:T(8,128)(2,1)}, bf16[384,512]{1,0:T(8,128)(2,1)}, u32[]{:S(2)}, u32[]{:S(2)}) collective-permute-start(bf16[384,512]{1,0:T(8,128)(2,1)} %get-tuple-element.61), channel_id=1, source_target_pairs={{0,1},{1,0},{2,3},{3,2},{4,5},{5,4},{6,7},{7,6},{8,9},{9,8},{10,11... | collective-permute-start | bytes 1179656 | tf_op jit(solution)/shard_map/ppermute | solution.py:443
  112.6 19.2 %collective-permute-start.21 = (bf16[384,512]{1,0:T(8,128)(2,1)}, bf16[384,512]{1,0:T(8,128)(2,1)}, u32[]{:S(2)}, u32[]{:S(2)}) collective-permute-start(bf16[384,512]{1,0:T(8,128)(2,1)} %get-tuple-element.62), channel_id=1, source_target_pairs={{0,1},{1,0},{2,3},{3,2},{4,5},{5,4},{6,7},{7,6},{8,9},{9,8},{10,11... | collective-permute-start | bytes 1179656 | tf_op jit(solution)/shard_map/ppermute | solution.py:443
  113.1 4.3 %copy-start.7 = (s32[4]{0:T(128)S(1)}, s32[4]{0:T(128)}, u32[]{:S(2)}) copy-start(s32[4]{0:T(128)} %param.14) | copy-start | bytes 52
  115.8 43.1 %collective-permute-start.26 = (bf16[256,1024]{1,0:T(8,128)(2,1)S(1)}, bf16[256,1024]{1,0:T(8,128)(2,1)}, u32[]{:S(2)}, u32[]{:S(2)}) collective-permute-start(bf16[256,1024]{1,0:T(8,128)(2,1)S(1)} %get-tuple-element.69.stepped_ref), channel_id=1, source_target_pairs={{0,8},{8,0},{16,24},{24,16},{1,9},{9,1},{17,25},{25,17},{2,10},{10... | collective-permute-start | bytes 1572872 | tf_op jit(solution)/shard_map/ppermute | solution.py:388
  115.8 43.8 %collective-permute-start.17 = (bf16[384,1024]{1,0:T(8,128)(2,1)}, bf16[384,1024]{1,0:T(8,128)(2,1)}, u32[]{:S(2)}, u32[]{:S(2)}) collective-permute-start(bf16[384,1024]{1,0:T(8,128)(2,1)} %get-tuple-element.57), channel_id=1, source_target_pairs={{0,1},{1,0},{2,3},{3,2},{4,5},{5,4},{6,7},{7,6},{8,9},{9,8},{10,11... | collective-permute-start | bytes 2359304 | tf_op jit(solution)/shard_map/ppermute | solution.py:444
  157.3 14.9 %collective-permute-start.29 = (bf16[256,1024]{1,0:T(8,128)(2,1)S(1)}, bf16[256,1024]{1,0:T(8,128)(2,1)S(1)}, u32[]{:S(2)}, u32[]{:S(2)}) collective-permute-start(bf16[256,1024]{1,0:T(8,128)(2,1)S(1)} %broadcast_select_fusion), channel_id=1, source_target_pairs={{0,16},{8,24},{16,0},{24,8},{1,17},{9,25},{17,1},{25,9},{2,18},{10... | collective-permute-start | bytes 1572872 | tf_op jit(solution)/shard_map/ppermute | solution.py:389
  159.0 22.8 %collective-permute-start.27 = (bf16[256,1024]{1,0:T(8,128)(2,1)S(1)}, bf16[256,1024]{1,0:T(8,128)(2,1)S(1)}, u32[]{:S(2)}, u32[]{:S(2)}) collective-permute-start(bf16[256,1024]{1,0:T(8,128)(2,1)S(1)} %broadcast_select_fusion.1), channel_id=1, source_target_pairs={{0,16},{8,24},{16,0},{24,8},{1,17},{9,25},{17,1},{25,9},{2,18},{10... | collective-permute-start | bytes 1572872 | tf_op jit(solution)/shard_map/ppermute | solution.py:389
  (6 other events, 17.9 us)

commit v2 on v1

v2 whole, which is shorter than its diff:
```python
import functools

import jax
import jax.numpy as jnp
import numpy as np
from jax import lax
from jax.experimental import pallas as pl
from jax.experimental.pallas import tpu as pltpu
from jax.sharding import PartitionSpec as P

beta_one = 0.9
beta_two = 0.999
learn_rate = 0.02
weight_decay = 0.1
adam_eps = 1e-08
corr_one = 1.0 - beta_one**10
corr_two = 1.0 - beta_two**10
mix_denom = 64.0

CHUNKS = 2
MIB = 1 << 20
ANY = pl.BlockSpec(memory_space=pl.ANY)

TN = (((0,), (0,)), ((), ()))
NT = (((1,), (1,)), ((), ()))


def dot(a, b, dims=(((1,), (0,)), ((), ()))):
    return lax.dot_general(a, b, dims, preferred_element_type=jnp.float32)


class Plan:
    def __init__(self, n):
        self.depth = depth = n // 2
        self.columns = {}
        self.rows = [[] for _ in range(n)]
        order = [
            sorted(range(depth), key=lambda q: (-abs(q - z), (q < z) != (2 * z >= depth)))
            for z in range(depth)
        ]
        self.sources = [set() for _ in range(depth)]
        arrivals = []
        for z in range(depth):
            below, above = ("b", "a") if z % 2 == 0 else ("a", "b")
            ups = [(z - t, (below, t)) for t in range(1, z + 1)]
            downs = [(z + t, (above, t)) for t in range(1, depth - z)]
            arrivals.append(downs + ups if 2 * z < depth else ups + downs)
            for j, (_, source) in enumerate(arrivals[z], 1):
                self.sources[j].add(source)
        self.sources = [sorted(s) for s in self.sources]
        for i in range(n):
            z, x = divmod(i, 2)
            put = functools.partial(self._put, i)
            put("own", i)
            for k in range(depth):
                put(f"pack{k}", 2 * order[z][k] + 1 - x)
            for s in range(2, depth + 1):
                up, down = z + 1 + depth - s, z - 1 - depth + s
                for link, q in zip("ab", (up, down) if z % 2 == 0 else (down, up)):
                    add = 0 <= q < depth
                    put(f"add_{link}{s}", int(add))
                    put(f"blk_{link}{s}", 2 * q + x if add else 0)
                    put(f"pos_{link}{s}", order[z].index(q) if add else 0)
            for j in range(depth):
                q, source = (z, None) if j == 0 else arrivals[z][j - 1]
                put(f"mine{j}", 2 * q + x)
                put(f"theirs{j}", 2 * q + 1 - x)
                put(f"piece{j}", order[z].index(q))
                put(f"source{j}", 0 if j == 0 else self.sources[j].index(source))
        self.table = np.asarray(self.rows, np.int32)

    def _put(self, i, name, value):
        column = self.columns.setdefault(name, len(self.columns))
        assert column == len(self.rows[i])
        self.rows[i].append(value)

    def __getitem__(self, name):
        return self.columns[name]


def call(kernel, row, ins, outs, grid=(1,), aliases=None, scratch=(), flops=0, moved=0, vmem=24):
    return pl.pallas_call(
        kernel,
        grid_spec=pltpu.PrefetchScalarGridSpec(
            num_scalar_prefetch=1,
            grid=grid,
            in_specs=[spec for _, spec in ins],
            out_specs=[spec for _, spec in outs],
            scratch_shapes=list(scratch),
        ),
        out_shape=[shape for shape, _ in outs],
        input_output_aliases=aliases or {},
        compiler_params=pltpu.CompilerParams(vmem_limit_bytes=vmem * MIB),
        cost_estimate=pl.CostEstimate(flops=flops, bytes_accessed=moved, transcendentals=0),
    )(row, *[array for array, _ in ins])


def whole(array):
    rank = array.ndim
    return pl.BlockSpec(array.shape, lambda g, row: (0,) * rank)


def block(shape, column, scale=1, offset=0):
    return pl.BlockSpec(shape, lambda g, row: (0, row[column] * scale + offset))


def struct(shape, dtype):
    return jax.ShapeDtypeStruct(shape, dtype)


class View:
    def __init__(self, array, start, count):
        assert start % count == 0
        self.array, self.start, self.count = array, start, count
        self.shape = (array.shape[0], count)

    def operand(self):
        at = self.start // self.count
        return self.array, pl.BlockSpec(self.shape, lambda g, row: (0, at))


def pack(plan, row, width, views, act=None, turns=(), after=()):
    count = len(views) + len(turns)
    ins = [v.operand() for v in views]
    tokens = views[0].shape[0] if views else act.shape[0]
    ins += [(act, block((tokens, width), plan[f"pack{k}"])) for k in turns]
    sizes = [v.count for v in views] + [width] * len(turns)

    def kernel(row_ref, *refs):
        at = 0
        for ref, size in zip(refs[:count], sizes):
            refs[-1][:, at : at + size] = ref[...]
            at += size

    out = struct((tokens, sum(sizes)), jnp.bfloat16)
    return call(
        kernel,
        row,
        ins + [(a, ANY) for a in after],
        [(out, whole(out))],
        moved=4 * tokens * sum(sizes),
    )[0]


def relay(plan, row, s, got, act, pieces, cot_own, cot_oth):
    (tokens, columns), rows = cot_own.shape, got["a"].shape[0]
    count = len(pieces)

    def kernel(row_ref, *refs):
        got_refs, act_refs = refs[0:2], refs[2:4]
        piece_refs = refs[4 : 4 + count]
        own_ref, oth_ref = refs[4 + count : 6 + count]
        out_refs = refs[6 + count : 8 + count]
        held = refs[8 + count]
        for d, link in enumerate("ab"):
            add = row_ref[plan[f"add_{link}{s}"]]
            pos = row_ref[plan[f"pos_{link}{s}"]]

            @pl.when(add == 0)
            def _():
                out_refs[d][...] = got_refs[d][...]

            @pl.when(add == 1)
            def _():
                for j in range(count):

                    @pl.when(pos == j)
                    def _():
                        held[...] = piece_refs[j][...]

                total = dot(act_refs[d][...], own_ref[...], TN)
                total = total + dot(held[...], oth_ref[...], TN)
                out_refs[d][...] = (total + got_refs[d][...].astype(jnp.float32)).astype(jnp.bfloat16)

    ins = [(got[link], whole(got[link])) for link in "ba"]
    ins += [(act, block((tokens, rows), plan[f"blk_{link}{s}"])) for link in "ab"]
    ins += [view.operand() for view in (*pieces, cot_own, cot_oth)]
    out = struct((rows, columns), jnp.bfloat16)
    a, b = call(
        kernel,
        row,
        ins,
        [(out, whole(out)), (out, whole(out))],
        scratch=[pltpu.VMEM((tokens, rows), jnp.bfloat16)],
        flops=8 * tokens * rows * columns,
        moved=8 * rows * columns + 4 * tokens * columns,
    )
    return {"a": a, "b": b}


def own_gradient(plan, row, act, piece, cot, cot_oth):
    tokens, columns = cot.shape
    rows = piece.shape[1]

    def kernel(row_ref, act_ref, piece_ref, own_ref, *refs):
        out_ref = refs[-1]
        at = 0
        for ref, view in zip(refs, cot_oth):
            part = slice(at, at + view.count)
            total = dot(act_ref[...], own_ref[:, part], TN)
            out_ref[:, part] = total + dot(piece_ref[...], ref[...], TN)
            at += view.count

    out = struct((rows, columns), jnp.float32)
    return call(
        kernel,
        row,
        [(act, block((tokens, rows), plan["own"])), piece.operand(), (cot, whole(cot))]
        + [view.operand() for view in cot_oth],
        [(out, whole(out))],
        flops=4 * tokens * rows * columns,
        moved=4 * rows * columns + 4 * tokens * columns,
    )[0]


def project(plan, row, j, candidates, act, cot, cot_oth, xg_before, turn=None, after=()):
    (tokens, columns), rows = cot.shape, candidates[0][0].shape[0]
    parts = len(candidates[0])
    flat = [c for candidate in candidates for c in candidate]
    n_w, n_c, extra = len(flat), len(cot_oth), turn is not None
    widths = [c.shape[1] for c in candidates[0]]
    starts = np.cumsum([0] + widths)

    def kernel(row_ref, *refs):
        w_refs, cot_refs = refs[:n_w], refs[n_w : n_w + n_c]
        own_ref = refs[n_w + n_c]
        xg_own, xg_oth, w_out, sems = refs[-4:]
        for c in range(len(candidates)):

            @pl.when(row_ref[plan[f"source{j}"]] == c)
            def _():
                copies = [
                    pltpu.make_async_copy(
                        w_refs[c * parts + p],
                        w_out.at[:, pl.ds(int(starts[p]), widths[p])],
                        sems.at[p],
                    )
                    for p in range(parts)
                ]
                for copy in copies:
                    copy.start()
                for copy in copies:
                    copy.wait()

        total, at = 0.0, 0
        for ref, view in zip(cot_refs, cot_oth):
            total = total + dot(ref[...], w_out[:, at : at + view.count], NT)
            at += view.count
        xg_oth[:, :rows] = total.astype(jnp.bfloat16)
        if extra:
            xg_oth[:, rows:] = refs[n_w + n_c + 1][...]
        xg_own[...] = dot(own_ref[...], w_out[...], NT).astype(jnp.bfloat16)

    ins = [(w, ANY) for w in flat] + [view.operand() for view in cot_oth] + [(cot, whole(cot))]
    if extra:
        ins.append((act, block((tokens, rows), plan[f"pack{turn}"])))
    aliases = {}
    if xg_before is not None:
        aliases = {1 + len(ins): 0}
        ins.append((xg_before, ANY))
    ins += [(a, ANY) for a in after]
    other = struct((tokens, rows * (1 + extra)), jnp.bfloat16)
    shard = struct((rows, columns), jnp.bfloat16)
    return call(
        kernel,
        row,
        ins,
        [
            (struct(act.shape, jnp.bfloat16), block((tokens, rows), plan[f"mine{j}"])),
            (other, whole(other)),
            (shard, whole(shard)),
        ],
        aliases=aliases,
        scratch=[pltpu.SemaphoreType.DMA((parts,))],
        flops=4 * tokens * rows * columns,
        moved=12 * tokens * columns,
    )


def values(plan, row, turns, shards, act, pieces, kept, last):
    rows, columns = shards[0].shape
    tokens = act.shape[0]
    count, n_p = len(turns), len(pieces)

    def kernel(row_ref, *refs):
        w_refs, act_refs = refs[:count], refs[count : 2 * count]
        piece_refs = refs[2 * count : 2 * count + n_p]
        own_out, oth_out, held = refs[-3:]
        own = oth = 0.0
        if kept is not None:
            own, oth = refs[2 * count + n_p][...], refs[2 * count + n_p + 1][...]
        for t, j in enumerate(turns):
            for p in range(n_p):

                @pl.when(row_ref[plan[f"piece{j}"]] == p)
                def _():
                    held[...] = piece_refs[p][...]

            oth = oth + dot(held[...], w_refs[t][...])
            own = own + dot(act_refs[t][...], w_refs[t][...])
        oth_out[...] = oth.astype(oth_out.dtype)
        own_out[...] = own

    ins = [(w, whole(w)) for w in shards]
    ins += [(act, block((tokens, rows), plan[f"mine{j}"])) for j in turns]
    ins += [p.operand() for p in pieces]
    if kept is not None:
        ins += [(k, whole(k)) for k in kept]
    own = struct((tokens, columns), jnp.float32)
    oth = struct((tokens, columns), jnp.bfloat16 if last else jnp.float32)
    return call(
        kernel,
        row,
        ins,
        [(own, whole(own)), (oth, whole(oth))],
        scratch=[pltpu.VMEM((tokens, rows), jnp.bfloat16)],
        flops=4 * tokens * rows * columns * count,
        moved=8 * tokens * columns,
        vmem=40,
    )


def finish(plan, row, xg, arrived, kv_own, kv_got, after):
    count = len(arrived)
    tokens, width = arrived[0].shape
    table = [plan[f"theirs{j}"] for j in range(count)]

    def kernel(row_ref, *refs):
        out_ref, kv_out = refs[-2:]
        g = pl.program_id(0)
        for j in range(count):

            @pl.when(g == j)
            def _():
                out_ref[...] = refs[j][...]

        kv_out[...] = (refs[count][...] + refs[count + 1][...].astype(jnp.float32)).astype(jnp.bfloat16)

    def place(g, row):
        at = row[table[0]]
        for j in range(1, count):
            at = jnp.where(g == j, row[table[j]], at)
        return (0, at)

    kv_block = pl.BlockSpec((tokens // count, kv_own.shape[1]), lambda g, row: (g, 0))
    ins = [view.operand() for view in arrived]
    ins += [(kv_own, kv_block), (kv_got, kv_block), (xg, ANY)] + [(a, ANY) for a in after]
    return call(
        kernel,
        row,
        ins,
        [
            (struct(xg.shape, xg.dtype), pl.BlockSpec((tokens, width), place)),
            (struct(kv_own.shape, jnp.bfloat16), kv_block),
        ],
        grid=(count,),
        aliases={count + 3: 0},
        moved=4 * count * tokens * width,
    )


def adam(row, h, got, grad, weights, first, second, kept):
    rows, columns = got["a"].shape
    steps = 4 if rows % 64 == 0 else 1
    size = rows // steps

    def kernel(row_ref, up_ref, dn_ref, grad_ref, w_ref, a_ref, b_ref, *refs):
        a_out, b_out, stepped = refs[-3:]
        gradient = grad_ref[...] + up_ref[...].astype(jnp.float32) + dn_ref[...].astype(jnp.float32)
        moment_a = beta_one * a_ref[...] + (1.0 - beta_one) * gradient
        moment_b = beta_two * b_ref[...] + (1.0 - beta_two) * gradient * gradient
        old = w_ref[...].astype(jnp.float32)
        update = moment_a / corr_one / (jnp.sqrt(moment_b / corr_two) + adam_eps) + weight_decay * old
        a_out[...] = moment_a
        b_out[...] = moment_b
        stepped[...] = (old - learn_rate * update).astype(jnp.bfloat16)

    local = pl.BlockSpec((size, columns), lambda g, row: (g, 0))
    part = pl.BlockSpec((size, columns), lambda g, row: (g, h))
    ins = [(got["a"], local), (got["b"], local)]
    ins += [(a, part) for a in (grad, weights, first, second)]
    aliases = {}
    if kept is not None:
        aliases = {1 + len(ins): 0, 2 + len(ins): 1}
        ins += [(a, ANY) for a in kept]
    return call(
        kernel,
        row,
        ins,
        [
            (struct(first.shape, jnp.float32), part),
            (struct(second.shape, jnp.float32), part),
            (struct((rows, columns), jnp.bfloat16), local),
        ],
        grid=(steps,),
        aliases=aliases,
        flops=16 * rows * columns,
        moved=28 * rows * columns,
    )


def average(mixing, h, stepped, chosen, kept, width):
    rows, columns = stepped.shape
    steps = 2 if rows % 32 == 0 else 1
    size = rows // steps

    def kernel(mix_ref, stepped_ref, chosen_ref, *refs):
        mix = mix_ref[0].astype(jnp.float32) / mix_denom
        refs[-1][...] = (
            (1.0 - mix) * stepped_ref[...].astype(jnp.float32)
            + mix * chosen_ref[...].astype(jnp.float32)
        ).astype(jnp.bfloat16)

    local = pl.BlockSpec((size, columns), lambda g, row: (g, 0))
    part = pl.BlockSpec((size, columns), lambda g, row: (g, h))
    ins = [(stepped, local), (chosen, local)]
    if kept is not None:
        ins.append((kept, ANY))
    return call(
        kernel,
        mixing,
        ins,
        [(struct((rows, width), jnp.bfloat16), part)],
        grid=(steps,),
        aliases={} if kept is None else {3: 0},
        moved=6 * rows * columns,
    )[0]


def partner_rows(stepped, partner, replica, n_rep):
    if n_rep != 4:
        gathered = lax.all_gather(stepped, "rep", axis=0, tiled=False)
        return lax.dynamic_index_in_dim(gathered, partner[replica], 0, keepdims=False)
    mask = partner[0]
    near = lax.ppermute(stepped, "rep", [(r, r ^ 1) for r in range(4)])
    far = lax.ppermute(
        jnp.where(mask == 3, near, stepped), "rep", [(r, r ^ 2) for r in range(4)]
    )
    return jnp.where(mask == 1, near, far)


def per_device(
    n_rep, n, activations, kv_weight, kv_cotangent, first_moment, second_moment, partner, mix_numerator
):
    act, weights, cot = activations[0], kv_weight[0], kv_cotangent[0]
    first, second = first_moment[0], second_moment[0]
    plan = Plan(n)
    depth = plan.depth
    rows, columns = weights.shape
    size = columns // CHUNKS
    row = lax.dynamic_index_in_dim(
        jnp.asarray(plan.table), lax.axis_index("fsdp"), 0, keepdims=False
    )
    links = {
        "a": [(i, i + 2 if i // 2 % 2 == 0 else i - 2) for i in range(n)],
        "b": [(i, i - 2 if i // 2 % 2 == 0 else i + 2) for i in range(n)],
    }
    links = {name: [p for p in pairs if 0 <= p[1] < n] for name, pairs in links.items()}
    swap = functools.partial(lax.ppermute, axis_name="fsdp", perm=[(i, i ^ 1) for i in range(n)])

    def exchange(bufs):
        return {name: lax.ppermute(bufs[name], "fsdp", links[name]) for name in links}

    def part(array, h):
        return View(array, h * size, size)

    got = {}
    for h in range(CHUNKS):
        own = weights[:, h * size : (h + 1) * size]
        got[1, h] = exchange({"a": own, "b": own})

    opening = swap(pack(plan, row, rows, [part(cot, 0)], act, [0]))
    cot_oth = [View(opening, 0, size)]
    pieces = [View(opening, size, rows)]
    for h in range(1, CHUNKS):
        cot_oth.append(part(swap(pack(plan, row, rows, [part(cot, h)], after=[opening])), 0))
    latest = cot_oth[-1].array
    for k in range(1, depth - 1, 2):
        turns = list(range(k, min(k + 2, depth - 1)))
        latest = swap(pack(plan, row, rows, [], act, turns, after=[latest]))
        pieces += [View(latest, t * rows, rows) for t in range(len(turns))]
    xg, both, shard = project(
        plan, row, 0, [[weights]], act, cot, cot_oth, None, turn=depth - 1, after=[latest]
    )
    both = swap(both)
    arrived, shards = [View(both, 0, rows)], [shard]
    pieces.append(View(both, rows, rows))

    for s in range(2, depth + 1):
        for h in range(CHUNKS):
            bufs = relay(
                plan, row, s, got[s - 1, h], act, pieces[: s - 1], part(cot, h), cot_oth[h]
            )
            got[s, h] = exchange(bufs)

    for j in range(1, depth):
        candidates = [
            [got[slot, h][link] for h in range(CHUNKS)] for link, slot in plan.sources[j]
        ]
        xg, xg_oth, shard = project(plan, row, j, candidates, act, cot, cot_oth, xg)
        arrived.append(View(swap(xg_oth), 0, rows))
        shards.append(shard)
    early = list(range(depth - 1))
    sums = values(plan, row, early, shards[:-1], act, pieces, None, False)
    kv_own, kv_oth = values(plan, row, [depth - 1], shards[-1:], act, pieces, sums, True)
    kv_got = swap(kv_oth)

    grad = own_gradient(plan, row, act, pieces[depth - 1], cot, cot_oth)
    replica = lax.axis_index("rep")
    mixing = lax.dynamic_slice(mix_numerator, (replica,), (1,))
    moments, averaged = None, None
    for h in range(CHUNKS):
        new_a, new_b, stepped = adam(row, h, got[depth, h], grad, weights, first, second, moments)
        moments = (new_a, new_b)
        chosen = partner_rows(stepped, partner, replica, n_rep)
        if h == CHUNKS - 1:
            x_grad, kv_out = finish(plan, row, xg, arrived, kv_own, kv_got, [averaged])
        averaged = average(mixing, h, stepped, chosen, averaged, columns)
    return (
        kv_out[None],
        x_grad[None],
        averaged[None],
        moments[0][None],
        moments[1][None],
    )


def solution(mesh):
    placed = P("rep", "fsdp", None)
    return jax.shard_map(
        functools.partial(per_device, mesh.shape["rep"], mesh.shape["fsdp"]),
        mesh=mesh,
        in_specs=(placed,) * 5 + (P(), P()),
        out_specs=(placed,) * 5,
        check_vma=False,
    )
```

time: 185 us -> 190 us (1.027)
  waiting for transfers between devices: 55.3 us -> 101 us
  starting transfers between devices: 61.2 us -> 36.4 us
  Pallas kernels: 58.6 us -> 42.4 us
    ppermute x26 -> x24, waiting for transfers between devices: 38 us -> 87.3 us  [the longest x16 44.6 us: exchange(): lax.ppermute(bufs[name], 'fsdp', links[name])]
    ppermute x26 -> x24, starting transfers between devices: 59 us -> 34.3 us  [the longest x16 24.3 us: exchange(): lax.ppermute(bufs[name], 'fsdp', links[name])]
    pallas_call x20 -> x21, Pallas kernels: 58.6 us -> 42.4 us  [call(): pl.pallas_call(kernel, grid_spec=pltpu.PrefetchScalarGridSpec(num_scalar_...]
    ppermute x2, waiting for transfers between devices: 17.4 us -> 14 us  [partner_rows(): lax.ppermute(jnp.where(mask == 3, near, stepped), 'rep', [(r, r ^ 2) for...]
    broadcast_in_dim x1 -> x0, other arithmetic: 2.27 us -> none  [per_device(): kv_out[None]]
    unnamed x16 -> x32, local copies, waits for them, and re-layouts: 2.29 us -> 3.83 us
  transfers between devices with their start and end apart: 30 -> 28, of which waited for: 12 -> 15; matrix products, arithmetic and copies ran while one was open for 2% -> 2% of each run, Pallas kernels for 31% -> 19%
where the time goes in v2:
time: 190 us; the launch traced here: 189 us
  waiting for transfers between devices  101 us (53%)
  Pallas kernels  42.4 us (22%)
  starting transfers between devices  36.4 us (19%)
  local copies, waits for them, and re-layouts  5.27 us (3%)
  other arithmetic  3.03 us (2%)
    ppermute x16, waiting for transfers between devices, exchange(): lax.ppermute(bufs[name], 'fsdp', links[name])  44.6 us
    pallas_call x21, Pallas kernels, call(): pl.pallas_call(kernel, grid_spec=pltpu.PrefetchScalarGridSpec(num_scalar_...  42.4 us
    ppermute x16, starting transfers between devices, exchange(): lax.ppermute(bufs[name], 'fsdp', links[name])  24.3 us
    ppermute x3, waiting for transfers between devices, per_device(): arrived.append(View(swap(xg_oth), 0, rows))  24.3 us
    ppermute x1, waiting for transfers between devices, per_device(): opening = swap(pack(plan, row, rows, [part(cot, 0)], act, [0]))  17.5 us
    ppermute x2, waiting for transfers between devices, partner_rows(): lax.ppermute(jnp.where(mask == 3, near, stepped), 'rep', [(r, r ^ 2) for...  14 us
    unnamed x32, local copies, waits for them, and re-layouts  3.83 us
  transfers between devices with their start and end apart: 28, of which 15 were waited for; matrix products, arithmetic and copies ran while one was open for 2% of the time, Pallas kernels for 19%

profile of v2, /device:TPU:0, one launch (start us, length us, event | category | flops | bytes accessed | tf_op | source)
XLA Modules:
  0.0 189.4 jit_solution(14088280403694213645)
XLA Ops:
  1.3 1.9 copy-done
  5.0 3.0 %collective-permute-start = (bf16[384,1024]{1,0:T(8,128)(2,1)S(1)}, bf16[384,1024]{1,0:T(8,128)(2,1)S(1)}, u32[]{:S(2)}, u32[]{:S(2)}) collective-permute-start(bf16[384,1024]{1,0:T(8,128)(2,1)S(1)} %shard_map.119), channel_id=1, source_target_pairs={{0,1},{1,0},{2,3},{3,2},{4,5},{5,4},{6,7},{7,6},{8,9},{9,8},{10,11... | collective-permute-start | bytes 2359304 | tf_op jit(solution)/shard_map/ppermute | solution.py:472
  8.0 17.5 %collective-permute-done.refs_1_.refs_4_.refs_6_.refs_7_.refs_2_.refs_8_.refs_0_ = bf16[384,1024]{1,0:T(8,128)(2,1)S(1)} collective-permute-done((bf16[384,1024]{1,0:T(8,128)(2,1)S(1)}, bf16[384,1024]{1,0:T(8,128)(2,1)S(1)}, u32[]{:S(2)}, u32[]{:S(2)}) %collective-permute-start) | collective-permute-done | bytes 786464 | tf_op jit(solution)/shard_map/ppermute | solution.py:472
  26.1 1.8 collective-permute-start.1
  28.7 4.4 %collective-permute-start.4 = (bf16[512,512]{1,0:T(8,128)(2,1)S(1)}, bf16[512,512]{1,0:T(8,128)(2,1)S(1)}, u32[]{:S(2)}, u32[]{:S(2)}) collective-permute-start(bf16[512,512]{1,0:T(8,128)(2,1)S(1)} %get-tuple-element.78), channel_id=1, source_target_pairs={{0,2},{1,3},{2,0},{3,1},{4,6},{5,7},{6,4},{7,5},{8,10},{9,11},{10,... | collective-permute-start | bytes 1572872 | tf_op jit(solution)/shard_map/ppermute | solution.py:462
  33.8 1.8 collective-permute-start.5
  38.6 7.4 %collective-permute-done.4.refs_0_.refs_1_ = bf16[512,512]{1,0:T(8,128)(2,1)S(1)} collective-permute-done((bf16[512,512]{1,0:T(8,128)(2,1)S(1)}, bf16[512,512]{1,0:T(8,128)(2,1)S(1)}, u32[]{:S(2)}, u32[]{:S(2)}) %collective-permute-start.4) | collective-permute-done | bytes 524320 | tf_op jit(solution)/shard_map/ppermute | solution.py:462
  49.5 7.7 %collective-permute-done.5.refs_1_ = bf16[512,512]{1,0:T(8,128)(2,1)S(1)} collective-permute-done((bf16[512,512]{1,0:T(8,128)(2,1)S(1)}, bf16[512,512]{1,0:T(8,128)(2,1)S(1)}, u32[]{:S(2)}, u32[]{:S(2)}) %collective-permute-start.5) | collective-permute-done | bytes 524320 | tf_op jit(solution)/shard_map/ppermute | solution.py:462
  60.7 7.7 %collective-permute-done.9.refs_0_.refs_1_ = bf16[512,512]{1,0:T(8,128)(2,1)S(1)} collective-permute-done((bf16[512,512]{1,0:T(8,128)(2,1)S(1)}, bf16[512,512]{1,0:T(8,128)(2,1)S(1)}, u32[]{:S(2)}, u32[]{:S(2)}) %collective-permute-start.9) | collective-permute-done | bytes 524320 | tf_op jit(solution)/shard_map/ppermute | solution.py:462
  69.9 2.1 %collective-permute-start.14 = (bf16[512,512]{1,0:T(8,128)(2,1)S(1)}, bf16[512,512]{1,0:T(8,128)(2,1)S(1)}, u32[]{:S(2)}, u32[]{:S(2)}) collective-permute-start(bf16[512,512]{1,0:T(8,128)(2,1)S(1)} %get-tuple-element.50), channel_id=1, source_target_pairs={{0,2},{1,3},{2,0},{3,1},{4,6},{5,7},{6,4},{7,5},{8,10},{9,11},{10,... | collective-permute-start | bytes 1572872 | tf_op jit(solution)/shard_map/ppermute | solution.py:462
  72.7 6.9 %collective-permute-done.10.refs_1_ = bf16[512,512]{1,0:T(8,128)(2,1)S(1)} collective-permute-done((bf16[512,512]{1,0:T(8,128)(2,1)S(1)}, bf16[512,512]{1,0:T(8,128)(2,1)S(1)}, u32[]{:S(2)}, u32[]{:S(2)}) %collective-permute-start.10) | collective-permute-done | bytes 524320 | tf_op jit(solution)/shard_map/ppermute | solution.py:462
  81.2 2.1 %collective-permute-start.15 = (bf16[512,512]{1,0:T(8,128)(2,1)S(1)}, bf16[512,512]{1,0:T(8,128)(2,1)S(1)}, u32[]{:S(2)}, u32[]{:S(2)}) collective-permute-start(bf16[512,512]{1,0:T(8,128)(2,1)S(1)} %get-tuple-element.51), channel_id=1, source_target_pairs={{0,2},{1,3},{2,0},{3,1},{4,6},{5,7},{6,4},{7,5},{8,10},{9,11},{10,... | collective-permute-start | bytes 1572872 | tf_op jit(solution)/shard_map/ppermute | solution.py:462
  83.9 2.4 %shard_map.122 = (bf16[384,4096]{1,0:T(8,128)(2,1)}, bf16[384,1024]{1,0:T(8,128)(2,1)S(1)}, bf16[512,1024]{1,0:T(8,128)(2,1)S(1)}) custom-call(s32[39]{0:T(128)S(1)} %dynamic-slice_bitcast_fusion.row_ref, bf16[512,1024]{1,0:T(8,128)(2,1)S(1)} %bitcast.50, bf16[384,1024]{1,0:T(8,128)(2,1)S(1)} %collective-permute-done.refs_1_.refs_4_.refs_6_.refs_7_.refs_2_.refs_8_.refs_0_, ...), custom_call_target="tpu_custom_call" | custom-call | flops 805306368 | bytes 4718592 | tf_op jit(solution)/shard_map/pallas_call | solution.py:82
  87.0 3.9 %collective-permute-done.14.refs_2_.refs_1_ = bf16[512,512]{1,0:T(8,128)(2,1)S(1)} collective-permute-done((bf16[512,512]{1,0:T(8,128)(2,1)S(1)}, bf16[512,512]{1,0:T(8,128)(2,1)S(1)}, u32[]{:S(2)}, u32[]{:S(2)}) %collective-permute-start.14) | collective-permute-done | bytes 524320 | tf_op jit(solution)/shard_map/ppermute | solution.py:462
  92.4 2.8 %collective-permute-start.19 = (bf16[512,512]{1,0:T(8,128)(2,1)S(1)}, bf16[512,512]{1,0:T(8,128)(2,1)S(1)}, u32[]{:S(2)}, u32[]{:S(2)}) collective-permute-start(bf16[512,512]{1,0:T(8,128)(2,1)S(1)} %get-tuple-element.64), channel_id=1, source_target_pairs={{0,2},{1,3},{2,0},{3,1},{4,6},{5,7},{6,4},{7,5},{8,10},{9,11},{10,... | collective-permute-start | bytes 1572872 | tf_op jit(solution)/shard_map/ppermute | solution.py:462
  95.9 6.2 %collective-permute-done.15.refs_3_.refs_1_ = bf16[512,512]{1,0:T(8,128)(2,1)S(1)} collective-permute-done((bf16[512,512]{1,0:T(8,128)(2,1)S(1)}, bf16[512,512]{1,0:T(8,128)(2,1)S(1)}, u32[]{:S(2)}, u32[]{:S(2)}) %collective-permute-start.15) | collective-permute-done | bytes 524320 | tf_op jit(solution)/shard_map/ppermute | solution.py:462
  103.7 2.8 %collective-permute-start.24 = (bf16[512,512]{1,0:T(8,128)(2,1)S(1)}, bf16[512,512]{1,0:T(8,128)(2,1)S(1)}, u32[]{:S(2)}, u32[]{:S(2)}) collective-permute-start(bf16[512,512]{1,0:T(8,128)(2,1)S(1)} %get-tuple-element.70), channel_id=1, source_target_pairs={{0,2},{1,3},{2,0},{3,1},{4,6},{5,7},{6,4},{7,5},{8,10},{9,11},{10,... | collective-permute-start | bytes 1572872 | tf_op jit(solution)/shard_map/ppermute | solution.py:462
  107.3 1.8 shard_map.133.grad_ref
  109.1 4.2 %collective-permute-done.19.up_ref = bf16[512,512]{1,0:T(8,128)(2,1)S(1)} collective-permute-done((bf16[512,512]{1,0:T(8,128)(2,1)S(1)}, bf16[512,512]{1,0:T(8,128)(2,1)S(1)}, u32[]{:S(2)}, u32[]{:S(2)}) %collective-permute-start.19) | collective-permute-done | bytes 524320 | tf_op jit(solution)/shard_map/ppermute | solution.py:462
  113.4 3.1 %shard_map.134 = (f32[512,1024]{1,0:T(8,128)}, f32[512,1024]{1,0:T(8,128)}, bf16[512,512]{1,0:T(8,128)(2,1)S(1)}) custom-call(s32[39]{0:T(128)S(1)} %dynamic-slice_bitcast_fusion.row_ref, bf16[512,512]{1,0:T(8,128)(2,1)S(1)} %collective-permute-done.19.up_ref, bf16[512,512]{1,0:T(8,128)(2,1)S(1)} %collective-permute-done.20.dn_ref, ...), custom_call_target="tpu_custom_call" | custom-call | flops 4194304 | bytes 7340032 | tf_op jit(solution)/shard_map/pallas_call | solution.py:82
  116.5 2.7 %shard_map.123 = (bf16[384,4096]{1,0:T(8,128)(2,1)}, bf16[384,512]{1,0:T(8,128)(2,1)S(1)}, bf16[512,1024]{1,0:T(8,128)(2,1)S(1)}) custom-call(s32[39]{0:T(128)S(1)} %dynamic-slice_bitcast_fusion.row_ref, bf16[512,512]{1,0:T(8,128)(2,1)S(1)} %collective-permute-done.4.refs_0_.refs_1_, ...), custom_call_target="tpu_custom_call", output_to_operand_aliasing={{0}: (8, {})} | custom-call | flops 805306368 | bytes 4718592 | tf_op jit(solution)/shard_map/pallas_call | solution.py:82
  119.2 2.5 %shard_map.126 = (bf16[384,4096]{1,0:T(8,128)(2,1)}, bf16[384,512]{1,0:T(8,128)(2,1)S(1)}, bf16[512,1024]{1,0:T(8,128)(2,1)S(1)}) custom-call(s32[39]{0:T(128)S(1)} %dynamic-slice_bitcast_fusion.row_ref, bf16[512,512]{1,0:T(8,128)(2,1)S(1)} %collective-permute-done.9.refs_0_.refs_1_, ...), custom_call_target="tpu_custom_call", output_to_operand_aliasing={{0}: (8, {})} | custom-call | flops 805306368 | bytes 4718592 | tf_op jit(solution)/shard_map/pallas_call | solution.py:82
  122.3 3.1 %shard_map.138 = (f32[512,1024]{1,0:T(8,128)}, f32[512,1024]{1,0:T(8,128)}, bf16[512,512]{1,0:T(8,128)(2,1)S(1)}) custom-call(s32[39]{0:T(128)S(1)} %dynamic-slice_bitcast_fusion.row_ref, bf16[512,512]{1,0:T(8,128)(2,1)S(1)} %collective-permute-done.24.up_ref, ...), custom_call_target="tpu_custom_call", output_to_operand_aliasing={{0}: (7, {}), {1}: (8, {})} | custom-call | flops 4194304 | bytes 7340032 | tf_op jit(solution)/shard_map/pallas_call | solution.py:82
  125.4 2.5 %shard_map.129 = (bf16[384,4096]{1,0:T(8,128)(2,1)}, bf16[384,512]{1,0:T(8,128)(2,1)S(1)}, bf16[512,1024]{1,0:T(8,128)(2,1)S(1)}) custom-call(s32[39]{0:T(128)S(1)} %dynamic-slice_bitcast_fusion.row_ref, bf16[512,512]{1,0:T(8,128)(2,1)S(1)} %collective-permute-done.4.refs_0_.refs_1_, ...), custom_call_target="tpu_custom_call", output_to_operand_aliasing={{0}: (8, {})} | custom-call | flops 805306368 | bytes 4718592 | tf_op jit(solution)/shard_map/pallas_call | solution.py:82
  128.6 3.8 %shard_map.130 = (f32[384,1024]{1,0:T(8,128)S(1)}, f32[384,1024]{1,0:T(8,128)S(1)}) custom-call(s32[39]{0:T(128)S(1)} %dynamic-slice_bitcast_fusion.row_ref, bf16[512,1024]{1,0:T(8,128)(2,1)S(1)} %get-tuple-element.55.refs_0_, bf16[512,1024]{1,0:T(8,128)(2,1)S(1)} %get-tuple-element.56.refs_1_, bf16[512,1024]{1,0:T(8,128)(2,1)S(1)} %get-tuple-element.57.refs_2_, ...), custom_call_target="tpu_custom_call" | custom-call | flops 2415919104 | bytes 3145728 | tf_op jit(solution)/shard_map/pallas_call | solution.py:82
  136.3 2.4 %shard_map.131 = (f32[384,1024]{1,0:T(8,128)S(1)}, bf16[384,1024]{1,0:T(8,128)(2,1)}) custom-call(s32[39]{0:T(128)S(1)} %dynamic-slice_bitcast_fusion.row_ref, bf16[512,1024]{1,0:T(8,128)(2,1)S(1)} %get-tuple-element.54.refs_0_, bf16[384,4096]{1,0:T(8,128)(2,1)S(1)} %bitcast.35, ...), custom_call_target="tpu_custom_call" | custom-call | flops 805306368 | bytes 3145728 | tf_op jit(solution)/shard_map/pallas_call | solution.py:82
  142.0 6.4 %collective-permute-done.22 = bf16[512,512]{1,0:T(8,128)(2,1)} collective-permute-done((bf16[512,512]{1,0:T(8,128)(2,1)}, bf16[512,512]{1,0:T(8,128)(2,1)}, u32[]{:S(2)}, u32[]{:S(2)}) %collective-permute-start.22) | collective-permute-done | bytes 524320 | tf_op jit(solution)/shard_map/ppermute | solution.py:436
  151.7 7.5 %collective-permute-done.27 = bf16[512,512]{1,0:T(8,128)(2,1)} collective-permute-done((bf16[512,512]{1,0:T(8,128)(2,1)}, bf16[512,512]{1,0:T(8,128)(2,1)}, u32[]{:S(2)}, u32[]{:S(2)}) %collective-permute-start.27) | collective-permute-done | bytes 524320 | tf_op jit(solution)/shard_map/ppermute | solution.py:436
  159.3 8.5 %collective-permute-done.8.refs_1_ = bf16[384,512]{1,0:T(8,128)(2,1)S(1)} collective-permute-done((bf16[384,512]{1,0:T(8,128)(2,1)}, bf16[384,512]{1,0:T(8,128)(2,1)S(1)}, u32[]{:S(2)}, u32[]{:S(2)}) %collective-permute-start.8) | collective-permute-done | bytes 393248 | tf_op jit(solution)/shard_map/ppermute | solution.py:501
  167.8 8.4 %collective-permute-done.13.refs_2_ = bf16[384,512]{1,0:T(8,128)(2,1)S(1)} collective-permute-done((bf16[384,512]{1,0:T(8,128)(2,1)}, bf16[384,512]{1,0:T(8,128)(2,1)S(1)}, u32[]{:S(2)}, u32[]{:S(2)}) %collective-permute-start.13) | collective-permute-done | bytes 393248 | tf_op jit(solution)/shard_map/ppermute | solution.py:501
  176.2 7.4 %collective-permute-done.16.refs_3_ = bf16[384,512]{1,0:T(8,128)(2,1)S(1)} collective-permute-done((bf16[384,512]{1,0:T(8,128)(2,1)}, bf16[384,512]{1,0:T(8,128)(2,1)S(1)}, u32[]{:S(2)}, u32[]{:S(2)}) %collective-permute-start.16) | collective-permute-done | bytes 393248 | tf_op jit(solution)/shard_map/ppermute | solution.py:501
  183.6 4.2 %shard_map.136 = (bf16[384,4096]{1,0:T(8,128)(2,1)}, bf16[384,1024]{1,0:T(8,128)(2,1)}) custom-call(s32[39]{0:T(128)S(1)} %dynamic-slice_bitcast_fusion.row_ref, bf16[384,1024]{1,0:T(8,128)(2,1)S(1)} %collective-permute-done.3.refs_9_.refs_5_.piece_ref.refs_0_, bf16[384,512]{1,0:T(8,128)(2,1)S(1)} %collective-permute-done.8.refs_1_, ...), custom_call_target="tpu_custom_call", output_to_operand_aliasing={{0}: (7, {})} | custom-call | bytes 3145728 | tf_op jit(solution)/shard_map/pallas_call | solution.py:82
  (84 shorter events, 37.4 us)
Async XLA Ops:
  4.4 23.5 %copy-start.4 = (bf16[1,512,1024]{2,1,0:T(8,128)(2,1)S(1)}, bf16[1,512,1024]{2,1,0:T(8,128)(2,1)}, u32[]{:S(2)}) copy-start(bf16[1,512,1024]{2,1,0:T(8,128)(2,1)} %param.9) | copy-start | bytes 3145732
  5.0 31.5 %copy-start.1 = (bf16[1,384,4096]{2,1,0:T(8,128)(2,1)S(1)}, bf16[1,384,4096]{2,1,0:T(8,128)(2,1)}, u32[]{:S(2)}) copy-start(bf16[1,384,4096]{2,1,0:T(8,128)(2,1)} %param.8) | copy-start | bytes 9437188
  5.0 20.5 %collective-permute-start = (bf16[384,1024]{1,0:T(8,128)(2,1)S(1)}, bf16[384,1024]{1,0:T(8,128)(2,1)S(1)}, u32[]{:S(2)}, u32[]{:S(2)}) collective-permute-start(bf16[384,1024]{1,0:T(8,128)(2,1)S(1)} %shard_map.119), channel_id=1, source_target_pairs={{0,1},{1,0},{2,3},{3,2},{4,5},{5,4},{6,7},{7,6},{8,9},{9,8},{10,11... | collective-permute-start | bytes 2359304 | tf_op jit(solution)/shard_map/ppermute | solution.py:472
  26.1 10.4 %collective-permute-start.1 = (bf16[384,512]{1,0:T(8,128)(2,1)S(1)}, bf16[384,512]{1,0:T(8,128)(2,1)S(1)}, u32[]{:S(2)}, u32[]{:S(2)}) collective-permute-start(bf16[384,512]{1,0:T(8,128)(2,1)S(1)} %shard_map.120), channel_id=1, source_target_pairs={{0,1},{1,0},{2,3},{3,2},{4,5},{5,4},{6,7},{7,6},{8,9},{9,8},{10,11... | collective-permute-start | bytes 1179656 | tf_op jit(solution)/shard_map/ppermute | solution.py:476
  28.0 10.6 %collective-permute-start.6 = (bf16[512,512]{1,0:T(8,128)(2,1)S(1)}, bf16[512,512]{1,0:T(8,128)(2,1)S(1)}, u32[]{:S(2)}, u32[]{:S(2)}) collective-permute-start(bf16[512,512]{1,0:T(8,128)(2,1)S(1)} %get-tuple-element.78), channel_id=1, source_target_pairs={{2,4},{3,5},{4,2},{5,3},{10,12},{11,13},{12,10},{13,11},{18,20},{1... | collective-permute-start | bytes 1572872 | tf_op jit(solution)/shard_map/ppermute | solution.py:462
  28.7 17.3 %collective-permute-start.4 = (bf16[512,512]{1,0:T(8,128)(2,1)S(1)}, bf16[512,512]{1,0:T(8,128)(2,1)S(1)}, u32[]{:S(2)}, u32[]{:S(2)}) collective-permute-start(bf16[512,512]{1,0:T(8,128)(2,1)S(1)} %get-tuple-element.78), channel_id=1, source_target_pairs={{0,2},{1,3},{2,0},{3,1},{4,6},{5,7},{6,4},{7,5},{8,10},{9,11},{10,... | collective-permute-start | bytes 1572872 | tf_op jit(solution)/shard_map/ppermute | solution.py:462
  33.1 16.4 %collective-permute-start.7 = (bf16[512,512]{1,0:T(8,128)(2,1)S(1)}, bf16[512,512]{1,0:T(8,128)(2,1)S(1)}, u32[]{:S(2)}, u32[]{:S(2)}) collective-permute-start(bf16[512,512]{1,0:T(8,128)(2,1)S(1)} %get-tuple-element.77), channel_id=1, source_target_pairs={{2,4},{3,5},{4,2},{5,3},{10,12},{11,13},{12,10},{13,11},{18,20},{1... | collective-permute-start | bytes 1572872 | tf_op jit(solution)/shard_map/ppermute | solution.py:462
  33.8 23.4 %collective-permute-start.5 = (bf16[512,512]{1,0:T(8,128)(2,1)S(1)}, bf16[512,512]{1,0:T(8,128)(2,1)S(1)}, u32[]{:S(2)}, u32[]{:S(2)}) collective-permute-start(bf16[512,512]{1,0:T(8,128)(2,1)S(1)} %get-tuple-element.77), channel_id=1, source_target_pairs={{0,2},{1,3},{2,0},{3,1},{4,6},{5,7},{6,4},{7,5},{8,10},{9,11},{10,... | collective-permute-start | bytes 1572872 | tf_op jit(solution)/shard_map/ppermute | solution.py:462
  37.1 31.4 %collective-permute-start.2 = (bf16[384,1024]{1,0:T(8,128)(2,1)S(1)}, bf16[384,1024]{1,0:T(8,128)(2,1)S(1)}, u32[]{:S(2)}, u32[]{:S(2)}) collective-permute-start(bf16[384,1024]{1,0:T(8,128)(2,1)S(1)} %shard_map.121), channel_id=1, source_target_pairs={{0,1},{1,0},{2,3},{3,2},{4,5},{5,4},{6,7},{7,6},{8,9},{9,8},{10,11... | collective-permute-start | bytes 2359304 | tf_op jit(solution)/shard_map/ppermute | solution.py:480
  47.4 21.0 %collective-permute-start.9 = (bf16[512,512]{1,0:T(8,128)(2,1)S(1)}, bf16[512,512]{1,0:T(8,128)(2,1)S(1)}, u32[]{:S(2)}, u32[]{:S(2)}) collective-permute-start(bf16[512,512]{1,0:T(8,128)(2,1)S(1)} %get-tuple-element.44), channel_id=1, source_target_pairs={{0,2},{1,3},{2,0},{3,1},{4,6},{5,7},{6,4},{7,5},{8,10},{9,11},{10,... | collective-permute-start | bytes 1572872 | tf_op jit(solution)/shard_map/ppermute | solution.py:462
  48.8 19.6 %collective-permute-start.11 = (bf16[512,512]{1,0:T(8,128)(2,1)S(1)}, bf16[512,512]{1,0:T(8,128)(2,1)S(1)}, u32[]{:S(2)}, u32[]{:S(2)}) collective-permute-start(bf16[512,512]{1,0:T(8,128)(2,1)S(1)} %get-tuple-element.46), channel_id=1, source_target_pairs={{2,4},{3,5},{4,2},{5,3},{10,12},{11,13},{12,10},{13,11},{18,20},{1... | collective-permute-start | bytes 1572872 | tf_op jit(solution)/shard_map/ppermute | solution.py:462
  58.7 21.0 %collective-permute-start.10 = (bf16[512,512]{1,0:T(8,128)(2,1)S(1)}, bf16[512,512]{1,0:T(8,128)(2,1)S(1)}, u32[]{:S(2)}, u32[]{:S(2)}) collective-permute-start(bf16[512,512]{1,0:T(8,128)(2,1)S(1)} %get-tuple-element.45), channel_id=1, source_target_pairs={{0,2},{1,3},{2,0},{3,1},{4,6},{5,7},{6,4},{7,5},{8,10},{9,11},{10,... | collective-permute-start | bytes 1572872 | tf_op jit(solution)/shard_map/ppermute | solution.py:462
  60.0 19.6 %collective-permute-start.12 = (bf16[512,512]{1,0:T(8,128)(2,1)S(1)}, bf16[512,512]{1,0:T(8,128)(2,1)S(1)}, u32[]{:S(2)}, u32[]{:S(2)}) collective-permute-start(bf16[512,512]{1,0:T(8,128)(2,1)S(1)} %get-tuple-element.47), channel_id=1, source_target_pairs={{2,4},{3,5},{4,2},{5,3},{10,12},{11,13},{12,10},{13,11},{18,20},{1... | collective-permute-start | bytes 1572872 | tf_op jit(solution)/shard_map/ppermute | solution.py:462
  69.9 21.0 %collective-permute-start.14 = (bf16[512,512]{1,0:T(8,128)(2,1)S(1)}, bf16[512,512]{1,0:T(8,128)(2,1)S(1)}, u32[]{:S(2)}, u32[]{:S(2)}) collective-permute-start(bf16[512,512]{1,0:T(8,128)(2,1)S(1)} %get-tuple-element.50), channel_id=1, source_target_pairs={{0,2},{1,3},{2,0},{3,1},{4,6},{5,7},{6,4},{7,5},{8,10},{9,11},{10,... | collective-permute-start | bytes 1572872 | tf_op jit(solution)/shard_map/ppermute | solution.py:462
  72.0 18.9 %collective-permute-start.18 = (bf16[512,512]{1,0:T(8,128)(2,1)S(1)}, bf16[512,512]{1,0:T(8,128)(2,1)S(1)}, u32[]{:S(2)}, u32[]{:S(2)}) collective-permute-start(bf16[512,512]{1,0:T(8,128)(2,1)S(1)} %get-tuple-element.63), channel_id=1, source_target_pairs={{2,4},{3,5},{4,2},{5,3},{10,12},{11,13},{12,10},{13,11},{18,20},{1... | collective-permute-start | bytes 1572872 | tf_op jit(solution)/shard_map/ppermute | solution.py:462
  81.2 21.0 %collective-permute-start.15 = (bf16[512,512]{1,0:T(8,128)(2,1)S(1)}, bf16[512,512]{1,0:T(8,128)(2,1)S(1)}, u32[]{:S(2)}, u32[]{:S(2)}) collective-permute-start(bf16[512,512]{1,0:T(8,128)(2,1)S(1)} %get-tuple-element.51), channel_id=1, source_target_pairs={{0,2},{1,3},{2,0},{3,1},{4,6},{5,7},{6,4},{7,5},{8,10},{9,11},{10,... | collective-permute-start | bytes 1572872 | tf_op jit(solution)/shard_map/ppermute | solution.py:462
  83.2 18.9 %collective-permute-start.23 = (bf16[512,512]{1,0:T(8,128)(2,1)S(1)}, bf16[512,512]{1,0:T(8,128)(2,1)S(1)}, u32[]{:S(2)}, u32[]{:S(2)}) collective-permute-start(bf16[512,512]{1,0:T(8,128)(2,1)S(1)} %get-tuple-element.69), channel_id=1, source_target_pairs={{2,4},{3,5},{4,2},{5,3},{10,12},{11,13},{12,10},{13,11},{18,20},{1... | collective-permute-start | bytes 1572872 | tf_op jit(solution)/shard_map/ppermute | solution.py:462
  86.4 20.9 %collective-permute-start.3 = (bf16[384,1024]{1,0:T(8,128)(2,1)S(1)}, bf16[384,1024]{1,0:T(8,128)(2,1)S(1)}, u32[]{:S(2)}, u32[]{:S(2)}) collective-permute-start(bf16[384,1024]{1,0:T(8,128)(2,1)S(1)} %get-tuple-element.41), channel_id=1, source_target_pairs={{0,1},{1,0},{2,3},{3,2},{4,5},{5,4},{6,7},{7,6},{8,9},{9,8},{10,11... | collective-permute-start | bytes 2359304 | tf_op jit(solution)/shard_map/ppermute | solution.py:485
  92.4 20.9 %collective-permute-start.19 = (bf16[512,512]{1,0:T(8,128)(2,1)S(1)}, bf16[512,512]{1,0:T(8,128)(2,1)S(1)}, u32[]{:S(2)}, u32[]{:S(2)}) collective-permute-start(bf16[512,512]{1,0:T(8,128)(2,1)S(1)} %get-tuple-element.64), channel_id=1, source_target_pairs={{0,2},{1,3},{2,0},{3,1},{4,6},{5,7},{6,4},{7,5},{8,10},{9,11},{10,... | collective-permute-start | bytes 1572872 | tf_op jit(solution)/shard_map/ppermute | solution.py:462
  95.2 18.1 %collective-permute-start.20 = (bf16[512,512]{1,0:T(8,128)(2,1)S(1)}, bf16[512,512]{1,0:T(8,128)(2,1)S(1)}, u32[]{:S(2)}, u32[]{:S(2)}) collective-permute-start(bf16[512,512]{1,0:T(8,128)(2,1)S(1)} %get-tuple-element.65), channel_id=1, source_target_pairs={{2,4},{3,5},{4,2},{5,3},{10,12},{11,13},{12,10},{13,11},{18,20},{1... | collective-permute-start | bytes 1572872 | tf_op jit(solution)/shard_map/ppermute | solution.py:462
  103.7 18.6 %collective-permute-start.24 = (bf16[512,512]{1,0:T(8,128)(2,1)S(1)}, bf16[512,512]{1,0:T(8,128)(2,1)S(1)}, u32[]{:S(2)}, u32[]{:S(2)}) collective-permute-start(bf16[512,512]{1,0:T(8,128)(2,1)S(1)} %get-tuple-element.70), channel_id=1, source_target_pairs={{0,2},{1,3},{2,0},{3,1},{4,6},{5,7},{6,4},{7,5},{8,10},{9,11},{10,... | collective-permute-start | bytes 1572872 | tf_op jit(solution)/shard_map/ppermute | solution.py:462
  106.5 15.8 %collective-permute-start.25 = (bf16[512,512]{1,0:T(8,128)(2,1)S(1)}, bf16[512,512]{1,0:T(8,128)(2,1)S(1)}, u32[]{:S(2)}, u32[]{:S(2)}) collective-permute-start(bf16[512,512]{1,0:T(8,128)(2,1)S(1)} %get-tuple-element.71), channel_id=1, source_target_pairs={{2,4},{3,5},{4,2},{5,3},{10,12},{11,13},{12,10},{13,11},{18,20},{1... | collective-permute-start | bytes 1572872 | tf_op jit(solution)/shard_map/ppermute | solution.py:462
  116.5 16.0 %collective-permute-start.21 = (bf16[512,512]{1,0:T(8,128)(2,1)S(1)}, bf16[512,512]{1,0:T(8,128)(2,1)S(1)}, u32[]{:S(2)}, u32[]{:S(2)}) collective-permute-start(bf16[512,512]{1,0:T(8,128)(2,1)S(1)} %get-tuple-element.66.stepped_ref), channel_id=1, source_target_pairs={{0,8},{8,0},{16,24},{24,16},{1,9},{9,1},{17,25},{25,17},{2,10},{10... | collective-permute-start | bytes 1572872 | tf_op jit(solution)/shard_map/ppermute | solution.py:435
  125.3 9.6 %collective-permute-start.26 = (bf16[512,512]{1,0:T(8,128)(2,1)S(1)}, bf16[512,512]{1,0:T(8,128)(2,1)S(1)}, u32[]{:S(2)}, u32[]{:S(2)}) collective-permute-start(bf16[512,512]{1,0:T(8,128)(2,1)S(1)} %get-tuple-element.74.stepped_ref), channel_id=1, source_target_pairs={{0,8},{8,0},{16,24},{24,16},{1,9},{9,1},{17,25},{25,17},{2,10},{10... | collective-permute-start | bytes 1572872 | tf_op jit(solution)/shard_map/ppermute | solution.py:435
  133.4 15.0 %collective-permute-start.22 = (bf16[512,512]{1,0:T(8,128)(2,1)}, bf16[512,512]{1,0:T(8,128)(2,1)}, u32[]{:S(2)}, u32[]{:S(2)}) collective-permute-start(bf16[512,512]{1,0:T(8,128)(2,1)} %broadcast_select_fusion.1), channel_id=1, source_target_pairs={{0,16},{8,24},{16,0},{24,8},{1,17},{9,25},{17,1},{25,9},{2,18},{10... | collective-permute-start | bytes 1572872 | tf_op jit(solution)/shard_map/ppermute | solution.py:436
  135.8 23.4 %collective-permute-start.27 = (bf16[512,512]{1,0:T(8,128)(2,1)}, bf16[512,512]{1,0:T(8,128)(2,1)}, u32[]{:S(2)}, u32[]{:S(2)}) collective-permute-start(bf16[512,512]{1,0:T(8,128)(2,1)} %broadcast_select_fusion), channel_id=1, source_target_pairs={{0,16},{8,24},{16,0},{24,8},{1,17},{9,25},{17,1},{25,9},{2,18},{10... | collective-permute-start | bytes 1572872 | tf_op jit(solution)/shard_map/ppermute | solution.py:436
  138.7 44.9 %collective-permute-start.17 = (bf16[384,1024]{1,0:T(8,128)(2,1)}, bf16[384,1024]{1,0:T(8,128)(2,1)}, u32[]{:S(2)}, u32[]{:S(2)}) collective-permute-start(bf16[384,1024]{1,0:T(8,128)(2,1)} %get-tuple-element.61), channel_id=1, source_target_pairs={{0,1},{1,0},{2,3},{3,2},{4,5},{5,4},{6,7},{7,6},{8,9},{9,8},{10,11... | collective-permute-start | bytes 2359304 | tf_op jit(solution)/shard_map/ppermute | solution.py:506
  139.3 19.9 %copy-start.13 = (bf16[512,512]{1,0:T(8,128)(2,1)S(1)}, bf16[512,512]{1,0:T(8,128)(2,1)}, u32[]{:S(2)}) copy-start(bf16[512,512]{1,0:T(8,128)(2,1)} %copy-done.12) | copy-start | bytes 1572868
  140.0 27.8 %collective-permute-start.8 = (bf16[384,512]{1,0:T(8,128)(2,1)}, bf16[384,512]{1,0:T(8,128)(2,1)S(1)}, u32[]{:S(2)}, u32[]{:S(2)}) collective-permute-start(bf16[384,512]{1,0:T(8,128)(2,1)} %copy-done.8), channel_id=1, source_target_pairs={{0,1},{1,0},{2,3},{3,2},{4,5},{5,4},{6,7},{7,6},{8,9},{9,8},{10,11... | collective-permute-start | bytes 1179656 | tf_op jit(solution)/shard_map/ppermute | solution.py:501
  141.5 34.7 %collective-permute-start.13 = (bf16[384,512]{1,0:T(8,128)(2,1)}, bf16[384,512]{1,0:T(8,128)(2,1)S(1)}, u32[]{:S(2)}, u32[]{:S(2)}) collective-permute-start(bf16[384,512]{1,0:T(8,128)(2,1)} %copy-done.9), channel_id=1, source_target_pairs={{0,1},{1,0},{2,3},{3,2},{4,5},{5,4},{6,7},{7,6},{8,9},{9,8},{10,11... | collective-permute-start | bytes 1179656 | tf_op jit(solution)/shard_map/ppermute | solution.py:501
  148.4 35.1 %collective-permute-start.16 = (bf16[384,512]{1,0:T(8,128)(2,1)}, bf16[384,512]{1,0:T(8,128)(2,1)S(1)}, u32[]{:S(2)}, u32[]{:S(2)}) collective-permute-start(bf16[384,512]{1,0:T(8,128)(2,1)} %copy-done.10), channel_id=1, source_target_pairs={{0,1},{1,0},{2,3},{3,2},{4,5},{5,4},{6,7},{7,6},{8,9},{9,8},{10,11... | collective-permute-start | bytes 1179656 | tf_op jit(solution)/shard_map/ppermute | solution.py:501
  151.7 31.9 %copy-start.5 = (bf16[512,1024]{1,0:T(8,128)(2,1)S(1)}, bf16[512,1024]{1,0:T(8,128)(2,1)}, u32[]{:S(2)}) copy-start(bf16[512,1024]{1,0:T(8,128)(2,1)} %shard_map.135.refs_7_.refs_0_) | copy-start | bytes 3145732
  (12 other events, 42.9 us)

commit v3 on v2

--- a/solution.py
+++ b/solution.py
@@ -142,7 +142,7 @@
     )[0]
 
 
-def relay(plan, row, s, got, act, pieces, cot_own, cot_oth):
+def relay(plan, row, s, got, act, pieces, cot_own, cot_oth, after=()):
     (tokens, columns), rows = cot_own.shape, got["a"].shape[0]
     count = len(pieces)
 
@@ -150,8 +150,7 @@
         got_refs, act_refs = refs[0:2], refs[2:4]
         piece_refs = refs[4 : 4 + count]
         own_ref, oth_ref = refs[4 + count : 6 + count]
-        out_refs = refs[6 + count : 8 + count]
-        held = refs[8 + count]
+        out_refs, held = refs[-3:-1], refs[-1]
         for d, link in enumerate("ab"):
             add = row_ref[plan[f"add_{link}{s}"]]
             pos = row_ref[plan[f"pos_{link}{s}"]]
@@ -172,9 +171,10 @@
                 total = total + dot(held[...], oth_ref[...], TN)
                 out_refs[d][...] = (total + got_refs[d][...].astype(jnp.float32)).astype(jnp.bfloat16)
 
-    ins = [(got[link], whole(got[link])) for link in "ba"]
+    ins = [got[link].operand() for link in "ba"]
     ins += [(act, block((tokens, rows), plan[f"blk_{link}{s}"])) for link in "ab"]
     ins += [view.operand() for view in (*pieces, cot_own, cot_oth)]
+    ins += [(a, ANY) for a in after]
     out = struct((rows, columns), jnp.bfloat16)
     a, b = call(
         kernel,
@@ -213,13 +213,14 @@
     )[0]
 
 
-def project(plan, row, j, candidates, act, cot, cot_oth, xg_before, turn=None, after=()):
+def project(plan, row, j, candidates, act, cot, cot_oth, xg_before, turn=None, front=None, after=()):
     (tokens, columns), rows = cot.shape, candidates[0][0].shape[0]
-    parts = len(candidates[0])
     flat = [c for candidate in candidates for c in candidate]
-    n_w, n_c, extra = len(flat), len(cot_oth), turn is not None
-    widths = [c.shape[1] for c in candidates[0]]
-    starts = np.cumsum([0] + widths)
+    starts = np.cumsum([0] + [len(candidate) for candidate in candidates])
+    parts = max(len(candidate) for candidate in candidates)
+    n_w, n_c = len(flat), len(cot_oth)
+    ahead = 0 if front is None else front.count
+    width = ahead + rows + (0 if turn is None else rows)
 
     def kernel(row_ref, *refs):
         w_refs, cot_refs = refs[:n_w], refs[n_w : n_w + n_c]
@@ -229,14 +230,11 @@
 
             @pl.when(row_ref[plan[f"source{j}"]] == c)
             def _():
-                copies = [
-                    pltpu.make_async_copy(
-                        w_refs[c * parts + p],
-                        w_out.at[:, pl.ds(int(starts[p]), widths[p])],
-                        sems.at[p],
-                    )
-                    for p in range(parts)
-                ]
+                copies, at = [], 0
+                for p in range(starts[c], starts[c + 1]):
+                    to = w_out.at[:, pl.ds(at, flat[p].shape[1])]
+                    copies.append(pltpu.make_async_copy(w_refs[p], to, sems.at[len(copies)]))
+                    at += flat[p].shape[1]
                 for copy in copies:
                     copy.start()
                 for copy in copies:
@@ -246,20 +244,25 @@
         for ref, view in zip(cot_refs, cot_oth):
             total = total + dot(ref[...], w_out[:, at : at + view.count], NT)
             at += view.count
-        xg_oth[:, :rows] = total.astype(jnp.bfloat16)
-        if extra:
-            xg_oth[:, rows:] = refs[n_w + n_c + 1][...]
+        xg_oth[:, ahead : ahead + rows] = total.astype(jnp.bfloat16)
+        rest = list(refs[n_w + n_c + 1 :])
+        if front is not None:
+            xg_oth[:, :ahead] = rest.pop(0)[...]
+        if turn is not None:
+            xg_oth[:, ahead + rows :] = rest.pop(0)[...]
         xg_own[...] = dot(own_ref[...], w_out[...], NT).astype(jnp.bfloat16)
 
     ins = [(w, ANY) for w in flat] + [view.operand() for view in cot_oth] + [(cot, whole(cot))]
-    if extra:
+    if front is not None:
+        ins.append(front.operand())
+    if turn is not None:
         ins.append((act, block((tokens, rows), plan[f"pack{turn}"])))
     aliases = {}
     if xg_before is not None:
         aliases = {1 + len(ins): 0}
         ins.append((xg_before, ANY))
     ins += [(a, ANY) for a in after]
-    other = struct((tokens, rows * (1 + extra)), jnp.bfloat16)
+    other = struct((tokens, width), jnp.bfloat16)
     shard = struct((rows, columns), jnp.bfloat16)
     return call(
         kernel,
@@ -359,8 +362,9 @@
     )
 
 
-def adam(row, h, got, grad, weights, first, second, kept):
+def adam(row, h, got, grad, weights, first, second, kept, after=()):
     rows, columns = got["a"].shape
+    assert got["a"].start == 0
     steps = 4 if rows % 64 == 0 else 1
     size = rows // steps
 
@@ -377,12 +381,13 @@
 
     local = pl.BlockSpec((size, columns), lambda g, row: (g, 0))
     part = pl.BlockSpec((size, columns), lambda g, row: (g, h))
-    ins = [(got["a"], local), (got["b"], local)]
+    ins = [(got["a"].array, local), (got["b"].array, local)]
     ins += [(a, part) for a in (grad, weights, first, second)]
     aliases = {}
     if kept is not None:
         aliases = {1 + len(ins): 0, 2 + len(ins): 1}
         ins += [(a, ANY) for a in kept]
+    ins += [(a, ANY) for a in after]
     return call(
         kernel,
         row,
@@ -399,30 +404,36 @@
     )
 
 
-def average(mixing, h, stepped, chosen, kept, width):
+def average(scalars, h, stepped, others, kept, width, after):
     rows, columns = stepped.shape
     steps = 2 if rows % 32 == 0 else 1
     size = rows // steps
-
-    def kernel(mix_ref, stepped_ref, chosen_ref, *refs):
-        mix = mix_ref[0].astype(jnp.float32) / mix_denom
-        refs[-1][...] = (
-            (1.0 - mix) * stepped_ref[...].astype(jnp.float32)
-            + mix * chosen_ref[...].astype(jnp.float32)
-        ).astype(jnp.bfloat16)
+    count = len(others)
+
+    def kernel(scalar_ref, stepped_ref, *refs):
+        mix = scalar_ref[0].astype(jnp.float32) / mix_denom
+        for j in range(count):
+
+            @pl.when(scalar_ref[1] == j)
+            def _():
+                refs[-1][...] = (
+                    (1.0 - mix) * stepped_ref[...].astype(jnp.float32)
+                    + mix * refs[j][...].astype(jnp.float32)
+                ).astype(jnp.bfloat16)
 
     local = pl.BlockSpec((size, columns), lambda g, row: (g, 0))
     part = pl.BlockSpec((size, columns), lambda g, row: (g, h))
-    ins = [(stepped, local), (chosen, local)]
+    ins = [(a, local) for a in (stepped, *others)]
     if kept is not None:
         ins.append((kept, ANY))
-    return call(
-        kernel,
-        mixing,
+    ins += [(a, ANY) for a in after]
+    return call(
+        kernel,
+        scalars,
         ins,
         [(struct((rows, width), jnp.bfloat16), part)],
         grid=(steps,),
-        aliases={} if kept is None else {3: 0},
+        aliases={} if kept is None else {count + 2: 0},
         moved=6 * rows * columns,
     )[0]
 
@@ -430,13 +441,10 @@
 def partner_rows(stepped, partner, replica, n_rep):
     if n_rep != 4:
         gathered = lax.all_gather(stepped, "rep", axis=0, tiled=False)
-        return lax.dynamic_index_in_dim(gathered, partner[replica], 0, keepdims=False)
-    mask = partner[0]
-    near = lax.ppermute(stepped, "rep", [(r, r ^ 1) for r in range(4)])
-    far = lax.ppermute(
-        jnp.where(mask == 3, near, stepped), "rep", [(r, r ^ 2) for r in range(4)]
-    )
-    return jnp.where(mask == 1, near, far)
+        return [lax.dynamic_index_in_dim(gathered, partner[replica], 0, keepdims=False)]
+    far = lax.ppermute(stepped, "rep", [(r, r ^ 2) for r in range(4)])
+    core = [(r, r ^ 1) for r in range(4)]
+    return [lax.ppermute(stepped, "rep", core), far, lax.ppermute(far, "rep", core)]
 
 
 def per_device(
@@ -464,58 +472,76 @@
     def part(array, h):
         return View(array, h * size, size)
 
-    got = {}
-    for h in range(CHUNKS):
-        own = weights[:, h * size : (h + 1) * size]
-        got[1, h] = exchange({"a": own, "b": own})
-
-    opening = swap(pack(plan, row, rows, [part(cot, 0)], act, [0]))
-    cot_oth = [View(opening, 0, size)]
-    pieces = [View(opening, size, rows)]
+    opening = exchange({"a": weights, "b": weights})
+    got = {(1, h): {link: part(opening[link], h) for link in links} for h in range(CHUNKS)}
+
+    def arrivals(link, slot):
+        if slot == 1:
+            return [opening[link]]
+        return [got[slot, h][link].array for h in range(CHUNKS)]
+
+    def send(views, *turns, after=()):
+        return swap(pack(plan, row, rows, views, act, turns, after))
+
+    parcel = send([part(cot, 0)], 0)
+    cot_oth = [View(parcel, 0, size)]
+    pieces = [View(parcel, size, rows)]
     for h in range(1, CHUNKS):
-        cot_oth.append(part(swap(pack(plan, row, rows, [part(cot, h)], after=[opening])), 0))
-    latest = cot_oth[-1].array
-    for k in range(1, depth - 1, 2):
-        turns = list(range(k, min(k + 2, depth - 1)))
-        latest = swap(pack(plan, row, rows, [], act, turns, after=[latest]))
-        pieces += [View(latest, t * rows, rows) for t in range(len(turns))]
-    xg, both, shard = project(
-        plan, row, 0, [[weights]], act, cot, cot_oth, None, turn=depth - 1, after=[latest]
-    )
-    both = swap(both)
-    arrived, shards = [View(both, 0, rows)], [shard]
-    pieces.append(View(both, rows, rows))
-
+        cot_oth.append(part(send([part(cot, h)]), 0))
+    parcel = send([], *range(1, depth - 1), after=[parcel])
+    pieces += [View(parcel, k * rows, rows) for k in range(depth - 2)]
+
+    arrived, shards = [], []
+    xg, held = None, None
+
+    def shard_step(j, xg, held):
+        candidates = [[weights]]
+        if j > 0:
+            candidates = [arrivals(*source) for source in plan.sources[j]]
+        turn = depth - 1 if j == depth - 3 else None
+        xg, parcel, shard = project(plan, row, j, candidates, act, cot, cot_oth, xg, turn, held)
+        shards.append(shard)
+        if turn is None and j < depth - 1:
+            return xg, View(parcel, 0, parcel.shape[1])
+        parcel = swap(parcel)
+        arrived.extend(View(parcel, t * rows, rows) for t in range(j + 1 - len(arrived)))
+        if turn is not None:
+            pieces.append(View(parcel, parcel.shape[1] - rows, rows))
+        return xg, None
+
+    xg, held = shard_step(0, xg, held)
     for s in range(2, depth + 1):
+        if s > 2:
+            xg, held = shard_step(s - 2, xg, held)
+        if s == depth:
+            grad = own_gradient(plan, row, act, pieces[depth - 1], cot, cot_oth)
         for h in range(CHUNKS):
+            after = [bufs["a"]] if h > 0 else []
             bufs = relay(
-                plan, row, s, got[s - 1, h], act, pieces[: s - 1], part(cot, h), cot_oth[h]
+                plan, row, s, got[s - 1, h], act, pieces[: s - 1], part(cot, h), cot_oth[h], after
             )
-            got[s, h] = exchange(bufs)
-
-    for j in range(1, depth):
-        candidates = [
-            [got[slot, h][link] for h in range(CHUNKS)] for link, slot in plan.sources[j]
-        ]
-        xg, xg_oth, shard = project(plan, row, j, candidates, act, cot, cot_oth, xg)
-        arrived.append(View(swap(xg_oth), 0, rows))
-        shards.append(shard)
+            got[s, h] = {link: part(array, 0) for link, array in exchange(bufs).items()}
+    xg, held = shard_step(depth - 1, xg, held)
     early = list(range(depth - 1))
     sums = values(plan, row, early, shards[:-1], act, pieces, None, False)
     kv_own, kv_oth = values(plan, row, [depth - 1], shards[-1:], act, pieces, sums, True)
     kv_got = swap(kv_oth)
 
-    grad = own_gradient(plan, row, act, pieces[depth - 1], cot, cot_oth)
     replica = lax.axis_index("rep")
-    mixing = lax.dynamic_slice(mix_numerator, (replica,), (1,))
+    choice = (partner[0] if n_rep == 4 else jnp.int32(1)) - 1
+    scalars = jnp.stack([mix_numerator[replica], choice])
     moments, averaged = None, None
     for h in range(CHUNKS):
-        new_a, new_b, stepped = adam(row, h, got[depth, h], grad, weights, first, second, moments)
-        moments = (new_a, new_b)
-        chosen = partner_rows(stepped, partner, replica, n_rep)
+        after = [arrived[-1].array, kv_oth] if h == CHUNKS - 1 else []
+        *moments, stepped = adam(
+            row, h, got[depth, h], grad, weights, first, second, moments, after
+        )
+        others = partner_rows(stepped, partner, replica, n_rep)
         if h == CHUNKS - 1:
             x_grad, kv_out = finish(plan, row, xg, arrived, kv_own, kv_got, [averaged])
-        averaged = average(mixing, h, stepped, chosen, averaged, columns)
+        averaged = average(
+            scalars, h, stepped, others, averaged, columns, []
+        )
     return (
         kv_out[None],
         x_grad[None],

time: 190 us -> 151 us (0.79)
  waiting for transfers between devices: 101 us -> 56.1 us
  Pallas kernels: 42.4 us -> 49.8 us
  local copies, waits for them, and re-layouts: 5.27 us -> 11.9 us
  starting transfers between devices: 36.4 us -> 30.9 us
  other arithmetic: 3.03 us -> 0.72 us
    ppermute x16 -> x14, waiting for transfers between devices: 44.6 us -> 15.4 us  [exchange(): lax.ppermute(bufs[name], 'fsdp', links[name])]
    ppermute x11, waiting for transfers between devices: 56.7 us -> 40.7 us  [the longest x3 26.7 us: send(): return swap(pack(plan, row, rows, views, act, turns, after))]
    pallas_call x21, Pallas kernels: 42.4 us -> 49.8 us  [call(): pl.pallas_call(kernel, grid_spec=pltpu.PrefetchScalarGridSpec(num_scalar_...]
    unnamed x32 -> x30, local copies, waits for them, and re-layouts: 3.83 us -> 10.6 us
    ppermute x16 -> x14, starting transfers between devices: 24.3 us -> 20.5 us  [exchange(): lax.ppermute(bufs[name], 'fsdp', links[name])]
    select_n x4 -> x0, other arithmetic: 3.03 us -> none  [the longest x2 1.86 us: partner_rows(): jnp.where(mask == 3, near, stepped)]
    ppermute x11, starting transfers between devices: 11.5 us -> 9.36 us  [the longest x3 3.72 us: send(): return swap(pack(plan, row, rows, views, act, turns, after))]
  transfers between devices with their start and end apart: 28 -> 26, of which waited for: 15 -> 8; matrix products, arithmetic and copies ran while one was open for 2% -> 1% of each run, Pallas kernels for 19% -> 31%
where the time goes in v3:
time: 151 us; the launch traced here: 150 us
  waiting for transfers between devices  56.1 us (37%)
  Pallas kernels  49.8 us (33%)
  starting transfers between devices  30.9 us (20%)
  local copies, waits for them, and re-layouts  11.9 us (8%)
    pallas_call x21, Pallas kernels, call(): pl.pallas_call(kernel, grid_spec=pltpu.PrefetchScalarGridSpec(num_scalar_...  49.8 us
    ppermute x3, waiting for transfers between devices, send(): return swap(pack(plan, row, rows, views, act, turns, after))  26.7 us
    ppermute x14, starting transfers between devices, exchange(): lax.ppermute(bufs[name], 'fsdp', links[name])  20.5 us
    ppermute x14, waiting for transfers between devices, exchange(): lax.ppermute(bufs[name], 'fsdp', links[name])  15.4 us
    ppermute x2, waiting for transfers between devices, partner_rows(): far = lax.ppermute(stepped, 'rep', [(r, r ^ 2) for r in range(4)])  14 us
    unnamed x30, local copies, waits for them, and re-layouts  10.6 us
    ppermute x3, starting transfers between devices, send(): return swap(pack(plan, row, rows, views, act, turns, after))  3.72 us
    ppermute x2, starting transfers between devices, shard_step(): parcel = swap(parcel)  3.1 us
  transfers between devices with their start and end apart: 26, of which 8 were waited for; matrix products, arithmetic and copies ran while one was open for 1% of the time, Pallas kernels for 31%

profile of v3, /device:TPU:0, one launch (start us, length us, event | category | flops | bytes accessed | tf_op | source)
XLA Modules:
  0.0 150.4 jit_solution(14232358729629335223)
XLA Ops:
  1.4 5.8 %collective-permute-start = (bf16[512,1024]{1,0:T(8,128)(2,1)}, bf16[512,1024]{1,0:T(8,128)(2,1)S(1)}, u32[]{:S(2)}, u32[]{:S(2)}) collective-permute-start(bf16[512,1024]{1,0:T(8,128)(2,1)} %bitcast.48), channel_id=1, source_target_pairs={{0,2},{1,3},{2,0},{3,1},{4,6},{5,7},{6,4},{7,5},{8,10},{9,11},{10,... | collective-permute-start | bytes 3145736 | tf_op jit(solution)/shard_map/ppermute | solution.py:470
  7.9 1.9 %copy-done = bf16[1,384,4096]{2,1,0:T(8,128)(2,1)S(1)} copy-done((bf16[1,384,4096]{2,1,0:T(8,128)(2,1)S(1)}, bf16[1,384,4096]{2,1,0:T(8,128)(2,1)}, u32[]{:S(2)}) %copy-start) | copy-done | bytes 3145752
  11.5 1.6 %collective-permute-start.2 = (bf16[384,1024]{1,0:T(8,128)(2,1)S(1)}, bf16[384,1024]{1,0:T(8,128)(2,1)S(1)}, u32[]{:S(2)}, u32[]{:S(2)}) collective-permute-start(bf16[384,1024]{1,0:T(8,128)(2,1)S(1)} %shard_map.119), channel_id=1, source_target_pairs={{0,1},{1,0},{2,3},{3,2},{4,5},{5,4},{6,7},{7,6},{8,9},{9,8},{10,11... | collective-permute-start | bytes 2359304 | tf_op jit(solution)/shard_map/ppermute | solution.py:484
  14.3 17.8 %collective-permute-done.2.refs_1_.refs_2_.refs_4_.refs_6_.refs_7_.refs_3_.refs_8_.refs_0_ = bf16[384,1024]{1,0:T(8,128)(2,1)S(1)} collective-permute-done((bf16[384,1024]{1,0:T(8,128)(2,1)S(1)}, bf16[384,1024]{1,0:T(8,128)(2,1)S(1)}, u32[]{:S(2)}, u32[]{:S(2)}) %collective-permute-start.2) | collective-permute-done | bytes 786464 | tf_op jit(solution)/shard_map/ppermute | solution.py:484
  32.7 1.6 %collective-permute-start.7 = (bf16[384,1024]{1,0:T(8,128)(2,1)S(1)}, bf16[384,1024]{1,0:T(8,128)(2,1)S(1)}, u32[]{:S(2)}, u32[]{:S(2)}) collective-permute-start(bf16[384,1024]{1,0:T(8,128)(2,1)S(1)} %shard_map.124), channel_id=1, source_target_pairs={{0,1},{1,0},{2,3},{3,2},{4,5},{5,4},{6,7},{7,6},{8,9},{9,8},{10,11... | collective-permute-start | bytes 2359304 | tf_op jit(solution)/shard_map/ppermute | solution.py:484
  34.3 1.6 %shard_map.123 = (bf16[512,512]{1,0:T(8,128)(2,1)S(1)}, bf16[512,512]{1,0:T(8,128)(2,1)S(1)}) custom-call(s32[39]{0:T(128)S(1)} %dynamic-slice_bitcast_fusion.row_ref, bf16[512,1024]{1,0:T(8,128)(2,1)S(1)} %collective-permute-done.1.refs_1_.refs_0_, bf16[512,1024]{1,0:T(8,128)(2,1)S(1)} %collective-permute-done.refs_0_.refs_1_, ...), custom_call_target="tpu_custom_call" | custom-call | flops 805306368 | bytes 2883584 | tf_op jit(solution)/shard_map/pallas_call | solution.py:82
  37.5 3.0 %collective-permute-done.3.refs_2_.refs_3_.refs_6_.refs_7_.refs_5_.refs_4_.refs_1_.refs_8_ = bf16[384,512]{1,0:T(8,128)(2,1)S(1)} collective-permute-done((bf16[384,512]{1,0:T(8,128)(2,1)S(1)}, bf16[384,512]{1,0:T(8,128)(2,1)S(1)}, u32[]{:S(2)}, u32[]{:S(2)}) %collective-permute-start.3) | collective-permute-done | bytes 393248 | tf_op jit(solution)/shard_map/ppermute | solution.py:484
  40.5 1.5 %shard_map.126 = (bf16[512,512]{1,0:T(8,128)(2,1)S(1)}, bf16[512,512]{1,0:T(8,128)(2,1)S(1)}) custom-call(s32[39]{0:T(128)S(1)} %dynamic-slice_bitcast_fusion.row_ref, bf16[512,1024]{1,0:T(8,128)(2,1)S(1)} %collective-permute-done.1.refs_1_.refs_0_, bf16[512,1024]{1,0:T(8,128)(2,1)S(1)} %collective-permute-done.refs_0_.refs_1_, ...), custom_call_target="tpu_custom_call" | custom-call | flops 805306368 | bytes 2883584 | tf_op jit(solution)/shard_map/pallas_call | solution.py:82
  43.8 2.4 %shard_map.121 = (bf16[384,4096]{1,0:T(8,128)(2,1)}, bf16[384,512]{1,0:T(8,128)(2,1)S(1)}, bf16[512,1024]{1,0:T(8,128)(2,1)S(1)}) custom-call(s32[39]{0:T(128)S(1)} %dynamic-slice_bitcast_fusion.row_ref, bf16[512,1024]{1,0:T(8,128)(2,1)S(1)} %bitcast.49, ...), custom_call_target="tpu_custom_call" | custom-call | flops 805306368 | bytes 4718592 | tf_op jit(solution)/shard_map/pallas_call | solution.py:82
  46.2 2.5 %shard_map.122 = (bf16[384,4096]{1,0:T(8,128)(2,1)}, bf16[384,1536]{1,0:T(8,128)(2,1)S(1)}, bf16[512,1024]{1,0:T(8,128)(2,1)S(1)}) custom-call(s32[39]{0:T(128)S(1)} %dynamic-slice_bitcast_fusion.row_ref, bf16[512,1024]{1,0:T(8,128)(2,1)S(1)} %collective-permute-done.refs_0_.refs_1_, ...), custom_call_target="tpu_custom_call", output_to_operand_aliasing={{0}: (8, {})} | custom-call | flops 805306368 | bytes 4718592 | tf_op jit(solution)/shard_map/pallas_call | solution.py:82
  48.7 1.6 %collective-permute-start.4 = (bf16[384,1536]{1,0:T(8,128)(2,1)S(1)}, bf16[384,1536]{1,0:T(8,128)(2,1)S(1)}, u32[]{:S(2)}, u32[]{:S(2)}) collective-permute-start(bf16[384,1536]{1,0:T(8,128)(2,1)S(1)} %get-tuple-element.43), channel_id=1, source_target_pairs={{0,1},{1,0},{2,3},{3,2},{4,5},{5,4},{6,7},{7,6},{8,9},{9,8},{10,11... | collective-permute-start | bytes 3538952 | tf_op jit(solution)/shard_map/ppermute | solution.py:506
  51.5 5.9 %collective-permute-done.7.refs_5_.refs_7_.refs_8_.refs_3_.refs_4_.refs_6_ = bf16[384,1024]{1,0:T(8,128)(2,1)S(1)} collective-permute-done((bf16[384,1024]{1,0:T(8,128)(2,1)S(1)}, bf16[384,1024]{1,0:T(8,128)(2,1)S(1)}, u32[]{:S(2)}, u32[]{:S(2)}) %collective-permute-start.7) | collective-permute-done | bytes 786464 | tf_op jit(solution)/shard_map/ppermute | solution.py:484
  60.5 2.1 %collective-permute-start.11 = (bf16[512,512]{1,0:T(8,128)(2,1)S(1)}, bf16[512,512]{1,0:T(8,128)(2,1)S(1)}, u32[]{:S(2)}, u32[]{:S(2)}) collective-permute-start(bf16[512,512]{1,0:T(8,128)(2,1)S(1)} %get-tuple-element.49), channel_id=1, source_target_pairs={{0,2},{1,3},{2,0},{3,1},{4,6},{5,7},{6,4},{7,5},{8,10},{9,11},{10,... | collective-permute-start | bytes 1572872 | tf_op jit(solution)/shard_map/ppermute | solution.py:470
  63.9 2.5 %shard_map.128 = (bf16[384,4096]{1,0:T(8,128)(2,1)}, bf16[384,512]{1,0:T(8,128)(2,1)S(1)}, bf16[512,1024]{1,0:T(8,128)(2,1)S(1)}) custom-call(s32[39]{0:T(128)S(1)} %dynamic-slice_bitcast_fusion.row_ref, bf16[512,512]{1,0:T(8,128)(2,1)S(1)} %collective-permute-done.6.refs_1_.refs_0_, ...), custom_call_target="tpu_custom_call", output_to_operand_aliasing={{0}: (8, {})} | custom-call | flops 805306368 | bytes 4718592 | tf_op jit(solution)/shard_map/pallas_call | solution.py:82
  66.4 7.4 %collective-permute-done.8.refs_1_ = bf16[512,512]{1,0:T(8,128)(2,1)S(1)} collective-permute-done((bf16[512,512]{1,0:T(8,128)(2,1)S(1)}, bf16[512,512]{1,0:T(8,128)(2,1)S(1)}, u32[]{:S(2)}, u32[]{:S(2)}) %collective-permute-start.8) | collective-permute-done | bytes 524320 | tf_op jit(solution)/shard_map/ppermute | solution.py:470
  73.8 6.8 %collective-permute-done.11.refs_2_.refs_1_ = bf16[512,512]{1,0:T(8,128)(2,1)S(1)} collective-permute-done((bf16[512,512]{1,0:T(8,128)(2,1)S(1)}, bf16[512,512]{1,0:T(8,128)(2,1)S(1)}, u32[]{:S(2)}, u32[]{:S(2)}) %collective-permute-start.11) | collective-permute-done | bytes 524320 | tf_op jit(solution)/shard_map/ppermute | solution.py:470
  80.6 2.7 %shard_map.129 = (bf16[384,4096]{1,0:T(8,128)(2,1)}, bf16[384,1024]{1,0:T(8,128)(2,1)}, bf16[512,1024]{1,0:T(8,128)(2,1)S(1)}) custom-call(s32[39]{0:T(128)S(1)} %dynamic-slice_bitcast_fusion.row_ref, bf16[512,1024]{1,0:T(8,128)(2,1)S(1)} %collective-permute-done.refs_0_.refs_1_, ...), custom_call_target="tpu_custom_call", output_to_operand_aliasing={{0}: (8, {})} | custom-call | flops 805306368 | bytes 4718592 | tf_op jit(solution)/shard_map/pallas_call | solution.py:82
  83.3 1.6 %collective-permute-start.12 = (bf16[384,1024]{1,0:T(8,128)(2,1)}, bf16[384,1024]{1,0:T(8,128)(2,1)S(1)}, u32[]{:S(2)}, u32[]{:S(2)}) collective-permute-start(bf16[384,1024]{1,0:T(8,128)(2,1)} %get-tuple-element.53), channel_id=1, source_target_pairs={{0,1},{1,0},{2,3},{3,2},{4,5},{5,4},{6,7},{7,6},{8,9},{9,8},{10,11... | collective-permute-start | bytes 2359304 | tf_op jit(solution)/shard_map/ppermute | solution.py:506
  84.9 2.5 %shard_map.132 = (bf16[512,512]{1,0:T(8,128)(2,1)}, bf16[512,512]{1,0:T(8,128)(2,1)}) custom-call(s32[39]{0:T(128)S(1)} %dynamic-slice_bitcast_fusion.row_ref, bf16[512,512]{1,0:T(8,128)(2,1)S(1)} %collective-permute-done.14.refs_0_, bf16[512,512]{1,0:T(8,128)(2,1)S(1)} %collective-permute-done.8.refs_1_, bf16[384,4096]{1,0:T(8,128)(2,1)S(1)} %bitcast.25, ...), custom_call_target="tpu_custom_call" | custom-call | flops 805306368 | bytes 2883584 | tf_op jit(solution)/shard_map/pallas_call | solution.py:82
  88.9 3.4 %collective-permute-start.15 = (bf16[512,512]{1,0:T(8,128)(2,1)}, bf16[512,512]{1,0:T(8,128)(2,1)}, u32[]{:S(2)}, u32[]{:S(2)}) collective-permute-start(bf16[512,512]{1,0:T(8,128)(2,1)} %get-tuple-element.64.refs_9_), channel_id=1, source_target_pairs={{0,2},{1,3},{2,0},{3,1},{4,6},{5,7},{6,4},{7,5},{8,10},{9,11},{10,... | collective-permute-start | bytes 1572872 | tf_op jit(solution)/shard_map/ppermute | solution.py:470
  92.2 2.7 %shard_map.137 = (bf16[512,512]{1,0:T(8,128)(2,1)}, bf16[512,512]{1,0:T(8,128)(2,1)}) custom-call(s32[39]{0:T(128)S(1)} %dynamic-slice_bitcast_fusion.row_ref, bf16[512,512]{1,0:T(8,128)(2,1)S(1)} %collective-permute-done.20.refs_0_, bf16[512,512]{1,0:T(8,128)(2,1)S(1)} %collective-permute-done.11.refs_2_.refs_1_, bf16[384,4096]{1,0:T(8,128)(2,1)S(1)} %bitcast.27, ...), custom_call_target="tpu_custom_call" | custom-call | flops 805306368 | bytes 2883584 | tf_op jit(solution)/shard_map/pallas_call | solution.py:82
  97.1 1.8 %shard_map.133.grad_ref = f32[512,1024]{1,0:T(8,128)S(1)} custom-call(s32[39]{0:T(128)S(1)} %dynamic-slice_bitcast_fusion.row_ref, bf16[384,4096]{1,0:T(8,128)(2,1)S(1)} %bitcast.29, bf16[384,1536]{1,0:T(8,128)(2,1)S(1)} %collective-permute-done.4.refs_9_.refs_5_.piece_ref.refs_0_.refs_1_, bf16[384,1024]{1,0:T(8,128)(2,1)S(1)} %bitcast.46, ...), custom_call_target="tpu_custom_call" | custom-call | flops 805306368 | bytes 3670016 | tf_op jit(solution)/shard_map/pallas_call | solution.py:82
  98.9 3.8 %shard_map.130 = (f32[384,1024]{1,0:T(8,128)S(1)}, f32[384,1024]{1,0:T(8,128)S(1)}) custom-call(s32[39]{0:T(128)S(1)} %dynamic-slice_bitcast_fusion.row_ref, bf16[512,1024]{1,0:T(8,128)(2,1)S(1)} %get-tuple-element.55.refs_0_, bf16[512,1024]{1,0:T(8,128)(2,1)S(1)} %get-tuple-element.56.refs_1_, bf16[512,1024]{1,0:T(8,128)(2,1)S(1)} %get-tuple-element.57.refs_2_, ...), custom_call_target="tpu_custom_call" | custom-call | flops 2415919104 | bytes 3145728 | tf_op jit(solution)/shard_map/pallas_call | solution.py:82
  109.0 2.4 %shard_map.131 = (f32[384,1024]{1,0:T(8,128)S(1)}, bf16[384,1024]{1,0:T(8,128)(2,1)}) custom-call(s32[39]{0:T(128)S(1)} %dynamic-slice_bitcast_fusion.row_ref, bf16[512,1024]{1,0:T(8,128)(2,1)S(1)} %copy-done.12, bf16[384,4096]{1,0:T(8,128)(2,1)S(1)} %bitcast.33, ...), custom_call_target="tpu_custom_call" | custom-call | flops 805306368 | bytes 3145728 | tf_op jit(solution)/shard_map/pallas_call | solution.py:82
  111.5 4.5 %shard_map.134 = (f32[512,1024]{1,0:T(8,128)}, f32[512,1024]{1,0:T(8,128)}, bf16[512,512]{1,0:T(8,128)(2,1)}) custom-call(s32[39]{0:T(128)S(1)} %dynamic-slice_bitcast_fusion.row_ref, bf16[512,512]{1,0:T(8,128)(2,1)} %collective-permute-done.15.up_ref, bf16[512,512]{1,0:T(8,128)(2,1)} %collective-permute-done.16.dn_ref, ...), custom_call_target="tpu_custom_call" | custom-call | flops 4194304 | bytes 7340032 | tf_op jit(solution)/shard_map/pallas_call | solution.py:82
  116.0 1.5 %collective-permute-start.18 = (bf16[512,512]{1,0:T(8,128)(2,1)}, bf16[512,512]{1,0:T(8,128)(2,1)}, u32[]{:S(2)}, u32[]{:S(2)}) collective-permute-start(bf16[512,512]{1,0:T(8,128)(2,1)} %get-tuple-element.66.stepped_ref), channel_id=1, source_target_pairs={{0,16},{8,24},{16,0},{24,8},{1,17},{9,25},{17,1},{25,9},{2,18},{10... | collective-permute-start | bytes 1572872 | tf_op jit(solution)/shard_map/ppermute | solution.py:445
  117.5 4.4 %shard_map.138 = (f32[512,1024]{1,0:T(8,128)}, f32[512,1024]{1,0:T(8,128)}, bf16[512,512]{1,0:T(8,128)(2,1)}) custom-call(s32[39]{0:T(128)S(1)} %dynamic-slice_bitcast_fusion.row_ref, bf16[512,512]{1,0:T(8,128)(2,1)S(1)} %collective-permute-done.21.up_ref, ...), custom_call_target="tpu_custom_call", output_to_operand_aliasing={{0}: (7, {}), {1}: (8, {})} | custom-call | flops 4194304 | bytes 7340032 | tf_op jit(solution)/shard_map/pallas_call | solution.py:82
  123.4 7.7 %collective-permute-done.18.refs_1_ = bf16[512,512]{1,0:T(8,128)(2,1)} collective-permute-done((bf16[512,512]{1,0:T(8,128)(2,1)}, bf16[512,512]{1,0:T(8,128)(2,1)}, u32[]{:S(2)}, u32[]{:S(2)}) %collective-permute-start.18) | collective-permute-done | bytes 524320 | tf_op jit(solution)/shard_map/ppermute | solution.py:445
  131.6 6.3 %collective-permute-done.24.refs_1_ = bf16[512,512]{1,0:T(8,128)(2,1)} collective-permute-done((bf16[512,512]{1,0:T(8,128)(2,1)}, bf16[512,512]{1,0:T(8,128)(2,1)}, u32[]{:S(2)}, u32[]{:S(2)}) %collective-permute-start.24) | collective-permute-done | bytes 524320 | tf_op jit(solution)/shard_map/ppermute | solution.py:445
  139.3 2.9 %shard_map.135.refs_7_.refs_3_ = bf16[512,1024]{1,0:T(8,128)(2,1)} custom-call(s32[2]{0:T(128)S(1)} %pad_add_fusion.scalar_ref, bf16[512,512]{1,0:T(8,128)(2,1)} %get-tuple-element.66.stepped_ref, bf16[512,512]{1,0:T(8,128)(2,1)} %collective-permute-done.17.refs_0_, bf16[512,512]{1,0:T(8,128)(2,1)} %collective-permute-done.18.refs_1_, ...), custom_call_target="tpu_custom_call" | custom-call | bytes 1572864 | tf_op jit(solution)/shard_map/pallas_call | solution.py:82
  143.4 4.2 %shard_map.136 = (bf16[384,4096]{1,0:T(8,128)(2,1)}, bf16[384,1024]{1,0:T(8,128)(2,1)}) custom-call(s32[39]{0:T(128)S(1)} %dynamic-slice_bitcast_fusion.row_ref, bf16[384,1536]{1,0:T(8,128)(2,1)S(1)} %collective-permute-done.4.refs_9_.refs_5_.piece_ref.refs_0_.refs_1_, ...), custom_call_target="tpu_custom_call", output_to_operand_aliasing={{0}: (7, {})} | custom-call | bytes 3145728 | tf_op jit(solution)/shard_map/pallas_call | solution.py:82
  147.5 2.9 %shard_map.139 = bf16[512,1024]{1,0:T(8,128)(2,1)} custom-call(s32[2]{0:T(128)S(1)} %pad_add_fusion.scalar_ref, bf16[512,512]{1,0:T(8,128)(2,1)} %get-tuple-element.74.stepped_ref, bf16[512,512]{1,0:T(8,128)(2,1)} %collective-permute-done.23.refs_0_, bf16[512,512]{1,0:T(8,128)(2,1)} %collective-permute-done.24.refs_1_, ...), custom_call_target="tpu_custom_call", output_to_operand_aliasing={{}: (5, {})} | custom-call | bytes 1572864 | tf_op jit(solution)/shard_map/pallas_call | solution.py:82
  (74 shorter events, 28.6 us)
Async XLA Ops:
  0.6 33.6 %collective-permute-start.1 = (bf16[512,1024]{1,0:T(8,128)(2,1)}, bf16[512,1024]{1,0:T(8,128)(2,1)S(1)}, u32[]{:S(2)}, u32[]{:S(2)}) collective-permute-start(bf16[512,1024]{1,0:T(8,128)(2,1)} %bitcast.47), channel_id=1, source_target_pairs={{2,4},{3,5},{4,2},{5,3},{10,12},{11,13},{12,10},{13,11},{18,20},{1... | collective-permute-start | bytes 3145736 | tf_op jit(solution)/shard_map/ppermute | solution.py:470
  1.4 32.9 %collective-permute-start = (bf16[512,1024]{1,0:T(8,128)(2,1)}, bf16[512,1024]{1,0:T(8,128)(2,1)S(1)}, u32[]{:S(2)}, u32[]{:S(2)}) collective-permute-start(bf16[512,1024]{1,0:T(8,128)(2,1)} %bitcast.48), channel_id=1, source_target_pairs={{0,2},{1,3},{2,0},{3,1},{4,6},{5,7},{6,4},{7,5},{8,10},{9,11},{10,... | collective-permute-start | bytes 3145736 | tf_op jit(solution)/shard_map/ppermute | solution.py:470
  10.9 21.2 %copy-start.1 = (bf16[1,384,4096]{2,1,0:T(8,128)(2,1)S(1)}, bf16[1,384,4096]{2,1,0:T(8,128)(2,1)}, u32[]{:S(2)}) copy-start(bf16[1,384,4096]{2,1,0:T(8,128)(2,1)} %param.8) | copy-start | bytes 9437188
  11.5 20.5 %collective-permute-start.2 = (bf16[384,1024]{1,0:T(8,128)(2,1)S(1)}, bf16[384,1024]{1,0:T(8,128)(2,1)S(1)}, u32[]{:S(2)}, u32[]{:S(2)}) collective-permute-start(bf16[384,1024]{1,0:T(8,128)(2,1)S(1)} %shard_map.119), channel_id=1, source_target_pairs={{0,1},{1,0},{2,3},{3,2},{4,5},{5,4},{6,7},{7,6},{8,9},{9,8},{10,11... | collective-permute-start | bytes 2359304 | tf_op jit(solution)/shard_map/ppermute | solution.py:484
  13.7 26.8 %collective-permute-start.3 = (bf16[384,512]{1,0:T(8,128)(2,1)S(1)}, bf16[384,512]{1,0:T(8,128)(2,1)S(1)}, u32[]{:S(2)}, u32[]{:S(2)}) collective-permute-start(bf16[384,512]{1,0:T(8,128)(2,1)S(1)} %shard_map.120), channel_id=1, source_target_pairs={{0,1},{1,0},{2,3},{3,2},{4,5},{5,4},{6,7},{7,6},{8,9},{9,8},{10,11... | collective-permute-start | bytes 1179656 | tf_op jit(solution)/shard_map/ppermute | solution.py:484
  32.7 24.7 %collective-permute-start.7 = (bf16[384,1024]{1,0:T(8,128)(2,1)S(1)}, bf16[384,1024]{1,0:T(8,128)(2,1)S(1)}, u32[]{:S(2)}, u32[]{:S(2)}) collective-permute-start(bf16[384,1024]{1,0:T(8,128)(2,1)S(1)} %shard_map.124), channel_id=1, source_target_pairs={{0,1},{1,0},{2,3},{3,2},{4,5},{5,4},{6,7},{7,6},{8,9},{9,8},{10,11... | collective-permute-start | bytes 2359304 | tf_op jit(solution)/shard_map/ppermute | solution.py:484
  35.8 12.8 %collective-permute-start.5 = (bf16[512,512]{1,0:T(8,128)(2,1)S(1)}, bf16[512,512]{1,0:T(8,128)(2,1)S(1)}, u32[]{:S(2)}, u32[]{:S(2)}) collective-permute-start(bf16[512,512]{1,0:T(8,128)(2,1)S(1)} %get-tuple-element.44), channel_id=1, source_target_pairs={{2,4},{3,5},{4,2},{5,3},{10,12},{11,13},{12,10},{13,11},{18,20},{1... | collective-permute-start | bytes 1572872 | tf_op jit(solution)/shard_map/ppermute | solution.py:470
  36.5 7.2 %copy-start.3 = (bf16[1,512,1024]{2,1,0:T(8,128)(2,1)S(1)}, bf16[1,512,1024]{2,1,0:T(8,128)(2,1)}, u32[]{:S(2)}) copy-start(bf16[1,512,1024]{2,1,0:T(8,128)(2,1)} %param.9) | copy-start | bytes 3145732
  36.5 14.9 %collective-permute-start.6 = (bf16[512,512]{1,0:T(8,128)(2,1)S(1)}, bf16[512,512]{1,0:T(8,128)(2,1)S(1)}, u32[]{:S(2)}, u32[]{:S(2)}) collective-permute-start(bf16[512,512]{1,0:T(8,128)(2,1)S(1)} %get-tuple-element.45.refs_7_), channel_id=1, source_target_pairs={{0,2},{1,3},{2,0},{3,1},{4,6},{5,7},{6,4},{7,5},{8,10},{9,11},{10,... | collective-permute-start | bytes 1572872 | tf_op jit(solution)/shard_map/ppermute | solution.py:470
  42.0 16.9 %collective-permute-start.9 = (bf16[512,512]{1,0:T(8,128)(2,1)S(1)}, bf16[512,512]{1,0:T(8,128)(2,1)S(1)}, u32[]{:S(2)}, u32[]{:S(2)}) collective-permute-start(bf16[512,512]{1,0:T(8,128)(2,1)S(1)} %get-tuple-element.47), channel_id=1, source_target_pairs={{2,4},{3,5},{4,2},{5,3},{10,12},{11,13},{12,10},{13,11},{18,20},{1... | collective-permute-start | bytes 1572872 | tf_op jit(solution)/shard_map/ppermute | solution.py:470
  42.7 16.2 %collective-permute-start.10 = (bf16[512,512]{1,0:T(8,128)(2,1)S(1)}, bf16[512,512]{1,0:T(8,128)(2,1)S(1)}, u32[]{:S(2)}, u32[]{:S(2)}) collective-permute-start(bf16[512,512]{1,0:T(8,128)(2,1)S(1)} %get-tuple-element.48), channel_id=1, source_target_pairs={{0,2},{1,3},{2,0},{3,1},{4,6},{5,7},{6,4},{7,5},{8,10},{9,11},{10,... | collective-permute-start | bytes 1572872 | tf_op jit(solution)/shard_map/ppermute | solution.py:470
  48.7 47.0 %collective-permute-start.4 = (bf16[384,1536]{1,0:T(8,128)(2,1)S(1)}, bf16[384,1536]{1,0:T(8,128)(2,1)S(1)}, u32[]{:S(2)}, u32[]{:S(2)}) collective-permute-start(bf16[384,1536]{1,0:T(8,128)(2,1)S(1)} %get-tuple-element.43), channel_id=1, source_target_pairs={{0,1},{1,0},{2,3},{3,2},{4,5},{5,4},{6,7},{7,6},{8,9},{9,8},{10,11... | collective-permute-start | bytes 3538952 | tf_op jit(solution)/shard_map/ppermute | solution.py:506
  58.9 14.9 %collective-permute-start.8 = (bf16[512,512]{1,0:T(8,128)(2,1)S(1)}, bf16[512,512]{1,0:T(8,128)(2,1)S(1)}, u32[]{:S(2)}, u32[]{:S(2)}) collective-permute-start(bf16[512,512]{1,0:T(8,128)(2,1)S(1)} %get-tuple-element.46.refs_8_), channel_id=1, source_target_pairs={{0,2},{1,3},{2,0},{3,1},{4,6},{5,7},{6,4},{7,5},{8,10},{9,11},{10,... | collective-permute-start | bytes 1572872 | tf_op jit(solution)/shard_map/ppermute | solution.py:470
  60.5 20.1 %collective-permute-start.11 = (bf16[512,512]{1,0:T(8,128)(2,1)S(1)}, bf16[512,512]{1,0:T(8,128)(2,1)S(1)}, u32[]{:S(2)}, u32[]{:S(2)}) collective-permute-start(bf16[512,512]{1,0:T(8,128)(2,1)S(1)} %get-tuple-element.49), channel_id=1, source_target_pairs={{0,2},{1,3},{2,0},{3,1},{4,6},{5,7},{6,4},{7,5},{8,10},{9,11},{10,... | collective-permute-start | bytes 1572872 | tf_op jit(solution)/shard_map/ppermute | solution.py:470
  62.5 22.4 %collective-permute-start.14 = (bf16[512,512]{1,0:T(8,128)(2,1)S(1)}, bf16[512,512]{1,0:T(8,128)(2,1)S(1)}, u32[]{:S(2)}, u32[]{:S(2)}) collective-permute-start(bf16[512,512]{1,0:T(8,128)(2,1)S(1)} %get-tuple-element.63), channel_id=1, source_target_pairs={{2,4},{3,5},{4,2},{5,3},{10,12},{11,13},{12,10},{13,11},{18,20},{1... | collective-permute-start | bytes 1572872 | tf_op jit(solution)/shard_map/ppermute | solution.py:470
  63.2 29.0 %collective-permute-start.20 = (bf16[512,512]{1,0:T(8,128)(2,1)S(1)}, bf16[512,512]{1,0:T(8,128)(2,1)S(1)}, u32[]{:S(2)}, u32[]{:S(2)}) collective-permute-start(bf16[512,512]{1,0:T(8,128)(2,1)S(1)} %get-tuple-element.69), channel_id=1, source_target_pairs={{2,4},{3,5},{4,2},{5,3},{10,12},{11,13},{12,10},{13,11},{18,20},{1... | collective-permute-start | bytes 1572872 | tf_op jit(solution)/shard_map/ppermute | solution.py:470
  83.3 4.1 %copy-start.11 = (bf16[512,1024]{1,0:T(8,128)(2,1)}, bf16[512,1024]{1,0:T(8,128)(2,1)S(1)}, u32[]{:S(2)}) copy-start(bf16[512,1024]{1,0:T(8,128)(2,1)S(1)} %get-tuple-element.54.refs_0_) | copy-start | bytes 3145732
  83.3 34.2 %collective-permute-start.12 = (bf16[384,1024]{1,0:T(8,128)(2,1)}, bf16[384,1024]{1,0:T(8,128)(2,1)S(1)}, u32[]{:S(2)}, u32[]{:S(2)}) collective-permute-start(bf16[384,1024]{1,0:T(8,128)(2,1)} %get-tuple-element.53), channel_id=1, source_target_pairs={{0,1},{1,0},{2,3},{3,2},{4,5},{5,4},{6,7},{7,6},{8,9},{9,8},{10,11... | collective-permute-start | bytes 2359304 | tf_op jit(solution)/shard_map/ppermute | solution.py:506
  87.4 24.1 %collective-permute-start.16 = (bf16[512,512]{1,0:T(8,128)(2,1)}, bf16[512,512]{1,0:T(8,128)(2,1)}, u32[]{:S(2)}, u32[]{:S(2)}) collective-permute-start(bf16[512,512]{1,0:T(8,128)(2,1)} %get-tuple-element.65), channel_id=1, source_target_pairs={{2,4},{3,5},{4,2},{5,3},{10,12},{11,13},{12,10},{13,11},{18,20},{1... | collective-permute-start | bytes 1572872 | tf_op jit(solution)/shard_map/ppermute | solution.py:470
  88.9 22.6 %collective-permute-start.15 = (bf16[512,512]{1,0:T(8,128)(2,1)}, bf16[512,512]{1,0:T(8,128)(2,1)}, u32[]{:S(2)}, u32[]{:S(2)}) collective-permute-start(bf16[512,512]{1,0:T(8,128)(2,1)} %get-tuple-element.64.refs_9_), channel_id=1, source_target_pairs={{0,2},{1,3},{2,0},{3,1},{4,6},{5,7},{6,4},{7,5},{8,10},{9,11},{10,... | collective-permute-start | bytes 1572872 | tf_op jit(solution)/shard_map/ppermute | solution.py:470
  94.9 22.6 %collective-permute-start.21 = (bf16[512,512]{1,0:T(8,128)(2,1)}, bf16[512,512]{1,0:T(8,128)(2,1)S(1)}, u32[]{:S(2)}, u32[]{:S(2)}) collective-permute-start(bf16[512,512]{1,0:T(8,128)(2,1)} %get-tuple-element.70), channel_id=1, source_target_pairs={{0,2},{1,3},{2,0},{3,1},{4,6},{5,7},{6,4},{7,5},{8,10},{9,11},{10,... | collective-permute-start | bytes 1572872 | tf_op jit(solution)/shard_map/ppermute | solution.py:470
  95.7 21.8 %collective-permute-start.22 = (bf16[512,512]{1,0:T(8,128)(2,1)}, bf16[512,512]{1,0:T(8,128)(2,1)}, u32[]{:S(2)}, u32[]{:S(2)}) collective-permute-start(bf16[512,512]{1,0:T(8,128)(2,1)} %get-tuple-element.71), channel_id=1, source_target_pairs={{2,4},{3,5},{4,2},{5,3},{10,12},{11,13},{12,10},{13,11},{18,20},{1... | collective-permute-start | bytes 1572872 | tf_op jit(solution)/shard_map/ppermute | solution.py:470
  109.0 2.4 %copy-start.6 = (f32[1,512,1024]{2,1,0:T(8,128)S(1)}, f32[1,512,1024]{2,1,0:T(8,128)}, u32[]{:S(2)}) copy-start(f32[1,512,1024]{2,1,0:T(8,128)} %param.12) | copy-start | bytes 6291460
  116.0 15.2 %collective-permute-start.18 = (bf16[512,512]{1,0:T(8,128)(2,1)}, bf16[512,512]{1,0:T(8,128)(2,1)}, u32[]{:S(2)}, u32[]{:S(2)}) collective-permute-start(bf16[512,512]{1,0:T(8,128)(2,1)} %get-tuple-element.66.stepped_ref), channel_id=1, source_target_pairs={{0,16},{8,24},{16,0},{24,8},{1,17},{9,25},{17,1},{25,9},{2,18},{10... | collective-permute-start | bytes 1572872 | tf_op jit(solution)/shard_map/ppermute | solution.py:445
  117.5 20.4 %copy-start.13 = (s32[4]{0:T(128)S(1)}, s32[4]{0:T(128)}, u32[]{:S(2)}) copy-start(s32[4]{0:T(128)} %param.14) | copy-start | bytes 52
  117.5 21.0 %copy-start.14 = (s32[4]{0:T(128)S(1)}, s32[4]{0:T(128)}, u32[]{:S(2)}) copy-start(s32[4]{0:T(128)} %param.13) | copy-start | bytes 52
  121.9 16.0 %collective-permute-start.24 = (bf16[512,512]{1,0:T(8,128)(2,1)}, bf16[512,512]{1,0:T(8,128)(2,1)}, u32[]{:S(2)}, u32[]{:S(2)}) collective-permute-start(bf16[512,512]{1,0:T(8,128)(2,1)} %get-tuple-element.74.stepped_ref), channel_id=1, source_target_pairs={{0,16},{8,24},{16,0},{24,8},{1,17},{9,25},{17,1},{25,9},{2,18},{10... | collective-permute-start | bytes 1572872 | tf_op jit(solution)/shard_map/ppermute | solution.py:445
  122.4 19.8 %collective-permute-start.13 = (bf16[384,1024]{1,0:T(8,128)(2,1)}, bf16[384,1024]{1,0:T(8,128)(2,1)}, u32[]{:S(2)}, u32[]{:S(2)}) collective-permute-start(bf16[384,1024]{1,0:T(8,128)(2,1)} %get-tuple-element.61.refs_3_), channel_id=1, source_target_pairs={{0,1},{1,0},{2,3},{3,2},{4,5},{5,4},{6,7},{7,6},{8,9},{9,8},{10,11... | collective-permute-start | bytes 2359304 | tf_op jit(solution)/shard_map/ppermute | solution.py:528
  123.4 15.9 %collective-permute-start.17 = (bf16[512,512]{1,0:T(8,128)(2,1)}, bf16[512,512]{1,0:T(8,128)(2,1)}, u32[]{:S(2)}, u32[]{:S(2)}) collective-permute-start(bf16[512,512]{1,0:T(8,128)(2,1)} %get-tuple-element.66.stepped_ref), channel_id=1, source_target_pairs={{0,8},{8,0},{16,24},{24,16},{1,9},{9,1},{17,25},{25,17},{2,10},{10... | collective-permute-start | bytes 1572872 | tf_op jit(solution)/shard_map/ppermute | solution.py:447
  131.1 8.1 %collective-permute-start.19 = (bf16[512,512]{1,0:T(8,128)(2,1)}, bf16[512,512]{1,0:T(8,128)(2,1)}, u32[]{:S(2)}, u32[]{:S(2)}) collective-permute-start(bf16[512,512]{1,0:T(8,128)(2,1)} %collective-permute-done.18.refs_1_), channel_id=1, source_target_pairs={{0,8},{8,0},{16,24},{24,16},{1,9},{9,1},{17,25},{25,17},{2,10},{10... | collective-permute-start | bytes 1572872 | tf_op jit(solution)/shard_map/ppermute | solution.py:447
  131.1 16.4 %collective-permute-start.23 = (bf16[512,512]{1,0:T(8,128)(2,1)}, bf16[512,512]{1,0:T(8,128)(2,1)}, u32[]{:S(2)}, u32[]{:S(2)}) collective-permute-start(bf16[512,512]{1,0:T(8,128)(2,1)} %get-tuple-element.74.stepped_ref), channel_id=1, source_target_pairs={{0,8},{8,0},{16,24},{24,16},{1,9},{9,1},{17,25},{25,17},{2,10},{10... | collective-permute-start | bytes 1572872 | tf_op jit(solution)/shard_map/ppermute | solution.py:447
  137.9 9.6 %collective-permute-start.25 = (bf16[512,512]{1,0:T(8,128)(2,1)}, bf16[512,512]{1,0:T(8,128)(2,1)}, u32[]{:S(2)}, u32[]{:S(2)}) collective-permute-start(bf16[512,512]{1,0:T(8,128)(2,1)} %collective-permute-done.24.refs_1_), channel_id=1, source_target_pairs={{0,8},{8,0},{16,24},{24,16},{1,9},{9,1},{17,25},{25,17},{2,10},{10... | collective-permute-start | bytes 1572872 | tf_op jit(solution)/shard_map/ppermute | solution.py:447
  (9 other events, 13.0 us)

commit v4 on v3

--- a/solution.py
+++ b/solution.py
@@ -30,10 +30,10 @@
 
 
 class Plan:
-    def __init__(self, n):
+    def __init__(self, n_rep, n):
         self.depth = depth = n // 2
         self.columns = {}
-        self.rows = [[] for _ in range(n)]
+        self.rows = [[] for _ in range(n_rep * n)]
         order = [
             sorted(range(depth), key=lambda q: (-abs(q - z), (q < z) != (2 * z >= depth)))
             for z in range(depth)
@@ -48,9 +48,11 @@
             for j, (_, source) in enumerate(arrivals[z], 1):
                 self.sources[j].add(source)
         self.sources = [sorted(s) for s in self.sources]
-        for i in range(n):
+        for device in range(n_rep * n):
+            replica, i = divmod(device, n)
             z, x = divmod(i, 2)
-            put = functools.partial(self._put, i)
+            put = functools.partial(self._put, device)
+            put("replica", replica)
             put("own", i)
             for k in range(depth):
                 put(f"pack{k}", 2 * order[z][k] + 1 - x)
@@ -78,11 +80,12 @@
         return self.columns[name]
 
 
-def call(kernel, row, ins, outs, grid=(1,), aliases=None, scratch=(), flops=0, moved=0, vmem=24):
+def call(kernel, row, ins, outs, grid=(1,), aliases=None, scratch=(), flops=0, moved=0, vmem=16):
+    scalars = row if isinstance(row, tuple) else (row,)
     return pl.pallas_call(
         kernel,
         grid_spec=pltpu.PrefetchScalarGridSpec(
-            num_scalar_prefetch=1,
+            num_scalar_prefetch=len(scalars),
             grid=grid,
             in_specs=[spec for _, spec in ins],
             out_specs=[spec for _, spec in outs],
@@ -92,7 +95,7 @@
         input_output_aliases=aliases or {},
         compiler_params=pltpu.CompilerParams(vmem_limit_bytes=vmem * MIB),
         cost_estimate=pl.CostEstimate(flops=flops, bytes_accessed=moved, transcendentals=0),
-    )(row, *[array for array, _ in ins])
+    )(*scalars, *[array for array, _ in ins])
 
 
 def whole(array):
@@ -277,21 +280,24 @@
         scratch=[pltpu.SemaphoreType.DMA((parts,))],
         flops=4 * tokens * rows * columns,
         moved=12 * tokens * columns,
-    )
-
-
-def values(plan, row, turns, shards, act, pieces, kept, last):
+        vmem=20,
+    )
+
+
+def values(plan, row, turns, shards, act, pieces, kept, behind=None):
     rows, columns = shards[0].shape
     tokens = act.shape[0]
     count, n_p = len(turns), len(pieces)
+    extra = 0 if behind is None else behind.count
 
     def kernel(row_ref, *refs):
         w_refs, act_refs = refs[:count], refs[count : 2 * count]
         piece_refs = refs[2 * count : 2 * count + n_p]
+        rest = list(refs[2 * count + n_p : -3])
         own_out, oth_out, held = refs[-3:]
         own = oth = 0.0
         if kept is not None:
-            own, oth = refs[2 * count + n_p][...], refs[2 * count + n_p + 1][...]
+            own, oth = rest.pop(0)[...], rest.pop(0)[...]
         for t, j in enumerate(turns):
             for p in range(n_p):
 
@@ -301,7 +307,9 @@
 
             oth = oth + dot(held[...], w_refs[t][...])
             own = own + dot(act_refs[t][...], w_refs[t][...])
-        oth_out[...] = oth.astype(oth_out.dtype)
+        oth_out[:, :columns] = oth.astype(oth_out.dtype)
+        if behind is not None:
+            oth_out[:, columns:] = rest.pop(0)[...]
         own_out[...] = own
 
     ins = [(w, whole(w)) for w in shards]
@@ -309,8 +317,10 @@
     ins += [p.operand() for p in pieces]
     if kept is not None:
         ins += [(k, whole(k)) for k in kept]
+    if behind is not None:
+        ins.append(behind.operand())
     own = struct((tokens, columns), jnp.float32)
-    oth = struct((tokens, columns), jnp.bfloat16 if last else jnp.float32)
+    oth = struct((tokens, columns + extra), jnp.float32 if behind is None else jnp.bfloat16)
     return call(
         kernel,
         row,
@@ -319,45 +329,50 @@
         scratch=[pltpu.VMEM((tokens, rows), jnp.bfloat16)],
         flops=4 * tokens * rows * columns * count,
         moved=8 * tokens * columns,
-        vmem=40,
-    )
-
-
-def finish(plan, row, xg, arrived, kv_own, kv_got, after):
+        vmem=28,
+    )
+
+
+def place(plan, row, xg, arrived, first, sums=None):
     count = len(arrived)
     tokens, width = arrived[0].shape
-    table = [plan[f"theirs{j}"] for j in range(count)]
+    table = [plan[f"theirs{first + j}"] for j in range(count)]
 
     def kernel(row_ref, *refs):
-        out_ref, kv_out = refs[-2:]
         g = pl.program_id(0)
+        out_ref = refs[-1] if sums is None else refs[-2]
         for j in range(count):
 
             @pl.when(g == j)
             def _():
                 out_ref[...] = refs[j][...]
 
-        kv_out[...] = (refs[count][...] + refs[count + 1][...].astype(jnp.float32)).astype(jnp.bfloat16)
-
-    def place(g, row):
+        if sums is not None:
+            total = refs[count][...] + refs[count + 1][...].astype(jnp.float32)
+            refs[-1][...] = total.astype(jnp.bfloat16)
+
+    def column(g, row):
         at = row[table[0]]
         for j in range(1, count):
             at = jnp.where(g == j, row[table[j]], at)
         return (0, at)
 
-    kv_block = pl.BlockSpec((tokens // count, kv_own.shape[1]), lambda g, row: (g, 0))
     ins = [view.operand() for view in arrived]
-    ins += [(kv_own, kv_block), (kv_got, kv_block), (xg, ANY)] + [(a, ANY) for a in after]
-    return call(
-        kernel,
-        row,
-        ins,
-        [
-            (struct(xg.shape, xg.dtype), pl.BlockSpec((tokens, width), place)),
-            (struct(kv_own.shape, jnp.bfloat16), kv_block),
-        ],
+    outs = [(struct(xg.shape, xg.dtype), pl.BlockSpec((tokens, width), column))]
+    if sums is not None:
+        own, other = sums
+        kv_block = pl.BlockSpec((tokens // count, own.shape[1]), lambda g, row: (g, 0))
+        assert other.start == 0
+        ins += [(own, kv_block), (other.array, kv_block)]
+        outs.append((struct(own.shape, jnp.bfloat16), kv_block))
+    aliases = {1 + len(ins): 0}
+    return call(
+        kernel,
+        row,
+        ins + [(xg, ANY)],
+        outs,
         grid=(count,),
-        aliases={count + 3: 0},
+        aliases=aliases,
         moved=4 * count * tokens * width,
     )
 
@@ -404,25 +419,25 @@
     )
 
 
-def average(scalars, h, stepped, others, kept, width, after):
+def average(plan, scalars, h, stepped, others, kept, width, after=()):
     rows, columns = stepped.shape
     steps = 2 if rows % 32 == 0 else 1
     size = rows // steps
     count = len(others)
 
-    def kernel(scalar_ref, stepped_ref, *refs):
-        mix = scalar_ref[0].astype(jnp.float32) / mix_denom
+    def kernel(row_ref, numerator_ref, partner_ref, stepped_ref, *refs):
+        mix = numerator_ref[row_ref[plan["replica"]]].astype(jnp.float32) / mix_denom
         for j in range(count):
 
-            @pl.when(scalar_ref[1] == j)
+            @pl.when((partner_ref[0] == j + 1) | (count == 1))
             def _():
                 refs[-1][...] = (
                     (1.0 - mix) * stepped_ref[...].astype(jnp.float32)
                     + mix * refs[j][...].astype(jnp.float32)
                 ).astype(jnp.bfloat16)
 
-    local = pl.BlockSpec((size, columns), lambda g, row: (g, 0))
-    part = pl.BlockSpec((size, columns), lambda g, row: (g, h))
+    local = pl.BlockSpec((size, columns), lambda g, *scalars: (g, 0))
+    part = pl.BlockSpec((size, columns), lambda g, *scalars: (g, h))
     ins = [(a, local) for a in (stepped, *others)]
     if kept is not None:
         ins.append((kept, ANY))
@@ -433,7 +448,7 @@
         ins,
         [(struct((rows, width), jnp.bfloat16), part)],
         grid=(steps,),
-        aliases={} if kept is None else {count + 2: 0},
+        aliases={} if kept is None else {count + 4: 0},
         moved=6 * rows * columns,
     )[0]
 
@@ -452,12 +467,12 @@
 ):
     act, weights, cot = activations[0], kv_weight[0], kv_cotangent[0]
     first, second = first_moment[0], second_moment[0]
-    plan = Plan(n)
+    plan = Plan(n_rep, n)
     depth = plan.depth
     rows, columns = weights.shape
     size = columns // CHUNKS
     row = lax.dynamic_index_in_dim(
-        jnp.asarray(plan.table), lax.axis_index("fsdp"), 0, keepdims=False
+        jnp.asarray(plan.table), lax.axis_index(("rep", "fsdp")), 0, keepdims=False
     )
     links = {
         "a": [(i, i + 2 if i // 2 % 2 == 0 else i - 2) for i in range(n)],
@@ -480,18 +495,16 @@
             return [opening[link]]
         return [got[slot, h][link].array for h in range(CHUNKS)]
 
-    def send(views, *turns, after=()):
-        return swap(pack(plan, row, rows, views, act, turns, after))
-
-    parcel = send([part(cot, 0)], 0)
-    cot_oth = [View(parcel, 0, size)]
-    pieces = [View(parcel, size, rows)]
-    for h in range(1, CHUNKS):
-        cot_oth.append(part(send([part(cot, h)]), 0))
-    parcel = send([], *range(1, depth - 1), after=[parcel])
+    def send(*turns, after=()):
+        return swap(pack(plan, row, rows, [], act, turns, after))
+
+    parcel = swap(cot)
+    cot_oth = [part(parcel, h) for h in range(CHUNKS)]
+    pieces = [View(send(0), 0, rows)]
+    parcel = send(*range(1, depth - 1), after=[parcel])
     pieces += [View(parcel, k * rows, rows) for k in range(depth - 2)]
 
-    arrived, shards = [], []
+    arrived, shards, sent = [], [], []
     xg, held = None, None
 
     def shard_step(j, xg, held):
@@ -499,14 +512,17 @@
         if j > 0:
             candidates = [arrivals(*source) for source in plan.sources[j]]
         turn = depth - 1 if j == depth - 3 else None
-        xg, parcel, shard = project(plan, row, j, candidates, act, cot, cot_oth, xg, turn, held)
+        after = [sent[-1]] if j == depth - 2 else []
+        xg, parcel, shard = project(
+            plan, row, j, candidates, act, cot, cot_oth, xg, turn, held, after
+        )
         shards.append(shard)
-        if turn is None and j < depth - 1:
+        if j < depth - 3 or j == depth - 1:
             return xg, View(parcel, 0, parcel.shape[1])
-        parcel = swap(parcel)
-        arrived.extend(View(parcel, t * rows, rows) for t in range(j + 1 - len(arrived)))
+        sent.append(swap(parcel))
+        arrived.extend(View(sent[-1], t * rows, rows) for t in range(j + 1 - len(arrived)))
         if turn is not None:
-            pieces.append(View(parcel, parcel.shape[1] - rows, rows))
+            pieces.append(View(sent[-1], parcel.shape[1] - rows, rows))
         return xg, None
 
     xg, held = shard_step(0, xg, held)
@@ -515,32 +531,36 @@
             xg, held = shard_step(s - 2, xg, held)
         if s == depth:
             grad = own_gradient(plan, row, act, pieces[depth - 1], cot, cot_oth)
+            sums = values(plan, row, list(range(depth - 1)), shards, act, pieces, None)
         for h in range(CHUNKS):
             after = [bufs["a"]] if h > 0 else []
+            if s == depth and h == CHUNKS - 1:
+                after.append(sums[0])
             bufs = relay(
                 plan, row, s, got[s - 1, h], act, pieces[: s - 1], part(cot, h), cot_oth[h], after
             )
             got[s, h] = {link: part(array, 0) for link, array in exchange(bufs).items()}
     xg, held = shard_step(depth - 1, xg, held)
-    early = list(range(depth - 1))
-    sums = values(plan, row, early, shards[:-1], act, pieces, None, False)
-    kv_own, kv_oth = values(plan, row, [depth - 1], shards[-1:], act, pieces, sums, True)
-    kv_got = swap(kv_oth)
-
-    replica = lax.axis_index("rep")
-    choice = (partner[0] if n_rep == 4 else jnp.int32(1)) - 1
-    scalars = jnp.stack([mix_numerator[replica], choice])
-    moments, averaged = None, None
+    kv_own, parcel = values(plan, row, [depth - 1], shards[-1:], act, pieces, sums, held)
+    final = swap(parcel)
+
+    scalars = (row, mix_numerator, partner)
+    moments, averaged, placed = None, None, None
     for h in range(CHUNKS):
-        after = [arrived[-1].array, kv_oth] if h == CHUNKS - 1 else []
+        last = h == CHUNKS - 1
+        after = [] if h == 0 else [sent[-1]]
         *moments, stepped = adam(
-            row, h, got[depth, h], grad, weights, first, second, moments, after
+            row, h, got[depth, h], grad, weights, first, second, moments, after + [parcel]
         )
-        others = partner_rows(stepped, partner, replica, n_rep)
-        if h == CHUNKS - 1:
-            x_grad, kv_out = finish(plan, row, xg, arrived, kv_own, kv_got, [averaged])
+        if placed is None:
+            placed = place(plan, row, xg, arrived, 0)[0]
+        others = partner_rows(stepped, partner, row[plan["replica"]], n_rep)
+        if last:
+            views = [View(final, columns, rows)]
+            kv_views = (kv_own, View(final, 0, columns))
+            x_grad, kv_out = place(plan, row, placed, views, depth - 1, kv_views)
         averaged = average(
-            scalars, h, stepped, others, averaged, columns, []
+            plan, scalars, h, stepped, others, averaged, columns, [kv_out] if last else [final]
         )
     return (
         kv_out[None],

time: 151 us -> 134 us (0.89)
  local copies, waits for them, and re-layouts: 11.9 us -> 2.62 us
  Pallas kernels: 49.8 us -> 40.8 us
  starting transfers between devices: 30.9 us -> 38.7 us
  waiting for transfers between devices: 56.1 us -> 50.8 us
    pallas_call x21, Pallas kernels: 49.8 us -> 40.8 us  [call(): pl.pallas_call(kernel, grid_spec=pltpu.PrefetchScalarGridSpec(num_scalar_...]
    unnamed x30 -> x18, local copies, waits for them, and re-layouts: 10.6 us -> 1.93 us
    ppermute x14, starting transfers between devices: 20.5 us -> 28 us  [exchange(): lax.ppermute(bufs[name], 'fsdp', links[name])]
    ppermute x6, waiting for transfers between devices: 26.7 us -> 21.7 us  [the longest x1 15.4 us: per_device(): parcel = swap(cot)]
  transfers between devices with their start and end apart: 26 -> 26, of which waited for: 8 -> 7; matrix products, arithmetic and copies ran while one was open for 1% -> 1% of each run, Pallas kernels for 31% -> 29%
where the time goes in v4:
time: 134 us
  waiting for transfers between devices  50.8 us (38%)
  Pallas kernels  40.8 us (30%)
  starting transfers between devices  38.7 us (29%)
  local copies, waits for them, and re-layouts  2.62 us (2%)
    pallas_call x21, Pallas kernels, call(): pl.pallas_call(kernel, grid_spec=pltpu.PrefetchScalarGridSpec(num_scalar_...  40.8 us
    ppermute x14, starting transfers between devices, exchange(): lax.ppermute(bufs[name], 'fsdp', links[name])  28 us
    ppermute x1, waiting for transfers between devices, per_device(): parcel = swap(cot)  15.4 us
    ppermute x14, waiting for transfers between devices, exchange(): lax.ppermute(bufs[name], 'fsdp', links[name])  15.1 us
    ppermute x2, waiting for transfers between devices, partner_rows(): far = lax.ppermute(stepped, 'rep', [(r, r ^ 2) for r in range(4)])  14 us
    ppermute x2, waiting for transfers between devices, send(): return swap(pack(plan, row, rows, [], act, turns, after))  6.25 us
    ppermute x2, starting transfers between devices, shard_step(): sent.append(swap(parcel))  3.12 us
    ppermute x2, starting transfers between devices, partner_rows(): far = lax.ppermute(stepped, 'rep', [(r, r ^ 2) for r in range(4)])  2.75 us
  transfers between devices with their start and end apart: 26, of which 7 were waited for; matrix products, arithmetic and copies ran while one was open for 1% of the time, Pallas kernels for 29%

profile of v4, /device:TPU:0, one launch (start us, length us, event | category | flops | bytes accessed | tf_op | source)
XLA Modules:
  0.0 133.9 jit_solution(5292152589748811334)
XLA Ops:
  1.4 5.8 %collective-permute-start = (bf16[512,1024]{1,0:T(8,128)(2,1)}, bf16[512,1024]{1,0:T(8,128)(2,1)S(1)}, u32[]{:S(2)}, u32[]{:S(2)}) collective-permute-start(bf16[512,1024]{1,0:T(8,128)(2,1)} %bitcast.46), channel_id=1, source_target_pairs={{0,2},{1,3},{2,0},{3,1},{4,6},{5,7},{6,4},{7,5},{8,10},{9,11},{10,... | collective-permute-start | bytes 3145736 | tf_op jit(solution)/shard_map/ppermute | solution.py:485
  9.4 1.9 %copy-done = bf16[1,384,4096]{2,1,0:T(8,128)(2,1)S(1)} copy-done((bf16[1,384,4096]{2,1,0:T(8,128)(2,1)S(1)}, bf16[1,384,4096]{2,1,0:T(8,128)(2,1)}, u32[]{:S(2)}) %copy-start) | copy-done | bytes 3145752
  12.5 15.4 %collective-permute-done.3.refs_6_.refs_2_.refs_7_.refs_1_.refs_3_.refs_4_.refs_5_.refs_8_.refs_0_ = bf16[384,1024]{1,0:T(8,128)(2,1)S(1)} collective-permute-done((bf16[384,1024]{1,0:T(8,128)(2,1)}, bf16[384,1024]{1,0:T(8,128)(2,1)S(1)}, u32[]{:S(2)}, u32[]{:S(2)}) %collective-permute-start.3) | collective-permute-done | bytes 786464 | tf_op jit(solution)/shard_map/ppermute | solution.py:501
  28.5 1.6 %collective-permute-start.6 = (bf16[384,1024]{1,0:T(8,128)(2,1)S(1)}, bf16[384,1024]{1,0:T(8,128)(2,1)S(1)}, u32[]{:S(2)}, u32[]{:S(2)}) collective-permute-start(bf16[384,1024]{1,0:T(8,128)(2,1)S(1)} %shard_map.121), channel_id=1, source_target_pairs={{0,1},{1,0},{2,3},{3,2},{4,5},{5,4},{6,7},{7,6},{8,9},{9,8},{10,11... | collective-permute-start | bytes 2359304 | tf_op jit(solution)/shard_map/ppermute | solution.py:499
  30.1 6.2 %collective-permute-done.2.refs_4_.refs_6_.refs_2_ = bf16[384,512]{1,0:T(8,128)(2,1)S(1)} collective-permute-done((bf16[384,512]{1,0:T(8,128)(2,1)S(1)}, bf16[384,512]{1,0:T(8,128)(2,1)S(1)}, u32[]{:S(2)}, u32[]{:S(2)}) %collective-permute-start.2) | collective-permute-done | bytes 393248 | tf_op jit(solution)/shard_map/ppermute | solution.py:499
  36.3 1.5 %shard_map.120 = (bf16[512,512]{1,0:T(8,128)(2,1)S(1)}, bf16[512,512]{1,0:T(8,128)(2,1)S(1)}) custom-call(s32[40]{0:T(128)S(1)} %dynamic-slice_bitcast_fusion.row_ref, bf16[512,1024]{1,0:T(8,128)(2,1)S(1)} %collective-permute-done.1.refs_0_.refs_1_, bf16[512,1024]{1,0:T(8,128)(2,1)S(1)} %collective-permute-done.refs_1_.refs_0_, ...), custom_call_target="tpu_custom_call" | custom-call | flops 805306368 | bytes 2883584 | tf_op jit(solution)/shard_map/pallas_call | solution.py:85
  38.7 2.4 %shard_map.125 = (bf16[384,4096]{1,0:T(8,128)(2,1)}, bf16[384,512]{1,0:T(8,128)(2,1)S(1)}, bf16[512,1024]{1,0:T(8,128)(2,1)S(1)}) custom-call(s32[40]{0:T(128)S(1)} %dynamic-slice_bitcast_fusion.row_ref, bf16[512,1024]{1,0:T(8,128)(2,1)S(1)} %bitcast.47, ...), custom_call_target="tpu_custom_call" | custom-call | flops 805306368 | bytes 4718592 | tf_op jit(solution)/shard_map/pallas_call | solution.py:85
  42.4 2.5 %shard_map.126 = (bf16[384,4096]{1,0:T(8,128)(2,1)}, bf16[384,1536]{1,0:T(8,128)(2,1)S(1)}, bf16[512,1024]{1,0:T(8,128)(2,1)S(1)}) custom-call(s32[40]{0:T(128)S(1)} %dynamic-slice_bitcast_fusion.row_ref, bf16[512,1024]{1,0:T(8,128)(2,1)S(1)} %collective-permute-done.refs_1_.refs_0_, ...), custom_call_target="tpu_custom_call", output_to_operand_aliasing={{0}: (8, {})} | custom-call | flops 805306368 | bytes 4718592 | tf_op jit(solution)/shard_map/pallas_call | solution.py:85
  44.9 1.6 %collective-permute-start.11 = (bf16[384,1536]{1,0:T(8,128)(2,1)S(1)}, bf16[384,1536]{1,0:T(8,128)(2,1)S(1)}, u32[]{:S(2)}, u32[]{:S(2)}) collective-permute-start(bf16[384,1536]{1,0:T(8,128)(2,1)S(1)} %get-tuple-element.50), channel_id=1, source_target_pairs={{0,1},{1,0},{2,3},{3,2},{4,5},{5,4},{6,7},{7,6},{8,9},{9,8},{10,11... | collective-permute-start | bytes 3538952 | tf_op jit(solution)/shard_map/ppermute | solution.py:522
  46.4 1.5 %shard_map.123 = (bf16[512,512]{1,0:T(8,128)(2,1)S(1)}, bf16[512,512]{1,0:T(8,128)(2,1)S(1)}) custom-call(s32[40]{0:T(128)S(1)} %dynamic-slice_bitcast_fusion.row_ref, bf16[512,1024]{1,0:T(8,128)(2,1)S(1)} %collective-permute-done.1.refs_0_.refs_1_, bf16[512,1024]{1,0:T(8,128)(2,1)S(1)} %collective-permute-done.refs_1_.refs_0_, ...), custom_call_target="tpu_custom_call" | custom-call | flops 805306368 | bytes 2883584 | tf_op jit(solution)/shard_map/pallas_call | solution.py:85
  48.7 3.4 %collective-permute-start.9 = (bf16[512,512]{1,0:T(8,128)(2,1)S(1)}, bf16[512,512]{1,0:T(8,128)(2,1)S(1)}, u32[]{:S(2)}, u32[]{:S(2)}) collective-permute-start(bf16[512,512]{1,0:T(8,128)(2,1)S(1)} %get-tuple-element.45), channel_id=1, source_target_pairs={{0,2},{1,3},{2,0},{3,1},{4,6},{5,7},{6,4},{7,5},{8,10},{9,11},{10,... | collective-permute-start | bytes 1572872 | tf_op jit(solution)/shard_map/ppermute | solution.py:485
  52.1 3.1 %collective-permute-done.5.refs_1_.refs_0_ = bf16[512,512]{1,0:T(8,128)(2,1)S(1)} collective-permute-done((bf16[512,512]{1,0:T(8,128)(2,1)S(1)}, bf16[512,512]{1,0:T(8,128)(2,1)S(1)}, u32[]{:S(2)}, u32[]{:S(2)}) %collective-permute-start.5) | collective-permute-done | bytes 524320 | tf_op jit(solution)/shard_map/ppermute | solution.py:485
  57.4 4.9 %collective-permute-start.7 = (bf16[512,512]{1,0:T(8,128)(2,1)S(1)}, bf16[512,512]{1,0:T(8,128)(2,1)S(1)}, u32[]{:S(2)}, u32[]{:S(2)}) collective-permute-start(bf16[512,512]{1,0:T(8,128)(2,1)S(1)} %get-tuple-element.43.refs_8_), channel_id=1, source_target_pairs={{0,2},{1,3},{2,0},{3,1},{4,6},{5,7},{6,4},{7,5},{8,10},{9,11},{10,... | collective-permute-start | bytes 1572872 | tf_op jit(solution)/shard_map/ppermute | solution.py:485
  62.3 4.2 %collective-permute-done.9.refs_1_ = bf16[512,512]{1,0:T(8,128)(2,1)S(1)} collective-permute-done((bf16[512,512]{1,0:T(8,128)(2,1)S(1)}, bf16[512,512]{1,0:T(8,128)(2,1)S(1)}, u32[]{:S(2)}, u32[]{:S(2)}) %collective-permute-start.9) | collective-permute-done | bytes 524320 | tf_op jit(solution)/shard_map/ppermute | solution.py:485
  69.9 7.8 %collective-permute-done.7.refs_1_ = bf16[512,512]{1,0:T(8,128)(2,1)S(1)} collective-permute-done((bf16[512,512]{1,0:T(8,128)(2,1)S(1)}, bf16[512,512]{1,0:T(8,128)(2,1)S(1)}, u32[]{:S(2)}, u32[]{:S(2)}) %collective-permute-start.7) | collective-permute-done | bytes 524320 | tf_op jit(solution)/shard_map/ppermute | solution.py:485
  79.9 5.6 %collective-permute-start.18 = (bf16[512,512]{1,0:T(8,128)(2,1)S(1)}, bf16[512,512]{1,0:T(8,128)(2,1)S(1)}, u32[]{:S(2)}, u32[]{:S(2)}) collective-permute-start(bf16[512,512]{1,0:T(8,128)(2,1)S(1)} %get-tuple-element.67.refs_9_), channel_id=1, source_target_pairs={{0,2},{1,3},{2,0},{3,1},{4,6},{5,7},{6,4},{7,5},{8,10},{9,11},{10,... | collective-permute-start | bytes 1572872 | tf_op jit(solution)/shard_map/ppermute | solution.py:485
  85.5 2.5 %shard_map.127 = (bf16[384,4096]{1,0:T(8,128)(2,1)}, bf16[384,512]{1,0:T(8,128)(2,1)S(1)}, bf16[512,1024]{1,0:T(8,128)(2,1)S(1)}) custom-call(s32[40]{0:T(128)S(1)} %dynamic-slice_bitcast_fusion.row_ref, bf16[512,512]{1,0:T(8,128)(2,1)S(1)} %collective-permute-done.5.refs_1_.refs_0_, ...), custom_call_target="tpu_custom_call", output_to_operand_aliasing={{0}: (8, {})} | custom-call | flops 805306368 | bytes 4718592 | tf_op jit(solution)/shard_map/pallas_call | solution.py:85
  88.0 3.9 %shard_map.129 = (f32[384,1024]{1,0:T(8,128)S(1)}, f32[384,1024]{1,0:T(8,128)S(1)}) custom-call(s32[40]{0:T(128)S(1)} %dynamic-slice_bitcast_fusion.row_ref, bf16[512,1024]{1,0:T(8,128)(2,1)S(1)} %get-tuple-element.53.refs_0_, bf16[512,1024]{1,0:T(8,128)(2,1)S(1)} %get-tuple-element.54.refs_1_, bf16[512,1024]{1,0:T(8,128)(2,1)S(1)} %get-tuple-element.55.refs_2_, ...), custom_call_target="tpu_custom_call" | custom-call | flops 2415919104 | bytes 3145728 | tf_op jit(solution)/shard_map/pallas_call | solution.py:85
  92.0 1.5 %shard_map.134 = (bf16[512,512]{1,0:T(8,128)(2,1)S(1)}, bf16[512,512]{1,0:T(8,128)(2,1)S(1)}) custom-call(s32[40]{0:T(128)S(1)} %dynamic-slice_bitcast_fusion.row_ref, bf16[512,512]{1,0:T(8,128)(2,1)S(1)} %collective-permute-done.14.refs_0_, bf16[512,512]{1,0:T(8,128)(2,1)S(1)} %collective-permute-done.10.refs_2_.refs_1_, bf16[384,4096]{1,0:T(8,128)(2,1)S(1)} %bitcast.29, ...), custom_call_target="tpu_custom_call" | custom-call | flops 805306368 | bytes 2883584 | tf_op jit(solution)/shard_map/pallas_call | solution.py:85
  95.0 1.6 %collective-permute-start.13 = (bf16[384,512]{1,0:T(8,128)(2,1)S(1)}, bf16[384,512]{1,0:T(8,128)(2,1)S(1)}, u32[]{:S(2)}, u32[]{:S(2)}) collective-permute-start(bf16[384,512]{1,0:T(8,128)(2,1)S(1)} %get-tuple-element.61), channel_id=1, source_target_pairs={{0,1},{1,0},{2,3},{3,2},{4,5},{5,4},{6,7},{7,6},{8,9},{9,8},{10,11... | collective-permute-start | bytes 1179656 | tf_op jit(solution)/shard_map/ppermute | solution.py:522
  96.6 2.5 %shard_map.128 = (bf16[384,4096]{1,0:T(8,128)(2,1)}, bf16[384,512]{1,0:T(8,128)(2,1)S(1)}, bf16[512,1024]{1,0:T(8,128)(2,1)S(1)}) custom-call(s32[40]{0:T(128)S(1)} %dynamic-slice_bitcast_fusion.row_ref, bf16[512,1024]{1,0:T(8,128)(2,1)S(1)} %collective-permute-done.refs_1_.refs_0_, ...), custom_call_target="tpu_custom_call", output_to_operand_aliasing={{0}: (7, {})} | custom-call | flops 805306368 | bytes 4718592 | tf_op jit(solution)/shard_map/pallas_call | solution.py:85
  99.1 1.9 %shard_map.130 = (f32[384,1024]{1,0:T(8,128)S(1)}, bf16[384,1536]{1,0:T(8,128)(2,1)S(1)}) custom-call(s32[40]{0:T(128)S(1)} %dynamic-slice_bitcast_fusion.row_ref, bf16[512,1024]{1,0:T(8,128)(2,1)S(1)} %get-tuple-element.52.refs_0_, bf16[384,4096]{1,0:T(8,128)(2,1)S(1)} %bitcast.31, bf16[384,512]{1,0:T(8,128)(2,1)S(1)} %collective-permute-done.2.refs_4_.refs_6_.refs_2_, ...), custom_call_target="tpu_custom_call" | custom-call | flops 805306368 | bytes 3145728 | tf_op jit(solution)/shard_map/pallas_call | solution.py:85
  101.7 1.8 %shard_map.135.grad_ref = f32[512,1024]{1,0:T(8,128)S(1)} custom-call(s32[40]{0:T(128)S(1)} %dynamic-slice_bitcast_fusion.row_ref, bf16[384,4096]{1,0:T(8,128)(2,1)S(1)} %bitcast.32, bf16[384,1536]{1,0:T(8,128)(2,1)S(1)} %collective-permute-done.11.refs_8_.refs_9_.refs_5_.refs_0_.refs_1_.piece_ref, bf16[384,1024]{1,0:T(8,128)(2,1)S(1)} %bitcast.44, ...), custom_call_target="tpu_custom_call" | custom-call | flops 805306368 | bytes 3670016 | tf_op jit(solution)/shard_map/pallas_call | solution.py:85
  103.5 3.1 %shard_map.136 = (f32[512,1024]{1,0:T(8,128)}, f32[512,1024]{1,0:T(8,128)}, bf16[512,512]{1,0:T(8,128)(2,1)S(1)}) custom-call(s32[40]{0:T(128)S(1)} %dynamic-slice_bitcast_fusion.row_ref, bf16[512,512]{1,0:T(8,128)(2,1)S(1)} %collective-permute-done.18.up_ref, bf16[512,512]{1,0:T(8,128)(2,1)S(1)} %collective-permute-done.19.dn_ref, ...), custom_call_target="tpu_custom_call" | custom-call | flops 4194304 | bytes 7340032 | tf_op jit(solution)/shard_map/pallas_call | solution.py:85
  106.6 1.5 %collective-permute-start.24 = (bf16[512,512]{1,0:T(8,128)(2,1)S(1)}, bf16[512,512]{1,0:T(8,128)(2,1)S(1)}, u32[]{:S(2)}, u32[]{:S(2)}) collective-permute-start(bf16[512,512]{1,0:T(8,128)(2,1)S(1)} %get-tuple-element.74.stepped_ref), channel_id=1, source_target_pairs={{0,16},{8,24},{16,0},{24,8},{1,17},{9,25},{17,1},{25,9},{2,18},{10... | collective-permute-start | bytes 1572872 | tf_op jit(solution)/shard_map/ppermute | solution.py:460
  108.1 3.1 %shard_map.137 = (f32[512,1024]{1,0:T(8,128)}, f32[512,1024]{1,0:T(8,128)}, bf16[512,512]{1,0:T(8,128)(2,1)S(1)}) custom-call(s32[40]{0:T(128)S(1)} %dynamic-slice_bitcast_fusion.row_ref, bf16[512,512]{1,0:T(8,128)(2,1)S(1)} %collective-permute-done.16.up_ref, ...), custom_call_target="tpu_custom_call", output_to_operand_aliasing={{0}: (7, {}), {1}: (8, {})} | custom-call | flops 4194304 | bytes 7340032 | tf_op jit(solution)/shard_map/pallas_call | solution.py:85
  112.4 8.9 %collective-permute-done.24.refs_1_ = bf16[512,512]{1,0:T(8,128)(2,1)S(1)} collective-permute-done((bf16[512,512]{1,0:T(8,128)(2,1)S(1)}, bf16[512,512]{1,0:T(8,128)(2,1)S(1)}, u32[]{:S(2)}, u32[]{:S(2)}) %collective-permute-start.24) | collective-permute-done | bytes 524320 | tf_op jit(solution)/shard_map/ppermute | solution.py:460
  121.8 5.1 %collective-permute-done.21.refs_1_ = bf16[512,512]{1,0:T(8,128)(2,1)S(1)} collective-permute-done((bf16[512,512]{1,0:T(8,128)(2,1)S(1)}, bf16[512,512]{1,0:T(8,128)(2,1)S(1)}, u32[]{:S(2)}, u32[]{:S(2)}) %collective-permute-start.21) | collective-permute-done | bytes 524320 | tf_op jit(solution)/shard_map/ppermute | solution.py:460
  126.9 2.2 %shard_map.131.refs_3_ = bf16[384,4096]{1,0:T(8,128)(2,1)} custom-call(s32[40]{0:T(128)S(1)} %dynamic-slice_bitcast_fusion.row_ref, bf16[384,1536]{1,0:T(8,128)(2,1)S(1)} %collective-permute-done.11.refs_8_.refs_9_.refs_5_.refs_0_.refs_1_.piece_ref, ...), custom_call_target="tpu_custom_call", output_to_operand_aliasing={{}: (4, {})} | custom-call | bytes 2359296 | tf_op jit(solution)/shard_map/pallas_call | solution.py:85
  129.1 1.7 %shard_map.132 = (bf16[384,4096]{1,0:T(8,128)(2,1)}, bf16[384,1024]{1,0:T(8,128)(2,1)}) custom-call(s32[40]{0:T(128)S(1)} %dynamic-slice_bitcast_fusion.row_ref, bf16[384,1536]{1,0:T(8,128)(2,1)S(1)} %collective-permute-done.12.refs_0_.refs_2_.refs_3_, f32[384,1024]{1,0:T(8,128)S(1)} %get-tuple-element.60.refs_1_, ...), custom_call_target="tpu_custom_call", output_to_operand_aliasing={{0}: (4, {})} | custom-call | bytes 786432 | tf_op jit(solution)/shard_map/pallas_call | solution.py:85
  130.8 1.5 %shard_map.138.refs_3_ = bf16[512,1024]{1,0:T(8,128)(2,1)} custom-call(s32[40]{0:T(128)S(1)} %dynamic-slice_bitcast_fusion.row_ref, s32[4]{0:T(128)S(1)} %copy-done.7, s32[4]{0:T(128)S(1)} %copy-done.8, bf16[512,512]{1,0:T(8,128)(2,1)S(1)} %get-tuple-element.74.stepped_ref, bf16[512,512]{1,0:T(8,128)(2,1)S(1)} %collective-permute-done.23.refs_0_, ...), custom_call_target="tpu_custom_call" | custom-call | bytes 1572864 | tf_op jit(solution)/shard_map/pallas_call | solution.py:85
  132.3 1.5 %shard_map.139 = bf16[512,1024]{1,0:T(8,128)(2,1)} custom-call(s32[40]{0:T(128)S(1)} %dynamic-slice_bitcast_fusion.row_ref, s32[4]{0:T(128)S(1)} %copy-done.7, s32[4]{0:T(128)S(1)} %copy-done.8, bf16[512,512]{1,0:T(8,128)(2,1)S(1)} %get-tuple-element.73.stepped_ref, ...), custom_call_target="tpu_custom_call", output_to_operand_aliasing={{}: (7, {})} | custom-call | bytes 1572864 | tf_op jit(solution)/shard_map/pallas_call | solution.py:85
  (60 shorter events, 19.1 us)
Async XLA Ops:
  0.6 35.7 %collective-permute-start.1 = (bf16[512,1024]{1,0:T(8,128)(2,1)}, bf16[512,1024]{1,0:T(8,128)(2,1)S(1)}, u32[]{:S(2)}, u32[]{:S(2)}) collective-permute-start(bf16[512,1024]{1,0:T(8,128)(2,1)} %bitcast.45), channel_id=1, source_target_pairs={{2,4},{3,5},{4,2},{5,3},{10,12},{11,13},{12,10},{13,11},{18,20},{1... | collective-permute-start | bytes 3145736 | tf_op jit(solution)/shard_map/ppermute | solution.py:485
  1.4 35.0 %collective-permute-start = (bf16[512,1024]{1,0:T(8,128)(2,1)}, bf16[512,1024]{1,0:T(8,128)(2,1)S(1)}, u32[]{:S(2)}, u32[]{:S(2)}) collective-permute-start(bf16[512,1024]{1,0:T(8,128)(2,1)} %bitcast.46), channel_id=1, source_target_pairs={{0,2},{1,3},{2,0},{3,1},{4,6},{5,7},{6,4},{7,5},{8,10},{9,11},{10,... | collective-permute-start | bytes 3145736 | tf_op jit(solution)/shard_map/ppermute | solution.py:485
  7.2 20.7 %collective-permute-start.3 = (bf16[384,1024]{1,0:T(8,128)(2,1)}, bf16[384,1024]{1,0:T(8,128)(2,1)S(1)}, u32[]{:S(2)}, u32[]{:S(2)}) collective-permute-start(bf16[384,1024]{1,0:T(8,128)(2,1)} %bitcast.33), channel_id=1, source_target_pairs={{0,1},{1,0},{2,3},{3,2},{4,5},{5,4},{6,7},{7,6},{8,9},{9,8},{10,11... | collective-permute-start | bytes 2359304 | tf_op jit(solution)/shard_map/ppermute | solution.py:501
  9.4 1.9 %copy-start = (bf16[1,384,4096]{2,1,0:T(8,128)(2,1)S(1)}, bf16[1,384,4096]{2,1,0:T(8,128)(2,1)}, u32[]{:S(2)}) copy-start(bf16[1,384,4096]{2,1,0:T(8,128)(2,1)} %param.8) | copy-start | bytes 9437188
  11.9 24.5 %copy-start.2 = (bf16[1,384,1024]{2,1,0:T(8,128)(2,1)S(1)}, bf16[1,384,1024]{2,1,0:T(8,128)(2,1)}, u32[]{:S(2)}) copy-start(bf16[1,384,1024]{2,1,0:T(8,128)(2,1)} %param.10) | copy-start | bytes 2359300
  11.9 24.5 %collective-permute-start.2 = (bf16[384,512]{1,0:T(8,128)(2,1)S(1)}, bf16[384,512]{1,0:T(8,128)(2,1)S(1)}, u32[]{:S(2)}, u32[]{:S(2)}) collective-permute-start(bf16[384,512]{1,0:T(8,128)(2,1)S(1)} %shard_map.119), channel_id=1, source_target_pairs={{0,1},{1,0},{2,3},{3,2},{4,5},{5,4},{6,7},{7,6},{8,9},{9,8},{10,11... | collective-permute-start | bytes 1179656 | tf_op jit(solution)/shard_map/ppermute | solution.py:499
  28.5 10.2 %copy-start.3 = (bf16[1,512,1024]{2,1,0:T(8,128)(2,1)S(1)}, bf16[1,512,1024]{2,1,0:T(8,128)(2,1)}, u32[]{:S(2)}) copy-start(bf16[1,512,1024]{2,1,0:T(8,128)(2,1)} %param.9) | copy-start | bytes 3145732
  28.5 26.7 %collective-permute-start.6 = (bf16[384,1024]{1,0:T(8,128)(2,1)S(1)}, bf16[384,1024]{1,0:T(8,128)(2,1)S(1)}, u32[]{:S(2)}, u32[]{:S(2)}) collective-permute-start(bf16[384,1024]{1,0:T(8,128)(2,1)S(1)} %shard_map.121), channel_id=1, source_target_pairs={{0,1},{1,0},{2,3},{3,2},{4,5},{5,4},{6,7},{7,6},{8,9},{9,8},{10,11... | collective-permute-start | bytes 2359304 | tf_op jit(solution)/shard_map/ppermute | solution.py:499
  37.9 4.5 %copy-start.1 = (bf16[1,384,4096]{2,1,0:T(8,128)(2,1)S(1)}, bf16[1,384,4096]{2,1,0:T(8,128)(2,1)}, u32[]{:S(2)}) copy-start(bf16[1,384,4096]{2,1,0:T(8,128)(2,1)} %param.8) | copy-start | bytes 9437188
  37.9 10.8 %collective-permute-start.4 = (bf16[512,512]{1,0:T(8,128)(2,1)S(1)}, bf16[512,512]{1,0:T(8,128)(2,1)S(1)}, u32[]{:S(2)}, u32[]{:S(2)}) collective-permute-start(bf16[512,512]{1,0:T(8,128)(2,1)S(1)} %get-tuple-element.41), channel_id=1, source_target_pairs={{2,4},{3,5},{4,2},{5,3},{10,12},{11,13},{12,10},{13,11},{18,20},{1... | collective-permute-start | bytes 1572872 | tf_op jit(solution)/shard_map/ppermute | solution.py:485
  41.2 14.0 %collective-permute-start.5 = (bf16[512,512]{1,0:T(8,128)(2,1)S(1)}, bf16[512,512]{1,0:T(8,128)(2,1)S(1)}, u32[]{:S(2)}, u32[]{:S(2)}) collective-permute-start(bf16[512,512]{1,0:T(8,128)(2,1)S(1)} %get-tuple-element.42.refs_7_), channel_id=1, source_target_pairs={{0,2},{1,3},{2,0},{3,1},{4,6},{5,7},{6,4},{7,5},{8,10},{9,11},{10,... | collective-permute-start | bytes 1572872 | tf_op jit(solution)/shard_map/ppermute | solution.py:485
  44.9 40.6 %collective-permute-start.11 = (bf16[384,1536]{1,0:T(8,128)(2,1)S(1)}, bf16[384,1536]{1,0:T(8,128)(2,1)S(1)}, u32[]{:S(2)}, u32[]{:S(2)}) collective-permute-start(bf16[384,1536]{1,0:T(8,128)(2,1)S(1)} %get-tuple-element.50), channel_id=1, source_target_pairs={{0,1},{1,0},{2,3},{3,2},{4,5},{5,4},{6,7},{7,6},{8,9},{9,8},{10,11... | collective-permute-start | bytes 3538952 | tf_op jit(solution)/shard_map/ppermute | solution.py:522
  48.0 14.3 %collective-permute-start.8 = (bf16[512,512]{1,0:T(8,128)(2,1)S(1)}, bf16[512,512]{1,0:T(8,128)(2,1)S(1)}, u32[]{:S(2)}, u32[]{:S(2)}) collective-permute-start(bf16[512,512]{1,0:T(8,128)(2,1)S(1)} %get-tuple-element.44), channel_id=1, source_target_pairs={{2,4},{3,5},{4,2},{5,3},{10,12},{11,13},{12,10},{13,11},{18,20},{1... | collective-permute-start | bytes 1572872 | tf_op jit(solution)/shard_map/ppermute | solution.py:485
  48.7 17.8 %collective-permute-start.9 = (bf16[512,512]{1,0:T(8,128)(2,1)S(1)}, bf16[512,512]{1,0:T(8,128)(2,1)S(1)}, u32[]{:S(2)}, u32[]{:S(2)}) collective-permute-start(bf16[512,512]{1,0:T(8,128)(2,1)S(1)} %get-tuple-element.45), channel_id=1, source_target_pairs={{0,2},{1,3},{2,0},{3,1},{4,6},{5,7},{6,4},{7,5},{8,10},{9,11},{10,... | collective-permute-start | bytes 1572872 | tf_op jit(solution)/shard_map/ppermute | solution.py:485
  56.7 13.2 %collective-permute-start.15 = (bf16[512,512]{1,0:T(8,128)(2,1)S(1)}, bf16[512,512]{1,0:T(8,128)(2,1)S(1)}, u32[]{:S(2)}, u32[]{:S(2)}) collective-permute-start(bf16[512,512]{1,0:T(8,128)(2,1)S(1)} %get-tuple-element.66), channel_id=1, source_target_pairs={{2,4},{3,5},{4,2},{5,3},{10,12},{11,13},{12,10},{13,11},{18,20},{1... | collective-permute-start | bytes 1572872 | tf_op jit(solution)/shard_map/ppermute | solution.py:485
  57.4 20.3 %collective-permute-start.7 = (bf16[512,512]{1,0:T(8,128)(2,1)S(1)}, bf16[512,512]{1,0:T(8,128)(2,1)S(1)}, u32[]{:S(2)}, u32[]{:S(2)}) collective-permute-start(bf16[512,512]{1,0:T(8,128)(2,1)S(1)} %get-tuple-element.43.refs_8_), channel_id=1, source_target_pairs={{0,2},{1,3},{2,0},{3,1},{4,6},{5,7},{6,4},{7,5},{8,10},{9,11},{10,... | collective-permute-start | bytes 1572872 | tf_op jit(solution)/shard_map/ppermute | solution.py:485
  67.9 24.0 %collective-permute-start.10 = (bf16[512,512]{1,0:T(8,128)(2,1)S(1)}, bf16[512,512]{1,0:T(8,128)(2,1)S(1)}, u32[]{:S(2)}, u32[]{:S(2)}) collective-permute-start(bf16[512,512]{1,0:T(8,128)(2,1)S(1)} %get-tuple-element.46), channel_id=1, source_target_pairs={{0,2},{1,3},{2,0},{3,1},{4,6},{5,7},{6,4},{7,5},{8,10},{9,11},{10,... | collective-permute-start | bytes 1572872 | tf_op jit(solution)/shard_map/ppermute | solution.py:485
  69.2 22.8 %collective-permute-start.14 = (bf16[512,512]{1,0:T(8,128)(2,1)S(1)}, bf16[512,512]{1,0:T(8,128)(2,1)S(1)}, u32[]{:S(2)}, u32[]{:S(2)}) collective-permute-start(bf16[512,512]{1,0:T(8,128)(2,1)S(1)} %get-tuple-element.65), channel_id=1, source_target_pairs={{2,4},{3,5},{4,2},{5,3},{10,12},{11,13},{12,10},{13,11},{18,20},{1... | collective-permute-start | bytes 1572872 | tf_op jit(solution)/shard_map/ppermute | solution.py:485
  79.2 21.8 %collective-permute-start.19 = (bf16[512,512]{1,0:T(8,128)(2,1)S(1)}, bf16[512,512]{1,0:T(8,128)(2,1)S(1)}, u32[]{:S(2)}, u32[]{:S(2)}) collective-permute-start(bf16[512,512]{1,0:T(8,128)(2,1)S(1)} %get-tuple-element.70), channel_id=1, source_target_pairs={{2,4},{3,5},{4,2},{5,3},{10,12},{11,13},{12,10},{13,11},{18,20},{1... | collective-permute-start | bytes 1572872 | tf_op jit(solution)/shard_map/ppermute | solution.py:485
  79.9 23.6 %collective-permute-start.18 = (bf16[512,512]{1,0:T(8,128)(2,1)S(1)}, bf16[512,512]{1,0:T(8,128)(2,1)S(1)}, u32[]{:S(2)}, u32[]{:S(2)}) collective-permute-start(bf16[512,512]{1,0:T(8,128)(2,1)S(1)} %get-tuple-element.67.refs_9_), channel_id=1, source_target_pairs={{0,2},{1,3},{2,0},{3,1},{4,6},{5,7},{6,4},{7,5},{8,10},{9,11},{10,... | collective-permute-start | bytes 1572872 | tf_op jit(solution)/shard_map/ppermute | solution.py:485
  93.5 14.6 %collective-permute-start.16 = (bf16[512,512]{1,0:T(8,128)(2,1)S(1)}, bf16[512,512]{1,0:T(8,128)(2,1)S(1)}, u32[]{:S(2)}, u32[]{:S(2)}) collective-permute-start(bf16[512,512]{1,0:T(8,128)(2,1)S(1)} %get-tuple-element.68), channel_id=1, source_target_pairs={{0,2},{1,3},{2,0},{3,1},{4,6},{5,7},{6,4},{7,5},{8,10},{9,11},{10,... | collective-permute-start | bytes 1572872 | tf_op jit(solution)/shard_map/ppermute | solution.py:485
  94.3 13.8 %collective-permute-start.17 = (bf16[512,512]{1,0:T(8,128)(2,1)S(1)}, bf16[512,512]{1,0:T(8,128)(2,1)S(1)}, u32[]{:S(2)}, u32[]{:S(2)}) collective-permute-start(bf16[512,512]{1,0:T(8,128)(2,1)S(1)} %get-tuple-element.69), channel_id=1, source_target_pairs={{2,4},{3,5},{4,2},{5,3},{10,12},{11,13},{12,10},{13,11},{18,20},{1... | collective-permute-start | bytes 1572872 | tf_op jit(solution)/shard_map/ppermute | solution.py:485
  95.0 13.1 %collective-permute-start.13 = (bf16[384,512]{1,0:T(8,128)(2,1)S(1)}, bf16[384,512]{1,0:T(8,128)(2,1)S(1)}, u32[]{:S(2)}, u32[]{:S(2)}) collective-permute-start(bf16[384,512]{1,0:T(8,128)(2,1)S(1)} %get-tuple-element.61), channel_id=1, source_target_pairs={{0,1},{1,0},{2,3},{3,2},{4,5},{5,4},{6,7},{7,6},{8,9},{9,8},{10,11... | collective-permute-start | bytes 1179656 | tf_op jit(solution)/shard_map/ppermute | solution.py:522
  101.0 2.5 %copy-start.4 = (f32[1,512,1024]{2,1,0:T(8,128)S(1)}, f32[1,512,1024]{2,1,0:T(8,128)}, u32[]{:S(2)}) copy-start(f32[1,512,1024]{2,1,0:T(8,128)} %param.11) | copy-start | bytes 6291460
  101.1 2.5 %copy-start.5 = (f32[1,512,1024]{2,1,0:T(8,128)S(1)}, f32[1,512,1024]{2,1,0:T(8,128)}, u32[]{:S(2)}) copy-start(f32[1,512,1024]{2,1,0:T(8,128)} %param.12) | copy-start | bytes 6291460
  101.1 28.0 %collective-permute-start.12 = (bf16[384,1536]{1,0:T(8,128)(2,1)S(1)}, bf16[384,1536]{1,0:T(8,128)(2,1)S(1)}, u32[]{:S(2)}, u32[]{:S(2)}) collective-permute-start(bf16[384,1536]{1,0:T(8,128)(2,1)S(1)} %get-tuple-element.59.refs_0_.refs_3_), channel_id=1, source_target_pairs={{0,1},{1,0},{2,3},{3,2},{4,5},{5,4},{6,7},{7,6},{8,9},{9,8},{10,11... | collective-permute-start | bytes 3538952 | tf_op jit(solution)/shard_map/ppermute | solution.py:545
  106.6 14.7 %collective-permute-start.24 = (bf16[512,512]{1,0:T(8,128)(2,1)S(1)}, bf16[512,512]{1,0:T(8,128)(2,1)S(1)}, u32[]{:S(2)}, u32[]{:S(2)}) collective-permute-start(bf16[512,512]{1,0:T(8,128)(2,1)S(1)} %get-tuple-element.74.stepped_ref), channel_id=1, source_target_pairs={{0,16},{8,24},{16,0},{24,8},{1,17},{9,25},{17,1},{25,9},{2,18},{10... | collective-permute-start | bytes 1572872 | tf_op jit(solution)/shard_map/ppermute | solution.py:460
  111.2 15.7 %collective-permute-start.21 = (bf16[512,512]{1,0:T(8,128)(2,1)S(1)}, bf16[512,512]{1,0:T(8,128)(2,1)S(1)}, u32[]{:S(2)}, u32[]{:S(2)}) collective-permute-start(bf16[512,512]{1,0:T(8,128)(2,1)S(1)} %get-tuple-element.73.stepped_ref), channel_id=1, source_target_pairs={{0,16},{8,24},{16,0},{24,8},{1,17},{9,25},{17,1},{25,9},{2,18},{10... | collective-permute-start | bytes 1572872 | tf_op jit(solution)/shard_map/ppermute | solution.py:460
  112.4 18.3 %collective-permute-start.23 = (bf16[512,512]{1,0:T(8,128)(2,1)S(1)}, bf16[512,512]{1,0:T(8,128)(2,1)S(1)}, u32[]{:S(2)}, u32[]{:S(2)}) collective-permute-start(bf16[512,512]{1,0:T(8,128)(2,1)S(1)} %get-tuple-element.74.stepped_ref), channel_id=1, source_target_pairs={{0,8},{8,0},{16,24},{24,16},{1,9},{9,1},{17,25},{25,17},{2,10},{10... | collective-permute-start | bytes 1572872 | tf_op jit(solution)/shard_map/ppermute | solution.py:462
  121.3 9.5 %collective-permute-start.25 = (bf16[512,512]{1,0:T(8,128)(2,1)S(1)}, bf16[512,512]{1,0:T(8,128)(2,1)S(1)}, u32[]{:S(2)}, u32[]{:S(2)}) collective-permute-start(bf16[512,512]{1,0:T(8,128)(2,1)S(1)} %collective-permute-done.24.refs_1_), channel_id=1, source_target_pairs={{0,8},{8,0},{16,24},{24,16},{1,9},{9,1},{17,25},{25,17},{2,10},{10... | collective-permute-start | bytes 1572872 | tf_op jit(solution)/shard_map/ppermute | solution.py:462
  121.3 11.0 %collective-permute-start.20 = (bf16[512,512]{1,0:T(8,128)(2,1)S(1)}, bf16[512,512]{1,0:T(8,128)(2,1)S(1)}, u32[]{:S(2)}, u32[]{:S(2)}) collective-permute-start(bf16[512,512]{1,0:T(8,128)(2,1)S(1)} %get-tuple-element.73.stepped_ref), channel_id=1, source_target_pairs={{0,8},{8,0},{16,24},{24,16},{1,9},{9,1},{17,25},{25,17},{2,10},{10... | collective-permute-start | bytes 1572872 | tf_op jit(solution)/shard_map/ppermute | solution.py:462
  126.9 5.4 %collective-permute-start.22 = (bf16[512,512]{1,0:T(8,128)(2,1)S(1)}, bf16[512,512]{1,0:T(8,128)(2,1)S(1)}, u32[]{:S(2)}, u32[]{:S(2)}) collective-permute-start(bf16[512,512]{1,0:T(8,128)(2,1)S(1)} %collective-permute-done.21.refs_1_), channel_id=1, source_target_pairs={{0,8},{8,0},{16,24},{24,16},{1,9},{9,1},{17,25},{25,17},{2,10},{10... | collective-permute-start | bytes 1572872 | tf_op jit(solution)/shard_map/ppermute | solution.py:462
  (3 other events, 5.0 us)

commit v5 on v4

--- a/solution.py
+++ b/solution.py
@@ -80,7 +80,7 @@
         return self.columns[name]
 
 
-def call(kernel, row, ins, outs, grid=(1,), aliases=None, scratch=(), flops=0, moved=0, vmem=16):
+def call(kernel, row, ins, outs, grid=(1,), aliases=None, scratch=(), vmem=16):
     scalars = row if isinstance(row, tuple) else (row,)
     return pl.pallas_call(
         kernel,
@@ -94,7 +94,7 @@
         out_shape=[shape for shape, _ in outs],
         input_output_aliases=aliases or {},
         compiler_params=pltpu.CompilerParams(vmem_limit_bytes=vmem * MIB),
-        cost_estimate=pl.CostEstimate(flops=flops, bytes_accessed=moved, transcendentals=0),
+        cost_estimate=pl.CostEstimate(flops=0, bytes_accessed=0, transcendentals=0),
     )(*scalars, *[array for array, _ in ins])
 
 
@@ -141,7 +141,6 @@
         row,
         ins + [(a, ANY) for a in after],
         [(out, whole(out))],
-        moved=4 * tokens * sum(sizes),
     )[0]
 
 
@@ -185,8 +184,6 @@
         ins,
         [(out, whole(out)), (out, whole(out))],
         scratch=[pltpu.VMEM((tokens, rows), jnp.bfloat16)],
-        flops=8 * tokens * rows * columns,
-        moved=8 * rows * columns + 4 * tokens * columns,
     )
     return {"a": a, "b": b}
 
@@ -211,8 +208,6 @@
         [(act, block((tokens, rows), plan["own"])), piece.operand(), (cot, whole(cot))]
         + [view.operand() for view in cot_oth],
         [(out, whole(out))],
-        flops=4 * tokens * rows * columns,
-        moved=4 * rows * columns + 4 * tokens * columns,
     )[0]
 
 
@@ -278,8 +273,6 @@
         ],
         aliases=aliases,
         scratch=[pltpu.SemaphoreType.DMA((parts,))],
-        flops=4 * tokens * rows * columns,
-        moved=12 * tokens * columns,
         vmem=20,
     )
 
@@ -327,8 +320,6 @@
         ins,
         [(own, whole(own)), (oth, whole(oth))],
         scratch=[pltpu.VMEM((tokens, rows), jnp.bfloat16)],
-        flops=4 * tokens * rows * columns * count,
-        moved=8 * tokens * columns,
         vmem=28,
     )
 
@@ -373,7 +364,6 @@
         outs,
         grid=(count,),
         aliases=aliases,
-        moved=4 * count * tokens * width,
     )
 
 
@@ -414,8 +404,6 @@
         ],
         grid=(steps,),
         aliases=aliases,
-        flops=16 * rows * columns,
-        moved=28 * rows * columns,
     )
 
 
@@ -449,7 +437,6 @@
         [(struct((rows, width), jnp.bfloat16), part)],
         grid=(steps,),
         aliases={} if kept is None else {count + 4: 0},
-        moved=6 * rows * columns,
     )[0]
 
 
@@ -511,13 +498,13 @@
         candidates = [[weights]]
         if j > 0:
             candidates = [arrivals(*source) for source in plan.sources[j]]
-        turn = depth - 1 if j == depth - 3 else None
-        after = [sent[-1]] if j == depth - 2 else []
+        turn = depth - 1 if j == 0 else None
+        after = [sent[0]] if j == depth - 2 else list(bufs.values()) if j == 0 else []
         xg, parcel, shard = project(
             plan, row, j, candidates, act, cot, cot_oth, xg, turn, held, after
         )
         shards.append(shard)
-        if j < depth - 3 or j == depth - 1:
+        if 0 < j < depth - 2 or j == depth - 1:
             return xg, View(parcel, 0, parcel.shape[1])
         sent.append(swap(parcel))
         arrived.extend(View(sent[-1], t * rows, rows) for t in range(j + 1 - len(arrived)))
@@ -525,21 +512,23 @@
             pieces.append(View(sent[-1], parcel.shape[1] - rows, rows))
         return xg, None
 
-    xg, held = shard_step(0, xg, held)
+    bufs = {}
     for s in range(2, depth + 1):
-        if s > 2:
-            xg, held = shard_step(s - 2, xg, held)
         if s == depth:
+            for j in range(1, depth - 1):
+                xg, held = shard_step(j, xg, held)
             grad = own_gradient(plan, row, act, pieces[depth - 1], cot, cot_oth)
             sums = values(plan, row, list(range(depth - 1)), shards, act, pieces, None)
         for h in range(CHUNKS):
-            after = [bufs["a"]] if h > 0 else []
+            after = list(bufs.values())[:1]
             if s == depth and h == CHUNKS - 1:
-                after.append(sums[0])
+                after += [sums[0], grad]
             bufs = relay(
                 plan, row, s, got[s - 1, h], act, pieces[: s - 1], part(cot, h), cot_oth[h], after
             )
             got[s, h] = {link: part(array, 0) for link, array in exchange(bufs).items()}
+            if s == 3 and h == 0:
+                xg, held = shard_step(0, xg, held)
     xg, held = shard_step(depth - 1, xg, held)
     kv_own, parcel = values(plan, row, [depth - 1], shards[-1:], act, pieces, sums, held)
     final = swap(parcel)
@@ -548,7 +537,7 @@
     moments, averaged, placed = None, None, None
     for h in range(CHUNKS):
         last = h == CHUNKS - 1
-        after = [] if h == 0 else [sent[-1]]
+        after = [] if h == 0 else [placed]
         *moments, stepped = adam(
             row, h, got[depth, h], grad, weights, first, second, moments, after + [parcel]
         )

time: 134 us -> 128 us (0.955)
  waiting for transfers between devices: 50.8 us -> 44.5 us
  starting transfers between devices: 38.7 us -> 35.6 us
  local copies, waits for them, and re-layouts: 2.62 us -> 4.9 us
    ppermute x14, waiting for transfers between devices: 15.1 us -> 9.78 us  [exchange(): lax.ppermute(bufs[name], 'fsdp', links[name])]
    ppermute x2, waiting for transfers between devices: 14 us -> 9.71 us  [partner_rows(): far = lax.ppermute(stepped, 'rep', [(r, r ^ 2) for r in range(4)])]
    ppermute x14, starting transfers between devices: 28 us -> 24.4 us  [exchange(): lax.ppermute(bufs[name], 'fsdp', links[name])]
    ppermute x2, waiting for transfers between devices: 0.01 us -> 3.27 us  [shard_step(): sent.append(swap(parcel))]
    unnamed x18 -> x20, local copies, waits for them, and re-layouts: 1.93 us -> 4.21 us
  transfers between devices with their start and end apart: 26 -> 26, of which waited for: 7 -> 7; matrix products, arithmetic and copies ran while one was open for 1% -> 1% of each run, Pallas kernels for 29% -> 31%
where the time goes in v5:
time: 128 us; the launch traced here: 127 us
  waiting for transfers between devices  44.5 us (35%)
  Pallas kernels  40.8 us (32%)
  starting transfers between devices  35.6 us (28%)
  local copies, waits for them, and re-layouts  4.9 us (4%)
    pallas_call x21, Pallas kernels, call(): pl.pallas_call(kernel, grid_spec=pltpu.PrefetchScalarGridSpec(num_scalar_...  40.8 us
    ppermute x14, starting transfers between devices, exchange(): lax.ppermute(bufs[name], 'fsdp', links[name])  24.4 us
    ppermute x1, waiting for transfers between devices, per_device(): parcel = swap(cot)  15.4 us
    ppermute x14, waiting for transfers between devices, exchange(): lax.ppermute(bufs[name], 'fsdp', links[name])  9.78 us
    ppermute x2, waiting for transfers between devices, partner_rows(): far = lax.ppermute(stepped, 'rep', [(r, r ^ 2) for r in range(4)])  9.71 us
    ppermute x2, waiting for transfers between devices, send(): return swap(pack(plan, row, rows, [], act, turns, after))  6.26 us
    unnamed x20, local copies, waits for them, and re-layouts  4.21 us
    ppermute x2, waiting for transfers between devices, shard_step(): sent.append(swap(parcel))  3.27 us
  transfers between devices with their start and end apart: 26, of which 7 were waited for; matrix products, arithmetic and copies ran while one was open for 1% of the time, Pallas kernels for 31%

profile of v5, /device:TPU:0, one launch (start us, length us, event | category | flops | bytes accessed | tf_op | source)
XLA Modules:
  0.0 126.7 jit_solution(8510471405938575592)
XLA Ops:
  1.4 5.8 %collective-permute-start = (bf16[512,1024]{1,0:T(8,128)(2,1)}, bf16[512,1024]{1,0:T(8,128)(2,1)S(1)}, u32[]{:S(2)}, u32[]{:S(2)}) collective-permute-start(bf16[512,1024]{1,0:T(8,128)(2,1)} %bitcast.47), channel_id=1, source_target_pairs={{0,2},{1,3},{2,0},{3,1},{4,6},{5,7},{6,4},{7,5},{8,10},{9,11},{10,... | collective-permute-start | bytes 3145736 | tf_op jit(solution)/shard_map/ppermute | solution.py:472
  9.4 1.9 %copy-done = bf16[1,384,4096]{2,1,0:T(8,128)(2,1)S(1)} copy-done((bf16[1,384,4096]{2,1,0:T(8,128)(2,1)S(1)}, bf16[1,384,4096]{2,1,0:T(8,128)(2,1)}, u32[]{:S(2)}) %copy-start) | copy-done | bytes 3145752
  12.5 15.4 %collective-permute-done.3.refs_6_.refs_2_.refs_7_.refs_1_.refs_3_.refs_4_.refs_5_.refs_8_.refs_0_ = bf16[384,1024]{1,0:T(8,128)(2,1)S(1)} collective-permute-done((bf16[384,1024]{1,0:T(8,128)(2,1)}, bf16[384,1024]{1,0:T(8,128)(2,1)S(1)}, u32[]{:S(2)}, u32[]{:S(2)}) %collective-permute-start.3) | collective-permute-done | bytes 786464 | tf_op jit(solution)/shard_map/ppermute | solution.py:488
  28.5 1.6 %collective-permute-start.6 = (bf16[384,1024]{1,0:T(8,128)(2,1)S(1)}, bf16[384,1024]{1,0:T(8,128)(2,1)S(1)}, u32[]{:S(2)}, u32[]{:S(2)}) collective-permute-start(bf16[384,1024]{1,0:T(8,128)(2,1)S(1)} %shard_map.121), channel_id=1, source_target_pairs={{0,1},{1,0},{2,3},{3,2},{4,5},{5,4},{6,7},{7,6},{8,9},{9,8},{10,11... | collective-permute-start | bytes 2359304 | tf_op jit(solution)/shard_map/ppermute | solution.py:486
  30.1 6.3 %collective-permute-done.2.refs_4_.refs_6_.refs_2_ = bf16[384,512]{1,0:T(8,128)(2,1)S(1)} collective-permute-done((bf16[384,512]{1,0:T(8,128)(2,1)S(1)}, bf16[384,512]{1,0:T(8,128)(2,1)S(1)}, u32[]{:S(2)}, u32[]{:S(2)}) %collective-permute-start.2) | collective-permute-done | bytes 393248 | tf_op jit(solution)/shard_map/ppermute | solution.py:486
  36.3 1.5 %shard_map.120 = (bf16[512,512]{1,0:T(8,128)(2,1)S(1)}, bf16[512,512]{1,0:T(8,128)(2,1)S(1)}) custom-call(s32[40]{0:T(128)S(1)} %dynamic-slice_bitcast_fusion.row_ref, bf16[512,1024]{1,0:T(8,128)(2,1)S(1)} %collective-permute-done.1.refs_0_.refs_1_, bf16[512,1024]{1,0:T(8,128)(2,1)S(1)} %collective-permute-done.refs_1_.refs_0_, ...), custom_call_target="tpu_custom_call" | custom-call | tf_op jit(solution)/shard_map/pallas_call | solution.py:85
  39.7 1.5 %shard_map.122 = (bf16[512,512]{1,0:T(8,128)(2,1)S(1)}, bf16[512,512]{1,0:T(8,128)(2,1)S(1)}) custom-call(s32[40]{0:T(128)S(1)} %dynamic-slice_bitcast_fusion.row_ref, bf16[512,1024]{1,0:T(8,128)(2,1)S(1)} %collective-permute-done.1.refs_0_.refs_1_, bf16[512,1024]{1,0:T(8,128)(2,1)S(1)} %collective-permute-done.refs_1_.refs_0_, ...), custom_call_target="tpu_custom_call" | custom-call | tf_op jit(solution)/shard_map/pallas_call | solution.py:85
  41.9 2.2 %collective-permute-start.9 = (bf16[512,512]{1,0:T(8,128)(2,1)S(1)}, bf16[512,512]{1,0:T(8,128)(2,1)S(1)}, u32[]{:S(2)}, u32[]{:S(2)}) collective-permute-start(bf16[512,512]{1,0:T(8,128)(2,1)S(1)} %get-tuple-element.43.refs_8_), channel_id=1, source_target_pairs={{0,2},{1,3},{2,0},{3,1},{4,6},{5,7},{6,4},{7,5},{8,10},{9,11},{10,... | collective-permute-start | bytes 1572872 | tf_op jit(solution)/shard_map/ppermute | solution.py:472
  44.0 9.5 %collective-permute-done.5.refs_1_.refs_0_ = bf16[512,512]{1,0:T(8,128)(2,1)S(1)} collective-permute-done((bf16[512,512]{1,0:T(8,128)(2,1)S(1)}, bf16[512,512]{1,0:T(8,128)(2,1)S(1)}, u32[]{:S(2)}, u32[]{:S(2)}) %collective-permute-start.5) | collective-permute-done | bytes 524320 | tf_op jit(solution)/shard_map/ppermute | solution.py:472
  55.4 2.5 %shard_map.125 = (bf16[384,4096]{1,0:T(8,128)(2,1)}, bf16[384,1024]{1,0:T(8,128)(2,1)S(1)}, bf16[512,1024]{1,0:T(8,128)(2,1)S(1)}) custom-call(s32[40]{0:T(128)S(1)} %dynamic-slice_bitcast_fusion.row_ref, bf16[512,1024]{1,0:T(8,128)(2,1)S(1)} %bitcast.48, ...), custom_call_target="tpu_custom_call" | custom-call | tf_op jit(solution)/shard_map/pallas_call | solution.py:85
  57.9 1.6 %collective-permute-start.11 = (bf16[384,1024]{1,0:T(8,128)(2,1)S(1)}, bf16[384,1024]{1,0:T(8,128)(2,1)S(1)}, u32[]{:S(2)}, u32[]{:S(2)}) collective-permute-start(bf16[384,1024]{1,0:T(8,128)(2,1)S(1)} %get-tuple-element.51), channel_id=1, source_target_pairs={{0,1},{1,0},{2,3},{3,2},{4,5},{5,4},{6,7},{7,6},{8,9},{9,8},{10,11... | collective-permute-start | bytes 2359304 | tf_op jit(solution)/shard_map/ppermute | solution.py:509
  60.1 3.9 %collective-permute-start.7 = (bf16[512,512]{1,0:T(8,128)(2,1)S(1)}, bf16[512,512]{1,0:T(8,128)(2,1)S(1)}, u32[]{:S(2)}, u32[]{:S(2)}) collective-permute-start(bf16[512,512]{1,0:T(8,128)(2,1)S(1)} %get-tuple-element.44.refs_8_.refs_5_), channel_id=1, source_target_pairs={{0,2},{1,3},{2,0},{3,1},{4,6},{5,7},{6,4},{7,5},{8,10},{9,11},{10,... | collective-permute-start | bytes 1572872 | tf_op jit(solution)/shard_map/ppermute | solution.py:472
  66.2 1.8 %collective-permute-start.10 = (bf16[512,512]{1,0:T(8,128)(2,1)S(1)}, bf16[512,512]{1,0:T(8,128)(2,1)S(1)}, u32[]{:S(2)}, u32[]{:S(2)}) collective-permute-start(bf16[512,512]{1,0:T(8,128)(2,1)S(1)} %get-tuple-element.46.refs_9_), channel_id=1, source_target_pairs={{0,2},{1,3},{2,0},{3,1},{4,6},{5,7},{6,4},{7,5},{8,10},{9,11},{10,... | collective-permute-start | bytes 1572872 | tf_op jit(solution)/shard_map/ppermute | solution.py:472
  67.9 2.4 %shard_map.126 = (bf16[384,4096]{1,0:T(8,128)(2,1)}, bf16[384,512]{1,0:T(8,128)(2,1)S(1)}, bf16[512,1024]{1,0:T(8,128)(2,1)S(1)}) custom-call(s32[40]{0:T(128)S(1)} %dynamic-slice_bitcast_fusion.row_ref, bf16[512,1024]{1,0:T(8,128)(2,1)S(1)} %collective-permute-done.refs_1_.refs_0_, ...), custom_call_target="tpu_custom_call", output_to_operand_aliasing={{0}: (6, {})} | custom-call | tf_op jit(solution)/shard_map/pallas_call | solution.py:85
  70.4 3.3 %collective-permute-done.11.refs_9_.refs_5_.refs_0_.piece_ref = bf16[384,1024]{1,0:T(8,128)(2,1)S(1)} collective-permute-done((bf16[384,1024]{1,0:T(8,128)(2,1)S(1)}, bf16[384,1024]{1,0:T(8,128)(2,1)S(1)}, u32[]{:S(2)}, u32[]{:S(2)}) %collective-permute-start.11) | collective-permute-done | bytes 786464 | tf_op jit(solution)/shard_map/ppermute | solution.py:509
  73.7 2.5 %shard_map.127 = (bf16[384,4096]{1,0:T(8,128)(2,1)}, bf16[384,1024]{1,0:T(8,128)(2,1)S(1)}, bf16[512,1024]{1,0:T(8,128)(2,1)S(1)}) custom-call(s32[40]{0:T(128)S(1)} %dynamic-slice_bitcast_fusion.row_ref, bf16[512,512]{1,0:T(8,128)(2,1)S(1)} %collective-permute-done.5.refs_1_.refs_0_, ...), custom_call_target="tpu_custom_call", output_to_operand_aliasing={{0}: (9, {})} | custom-call | tf_op jit(solution)/shard_map/pallas_call | solution.py:85
  76.2 1.6 %collective-permute-start.13 = (bf16[384,1024]{1,0:T(8,128)(2,1)S(1)}, bf16[384,1024]{1,0:T(8,128)(2,1)S(1)}, u32[]{:S(2)}, u32[]{:S(2)}) collective-permute-start(bf16[384,1024]{1,0:T(8,128)(2,1)S(1)} %get-tuple-element.62), channel_id=1, source_target_pairs={{0,1},{1,0},{2,3},{3,2},{4,5},{5,4},{6,7},{7,6},{8,9},{9,8},{10,11... | collective-permute-start | bytes 2359304 | tf_op jit(solution)/shard_map/ppermute | solution.py:509
  80.0 4.0 %collective-permute-start.18 = (bf16[512,512]{1,0:T(8,128)(2,1)S(1)}, bf16[512,512]{1,0:T(8,128)(2,1)S(1)}, u32[]{:S(2)}, u32[]{:S(2)}) collective-permute-start(bf16[512,512]{1,0:T(8,128)(2,1)S(1)} %get-tuple-element.67.refs_9_), channel_id=1, source_target_pairs={{0,2},{1,3},{2,0},{3,1},{4,6},{5,7},{6,4},{7,5},{8,10},{9,11},{10,... | collective-permute-start | bytes 1572872 | tf_op jit(solution)/shard_map/ppermute | solution.py:472
  84.0 1.8 %shard_map.134.refs_11_.grad_ref = f32[512,1024]{1,0:T(8,128)S(1)} custom-call(s32[40]{0:T(128)S(1)} %dynamic-slice_bitcast_fusion.row_ref, bf16[384,4096]{1,0:T(8,128)(2,1)S(1)} %bitcast.26, bf16[384,1024]{1,0:T(8,128)(2,1)S(1)} %collective-permute-done.11.refs_9_.refs_5_.refs_0_.piece_ref, bf16[384,1024]{1,0:T(8,128)(2,1)S(1)} %bitcast.43, ...), custom_call_target="tpu_custom_call" | custom-call | tf_op jit(solution)/shard_map/pallas_call | solution.py:85
  85.8 3.9 %shard_map.129 = (f32[384,1024]{1,0:T(8,128)S(1)}, f32[384,1024]{1,0:T(8,128)S(1)}) custom-call(s32[40]{0:T(128)S(1)} %dynamic-slice_bitcast_fusion.row_ref, bf16[512,1024]{1,0:T(8,128)(2,1)S(1)} %get-tuple-element.54.refs_0_, bf16[512,1024]{1,0:T(8,128)(2,1)S(1)} %get-tuple-element.55.refs_1_, bf16[512,1024]{1,0:T(8,128)(2,1)S(1)} %get-tuple-element.56.refs_2_, ...), custom_call_target="tpu_custom_call" | custom-call | tf_op jit(solution)/shard_map/pallas_call | solution.py:85
  89.7 1.5 %shard_map.135 = (bf16[512,512]{1,0:T(8,128)(2,1)S(1)}, bf16[512,512]{1,0:T(8,128)(2,1)S(1)}) custom-call(s32[40]{0:T(128)S(1)} %dynamic-slice_bitcast_fusion.row_ref, bf16[512,512]{1,0:T(8,128)(2,1)S(1)} %collective-permute-done.14.refs_0_, bf16[512,512]{1,0:T(8,128)(2,1)S(1)} %collective-permute-done.10.refs_2_.refs_1_, bf16[384,4096]{1,0:T(8,128)(2,1)S(1)} %bitcast.30, ...), custom_call_target="tpu_custom_call" | custom-call | tf_op jit(solution)/shard_map/pallas_call | solution.py:85
  92.7 2.5 %shard_map.128 = (bf16[384,4096]{1,0:T(8,128)(2,1)}, bf16[384,512]{1,0:T(8,128)(2,1)S(1)}, bf16[512,1024]{1,0:T(8,128)(2,1)S(1)}) custom-call(s32[40]{0:T(128)S(1)} %dynamic-slice_bitcast_fusion.row_ref, bf16[512,1024]{1,0:T(8,128)(2,1)S(1)} %collective-permute-done.refs_1_.refs_0_, ...), custom_call_target="tpu_custom_call", output_to_operand_aliasing={{0}: (7, {})} | custom-call | tf_op jit(solution)/shard_map/pallas_call | solution.py:85
  95.3 1.9 %shard_map.130 = (f32[384,1024]{1,0:T(8,128)S(1)}, bf16[384,1536]{1,0:T(8,128)(2,1)S(1)}) custom-call(s32[40]{0:T(128)S(1)} %dynamic-slice_bitcast_fusion.row_ref, bf16[512,1024]{1,0:T(8,128)(2,1)S(1)} %get-tuple-element.53.refs_0_, bf16[384,4096]{1,0:T(8,128)(2,1)S(1)} %bitcast.32, bf16[384,512]{1,0:T(8,128)(2,1)S(1)} %collective-permute-done.2.refs_4_.refs_6_.refs_2_, ...), custom_call_target="tpu_custom_call" | custom-call | tf_op jit(solution)/shard_map/pallas_call | solution.py:85
  98.5 3.1 %shard_map.136 = (f32[512,1024]{1,0:T(8,128)}, f32[512,1024]{1,0:T(8,128)}, bf16[512,512]{1,0:T(8,128)(2,1)S(1)}) custom-call(s32[40]{0:T(128)S(1)} %dynamic-slice_bitcast_fusion.row_ref, bf16[512,512]{1,0:T(8,128)(2,1)S(1)} %collective-permute-done.18.up_ref, bf16[512,512]{1,0:T(8,128)(2,1)S(1)} %collective-permute-done.19.dn_ref, ...), custom_call_target="tpu_custom_call" | custom-call | tf_op jit(solution)/shard_map/pallas_call | solution.py:85
  101.5 1.5 %collective-permute-start.24 = (bf16[512,512]{1,0:T(8,128)(2,1)S(1)}, bf16[512,512]{1,0:T(8,128)(2,1)S(1)}, u32[]{:S(2)}, u32[]{:S(2)}) collective-permute-start(bf16[512,512]{1,0:T(8,128)(2,1)S(1)} %get-tuple-element.74.stepped_ref), channel_id=1, source_target_pairs={{0,16},{8,24},{16,0},{24,8},{1,17},{9,25},{17,1},{25,9},{2,18},{10... | collective-permute-start | bytes 1572872 | tf_op jit(solution)/shard_map/ppermute | solution.py:447
  103.0 2.2 %shard_map.131.refs_3_.refs_2_ = bf16[384,4096]{1,0:T(8,128)(2,1)} custom-call(s32[40]{0:T(128)S(1)} %dynamic-slice_bitcast_fusion.row_ref, bf16[384,1024]{1,0:T(8,128)(2,1)S(1)} %collective-permute-done.11.refs_9_.refs_5_.refs_0_.piece_ref, bf16[384,1024]{1,0:T(8,128)(2,1)S(1)} %collective-permute-done.13.refs_1_.refs_2_, ...), custom_call_target="tpu_custom_call", output_to_operand_aliasing={{}: (4, {})} | custom-call | tf_op jit(solution)/shard_map/pallas_call | solution.py:85
  105.3 1.9 %copy-done.2 = bf16[384,4096]{1,0:T(8,128)(2,1)S(1)} copy-done((bf16[384,4096]{1,0:T(8,128)(2,1)S(1)}, bf16[384,4096]{1,0:T(8,128)(2,1)}, u32[]{:S(2)}) %copy-start.2) | copy-done | bytes 3145752
  107.2 3.1 %shard_map.137 = (f32[512,1024]{1,0:T(8,128)}, f32[512,1024]{1,0:T(8,128)}, bf16[512,512]{1,0:T(8,128)(2,1)S(1)}) custom-call(s32[40]{0:T(128)S(1)} %dynamic-slice_bitcast_fusion.row_ref, bf16[512,512]{1,0:T(8,128)(2,1)S(1)} %collective-permute-done.16.up_ref, ...), custom_call_target="tpu_custom_call", output_to_operand_aliasing={{0}: (7, {}), {1}: (8, {})} | custom-call | tf_op jit(solution)/shard_map/pallas_call | solution.py:85
  113.4 8.5 %collective-permute-done.21.refs_1_ = bf16[512,512]{1,0:T(8,128)(2,1)S(1)} collective-permute-done((bf16[512,512]{1,0:T(8,128)(2,1)S(1)}, bf16[512,512]{1,0:T(8,128)(2,1)S(1)}, u32[]{:S(2)}, u32[]{:S(2)}) %collective-permute-start.21) | collective-permute-done | bytes 524320 | tf_op jit(solution)/shard_map/ppermute | solution.py:447
  122.0 1.7 %shard_map.132 = (bf16[384,4096]{1,0:T(8,128)(2,1)}, bf16[384,1024]{1,0:T(8,128)(2,1)}) custom-call(s32[40]{0:T(128)S(1)} %dynamic-slice_bitcast_fusion.row_ref, bf16[384,1536]{1,0:T(8,128)(2,1)S(1)} %collective-permute-done.12.refs_0_.refs_2_.refs_3_, f32[384,1024]{1,0:T(8,128)S(1)} %get-tuple-element.61.refs_1_, ...), custom_call_target="tpu_custom_call", output_to_operand_aliasing={{0}: (4, {})} | custom-call | tf_op jit(solution)/shard_map/pallas_call | solution.py:85
  123.7 1.5 %shard_map.138.refs_3_ = bf16[512,1024]{1,0:T(8,128)(2,1)} custom-call(s32[40]{0:T(128)S(1)} %dynamic-slice_bitcast_fusion.row_ref, s32[4]{0:T(128)S(1)} %copy-done.8, s32[4]{0:T(128)S(1)} %copy-done.9, bf16[512,512]{1,0:T(8,128)(2,1)S(1)} %get-tuple-element.74.stepped_ref, bf16[512,512]{1,0:T(8,128)(2,1)S(1)} %collective-permute-done.23.refs_0_, ...), custom_call_target="tpu_custom_call" | custom-call | tf_op jit(solution)/shard_map/pallas_call | solution.py:85
  125.2 1.5 %shard_map.139 = bf16[512,1024]{1,0:T(8,128)(2,1)} custom-call(s32[40]{0:T(128)S(1)} %dynamic-slice_bitcast_fusion.row_ref, s32[4]{0:T(128)S(1)} %copy-done.8, s32[4]{0:T(128)S(1)} %copy-done.9, bf16[512,512]{1,0:T(8,128)(2,1)S(1)} %get-tuple-element.73.stepped_ref, ...), custom_call_target="tpu_custom_call", output_to_operand_aliasing={{}: (7, {})} | custom-call | tf_op jit(solution)/shard_map/pallas_call | solution.py:85
  (62 shorter events, 20.1 us)
Async XLA Ops:
  0.6 35.7 %collective-permute-start.1 = (bf16[512,1024]{1,0:T(8,128)(2,1)}, bf16[512,1024]{1,0:T(8,128)(2,1)S(1)}, u32[]{:S(2)}, u32[]{:S(2)}) collective-permute-start(bf16[512,1024]{1,0:T(8,128)(2,1)} %bitcast.46), channel_id=1, source_target_pairs={{2,4},{3,5},{4,2},{5,3},{10,12},{11,13},{12,10},{13,11},{18,20},{1... | collective-permute-start | bytes 3145736 | tf_op jit(solution)/shard_map/ppermute | solution.py:472
  1.4 35.0 %collective-permute-start = (bf16[512,1024]{1,0:T(8,128)(2,1)}, bf16[512,1024]{1,0:T(8,128)(2,1)S(1)}, u32[]{:S(2)}, u32[]{:S(2)}) collective-permute-start(bf16[512,1024]{1,0:T(8,128)(2,1)} %bitcast.47), channel_id=1, source_target_pairs={{0,2},{1,3},{2,0},{3,1},{4,6},{5,7},{6,4},{7,5},{8,10},{9,11},{10,... | collective-permute-start | bytes 3145736 | tf_op jit(solution)/shard_map/ppermute | solution.py:472
  7.2 20.7 %collective-permute-start.3 = (bf16[384,1024]{1,0:T(8,128)(2,1)}, bf16[384,1024]{1,0:T(8,128)(2,1)S(1)}, u32[]{:S(2)}, u32[]{:S(2)}) collective-permute-start(bf16[384,1024]{1,0:T(8,128)(2,1)} %bitcast.34), channel_id=1, source_target_pairs={{0,1},{1,0},{2,3},{3,2},{4,5},{5,4},{6,7},{7,6},{8,9},{9,8},{10,11... | collective-permute-start | bytes 2359304 | tf_op jit(solution)/shard_map/ppermute | solution.py:488
  11.9 24.5 %copy-start.3 = (bf16[1,384,1024]{2,1,0:T(8,128)(2,1)S(1)}, bf16[1,384,1024]{2,1,0:T(8,128)(2,1)}, u32[]{:S(2)}) copy-start(bf16[1,384,1024]{2,1,0:T(8,128)(2,1)} %param.10) | copy-start | bytes 2359300
  11.9 24.5 %collective-permute-start.2 = (bf16[384,512]{1,0:T(8,128)(2,1)S(1)}, bf16[384,512]{1,0:T(8,128)(2,1)S(1)}, u32[]{:S(2)}, u32[]{:S(2)}) collective-permute-start(bf16[384,512]{1,0:T(8,128)(2,1)S(1)} %shard_map.119), channel_id=1, source_target_pairs={{0,1},{1,0},{2,3},{3,2},{4,5},{5,4},{6,7},{7,6},{8,9},{9,8},{10,11... | collective-permute-start | bytes 1179656 | tf_op jit(solution)/shard_map/ppermute | solution.py:486
  28.5 25.0 %collective-permute-start.6 = (bf16[384,1024]{1,0:T(8,128)(2,1)S(1)}, bf16[384,1024]{1,0:T(8,128)(2,1)S(1)}, u32[]{:S(2)}, u32[]{:S(2)}) collective-permute-start(bf16[384,1024]{1,0:T(8,128)(2,1)S(1)} %shard_map.121), channel_id=1, source_target_pairs={{0,1},{1,0},{2,3},{3,2},{4,5},{5,4},{6,7},{7,6},{8,9},{9,8},{10,11... | collective-permute-start | bytes 2359304 | tf_op jit(solution)/shard_map/ppermute | solution.py:486
  37.9 6.2 %collective-permute-start.4 = (bf16[512,512]{1,0:T(8,128)(2,1)S(1)}, bf16[512,512]{1,0:T(8,128)(2,1)S(1)}, u32[]{:S(2)}, u32[]{:S(2)}) collective-permute-start(bf16[512,512]{1,0:T(8,128)(2,1)S(1)} %get-tuple-element.41), channel_id=1, source_target_pairs={{2,4},{3,5},{4,2},{5,3},{10,12},{11,13},{12,10},{13,11},{18,20},{1... | collective-permute-start | bytes 1572872 | tf_op jit(solution)/shard_map/ppermute | solution.py:472
  38.6 14.9 %collective-permute-start.5 = (bf16[512,512]{1,0:T(8,128)(2,1)S(1)}, bf16[512,512]{1,0:T(8,128)(2,1)S(1)}, u32[]{:S(2)}, u32[]{:S(2)}) collective-permute-start(bf16[512,512]{1,0:T(8,128)(2,1)S(1)} %get-tuple-element.42.refs_7_), channel_id=1, source_target_pairs={{0,2},{1,3},{2,0},{3,1},{4,6},{5,7},{6,4},{7,5},{8,10},{9,11},{10,... | collective-permute-start | bytes 1572872 | tf_op jit(solution)/shard_map/ppermute | solution.py:472
  41.2 22.8 %collective-permute-start.8 = (bf16[512,512]{1,0:T(8,128)(2,1)S(1)}, bf16[512,512]{1,0:T(8,128)(2,1)S(1)}, u32[]{:S(2)}, u32[]{:S(2)}) collective-permute-start(bf16[512,512]{1,0:T(8,128)(2,1)S(1)} %get-tuple-element.45), channel_id=1, source_target_pairs={{2,4},{3,5},{4,2},{5,3},{10,12},{11,13},{12,10},{13,11},{18,20},{1... | collective-permute-start | bytes 1572872 | tf_op jit(solution)/shard_map/ppermute | solution.py:472
  41.9 13.1 %copy-start.4 = (bf16[1,512,1024]{2,1,0:T(8,128)(2,1)S(1)}, bf16[1,512,1024]{2,1,0:T(8,128)(2,1)}, u32[]{:S(2)}) copy-start(bf16[1,512,1024]{2,1,0:T(8,128)(2,1)} %param.9) | copy-start | bytes 3145732
  41.9 22.1 %collective-permute-start.9 = (bf16[512,512]{1,0:T(8,128)(2,1)S(1)}, bf16[512,512]{1,0:T(8,128)(2,1)S(1)}, u32[]{:S(2)}, u32[]{:S(2)}) collective-permute-start(bf16[512,512]{1,0:T(8,128)(2,1)S(1)} %get-tuple-element.43.refs_8_), channel_id=1, source_target_pairs={{0,2},{1,3},{2,0},{3,1},{4,6},{5,7},{6,4},{7,5},{8,10},{9,11},{10,... | collective-permute-start | bytes 1572872 | tf_op jit(solution)/shard_map/ppermute | solution.py:472
  53.5 1.9 %copy-start.1 = (bf16[1,384,4096]{2,1,0:T(8,128)(2,1)S(1)}, bf16[1,384,4096]{2,1,0:T(8,128)(2,1)}, u32[]{:S(2)}) copy-start(bf16[1,384,4096]{2,1,0:T(8,128)(2,1)} %param.8) | copy-start | bytes 9437188
  57.9 15.8 %collective-permute-start.11 = (bf16[384,1024]{1,0:T(8,128)(2,1)S(1)}, bf16[384,1024]{1,0:T(8,128)(2,1)S(1)}, u32[]{:S(2)}, u32[]{:S(2)}) collective-permute-start(bf16[384,1024]{1,0:T(8,128)(2,1)S(1)} %get-tuple-element.51), channel_id=1, source_target_pairs={{0,1},{1,0},{2,3},{3,2},{4,5},{5,4},{6,7},{7,6},{8,9},{9,8},{10,11... | collective-permute-start | bytes 2359304 | tf_op jit(solution)/shard_map/ppermute | solution.py:509
  59.4 18.3 %collective-permute-start.15 = (bf16[512,512]{1,0:T(8,128)(2,1)S(1)}, bf16[512,512]{1,0:T(8,128)(2,1)S(1)}, u32[]{:S(2)}, u32[]{:S(2)}) collective-permute-start(bf16[512,512]{1,0:T(8,128)(2,1)S(1)} %get-tuple-element.47.refs_6_), channel_id=1, source_target_pairs={{2,4},{3,5},{4,2},{5,3},{10,12},{11,13},{12,10},{13,11},{18,20},{1... | collective-permute-start | bytes 1572872 | tf_op jit(solution)/shard_map/ppermute | solution.py:472
  60.1 17.6 %collective-permute-start.7 = (bf16[512,512]{1,0:T(8,128)(2,1)S(1)}, bf16[512,512]{1,0:T(8,128)(2,1)S(1)}, u32[]{:S(2)}, u32[]{:S(2)}) collective-permute-start(bf16[512,512]{1,0:T(8,128)(2,1)S(1)} %get-tuple-element.44.refs_8_.refs_5_), channel_id=1, source_target_pairs={{0,2},{1,3},{2,0},{3,1},{4,6},{5,7},{6,4},{7,5},{8,10},{9,11},{10,... | collective-permute-start | bytes 1572872 | tf_op jit(solution)/shard_map/ppermute | solution.py:472
  65.5 24.2 %collective-permute-start.14 = (bf16[512,512]{1,0:T(8,128)(2,1)S(1)}, bf16[512,512]{1,0:T(8,128)(2,1)S(1)}, u32[]{:S(2)}, u32[]{:S(2)}) collective-permute-start(bf16[512,512]{1,0:T(8,128)(2,1)S(1)} %get-tuple-element.66), channel_id=1, source_target_pairs={{2,4},{3,5},{4,2},{5,3},{10,12},{11,13},{12,10},{13,11},{18,20},{1... | collective-permute-start | bytes 1572872 | tf_op jit(solution)/shard_map/ppermute | solution.py:472
  66.2 23.5 %collective-permute-start.10 = (bf16[512,512]{1,0:T(8,128)(2,1)S(1)}, bf16[512,512]{1,0:T(8,128)(2,1)S(1)}, u32[]{:S(2)}, u32[]{:S(2)}) collective-permute-start(bf16[512,512]{1,0:T(8,128)(2,1)S(1)} %get-tuple-element.46.refs_9_), channel_id=1, source_target_pairs={{0,2},{1,3},{2,0},{3,1},{4,6},{5,7},{6,4},{7,5},{8,10},{9,11},{10,... | collective-permute-start | bytes 1572872 | tf_op jit(solution)/shard_map/ppermute | solution.py:472
  76.2 26.8 %collective-permute-start.13 = (bf16[384,1024]{1,0:T(8,128)(2,1)S(1)}, bf16[384,1024]{1,0:T(8,128)(2,1)S(1)}, u32[]{:S(2)}, u32[]{:S(2)}) collective-permute-start(bf16[384,1024]{1,0:T(8,128)(2,1)S(1)} %get-tuple-element.62), channel_id=1, source_target_pairs={{0,1},{1,0},{2,3},{3,2},{4,5},{5,4},{6,7},{7,6},{8,9},{9,8},{10,11... | collective-permute-start | bytes 2359304 | tf_op jit(solution)/shard_map/ppermute | solution.py:509
  79.3 17.9 %collective-permute-start.19 = (bf16[512,512]{1,0:T(8,128)(2,1)S(1)}, bf16[512,512]{1,0:T(8,128)(2,1)S(1)}, u32[]{:S(2)}, u32[]{:S(2)}) collective-permute-start(bf16[512,512]{1,0:T(8,128)(2,1)S(1)} %get-tuple-element.70), channel_id=1, source_target_pairs={{2,4},{3,5},{4,2},{5,3},{10,12},{11,13},{12,10},{13,11},{18,20},{1... | collective-permute-start | bytes 1572872 | tf_op jit(solution)/shard_map/ppermute | solution.py:472
  80.0 18.5 %collective-permute-start.18 = (bf16[512,512]{1,0:T(8,128)(2,1)S(1)}, bf16[512,512]{1,0:T(8,128)(2,1)S(1)}, u32[]{:S(2)}, u32[]{:S(2)}) collective-permute-start(bf16[512,512]{1,0:T(8,128)(2,1)S(1)} %get-tuple-element.67.refs_9_), channel_id=1, source_target_pairs={{0,2},{1,3},{2,0},{3,1},{4,6},{5,7},{6,4},{7,5},{8,10},{9,11},{10,... | collective-permute-start | bytes 1572872 | tf_op jit(solution)/shard_map/ppermute | solution.py:472
  91.2 14.0 %collective-permute-start.16 = (bf16[512,512]{1,0:T(8,128)(2,1)S(1)}, bf16[512,512]{1,0:T(8,128)(2,1)S(1)}, u32[]{:S(2)}, u32[]{:S(2)}) collective-permute-start(bf16[512,512]{1,0:T(8,128)(2,1)S(1)} %get-tuple-element.68), channel_id=1, source_target_pairs={{0,2},{1,3},{2,0},{3,1},{4,6},{5,7},{6,4},{7,5},{8,10},{9,11},{10,... | collective-permute-start | bytes 1572872 | tf_op jit(solution)/shard_map/ppermute | solution.py:472
  92.1 13.2 %collective-permute-start.17 = (bf16[512,512]{1,0:T(8,128)(2,1)S(1)}, bf16[512,512]{1,0:T(8,128)(2,1)S(1)}, u32[]{:S(2)}, u32[]{:S(2)}) collective-permute-start(bf16[512,512]{1,0:T(8,128)(2,1)S(1)} %get-tuple-element.69), channel_id=1, source_target_pairs={{2,4},{3,5},{4,2},{5,3},{10,12},{11,13},{12,10},{13,11},{18,20},{1... | collective-permute-start | bytes 1572872 | tf_op jit(solution)/shard_map/ppermute | solution.py:472
  95.3 3.2 %copy-start.5 = (f32[1,512,1024]{2,1,0:T(8,128)S(1)}, f32[1,512,1024]{2,1,0:T(8,128)}, u32[]{:S(2)}) copy-start(f32[1,512,1024]{2,1,0:T(8,128)} %param.11) | copy-start | bytes 6291460
  95.3 3.2 %copy-start.6 = (f32[1,512,1024]{2,1,0:T(8,128)S(1)}, f32[1,512,1024]{2,1,0:T(8,128)}, u32[]{:S(2)}) copy-start(f32[1,512,1024]{2,1,0:T(8,128)} %param.12) | copy-start | bytes 6291460
  97.2 24.7 %collective-permute-start.12 = (bf16[384,1536]{1,0:T(8,128)(2,1)S(1)}, bf16[384,1536]{1,0:T(8,128)(2,1)S(1)}, u32[]{:S(2)}, u32[]{:S(2)}) collective-permute-start(bf16[384,1536]{1,0:T(8,128)(2,1)S(1)} %get-tuple-element.60.refs_0_.refs_3_), channel_id=1, source_target_pairs={{0,1},{1,0},{2,3},{3,2},{4,5},{5,4},{6,7},{7,6},{8,9},{9,8},{10,11... | collective-permute-start | bytes 3538952 | tf_op jit(solution)/shard_map/ppermute | solution.py:534
  101.5 11.4 %collective-permute-start.24 = (bf16[512,512]{1,0:T(8,128)(2,1)S(1)}, bf16[512,512]{1,0:T(8,128)(2,1)S(1)}, u32[]{:S(2)}, u32[]{:S(2)}) collective-permute-start(bf16[512,512]{1,0:T(8,128)(2,1)S(1)} %get-tuple-element.74.stepped_ref), channel_id=1, source_target_pairs={{0,16},{8,24},{16,0},{24,8},{1,17},{9,25},{17,1},{25,9},{2,18},{10... | collective-permute-start | bytes 1572872 | tf_op jit(solution)/shard_map/ppermute | solution.py:447
  105.3 1.9 %copy-start.2 = (bf16[384,4096]{1,0:T(8,128)(2,1)S(1)}, bf16[384,4096]{1,0:T(8,128)(2,1)}, u32[]{:S(2)}) copy-start(bf16[384,4096]{1,0:T(8,128)(2,1)} %shard_map.131.refs_3_.refs_2_) | copy-start | bytes 9437188
  110.2 11.7 %collective-permute-start.21 = (bf16[512,512]{1,0:T(8,128)(2,1)S(1)}, bf16[512,512]{1,0:T(8,128)(2,1)S(1)}, u32[]{:S(2)}, u32[]{:S(2)}) collective-permute-start(bf16[512,512]{1,0:T(8,128)(2,1)S(1)} %get-tuple-element.73.stepped_ref), channel_id=1, source_target_pairs={{0,16},{8,24},{16,0},{24,8},{1,17},{9,25},{17,1},{25,9},{2,18},{10... | collective-permute-start | bytes 1572872 | tf_op jit(solution)/shard_map/ppermute | solution.py:447
  111.7 11.9 %collective-permute-start.23 = (bf16[512,512]{1,0:T(8,128)(2,1)S(1)}, bf16[512,512]{1,0:T(8,128)(2,1)S(1)}, u32[]{:S(2)}, u32[]{:S(2)}) collective-permute-start(bf16[512,512]{1,0:T(8,128)(2,1)S(1)} %get-tuple-element.74.stepped_ref), channel_id=1, source_target_pairs={{0,8},{8,0},{16,24},{24,16},{1,9},{9,1},{17,25},{25,17},{2,10},{10... | collective-permute-start | bytes 1572872 | tf_op jit(solution)/shard_map/ppermute | solution.py:449
  112.9 10.7 %collective-permute-start.25 = (bf16[512,512]{1,0:T(8,128)(2,1)S(1)}, bf16[512,512]{1,0:T(8,128)(2,1)S(1)}, u32[]{:S(2)}, u32[]{:S(2)}) collective-permute-start(bf16[512,512]{1,0:T(8,128)(2,1)S(1)} %collective-permute-done.24.refs_1_), channel_id=1, source_target_pairs={{0,8},{8,0},{16,24},{24,16},{1,9},{9,1},{17,25},{25,17},{2,10},{10... | collective-permute-start | bytes 1572872 | tf_op jit(solution)/shard_map/ppermute | solution.py:449
  112.9 12.3 %collective-permute-start.20 = (bf16[512,512]{1,0:T(8,128)(2,1)S(1)}, bf16[512,512]{1,0:T(8,128)(2,1)S(1)}, u32[]{:S(2)}, u32[]{:S(2)}) collective-permute-start(bf16[512,512]{1,0:T(8,128)(2,1)S(1)} %get-tuple-element.73.stepped_ref), channel_id=1, source_target_pairs={{0,8},{8,0},{16,24},{24,16},{1,9},{9,1},{17,25},{25,17},{2,10},{10... | collective-permute-start | bytes 1572872 | tf_op jit(solution)/shard_map/ppermute | solution.py:449
  121.9 3.3 %collective-permute-start.22 = (bf16[512,512]{1,0:T(8,128)(2,1)S(1)}, bf16[512,512]{1,0:T(8,128)(2,1)S(1)}, u32[]{:S(2)}, u32[]{:S(2)}) collective-permute-start(bf16[512,512]{1,0:T(8,128)(2,1)S(1)} %collective-permute-done.21.refs_1_), channel_id=1, source_target_pairs={{0,8},{8,0},{16,24},{24,16},{1,9},{9,1},{17,25},{25,17},{2,10},{10... | collective-permute-start | bytes 1572872 | tf_op jit(solution)/shard_map/ppermute | solution.py:449
  (4 other events, 6.9 us)

commit v6 on v5

--- a/solution.py
+++ b/solution.py
@@ -211,14 +211,13 @@
     )[0]
 
 
-def project(plan, row, j, candidates, act, cot, cot_oth, xg_before, turn=None, front=None, after=()):
+def project(plan, row, j, candidates, act, cot, cot_oth, xg_before, turns=(), after=()):
     (tokens, columns), rows = cot.shape, candidates[0][0].shape[0]
     flat = [c for candidate in candidates for c in candidate]
     starts = np.cumsum([0] + [len(candidate) for candidate in candidates])
     parts = max(len(candidate) for candidate in candidates)
     n_w, n_c = len(flat), len(cot_oth)
-    ahead = 0 if front is None else front.count
-    width = ahead + rows + (0 if turn is None else rows)
+    width = rows * (1 + len(turns))
 
     def kernel(row_ref, *refs):
         w_refs, cot_refs = refs[:n_w], refs[n_w : n_w + n_c]
@@ -242,19 +241,14 @@
         for ref, view in zip(cot_refs, cot_oth):
             total = total + dot(ref[...], w_out[:, at : at + view.count], NT)
             at += view.count
-        xg_oth[:, ahead : ahead + rows] = total.astype(jnp.bfloat16)
-        rest = list(refs[n_w + n_c + 1 :])
-        if front is not None:
-            xg_oth[:, :ahead] = rest.pop(0)[...]
-        if turn is not None:
-            xg_oth[:, ahead + rows :] = rest.pop(0)[...]
+        xg_oth[:, :rows] = total.astype(jnp.bfloat16)
+        for t in range(len(turns)):
+            ref = refs[n_w + n_c + 1 + t]
+            xg_oth[:, (t + 1) * rows : (t + 2) * rows] = ref[...]
         xg_own[...] = dot(own_ref[...], w_out[...], NT).astype(jnp.bfloat16)
 
     ins = [(w, ANY) for w in flat] + [view.operand() for view in cot_oth] + [(cot, whole(cot))]
-    if front is not None:
-        ins.append(front.operand())
-    if turn is not None:
-        ins.append((act, block((tokens, rows), plan[f"pack{turn}"])))
+    ins += [(act, block((tokens, rows), plan[f"pack{turn}"])) for turn in turns]
     aliases = {}
     if xg_before is not None:
         aliases = {1 + len(ins): 0}
@@ -488,35 +482,33 @@
     parcel = swap(cot)
     cot_oth = [part(parcel, h) for h in range(CHUNKS)]
     pieces = [View(send(0), 0, rows)]
-    parcel = send(*range(1, depth - 1), after=[parcel])
-    pieces += [View(parcel, k * rows, rows) for k in range(depth - 2)]
-
-    arrived, shards, sent = [], [], []
-    xg, held = None, None
-
-    def shard_step(j, xg, held):
+
+    arrived, shards = [], []
+
+    def shard_step(j, xg, turns, after=()):
         candidates = [[weights]]
         if j > 0:
             candidates = [arrivals(*source) for source in plan.sources[j]]
-        turn = depth - 1 if j == 0 else None
-        after = [sent[0]] if j == depth - 2 else list(bufs.values()) if j == 0 else []
-        xg, parcel, shard = project(
-            plan, row, j, candidates, act, cot, cot_oth, xg, turn, held, after
-        )
+        ahead = turns if j > 0 else []
+        xg, parcel, shard = project(plan, row, j, candidates, act, cot, cot_oth, xg, ahead, after)
         shards.append(shard)
-        if 0 < j < depth - 2 or j == depth - 1:
-            return xg, View(parcel, 0, parcel.shape[1])
-        sent.append(swap(parcel))
-        arrived.extend(View(sent[-1], t * rows, rows) for t in range(j + 1 - len(arrived)))
-        if turn is not None:
-            pieces.append(View(sent[-1], parcel.shape[1] - rows, rows))
+        if j == 0:
+            front = View(parcel, 0, rows)
+            parcel = pack(plan, row, rows, [front], act, turns, [pieces[0].array])
+        if j == depth - 1:
+            return xg, View(parcel, 0, rows)
+        parcel = swap(parcel)
+        arrived.append(View(parcel, 0, rows))
+        pieces.extend(View(parcel, (t + 1) * rows, rows) for t in range(len(turns)))
         return xg, None
 
+    xg, _ = shard_step(0, None, range(1, depth - 1))
     bufs = {}
     for s in range(2, depth + 1):
         if s == depth:
             for j in range(1, depth - 1):
-                xg, held = shard_step(j, xg, held)
+                turns = [depth - 1] if j == 1 else []
+                xg, _ = shard_step(j, xg, turns, [arrived[-1].array])
             grad = own_gradient(plan, row, act, pieces[depth - 1], cot, cot_oth)
             sums = values(plan, row, list(range(depth - 1)), shards, act, pieces, None)
         for h in range(CHUNKS):
@@ -527,9 +519,7 @@
                 plan, row, s, got[s - 1, h], act, pieces[: s - 1], part(cot, h), cot_oth[h], after
             )
             got[s, h] = {link: part(array, 0) for link, array in exchange(bufs).items()}
-            if s == 3 and h == 0:
-                xg, held = shard_step(0, xg, held)
-    xg, held = shard_step(depth - 1, xg, held)
+    xg, held = shard_step(depth - 1, xg, [])
     kv_own, parcel = values(plan, row, [depth - 1], shards[-1:], act, pieces, sums, held)
     final = swap(parcel)
 

time: 128 us -> 136 us (1.062)
  waiting for transfers between devices: 44.5 us -> 49.4 us
  starting transfers between devices: 35.6 us -> 37.9 us
    ppermute x2 -> x3, waiting for transfers between devices: 3.27 us -> 13.9 us  [shard_step(): parcel = swap(parcel)]
    ppermute x1, waiting for transfers between devices: 15.4 us -> 9.52 us  [per_device(): parcel = swap(cot)]
    ppermute x14, waiting for transfers between devices: 9.78 us -> 12 us  [exchange(): lax.ppermute(bufs[name], 'fsdp', links[name])]
    ppermute x2 -> x1, starting transfers between devices: 2.16 us -> 0.09 us  [send(): return swap(pack(plan, row, rows, [], act, turns, after))]
    ppermute x1, starting transfers between devices: 1.49 us -> 3 us  [per_device(): parcel = swap(cot)]
    ppermute x14, starting transfers between devices: 24.4 us -> 25.8 us  [exchange(): lax.ppermute(bufs[name], 'fsdp', links[name])]
    ppermute x2 -> x1, waiting for transfers between devices: 6.26 us -> 5.16 us  [send(): return swap(pack(plan, row, rows, [], act, turns, after))]
    ppermute x2 -> x3, starting transfers between devices: 3.11 us -> 3.87 us  [shard_step(): parcel = swap(parcel)]
  transfers between devices with their start and end apart: 26 -> 26, of which waited for: 7 -> 8; matrix products, arithmetic and copies ran while one was open for 1% -> 1% of each run, Pallas kernels for 31% -> 29%
where the time goes in v6:
time: 136 us; the launch traced here: 134 us
  waiting for transfers between devices  49.4 us (36%)
  Pallas kernels  40.8 us (30%)
  starting transfers between devices  37.9 us (28%)
  local copies, waits for them, and re-layouts  5.04 us (4%)
    pallas_call x21, Pallas kernels, call(): pl.pallas_call(kernel, grid_spec=pltpu.PrefetchScalarGridSpec(num_scalar_...  40.8 us
    ppermute x14, starting transfers between devices, exchange(): lax.ppermute(bufs[name], 'fsdp', links[name])  25.8 us
    ppermute x3, waiting for transfers between devices, shard_step(): parcel = swap(parcel)  13.9 us
    ppermute x14, waiting for transfers between devices, exchange(): lax.ppermute(bufs[name], 'fsdp', links[name])  12 us
    ppermute x1, waiting for transfers between devices, per_device(): parcel = swap(cot)  9.52 us
    ppermute x2, waiting for transfers between devices, partner_rows(): far = lax.ppermute(stepped, 'rep', [(r, r ^ 2) for r in range(4)])  8.84 us
    ppermute x1, waiting for transfers between devices, send(): return swap(pack(plan, row, rows, [], act, turns, after))  5.16 us
    unnamed x20, local copies, waits for them, and re-layouts  4.35 us
  transfers between devices with their start and end apart: 26, of which 8 were waited for; matrix products, arithmetic and copies ran while one was open for 1% of the time, Pallas kernels for 29%

profile of v6, /device:TPU:0, one launch (start us, length us, event | category | flops | bytes accessed | tf_op | source)
XLA Modules:
  0.0 134.1 jit_solution(14322119022461839143)
XLA Ops:
  0.6 3.0 %collective-permute-start.3 = (bf16[384,1024]{1,0:T(8,128)(2,1)}, bf16[384,1024]{1,0:T(8,128)(2,1)S(1)}, u32[]{:S(2)}, u32[]{:S(2)}) collective-permute-start(bf16[384,1024]{1,0:T(8,128)(2,1)} %bitcast.34), channel_id=1, source_target_pairs={{0,1},{1,0},{2,3},{3,2},{4,5},{5,4},{6,7},{7,6},{8,9},{9,8},{10,11... | collective-permute-start | bytes 2359304 | tf_op jit(solution)/shard_map/ppermute | solution.py:482
  4.3 1.9 %copy-done = bf16[1,384,4096]{2,1,0:T(8,128)(2,1)S(1)} copy-done((bf16[1,384,4096]{2,1,0:T(8,128)(2,1)S(1)}, bf16[1,384,4096]{2,1,0:T(8,128)(2,1)}, u32[]{:S(2)}) %copy-start) | copy-done | bytes 3145752
  8.3 4.4 %collective-permute-start = (bf16[512,1024]{1,0:T(8,128)(2,1)S(1)}, bf16[512,1024]{1,0:T(8,128)(2,1)S(1)}, u32[]{:S(2)}, u32[]{:S(2)}) collective-permute-start(bf16[512,1024]{1,0:T(8,128)(2,1)S(1)} %bitcast.47), channel_id=1, source_target_pairs={{0,2},{1,3},{2,0},{3,1},{4,6},{5,7},{6,4},{7,5},{8,10},{9,11},{10,... | collective-permute-start | bytes 3145736 | tf_op jit(solution)/shard_map/ppermute | solution.py:466
  12.7 9.5 %collective-permute-done.3.refs_6_.refs_1_.refs_2_.refs_7_.refs_3_.refs_4_.refs_5_.refs_8_.refs_0_ = bf16[384,1024]{1,0:T(8,128)(2,1)S(1)} collective-permute-done((bf16[384,1024]{1,0:T(8,128)(2,1)}, bf16[384,1024]{1,0:T(8,128)(2,1)S(1)}, u32[]{:S(2)}, u32[]{:S(2)}) %collective-permute-start.3) | collective-permute-done | bytes 786464 | tf_op jit(solution)/shard_map/ppermute | solution.py:482
  22.2 2.4 %shard_map.121 = (bf16[384,4096]{1,0:T(8,128)(2,1)}, bf16[384,512]{1,0:T(8,128)(2,1)S(1)}, bf16[512,1024]{1,0:T(8,128)(2,1)S(1)}) custom-call(s32[40]{0:T(128)S(1)} %dynamic-slice_bitcast_fusion.row_ref, bf16[512,1024]{1,0:T(8,128)(2,1)S(1)} %bitcast.48, ...), custom_call_target="tpu_custom_call" | custom-call | tf_op jit(solution)/shard_map/pallas_call | solution.py:85
  24.7 5.2 %collective-permute-done.2.refs_4_.refs_3_.refs_6_.refs_2_ = bf16[384,512]{1,0:T(8,128)(2,1)S(1)} collective-permute-done((bf16[384,512]{1,0:T(8,128)(2,1)S(1)}, bf16[384,512]{1,0:T(8,128)(2,1)S(1)}, u32[]{:S(2)}, u32[]{:S(2)}) %collective-permute-start.2) | collective-permute-done | bytes 393248 | tf_op jit(solution)/shard_map/ppermute | solution.py:480
  30.4 1.8 %collective-permute-start.6 = (bf16[384,1536]{1,0:T(8,128)(2,1)S(1)}, bf16[384,1536]{1,0:T(8,128)(2,1)S(1)}, u32[]{:S(2)}, u32[]{:S(2)}) collective-permute-start(bf16[384,1536]{1,0:T(8,128)(2,1)S(1)} %shard_map.122), channel_id=1, source_target_pairs={{0,1},{1,0},{2,3},{3,2},{4,5},{5,4},{6,7},{7,6},{8,9},{9,8},{10,11... | collective-permute-start | bytes 3538952 | tf_op jit(solution)/shard_map/ppermute | solution.py:500
  32.3 3.0 %collective-permute-done.refs_1_.refs_0_ = bf16[512,1024]{1,0:T(8,128)(2,1)S(1)} collective-permute-done((bf16[512,1024]{1,0:T(8,128)(2,1)S(1)}, bf16[512,1024]{1,0:T(8,128)(2,1)S(1)}, u32[]{:S(2)}, u32[]{:S(2)}) %collective-permute-start) | collective-permute-done | bytes 1048608 | tf_op jit(solution)/shard_map/ppermute | solution.py:466
  35.3 1.5 %shard_map.120 = (bf16[512,512]{1,0:T(8,128)(2,1)S(1)}, bf16[512,512]{1,0:T(8,128)(2,1)S(1)}) custom-call(s32[40]{0:T(128)S(1)} %dynamic-slice_bitcast_fusion.row_ref, bf16[512,1024]{1,0:T(8,128)(2,1)S(1)} %collective-permute-done.1.refs_0_.refs_1_, bf16[512,1024]{1,0:T(8,128)(2,1)S(1)} %collective-permute-done.refs_1_.refs_0_, ...), custom_call_target="tpu_custom_call" | custom-call | tf_op jit(solution)/shard_map/pallas_call | solution.py:85
  37.5 2.8 %collective-permute-start.5 = (bf16[512,512]{1,0:T(8,128)(2,1)S(1)}, bf16[512,512]{1,0:T(8,128)(2,1)S(1)}, u32[]{:S(2)}, u32[]{:S(2)}) collective-permute-start(bf16[512,512]{1,0:T(8,128)(2,1)S(1)} %get-tuple-element.42.refs_7_), channel_id=1, source_target_pairs={{0,2},{1,3},{2,0},{3,1},{4,6},{5,7},{6,4},{7,5},{8,10},{9,11},{10,... | collective-permute-start | bytes 1572872 | tf_op jit(solution)/shard_map/ppermute | solution.py:466
  40.3 1.5 %shard_map.123 = (bf16[512,512]{1,0:T(8,128)(2,1)S(1)}, bf16[512,512]{1,0:T(8,128)(2,1)S(1)}) custom-call(s32[40]{0:T(128)S(1)} %dynamic-slice_bitcast_fusion.row_ref, bf16[512,1024]{1,0:T(8,128)(2,1)S(1)} %collective-permute-done.1.refs_0_.refs_1_, bf16[512,1024]{1,0:T(8,128)(2,1)S(1)} %collective-permute-done.refs_1_.refs_0_, ...), custom_call_target="tpu_custom_call" | custom-call | tf_op jit(solution)/shard_map/pallas_call | solution.py:85
  42.5 2.1 %collective-permute-start.9 = (bf16[512,512]{1,0:T(8,128)(2,1)S(1)}, bf16[512,512]{1,0:T(8,128)(2,1)S(1)}, u32[]{:S(2)}, u32[]{:S(2)}) collective-permute-start(bf16[512,512]{1,0:T(8,128)(2,1)S(1)} %get-tuple-element.44.refs_8_), channel_id=1, source_target_pairs={{0,2},{1,3},{2,0},{3,1},{4,6},{5,7},{6,4},{7,5},{8,10},{9,11},{10,... | collective-permute-start | bytes 1572872 | tf_op jit(solution)/shard_map/ppermute | solution.py:466
  44.7 13.0 %collective-permute-done.6.refs_5_.refs_7_.refs_8_.refs_3_.refs_4_.refs_0_.refs_6_ = bf16[384,1536]{1,0:T(8,128)(2,1)S(1)} collective-permute-done((bf16[384,1536]{1,0:T(8,128)(2,1)S(1)}, bf16[384,1536]{1,0:T(8,128)(2,1)S(1)}, u32[]{:S(2)}, u32[]{:S(2)}) %collective-permute-start.6) | collective-permute-done | bytes 1179680 | tf_op jit(solution)/shard_map/ppermute | solution.py:500
  57.7 2.5 %shard_map.126 = (bf16[384,4096]{1,0:T(8,128)(2,1)}, bf16[384,1024]{1,0:T(8,128)(2,1)S(1)}, bf16[512,1024]{1,0:T(8,128)(2,1)S(1)}) custom-call(s32[40]{0:T(128)S(1)} %dynamic-slice_bitcast_fusion.row_ref, bf16[512,1024]{1,0:T(8,128)(2,1)S(1)} %collective-permute-done.refs_1_.refs_0_, ...), custom_call_target="tpu_custom_call", output_to_operand_aliasing={{0}: (7, {})} | custom-call | tf_op jit(solution)/shard_map/pallas_call | solution.py:85
  63.8 4.4 %collective-permute-start.7 = (bf16[512,512]{1,0:T(8,128)(2,1)S(1)}, bf16[512,512]{1,0:T(8,128)(2,1)S(1)}, u32[]{:S(2)}, u32[]{:S(2)}) collective-permute-start(bf16[512,512]{1,0:T(8,128)(2,1)S(1)} %get-tuple-element.45.refs_8_), channel_id=1, source_target_pairs={{0,2},{1,3},{2,0},{3,1},{4,6},{5,7},{6,4},{7,5},{8,10},{9,11},{10,... | collective-permute-start | bytes 1572872 | tf_op jit(solution)/shard_map/ppermute | solution.py:466
  70.5 1.8 %collective-permute-start.10 = (bf16[512,512]{1,0:T(8,128)(2,1)S(1)}, bf16[512,512]{1,0:T(8,128)(2,1)S(1)}, u32[]{:S(2)}, u32[]{:S(2)}) collective-permute-start(bf16[512,512]{1,0:T(8,128)(2,1)S(1)} %get-tuple-element.47.refs_9_), channel_id=1, source_target_pairs={{0,2},{1,3},{2,0},{3,1},{4,6},{5,7},{6,4},{7,5},{8,10},{9,11},{10,... | collective-permute-start | bytes 1572872 | tf_op jit(solution)/shard_map/ppermute | solution.py:466
  72.2 8.9 %collective-permute-done.7.refs_1_ = bf16[512,512]{1,0:T(8,128)(2,1)S(1)} collective-permute-done((bf16[512,512]{1,0:T(8,128)(2,1)S(1)}, bf16[512,512]{1,0:T(8,128)(2,1)S(1)}, u32[]{:S(2)}, u32[]{:S(2)}) %collective-permute-start.7) | collective-permute-done | bytes 524320 | tf_op jit(solution)/shard_map/ppermute | solution.py:466
  83.3 4.5 %collective-permute-start.18 = (bf16[512,512]{1,0:T(8,128)(2,1)S(1)}, bf16[512,512]{1,0:T(8,128)(2,1)S(1)}, u32[]{:S(2)}, u32[]{:S(2)}) collective-permute-start(bf16[512,512]{1,0:T(8,128)(2,1)S(1)} %get-tuple-element.67.refs_9_), channel_id=1, source_target_pairs={{0,2},{1,3},{2,0},{3,1},{4,6},{5,7},{6,4},{7,5},{8,10},{9,11},{10,... | collective-permute-start | bytes 1572872 | tf_op jit(solution)/shard_map/ppermute | solution.py:466
  87.8 1.8 %shard_map.134.refs_11_.grad_ref = f32[512,1024]{1,0:T(8,128)S(1)} custom-call(s32[40]{0:T(128)S(1)} %dynamic-slice_bitcast_fusion.row_ref, bf16[384,4096]{1,0:T(8,128)(2,1)S(1)} %bitcast.26, bf16[384,1024]{1,0:T(8,128)(2,1)S(1)} %collective-permute-done.11.refs_8_.refs_9_.refs_5_.refs_1_.piece_ref, bf16[384,1024]{1,0:T(8,128)(2,1)S(1)} %bitcast.42, ...), custom_call_target="tpu_custom_call" | custom-call | tf_op jit(solution)/shard_map/pallas_call | solution.py:85
  89.6 2.5 %shard_map.127 = (bf16[384,4096]{1,0:T(8,128)(2,1)}, bf16[384,512]{1,0:T(8,128)(2,1)S(1)}, bf16[512,1024]{1,0:T(8,128)(2,1)S(1)}) custom-call(s32[40]{0:T(128)S(1)} %dynamic-slice_bitcast_fusion.row_ref, bf16[512,512]{1,0:T(8,128)(2,1)S(1)} %collective-permute-done.5.refs_1_.refs_0_, ...), custom_call_target="tpu_custom_call", output_to_operand_aliasing={{0}: (8, {})} | custom-call | tf_op jit(solution)/shard_map/pallas_call | solution.py:85
  92.2 3.9 %shard_map.129 = (f32[384,1024]{1,0:T(8,128)S(1)}, f32[384,1024]{1,0:T(8,128)S(1)}) custom-call(s32[40]{0:T(128)S(1)} %dynamic-slice_bitcast_fusion.row_ref, bf16[512,1024]{1,0:T(8,128)(2,1)S(1)} %get-tuple-element.53.refs_0_, bf16[512,1024]{1,0:T(8,128)(2,1)S(1)} %get-tuple-element.54.refs_1_, bf16[512,1024]{1,0:T(8,128)(2,1)S(1)} %get-tuple-element.55.refs_2_, ...), custom_call_target="tpu_custom_call" | custom-call | tf_op jit(solution)/shard_map/pallas_call | solution.py:85
  99.7 2.5 %shard_map.128 = (bf16[384,4096]{1,0:T(8,128)(2,1)}, bf16[384,512]{1,0:T(8,128)(2,1)S(1)}, bf16[512,1024]{1,0:T(8,128)(2,1)S(1)}) custom-call(s32[40]{0:T(128)S(1)} %dynamic-slice_bitcast_fusion.row_ref, bf16[512,1024]{1,0:T(8,128)(2,1)S(1)} %collective-permute-done.refs_1_.refs_0_, ...), custom_call_target="tpu_custom_call", output_to_operand_aliasing={{0}: (7, {})} | custom-call | tf_op jit(solution)/shard_map/pallas_call | solution.py:85
  102.3 1.9 %shard_map.130 = (f32[384,1024]{1,0:T(8,128)S(1)}, bf16[384,1536]{1,0:T(8,128)(2,1)S(1)}) custom-call(s32[40]{0:T(128)S(1)} %dynamic-slice_bitcast_fusion.row_ref, bf16[512,1024]{1,0:T(8,128)(2,1)S(1)} %get-tuple-element.52.refs_0_, bf16[384,4096]{1,0:T(8,128)(2,1)S(1)} %bitcast.32, ...), custom_call_target="tpu_custom_call" | custom-call | tf_op jit(solution)/shard_map/pallas_call | solution.py:85
  104.2 1.6 %collective-permute-start.12 = (bf16[384,1536]{1,0:T(8,128)(2,1)S(1)}, bf16[384,1536]{1,0:T(8,128)(2,1)S(1)}, u32[]{:S(2)}, u32[]{:S(2)}) collective-permute-start(bf16[384,1536]{1,0:T(8,128)(2,1)S(1)} %get-tuple-element.59.refs_0_.refs_3_), channel_id=1, source_target_pairs={{0,1},{1,0},{2,3},{3,2},{4,5},{5,4},{6,7},{7,6},{8,9},{9,8},{10,11... | collective-permute-start | bytes 3538952 | tf_op jit(solution)/shard_map/ppermute | solution.py:524
  105.8 3.1 %shard_map.136 = (f32[512,1024]{1,0:T(8,128)}, f32[512,1024]{1,0:T(8,128)}, bf16[512,512]{1,0:T(8,128)(2,1)S(1)}) custom-call(s32[40]{0:T(128)S(1)} %dynamic-slice_bitcast_fusion.row_ref, bf16[512,512]{1,0:T(8,128)(2,1)S(1)} %collective-permute-done.18.up_ref, bf16[512,512]{1,0:T(8,128)(2,1)S(1)} %collective-permute-done.19.dn_ref, ...), custom_call_target="tpu_custom_call" | custom-call | tf_op jit(solution)/shard_map/pallas_call | solution.py:85
  111.3 2.2 %shard_map.131.refs_3_.refs_2_ = bf16[384,4096]{1,0:T(8,128)(2,1)} custom-call(s32[40]{0:T(128)S(1)} %dynamic-slice_bitcast_fusion.row_ref, bf16[384,1536]{1,0:T(8,128)(2,1)S(1)} %collective-permute-done.6.refs_5_.refs_7_.refs_8_.refs_3_.refs_4_.refs_0_.refs_6_, ...), custom_call_target="tpu_custom_call", output_to_operand_aliasing={{}: (4, {})} | custom-call | tf_op jit(solution)/shard_map/pallas_call | solution.py:85
  113.5 1.9 %copy-done.2 = bf16[384,4096]{1,0:T(8,128)(2,1)S(1)} copy-done((bf16[384,4096]{1,0:T(8,128)(2,1)S(1)}, bf16[384,4096]{1,0:T(8,128)(2,1)}, u32[]{:S(2)}) %copy-start.2) | copy-done | bytes 3145752
  115.4 3.1 %shard_map.137 = (f32[512,1024]{1,0:T(8,128)}, f32[512,1024]{1,0:T(8,128)}, bf16[512,512]{1,0:T(8,128)(2,1)S(1)}) custom-call(s32[40]{0:T(128)S(1)} %dynamic-slice_bitcast_fusion.row_ref, bf16[512,512]{1,0:T(8,128)(2,1)S(1)} %collective-permute-done.16.up_ref, ...), custom_call_target="tpu_custom_call", output_to_operand_aliasing={{0}: (7, {}), {1}: (8, {})} | custom-call | tf_op jit(solution)/shard_map/pallas_call | solution.py:85
  120.6 8.7 %collective-permute-done.21.refs_1_ = bf16[512,512]{1,0:T(8,128)(2,1)S(1)} collective-permute-done((bf16[512,512]{1,0:T(8,128)(2,1)S(1)}, bf16[512,512]{1,0:T(8,128)(2,1)S(1)}, u32[]{:S(2)}, u32[]{:S(2)}) %collective-permute-start.21) | collective-permute-done | bytes 524320 | tf_op jit(solution)/shard_map/ppermute | solution.py:441
  129.3 1.7 %shard_map.132 = (bf16[384,4096]{1,0:T(8,128)(2,1)}, bf16[384,1024]{1,0:T(8,128)(2,1)}) custom-call(s32[40]{0:T(128)S(1)} %dynamic-slice_bitcast_fusion.row_ref, bf16[384,1536]{1,0:T(8,128)(2,1)S(1)} %collective-permute-done.12.refs_0_.refs_2_.refs_3_, f32[384,1024]{1,0:T(8,128)S(1)} %get-tuple-element.60.refs_1_, ...), custom_call_target="tpu_custom_call", output_to_operand_aliasing={{0}: (4, {})} | custom-call | tf_op jit(solution)/shard_map/pallas_call | solution.py:85
  131.0 1.5 %shard_map.138.refs_3_ = bf16[512,1024]{1,0:T(8,128)(2,1)} custom-call(s32[40]{0:T(128)S(1)} %dynamic-slice_bitcast_fusion.row_ref, s32[4]{0:T(128)S(1)} %copy-done.8, s32[4]{0:T(128)S(1)} %copy-done.9, bf16[512,512]{1,0:T(8,128)(2,1)S(1)} %get-tuple-element.74.stepped_ref, bf16[512,512]{1,0:T(8,128)(2,1)S(1)} %collective-permute-done.23.refs_0_, ...), custom_call_target="tpu_custom_call" | custom-call | tf_op jit(solution)/shard_map/pallas_call | solution.py:85
  132.6 1.5 %shard_map.139 = bf16[512,1024]{1,0:T(8,128)(2,1)} custom-call(s32[40]{0:T(128)S(1)} %dynamic-slice_bitcast_fusion.row_ref, s32[4]{0:T(128)S(1)} %copy-done.8, s32[4]{0:T(128)S(1)} %copy-done.9, bf16[512,512]{1,0:T(8,128)(2,1)S(1)} %get-tuple-element.73.stepped_ref, ...), custom_call_target="tpu_custom_call", output_to_operand_aliasing={{}: (7, {})} | custom-call | tf_op jit(solution)/shard_map/pallas_call | solution.py:85
  (62 shorter events, 21.1 us)
Async XLA Ops:
  0.6 21.6 %collective-permute-start.3 = (bf16[384,1024]{1,0:T(8,128)(2,1)}, bf16[384,1024]{1,0:T(8,128)(2,1)S(1)}, u32[]{:S(2)}, u32[]{:S(2)}) collective-permute-start(bf16[384,1024]{1,0:T(8,128)(2,1)} %bitcast.34), channel_id=1, source_target_pairs={{0,1},{1,0},{2,3},{3,2},{4,5},{5,4},{6,7},{7,6},{8,9},{9,8},{10,11... | collective-permute-start | bytes 2359304 | tf_op jit(solution)/shard_map/ppermute | solution.py:482
  4.3 1.9 %copy-start = (bf16[1,384,4096]{2,1,0:T(8,128)(2,1)S(1)}, bf16[1,384,4096]{2,1,0:T(8,128)(2,1)}, u32[]{:S(2)}) copy-start(bf16[1,384,4096]{2,1,0:T(8,128)(2,1)} %param.8) | copy-start | bytes 9437188
  6.2 16.0 %copy-start.3 = (bf16[1,384,1024]{2,1,0:T(8,128)(2,1)S(1)}, bf16[1,384,1024]{2,1,0:T(8,128)(2,1)}, u32[]{:S(2)}) copy-start(bf16[1,384,1024]{2,1,0:T(8,128)(2,1)} %param.10) | copy-start | bytes 2359300
  6.8 23.0 %copy-start.1 = (bf16[1,384,4096]{2,1,0:T(8,128)(2,1)S(1)}, bf16[1,384,4096]{2,1,0:T(8,128)(2,1)}, u32[]{:S(2)}) copy-start(bf16[1,384,4096]{2,1,0:T(8,128)(2,1)} %param.8) | copy-start | bytes 9437188
  6.8 23.0 %collective-permute-start.2 = (bf16[384,512]{1,0:T(8,128)(2,1)S(1)}, bf16[384,512]{1,0:T(8,128)(2,1)S(1)}, u32[]{:S(2)}, u32[]{:S(2)}) collective-permute-start(bf16[384,512]{1,0:T(8,128)(2,1)S(1)} %shard_map.119), channel_id=1, source_target_pairs={{0,1},{1,0},{2,3},{3,2},{4,5},{5,4},{6,7},{7,6},{8,9},{9,8},{10,11... | collective-permute-start | bytes 1179656 | tf_op jit(solution)/shard_map/ppermute | solution.py:480
  7.4 24.8 %collective-permute-start.1 = (bf16[512,1024]{1,0:T(8,128)(2,1)S(1)}, bf16[512,1024]{1,0:T(8,128)(2,1)S(1)}, u32[]{:S(2)}, u32[]{:S(2)}) collective-permute-start(bf16[512,1024]{1,0:T(8,128)(2,1)S(1)} %bitcast.46), channel_id=1, source_target_pairs={{2,4},{3,5},{4,2},{5,3},{10,12},{11,13},{12,10},{13,11},{18,20},{1... | collective-permute-start | bytes 3145736 | tf_op jit(solution)/shard_map/ppermute | solution.py:466
  8.3 27.0 %collective-permute-start = (bf16[512,1024]{1,0:T(8,128)(2,1)S(1)}, bf16[512,1024]{1,0:T(8,128)(2,1)S(1)}, u32[]{:S(2)}, u32[]{:S(2)}) collective-permute-start(bf16[512,1024]{1,0:T(8,128)(2,1)S(1)} %bitcast.47), channel_id=1, source_target_pairs={{0,2},{1,3},{2,0},{3,1},{4,6},{5,7},{6,4},{7,5},{8,10},{9,11},{10,... | collective-permute-start | bytes 3145736 | tf_op jit(solution)/shard_map/ppermute | solution.py:466
  30.4 27.2 %collective-permute-start.6 = (bf16[384,1536]{1,0:T(8,128)(2,1)S(1)}, bf16[384,1536]{1,0:T(8,128)(2,1)S(1)}, u32[]{:S(2)}, u32[]{:S(2)}) collective-permute-start(bf16[384,1536]{1,0:T(8,128)(2,1)S(1)} %shard_map.122), channel_id=1, source_target_pairs={{0,1},{1,0},{2,3},{3,2},{4,5},{5,4},{6,7},{7,6},{8,9},{9,8},{10,11... | collective-permute-start | bytes 3538952 | tf_op jit(solution)/shard_map/ppermute | solution.py:500
  36.8 24.8 %collective-permute-start.4 = (bf16[512,512]{1,0:T(8,128)(2,1)S(1)}, bf16[512,512]{1,0:T(8,128)(2,1)S(1)}, u32[]{:S(2)}, u32[]{:S(2)}) collective-permute-start(bf16[512,512]{1,0:T(8,128)(2,1)S(1)} %get-tuple-element.41), channel_id=1, source_target_pairs={{2,4},{3,5},{4,2},{5,3},{10,12},{11,13},{12,10},{13,11},{18,20},{1... | collective-permute-start | bytes 1572872 | tf_op jit(solution)/shard_map/ppermute | solution.py:466
  37.5 24.1 %collective-permute-start.5 = (bf16[512,512]{1,0:T(8,128)(2,1)S(1)}, bf16[512,512]{1,0:T(8,128)(2,1)S(1)}, u32[]{:S(2)}, u32[]{:S(2)}) collective-permute-start(bf16[512,512]{1,0:T(8,128)(2,1)S(1)} %get-tuple-element.42.refs_7_), channel_id=1, source_target_pairs={{0,2},{1,3},{2,0},{3,1},{4,6},{5,7},{6,4},{7,5},{8,10},{9,11},{10,... | collective-permute-start | bytes 1572872 | tf_op jit(solution)/shard_map/ppermute | solution.py:466
  41.8 26.5 %collective-permute-start.8 = (bf16[512,512]{1,0:T(8,128)(2,1)S(1)}, bf16[512,512]{1,0:T(8,128)(2,1)S(1)}, u32[]{:S(2)}, u32[]{:S(2)}) collective-permute-start(bf16[512,512]{1,0:T(8,128)(2,1)S(1)} %get-tuple-element.46), channel_id=1, source_target_pairs={{2,4},{3,5},{4,2},{5,3},{10,12},{11,13},{12,10},{13,11},{18,20},{1... | collective-permute-start | bytes 1572872 | tf_op jit(solution)/shard_map/ppermute | solution.py:466
  42.5 25.8 %collective-permute-start.9 = (bf16[512,512]{1,0:T(8,128)(2,1)S(1)}, bf16[512,512]{1,0:T(8,128)(2,1)S(1)}, u32[]{:S(2)}, u32[]{:S(2)}) collective-permute-start(bf16[512,512]{1,0:T(8,128)(2,1)S(1)} %get-tuple-element.44.refs_8_), channel_id=1, source_target_pairs={{0,2},{1,3},{2,0},{3,1},{4,6},{5,7},{6,4},{7,5},{8,10},{9,11},{10,... | collective-permute-start | bytes 1572872 | tf_op jit(solution)/shard_map/ppermute | solution.py:466
  60.1 27.7 %collective-permute-start.11 = (bf16[384,1024]{1,0:T(8,128)(2,1)S(1)}, bf16[384,1024]{1,0:T(8,128)(2,1)S(1)}, u32[]{:S(2)}, u32[]{:S(2)}) collective-permute-start(bf16[384,1024]{1,0:T(8,128)(2,1)S(1)} %get-tuple-element.50), channel_id=1, source_target_pairs={{0,1},{1,0},{2,3},{3,2},{4,5},{5,4},{6,7},{7,6},{8,9},{9,8},{10,11... | collective-permute-start | bytes 2359304 | tf_op jit(solution)/shard_map/ppermute | solution.py:500
  63.1 9.1 %collective-permute-start.15 = (bf16[512,512]{1,0:T(8,128)(2,1)S(1)}, bf16[512,512]{1,0:T(8,128)(2,1)S(1)}, u32[]{:S(2)}, u32[]{:S(2)}) collective-permute-start(bf16[512,512]{1,0:T(8,128)(2,1)S(1)} %get-tuple-element.66), channel_id=1, source_target_pairs={{2,4},{3,5},{4,2},{5,3},{10,12},{11,13},{12,10},{13,11},{18,20},{1... | collective-permute-start | bytes 1572872 | tf_op jit(solution)/shard_map/ppermute | solution.py:466
  63.8 17.3 %collective-permute-start.7 = (bf16[512,512]{1,0:T(8,128)(2,1)S(1)}, bf16[512,512]{1,0:T(8,128)(2,1)S(1)}, u32[]{:S(2)}, u32[]{:S(2)}) collective-permute-start(bf16[512,512]{1,0:T(8,128)(2,1)S(1)} %get-tuple-element.45.refs_8_), channel_id=1, source_target_pairs={{0,2},{1,3},{2,0},{3,1},{4,6},{5,7},{6,4},{7,5},{8,10},{9,11},{10,... | collective-permute-start | bytes 1572872 | tf_op jit(solution)/shard_map/ppermute | solution.py:466
  69.8 26.3 %collective-permute-start.14 = (bf16[512,512]{1,0:T(8,128)(2,1)S(1)}, bf16[512,512]{1,0:T(8,128)(2,1)S(1)}, u32[]{:S(2)}, u32[]{:S(2)}) collective-permute-start(bf16[512,512]{1,0:T(8,128)(2,1)S(1)} %get-tuple-element.65), channel_id=1, source_target_pairs={{2,4},{3,5},{4,2},{5,3},{10,12},{11,13},{12,10},{13,11},{18,20},{1... | collective-permute-start | bytes 1572872 | tf_op jit(solution)/shard_map/ppermute | solution.py:466
  70.5 25.6 %collective-permute-start.10 = (bf16[512,512]{1,0:T(8,128)(2,1)S(1)}, bf16[512,512]{1,0:T(8,128)(2,1)S(1)}, u32[]{:S(2)}, u32[]{:S(2)}) collective-permute-start(bf16[512,512]{1,0:T(8,128)(2,1)S(1)} %get-tuple-element.47.refs_9_), channel_id=1, source_target_pairs={{0,2},{1,3},{2,0},{3,1},{4,6},{5,7},{6,4},{7,5},{8,10},{9,11},{10,... | collective-permute-start | bytes 1572872 | tf_op jit(solution)/shard_map/ppermute | solution.py:466
  82.6 21.6 %collective-permute-start.19 = (bf16[512,512]{1,0:T(8,128)(2,1)S(1)}, bf16[512,512]{1,0:T(8,128)(2,1)S(1)}, u32[]{:S(2)}, u32[]{:S(2)}) collective-permute-start(bf16[512,512]{1,0:T(8,128)(2,1)S(1)} %get-tuple-element.70), channel_id=1, source_target_pairs={{2,4},{3,5},{4,2},{5,3},{10,12},{11,13},{12,10},{13,11},{18,20},{1... | collective-permute-start | bytes 1572872 | tf_op jit(solution)/shard_map/ppermute | solution.py:466
  83.3 22.5 %collective-permute-start.18 = (bf16[512,512]{1,0:T(8,128)(2,1)S(1)}, bf16[512,512]{1,0:T(8,128)(2,1)S(1)}, u32[]{:S(2)}, u32[]{:S(2)}) collective-permute-start(bf16[512,512]{1,0:T(8,128)(2,1)S(1)} %get-tuple-element.67.refs_9_), channel_id=1, source_target_pairs={{0,2},{1,3},{2,0},{3,1},{4,6},{5,7},{6,4},{7,5},{8,10},{9,11},{10,... | collective-permute-start | bytes 1572872 | tf_op jit(solution)/shard_map/ppermute | solution.py:466
  97.6 15.8 %collective-permute-start.16 = (bf16[512,512]{1,0:T(8,128)(2,1)S(1)}, bf16[512,512]{1,0:T(8,128)(2,1)S(1)}, u32[]{:S(2)}, u32[]{:S(2)}) collective-permute-start(bf16[512,512]{1,0:T(8,128)(2,1)S(1)} %get-tuple-element.68), channel_id=1, source_target_pairs={{0,2},{1,3},{2,0},{3,1},{4,6},{5,7},{6,4},{7,5},{8,10},{9,11},{10,... | collective-permute-start | bytes 1572872 | tf_op jit(solution)/shard_map/ppermute | solution.py:466
  98.5 15.0 %collective-permute-start.17 = (bf16[512,512]{1,0:T(8,128)(2,1)S(1)}, bf16[512,512]{1,0:T(8,128)(2,1)S(1)}, u32[]{:S(2)}, u32[]{:S(2)}) collective-permute-start(bf16[512,512]{1,0:T(8,128)(2,1)S(1)} %get-tuple-element.69), channel_id=1, source_target_pairs={{2,4},{3,5},{4,2},{5,3},{10,12},{11,13},{12,10},{13,11},{18,20},{1... | collective-permute-start | bytes 1572872 | tf_op jit(solution)/shard_map/ppermute | solution.py:466
  99.2 12.1 %collective-permute-start.13 = (bf16[384,512]{1,0:T(8,128)(2,1)S(1)}, bf16[384,512]{1,0:T(8,128)(2,1)S(1)}, u32[]{:S(2)}, u32[]{:S(2)}) collective-permute-start(bf16[384,512]{1,0:T(8,128)(2,1)S(1)} %get-tuple-element.61), channel_id=1, source_target_pairs={{0,1},{1,0},{2,3},{3,2},{4,5},{5,4},{6,7},{7,6},{8,9},{9,8},{10,11... | collective-permute-start | bytes 1179656 | tf_op jit(solution)/shard_map/ppermute | solution.py:500
  102.3 3.5 %copy-start.5 = (f32[1,512,1024]{2,1,0:T(8,128)S(1)}, f32[1,512,1024]{2,1,0:T(8,128)}, u32[]{:S(2)}) copy-start(f32[1,512,1024]{2,1,0:T(8,128)} %param.11) | copy-start | bytes 6291460
  102.3 3.5 %copy-start.6 = (f32[1,512,1024]{2,1,0:T(8,128)S(1)}, f32[1,512,1024]{2,1,0:T(8,128)}, u32[]{:S(2)}) copy-start(f32[1,512,1024]{2,1,0:T(8,128)} %param.12) | copy-start | bytes 6291460
  104.2 25.1 %collective-permute-start.12 = (bf16[384,1536]{1,0:T(8,128)(2,1)S(1)}, bf16[384,1536]{1,0:T(8,128)(2,1)S(1)}, u32[]{:S(2)}, u32[]{:S(2)}) collective-permute-start(bf16[384,1536]{1,0:T(8,128)(2,1)S(1)} %get-tuple-element.59.refs_0_.refs_3_), channel_id=1, source_target_pairs={{0,1},{1,0},{2,3},{3,2},{4,5},{5,4},{6,7},{7,6},{8,9},{9,8},{10,11... | collective-permute-start | bytes 3538952 | tf_op jit(solution)/shard_map/ppermute | solution.py:524
  108.9 11.2 %collective-permute-start.24 = (bf16[512,512]{1,0:T(8,128)(2,1)S(1)}, bf16[512,512]{1,0:T(8,128)(2,1)S(1)}, u32[]{:S(2)}, u32[]{:S(2)}) collective-permute-start(bf16[512,512]{1,0:T(8,128)(2,1)S(1)} %get-tuple-element.74.stepped_ref), channel_id=1, source_target_pairs={{0,16},{8,24},{16,0},{24,8},{1,17},{9,25},{17,1},{25,9},{2,18},{10... | collective-permute-start | bytes 1572872 | tf_op jit(solution)/shard_map/ppermute | solution.py:441
  113.5 1.9 %copy-start.2 = (bf16[384,4096]{1,0:T(8,128)(2,1)S(1)}, bf16[384,4096]{1,0:T(8,128)(2,1)}, u32[]{:S(2)}) copy-start(bf16[384,4096]{1,0:T(8,128)(2,1)} %shard_map.131.refs_3_.refs_2_) | copy-start | bytes 9437188
  118.4 10.9 %collective-permute-start.21 = (bf16[512,512]{1,0:T(8,128)(2,1)S(1)}, bf16[512,512]{1,0:T(8,128)(2,1)S(1)}, u32[]{:S(2)}, u32[]{:S(2)}) collective-permute-start(bf16[512,512]{1,0:T(8,128)(2,1)S(1)} %get-tuple-element.73.stepped_ref), channel_id=1, source_target_pairs={{0,16},{8,24},{16,0},{24,8},{1,17},{9,25},{17,1},{25,9},{2,18},{10... | collective-permute-start | bytes 1572872 | tf_op jit(solution)/shard_map/ppermute | solution.py:441
  119.9 11.1 %collective-permute-start.23 = (bf16[512,512]{1,0:T(8,128)(2,1)S(1)}, bf16[512,512]{1,0:T(8,128)(2,1)S(1)}, u32[]{:S(2)}, u32[]{:S(2)}) collective-permute-start(bf16[512,512]{1,0:T(8,128)(2,1)S(1)} %get-tuple-element.74.stepped_ref), channel_id=1, source_target_pairs={{0,8},{8,0},{16,24},{24,16},{1,9},{9,1},{17,25},{25,17},{2,10},{10... | collective-permute-start | bytes 1572872 | tf_op jit(solution)/shard_map/ppermute | solution.py:443
  120.1 10.9 %collective-permute-start.25 = (bf16[512,512]{1,0:T(8,128)(2,1)S(1)}, bf16[512,512]{1,0:T(8,128)(2,1)S(1)}, u32[]{:S(2)}, u32[]{:S(2)}) collective-permute-start(bf16[512,512]{1,0:T(8,128)(2,1)S(1)} %collective-permute-done.24.refs_1_), channel_id=1, source_target_pairs={{0,8},{8,0},{16,24},{24,16},{1,9},{9,1},{17,25},{25,17},{2,10},{10... | collective-permute-start | bytes 1572872 | tf_op jit(solution)/shard_map/ppermute | solution.py:443
  120.4 12.1 %collective-permute-start.20 = (bf16[512,512]{1,0:T(8,128)(2,1)S(1)}, bf16[512,512]{1,0:T(8,128)(2,1)S(1)}, u32[]{:S(2)}, u32[]{:S(2)}) collective-permute-start(bf16[512,512]{1,0:T(8,128)(2,1)S(1)} %get-tuple-element.73.stepped_ref), channel_id=1, source_target_pairs={{0,8},{8,0},{16,24},{24,16},{1,9},{9,1},{17,25},{25,17},{2,10},{10... | collective-permute-start | bytes 1572872 | tf_op jit(solution)/shard_map/ppermute | solution.py:443
  129.3 3.3 %collective-permute-start.22 = (bf16[512,512]{1,0:T(8,128)(2,1)S(1)}, bf16[512,512]{1,0:T(8,128)(2,1)S(1)}, u32[]{:S(2)}, u32[]{:S(2)}) collective-permute-start(bf16[512,512]{1,0:T(8,128)(2,1)S(1)} %collective-permute-done.21.refs_1_), channel_id=1, source_target_pairs={{0,8},{8,0},{16,24},{24,16},{1,9},{9,1},{17,25},{25,17},{2,10},{10... | collective-permute-start | bytes 1572872 | tf_op jit(solution)/shard_map/ppermute | solution.py:443
  (4 other events, 6.2 us)

commit v7 on v6

--- a/solution.py
+++ b/solution.py
@@ -20,6 +20,7 @@
 CHUNKS = 2
 MIB = 1 << 20
 ANY = pl.BlockSpec(memory_space=pl.ANY)
+HBM = pl.BlockSpec(memory_space=pltpu.HBM)
 
 TN = (((0,), (0,)), ((), ()))
 NT = (((1,), (1,)), ((), ()))
@@ -211,13 +212,12 @@
     )[0]
 
 
-def project(plan, row, j, candidates, act, cot, cot_oth, xg_before, turns=(), after=()):
+def project(plan, row, j, candidates, act, cot, cot_oth, xg_before):
     (tokens, columns), rows = cot.shape, candidates[0][0].shape[0]
     flat = [c for candidate in candidates for c in candidate]
     starts = np.cumsum([0] + [len(candidate) for candidate in candidates])
     parts = max(len(candidate) for candidate in candidates)
     n_w, n_c = len(flat), len(cot_oth)
-    width = rows * (1 + len(turns))
 
     def kernel(row_ref, *refs):
         w_refs, cot_refs = refs[:n_w], refs[n_w : n_w + n_c]
@@ -241,20 +241,15 @@
         for ref, view in zip(cot_refs, cot_oth):
             total = total + dot(ref[...], w_out[:, at : at + view.count], NT)
             at += view.count
-        xg_oth[:, :rows] = total.astype(jnp.bfloat16)
-        for t in range(len(turns)):
-            ref = refs[n_w + n_c + 1 + t]
-            xg_oth[:, (t + 1) * rows : (t + 2) * rows] = ref[...]
+        xg_oth[...] = total.astype(jnp.bfloat16)
         xg_own[...] = dot(own_ref[...], w_out[...], NT).astype(jnp.bfloat16)
 
     ins = [(w, ANY) for w in flat] + [view.operand() for view in cot_oth] + [(cot, whole(cot))]
-    ins += [(act, block((tokens, rows), plan[f"pack{turn}"])) for turn in turns]
     aliases = {}
     if xg_before is not None:
         aliases = {1 + len(ins): 0}
-        ins.append((xg_before, ANY))
-    ins += [(a, ANY) for a in after]
-    other = struct((tokens, width), jnp.bfloat16)
+        ins.append((xg_before, HBM))
+    other = struct((tokens, rows), jnp.bfloat16)
     shard = struct((rows, columns), jnp.bfloat16)
     return call(
         kernel,
@@ -354,7 +349,7 @@
     return call(
         kernel,
         row,
-        ins + [(xg, ANY)],
+        ins + [(xg, HBM)],
         outs,
         grid=(count,),
         aliases=aliases,
@@ -385,7 +380,7 @@
     aliases = {}
     if kept is not None:
         aliases = {1 + len(ins): 0, 2 + len(ins): 1}
-        ins += [(a, ANY) for a in kept]
+        ins += [(a, HBM) for a in kept]
     ins += [(a, ANY) for a in after]
     return call(
         kernel,
@@ -422,7 +417,7 @@
     part = pl.BlockSpec((size, columns), lambda g, *scalars: (g, h))
     ins = [(a, local) for a in (stepped, *others)]
     if kept is not None:
-        ins.append((kept, ANY))
+        ins.append((kept, HBM))
     ins += [(a, ANY) for a in after]
     return call(
         kernel,
@@ -483,44 +478,46 @@
     cot_oth = [part(parcel, h) for h in range(CHUNKS)]
     pieces = [View(send(0), 0, rows)]
 
-    arrived, shards = [], []
-
-    def shard_step(j, xg, turns, after=()):
+    parcel = send(*range(1, depth - 1), after=[parcel, pieces[0].array])
+    pieces += [View(parcel, k * rows, rows) for k in range(depth - 2)]
+
+    arrived, shards, parts = [], [], []
+
+    def shard_step(j, xg):
         candidates = [[weights]]
         if j > 0:
             candidates = [arrivals(*source) for source in plan.sources[j]]
-        ahead = turns if j > 0 else []
-        xg, parcel, shard = project(plan, row, j, candidates, act, cot, cot_oth, xg, ahead, after)
+        xg, parcel, shard = project(plan, row, j, candidates, act, cot, cot_oth, xg)
         shards.append(shard)
-        if j == 0:
-            front = View(parcel, 0, rows)
-            parcel = pack(plan, row, rows, [front], act, turns, [pieces[0].array])
-        if j == depth - 1:
-            return xg, View(parcel, 0, rows)
-        parcel = swap(parcel)
-        arrived.append(View(parcel, 0, rows))
-        pieces.extend(View(parcel, (t + 1) * rows, rows) for t in range(len(turns)))
-        return xg, None
-
-    xg, _ = shard_step(0, None, range(1, depth - 1))
+        parts.append(View(parcel, 0, rows))
+        return xg
+
+    def send_parts(views, turns, after):
+        parcel = swap(pack(plan, row, rows, views, act, turns, after))
+        arrived.extend(View(parcel, t * rows, rows) for t in range(len(views)))
+        return parcel
+
+    xg = shard_step(0, None)
+    parcel = send_parts(parts, [depth - 1], [parcel])
+    pieces.append(View(parcel, rows, rows))
     bufs = {}
     for s in range(2, depth + 1):
         if s == depth:
             for j in range(1, depth - 1):
-                turns = [depth - 1] if j == 1 else []
-                xg, _ = shard_step(j, xg, turns, [arrived[-1].array])
+                xg = shard_step(j, xg)
+            send_parts(parts[1:], [], [parcel])
             grad = own_gradient(plan, row, act, pieces[depth - 1], cot, cot_oth)
             sums = values(plan, row, list(range(depth - 1)), shards, act, pieces, None)
         for h in range(CHUNKS):
             after = list(bufs.values())[:1]
-            if s == depth and h == CHUNKS - 1:
-                after += [sums[0], grad]
+            if s == depth:
+                after.append(grad if h == 0 else sums[0])
             bufs = relay(
                 plan, row, s, got[s - 1, h], act, pieces[: s - 1], part(cot, h), cot_oth[h], after
             )
             got[s, h] = {link: part(array, 0) for link, array in exchange(bufs).items()}
-    xg, held = shard_step(depth - 1, xg, [])
-    kv_own, parcel = values(plan, row, [depth - 1], shards[-1:], act, pieces, sums, held)
+    xg = shard_step(depth - 1, xg)
+    kv_own, parcel = values(plan, row, [depth - 1], shards[-1:], act, pieces, sums, parts[-1])
     final = swap(parcel)
 
     scalars = (row, mix_numerator, partner)

time: 136 us -> 127 us (0.934); the launches traced: 134 us -> 127 us
  waiting for transfers between devices: 49.4 us -> 39 us
  starting transfers between devices: 37.9 us -> 40 us
    ppermute x1 -> x2, waiting for transfers between devices: 5.16 us -> 21.8 us  [send(): return swap(pack(plan, row, rows, [], act, turns, after))]
    ppermute x3 -> x2, waiting for transfers between devices: 13.9 us -> 0.01 us  [send_parts(): parcel = swap(pack(plan, row, rows, views, act, turns, after))]
    ppermute x1, waiting for transfers between devices: 9.52 us -> 0.01 us  [per_device(): parcel = swap(cot)]
    ppermute x14, waiting for transfers between devices: 12 us -> 7.61 us  [exchange(): lax.ppermute(bufs[name], 'fsdp', links[name])]
    ppermute x1 -> x2, starting transfers between devices: 0.09 us -> 2.41 us  [send(): return swap(pack(plan, row, rows, [], act, turns, after))]
    ppermute x14, starting transfers between devices: 25.8 us -> 28.1 us  [exchange(): lax.ppermute(bufs[name], 'fsdp', links[name])]
    ppermute x3 -> x2, starting transfers between devices: 3.87 us -> 2.08 us  [send_parts(): parcel = swap(pack(plan, row, rows, views, act, turns, after))]
    pallas_call x21 -> x23, Pallas kernels: 40.8 us -> 42 us  [call(): pl.pallas_call(kernel, grid_spec=pltpu.PrefetchScalarGridSpec(num_scalar_...]
  transfers between devices with their start and end apart: 26 -> 26, of which waited for: 8 -> 6; matrix products, arithmetic and copies ran while one was open for 1% -> 1% of each run, Pallas kernels for 29% -> 32%
where the time goes in v7:
time: 127 us
  Pallas kernels  42 us (33%)
  starting transfers between devices  40 us (31%)
  waiting for transfers between devices  39 us (31%)
  local copies, waits for them, and re-layouts  4.52 us (4%)
    pallas_call x23, Pallas kernels, call(): pl.pallas_call(kernel, grid_spec=pltpu.PrefetchScalarGridSpec(num_scalar_...  42 us
    ppermute x14, starting transfers between devices, exchange(): lax.ppermute(bufs[name], 'fsdp', links[name])  28.1 us
    ppermute x2, waiting for transfers between devices, send(): return swap(pack(plan, row, rows, [], act, turns, after))  21.8 us
    ppermute x2, waiting for transfers between devices, partner_rows(): far = lax.ppermute(stepped, 'rep', [(r, r ^ 2) for r in range(4)])  9.55 us
    ppermute x14, waiting for transfers between devices, exchange(): lax.ppermute(bufs[name], 'fsdp', links[name])  7.61 us
    unnamed x20, local copies, waits for them, and re-layouts  3.82 us
    ppermute x2, starting transfers between devices, partner_rows(): far = lax.ppermute(stepped, 'rep', [(r, r ^ 2) for r in range(4)])  3.04 us
    ppermute x1, starting transfers between devices, per_device(): parcel = swap(cot)  3 us
  transfers between devices with their start and end apart: 26, of which 6 were waited for; matrix products, arithmetic and copies ran while one was open for 1% of the time, Pallas kernels for 32%

profile of v7, /device:TPU:0, one launch (start us, length us, event | category | flops | bytes accessed | tf_op | source)
XLA Modules:
  0.0 126.5 jit_solution(12830379362557002936)
XLA Ops:
  0.6 3.0 %collective-permute-start.3 = (bf16[384,1024]{1,0:T(8,128)(2,1)}, bf16[384,1024]{1,0:T(8,128)(2,1)S(1)}, u32[]{:S(2)}, u32[]{:S(2)}) collective-permute-start(bf16[384,1024]{1,0:T(8,128)(2,1)} %bitcast.34), channel_id=1, source_target_pairs={{0,1},{1,0},{2,3},{3,2},{4,5},{5,4},{6,7},{7,6},{8,9},{9,8},{10,11... | collective-permute-start | bytes 2359304 | tf_op jit(solution)/shard_map/ppermute | solution.py:477
  4.4 4.4 %collective-permute-start = (bf16[512,1024]{1,0:T(8,128)(2,1)}, bf16[512,1024]{1,0:T(8,128)(2,1)S(1)}, u32[]{:S(2)}, u32[]{:S(2)}) collective-permute-start(bf16[512,1024]{1,0:T(8,128)(2,1)} %bitcast.47), channel_id=1, source_target_pairs={{0,2},{1,3},{2,0},{3,1},{4,6},{5,7},{6,4},{7,5},{8,10},{9,11},{10,... | collective-permute-start | bytes 3145736 | tf_op jit(solution)/shard_map/ppermute | solution.py:461
  9.5 1.9 %copy-done = bf16[1,384,4096]{2,1,0:T(8,128)(2,1)S(1)} copy-done((bf16[1,384,4096]{2,1,0:T(8,128)(2,1)S(1)}, bf16[1,384,4096]{2,1,0:T(8,128)(2,1)}, u32[]{:S(2)}) %copy-start) | copy-done | bytes 3145752
  12.5 17.3 %collective-permute-done.2.refs_4_.refs_3_.refs_6_.refs_2_ = bf16[384,512]{1,0:T(8,128)(2,1)S(1)} collective-permute-done((bf16[384,512]{1,0:T(8,128)(2,1)S(1)}, bf16[384,512]{1,0:T(8,128)(2,1)S(1)}, u32[]{:S(2)}, u32[]{:S(2)}) %collective-permute-start.2) | collective-permute-done | bytes 393248 | tf_op jit(solution)/shard_map/ppermute | solution.py:475
  30.4 1.8 %collective-permute-start.6 = (bf16[384,1024]{1,0:T(8,128)(2,1)S(1)}, bf16[384,1024]{1,0:T(8,128)(2,1)S(1)}, u32[]{:S(2)}, u32[]{:S(2)}) collective-permute-start(bf16[384,1024]{1,0:T(8,128)(2,1)S(1)} %shard_map.121), channel_id=1, source_target_pairs={{0,1},{1,0},{2,3},{3,2},{4,5},{5,4},{6,7},{7,6},{8,9},{9,8},{10,11... | collective-permute-start | bytes 2359304 | tf_op jit(solution)/shard_map/ppermute | solution.py:475
  32.3 1.5 %shard_map.120 = (bf16[512,512]{1,0:T(8,128)(2,1)S(1)}, bf16[512,512]{1,0:T(8,128)(2,1)S(1)}) custom-call(s32[40]{0:T(128)S(1)} %dynamic-slice_bitcast_fusion.row_ref, bf16[512,1024]{1,0:T(8,128)(2,1)S(1)} %collective-permute-done.1.refs_0_.refs_1_, bf16[512,1024]{1,0:T(8,128)(2,1)S(1)} %collective-permute-done.refs_1_.refs_0_, ...), custom_call_target="tpu_custom_call" | custom-call | tf_op jit(solution)/shard_map/pallas_call | solution.py:86
  34.6 3.8 %collective-permute-start.5 = (bf16[512,512]{1,0:T(8,128)(2,1)S(1)}, bf16[512,512]{1,0:T(8,128)(2,1)S(1)}, u32[]{:S(2)}, u32[]{:S(2)}) collective-permute-start(bf16[512,512]{1,0:T(8,128)(2,1)S(1)} %get-tuple-element.42.refs_7_), channel_id=1, source_target_pairs={{0,2},{1,3},{2,0},{3,1},{4,6},{5,7},{6,4},{7,5},{8,10},{9,11},{10,... | collective-permute-start | bytes 1572872 | tf_op jit(solution)/shard_map/ppermute | solution.py:461
  38.5 2.4 %shard_map.125 = (bf16[384,4096]{1,0:T(8,128)(2,1)}, bf16[384,512]{1,0:T(8,128)(2,1)S(1)}, bf16[512,1024]{1,0:T(8,128)(2,1)S(1)}) custom-call(s32[40]{0:T(128)S(1)} %dynamic-slice_bitcast_fusion.row_ref, bf16[512,1024]{1,0:T(8,128)(2,1)S(1)} %bitcast.48, ...), custom_call_target="tpu_custom_call" | custom-call | tf_op jit(solution)/shard_map/pallas_call | solution.py:86
  40.9 1.5 %shard_map.122 = (bf16[512,512]{1,0:T(8,128)(2,1)S(1)}, bf16[512,512]{1,0:T(8,128)(2,1)S(1)}) custom-call(s32[40]{0:T(128)S(1)} %dynamic-slice_bitcast_fusion.row_ref, bf16[512,1024]{1,0:T(8,128)(2,1)S(1)} %collective-permute-done.1.refs_0_.refs_1_, bf16[512,1024]{1,0:T(8,128)(2,1)S(1)} %collective-permute-done.refs_1_.refs_0_, ...), custom_call_target="tpu_custom_call" | custom-call | tf_op jit(solution)/shard_map/pallas_call | solution.py:86
  44.7 4.5 %collective-permute-done.6.refs_5_.refs_2_.refs_7_.refs_8_.refs_3_.refs_4_.refs_6_ = bf16[384,1024]{1,0:T(8,128)(2,1)S(1)} collective-permute-done((bf16[384,1024]{1,0:T(8,128)(2,1)S(1)}, bf16[384,1024]{1,0:T(8,128)(2,1)S(1)}, u32[]{:S(2)}, u32[]{:S(2)}) %collective-permute-start.6) | collective-permute-done | bytes 786464 | tf_op jit(solution)/shard_map/ppermute | solution.py:475
  53.5 4.4 %collective-permute-start.7 = (bf16[512,512]{1,0:T(8,128)(2,1)S(1)}, bf16[512,512]{1,0:T(8,128)(2,1)S(1)}, u32[]{:S(2)}, u32[]{:S(2)}) collective-permute-start(bf16[512,512]{1,0:T(8,128)(2,1)S(1)} %get-tuple-element.44.refs_8_), channel_id=1, source_target_pairs={{0,2},{1,3},{2,0},{3,1},{4,6},{5,7},{6,4},{7,5},{8,10},{9,11},{10,... | collective-permute-start | bytes 1572872 | tf_op jit(solution)/shard_map/ppermute | solution.py:461
  58.0 4.6 %collective-permute-done.9.refs_1_ = bf16[512,512]{1,0:T(8,128)(2,1)S(1)} collective-permute-done((bf16[512,512]{1,0:T(8,128)(2,1)S(1)}, bf16[512,512]{1,0:T(8,128)(2,1)S(1)}, u32[]{:S(2)}, u32[]{:S(2)}) %collective-permute-start.9) | collective-permute-done | bytes 524320 | tf_op jit(solution)/shard_map/ppermute | solution.py:461
  64.7 3.8 %collective-permute-start.10 = (bf16[512,512]{1,0:T(8,128)(2,1)S(1)}, bf16[512,512]{1,0:T(8,128)(2,1)S(1)}, u32[]{:S(2)}, u32[]{:S(2)}) collective-permute-start(bf16[512,512]{1,0:T(8,128)(2,1)S(1)} %get-tuple-element.46.refs_9_), channel_id=1, source_target_pairs={{0,2},{1,3},{2,0},{3,1},{4,6},{5,7},{6,4},{7,5},{8,10},{9,11},{10,... | collective-permute-start | bytes 1572872 | tf_op jit(solution)/shard_map/ppermute | solution.py:461
  68.5 2.4 %shard_map.126 = (bf16[384,4096]{1,0:T(8,128)(2,1)}, bf16[384,512]{1,0:T(8,128)(2,1)S(1)}, bf16[512,1024]{1,0:T(8,128)(2,1)S(1)}) custom-call(s32[40]{0:T(128)S(1)} %dynamic-slice_bitcast_fusion.row_ref, bf16[512,1024]{1,0:T(8,128)(2,1)S(1)} %collective-permute-done.refs_1_.refs_0_, ...), custom_call_target="tpu_custom_call", output_to_operand_aliasing={{0}: (6, {})} | custom-call | tf_op jit(solution)/shard_map/pallas_call | solution.py:86
  70.9 2.5 %shard_map.127 = (bf16[384,4096]{1,0:T(8,128)(2,1)}, bf16[384,512]{1,0:T(8,128)(2,1)S(1)}, bf16[512,1024]{1,0:T(8,128)(2,1)S(1)}) custom-call(s32[40]{0:T(128)S(1)} %dynamic-slice_bitcast_fusion.row_ref, bf16[512,512]{1,0:T(8,128)(2,1)S(1)} %collective-permute-done.5.refs_1_.refs_0_, ...), custom_call_target="tpu_custom_call", output_to_operand_aliasing={{0}: (8, {})} | custom-call | tf_op jit(solution)/shard_map/pallas_call | solution.py:86
  74.7 1.8 %shard_map.135.refs_10_.grad_ref = f32[512,1024]{1,0:T(8,128)S(1)} custom-call(s32[40]{0:T(128)S(1)} %dynamic-slice_bitcast_fusion.row_ref, bf16[384,4096]{1,0:T(8,128)(2,1)S(1)} %bitcast.24, bf16[384,1024]{1,0:T(8,128)(2,1)S(1)} %collective-permute-done.11.refs_9_.refs_5_.refs_2_.refs_0_.piece_ref, bf16[384,1024]{1,0:T(8,128)(2,1)S(1)} %bitcast.42, ...), custom_call_target="tpu_custom_call" | custom-call | tf_op jit(solution)/shard_map/pallas_call | solution.py:86
  78.7 3.6 %collective-permute-start.18 = (bf16[512,512]{1,0:T(8,128)(2,1)S(1)}, bf16[512,512]{1,0:T(8,128)(2,1)S(1)}, u32[]{:S(2)}, u32[]{:S(2)}) collective-permute-start(bf16[512,512]{1,0:T(8,128)(2,1)S(1)} %get-tuple-element.67.refs_9_), channel_id=1, source_target_pairs={{0,2},{1,3},{2,0},{3,1},{4,6},{5,7},{6,4},{7,5},{8,10},{9,11},{10,... | collective-permute-start | bytes 1572872 | tf_op jit(solution)/shard_map/ppermute | solution.py:461
  82.4 3.9 %shard_map.130 = (f32[384,1024]{1,0:T(8,128)S(1)}, f32[384,1024]{1,0:T(8,128)S(1)}) custom-call(s32[40]{0:T(128)S(1)} %dynamic-slice_bitcast_fusion.row_ref, bf16[512,1024]{1,0:T(8,128)(2,1)S(1)} %get-tuple-element.52.refs_0_, bf16[512,1024]{1,0:T(8,128)(2,1)S(1)} %get-tuple-element.53.refs_1_, bf16[512,1024]{1,0:T(8,128)(2,1)S(1)} %get-tuple-element.54.refs_2_, ...), custom_call_target="tpu_custom_call" | custom-call | tf_op jit(solution)/shard_map/pallas_call | solution.py:86
  87.8 1.5 %collective-permute-start.16 = (bf16[512,512]{1,0:T(8,128)(2,1)S(1)}, bf16[512,512]{1,0:T(8,128)(2,1)S(1)}, u32[]{:S(2)}, u32[]{:S(2)}) collective-permute-start(bf16[512,512]{1,0:T(8,128)(2,1)S(1)} %get-tuple-element.68), channel_id=1, source_target_pairs={{0,2},{1,3},{2,0},{3,1},{4,6},{5,7},{6,4},{7,5},{8,10},{9,11},{10,... | collective-permute-start | bytes 1572872 | tf_op jit(solution)/shard_map/ppermute | solution.py:461
  90.0 2.5 %shard_map.128 = (bf16[384,4096]{1,0:T(8,128)(2,1)}, bf16[384,512]{1,0:T(8,128)(2,1)S(1)}, bf16[512,1024]{1,0:T(8,128)(2,1)S(1)}) custom-call(s32[40]{0:T(128)S(1)} %dynamic-slice_bitcast_fusion.row_ref, bf16[512,1024]{1,0:T(8,128)(2,1)S(1)} %collective-permute-done.refs_1_.refs_0_, ...), custom_call_target="tpu_custom_call", output_to_operand_aliasing={{0}: (7, {})} | custom-call | tf_op jit(solution)/shard_map/pallas_call | solution.py:86
  92.6 1.9 %shard_map.131 = (f32[384,1024]{1,0:T(8,128)S(1)}, bf16[384,1536]{1,0:T(8,128)(2,1)S(1)}) custom-call(s32[40]{0:T(128)S(1)} %dynamic-slice_bitcast_fusion.row_ref, bf16[512,1024]{1,0:T(8,128)(2,1)S(1)} %get-tuple-element.50.refs_0_, bf16[384,4096]{1,0:T(8,128)(2,1)S(1)} %bitcast.32, ...), custom_call_target="tpu_custom_call" | custom-call | tf_op jit(solution)/shard_map/pallas_call | solution.py:86
  96.3 3.1 %shard_map.138 = (f32[512,1024]{1,0:T(8,128)}, f32[512,1024]{1,0:T(8,128)}, bf16[512,512]{1,0:T(8,128)(2,1)S(1)}) custom-call(s32[40]{0:T(128)S(1)} %dynamic-slice_bitcast_fusion.row_ref, bf16[512,512]{1,0:T(8,128)(2,1)S(1)} %collective-permute-done.18.up_ref, bf16[512,512]{1,0:T(8,128)(2,1)S(1)} %collective-permute-done.19.dn_ref, ...), custom_call_target="tpu_custom_call" | custom-call | tf_op jit(solution)/shard_map/pallas_call | solution.py:86
  99.3 1.5 %collective-permute-start.24 = (bf16[512,512]{1,0:T(8,128)(2,1)S(1)}, bf16[512,512]{1,0:T(8,128)(2,1)S(1)}, u32[]{:S(2)}, u32[]{:S(2)}) collective-permute-start(bf16[512,512]{1,0:T(8,128)(2,1)S(1)} %get-tuple-element.74.stepped_ref), channel_id=1, source_target_pairs={{0,16},{8,24},{16,0},{24,8},{1,17},{9,25},{17,1},{25,9},{2,18},{10... | collective-permute-start | bytes 1572872 | tf_op jit(solution)/shard_map/ppermute | solution.py:436
  100.8 2.2 %shard_map.133.refs_3_.refs_2_ = bf16[384,4096]{1,0:T(8,128)(2,1)} custom-call(s32[40]{0:T(128)S(1)} %dynamic-slice_bitcast_fusion.row_ref, bf16[384,1024]{1,0:T(8,128)(2,1)S(1)} %collective-permute-done.11.refs_9_.refs_5_.refs_2_.refs_0_.piece_ref, bf16[384,1024]{1,0:T(8,128)(2,1)S(1)} %collective-permute-done.13.refs_1_.refs_2_, ...), custom_call_target="tpu_custom_call", output_to_operand_aliasing={{}: (4, {})} | custom-call | tf_op jit(solution)/shard_map/pallas_call | solution.py:86
  103.1 2.1 %collective-permute-done.16.up_ref = bf16[512,512]{1,0:T(8,128)(2,1)S(1)} collective-permute-done((bf16[512,512]{1,0:T(8,128)(2,1)S(1)}, bf16[512,512]{1,0:T(8,128)(2,1)S(1)}, u32[]{:S(2)}, u32[]{:S(2)}) %collective-permute-start.16) | collective-permute-done | bytes 524320 | tf_op jit(solution)/shard_map/ppermute | solution.py:461
  105.2 1.9 %copy-done.2 = bf16[384,4096]{1,0:T(8,128)(2,1)S(1)} copy-done((bf16[384,4096]{1,0:T(8,128)(2,1)S(1)}, bf16[384,4096]{1,0:T(8,128)(2,1)}, u32[]{:S(2)}) %copy-start.2) | copy-done | bytes 3145752
  107.0 3.1 %shard_map.139 = (f32[512,1024]{1,0:T(8,128)}, f32[512,1024]{1,0:T(8,128)}, bf16[512,512]{1,0:T(8,128)(2,1)S(1)}) custom-call(s32[40]{0:T(128)S(1)} %dynamic-slice_bitcast_fusion.row_ref, bf16[512,512]{1,0:T(8,128)(2,1)S(1)} %collective-permute-done.16.up_ref, ...), custom_call_target="tpu_custom_call", output_to_operand_aliasing={{0}: (7, {}), {1}: (8, {})} | custom-call | tf_op jit(solution)/shard_map/pallas_call | solution.py:86
  110.1 1.5 %collective-permute-start.21 = (bf16[512,512]{1,0:T(8,128)(2,1)S(1)}, bf16[512,512]{1,0:T(8,128)(2,1)S(1)}, u32[]{:S(2)}, u32[]{:S(2)}) collective-permute-start(bf16[512,512]{1,0:T(8,128)(2,1)S(1)} %get-tuple-element.73.stepped_ref), channel_id=1, source_target_pairs={{0,16},{8,24},{16,0},{24,8},{1,17},{9,25},{17,1},{25,9},{2,18},{10... | collective-permute-start | bytes 1572872 | tf_op jit(solution)/shard_map/ppermute | solution.py:436
  112.1 9.6 %collective-permute-done.21.refs_1_ = bf16[512,512]{1,0:T(8,128)(2,1)S(1)} collective-permute-done((bf16[512,512]{1,0:T(8,128)(2,1)S(1)}, bf16[512,512]{1,0:T(8,128)(2,1)S(1)}, u32[]{:S(2)}, u32[]{:S(2)}) %collective-permute-start.21) | collective-permute-done | bytes 524320 | tf_op jit(solution)/shard_map/ppermute | solution.py:436
  121.7 1.7 %shard_map.134 = (bf16[384,4096]{1,0:T(8,128)(2,1)}, bf16[384,1024]{1,0:T(8,128)(2,1)}) custom-call(s32[40]{0:T(128)S(1)} %dynamic-slice_bitcast_fusion.row_ref, bf16[384,1536]{1,0:T(8,128)(2,1)S(1)} %collective-permute-done.12.refs_0_.refs_2_.refs_3_, f32[384,1024]{1,0:T(8,128)S(1)} %get-tuple-element.59.refs_1_, ...), custom_call_target="tpu_custom_call", output_to_operand_aliasing={{0}: (4, {})} | custom-call | tf_op jit(solution)/shard_map/pallas_call | solution.py:86
  123.4 1.5 %shard_map.140.refs_3_ = bf16[512,1024]{1,0:T(8,128)(2,1)} custom-call(s32[40]{0:T(128)S(1)} %dynamic-slice_bitcast_fusion.row_ref, s32[4]{0:T(128)S(1)} %copy-done.8, s32[4]{0:T(128)S(1)} %copy-done.9, bf16[512,512]{1,0:T(8,128)(2,1)S(1)} %get-tuple-element.74.stepped_ref, bf16[512,512]{1,0:T(8,128)(2,1)S(1)} %collective-permute-done.23.refs_0_, ...), custom_call_target="tpu_custom_call" | custom-call | tf_op jit(solution)/shard_map/pallas_call | solution.py:86
  125.0 1.5 %shard_map.141 = bf16[512,1024]{1,0:T(8,128)(2,1)} custom-call(s32[40]{0:T(128)S(1)} %dynamic-slice_bitcast_fusion.row_ref, s32[4]{0:T(128)S(1)} %copy-done.8, s32[4]{0:T(128)S(1)} %copy-done.9, bf16[512,512]{1,0:T(8,128)(2,1)S(1)} %get-tuple-element.73.stepped_ref, ...), custom_call_target="tpu_custom_call", output_to_operand_aliasing={{}: (7, {})} | custom-call | tf_op jit(solution)/shard_map/pallas_call | solution.py:86
  (64 shorter events, 20.6 us)
Async XLA Ops:
  0.6 29.2 %collective-permute-start.3 = (bf16[384,1024]{1,0:T(8,128)(2,1)}, bf16[384,1024]{1,0:T(8,128)(2,1)S(1)}, u32[]{:S(2)}, u32[]{:S(2)}) collective-permute-start(bf16[384,1024]{1,0:T(8,128)(2,1)} %bitcast.34), channel_id=1, source_target_pairs={{0,1},{1,0},{2,3},{3,2},{4,5},{5,4},{6,7},{7,6},{8,9},{9,8},{10,11... | collective-permute-start | bytes 2359304 | tf_op jit(solution)/shard_map/ppermute | solution.py:477
  3.6 28.6 %collective-permute-start.1 = (bf16[512,1024]{1,0:T(8,128)(2,1)}, bf16[512,1024]{1,0:T(8,128)(2,1)S(1)}, u32[]{:S(2)}, u32[]{:S(2)}) collective-permute-start(bf16[512,1024]{1,0:T(8,128)(2,1)} %bitcast.46), channel_id=1, source_target_pairs={{2,4},{3,5},{4,2},{5,3},{10,12},{11,13},{12,10},{13,11},{18,20},{1... | collective-permute-start | bytes 3145736 | tf_op jit(solution)/shard_map/ppermute | solution.py:461
  4.4 27.9 %collective-permute-start = (bf16[512,1024]{1,0:T(8,128)(2,1)}, bf16[512,1024]{1,0:T(8,128)(2,1)S(1)}, u32[]{:S(2)}, u32[]{:S(2)}) collective-permute-start(bf16[512,1024]{1,0:T(8,128)(2,1)} %bitcast.47), channel_id=1, source_target_pairs={{0,2},{1,3},{2,0},{3,1},{4,6},{5,7},{6,4},{7,5},{8,10},{9,11},{10,... | collective-permute-start | bytes 3145736 | tf_op jit(solution)/shard_map/ppermute | solution.py:461
  11.9 20.3 %copy-start.3 = (bf16[1,384,1024]{2,1,0:T(8,128)(2,1)S(1)}, bf16[1,384,1024]{2,1,0:T(8,128)(2,1)}, u32[]{:S(2)}) copy-start(bf16[1,384,1024]{2,1,0:T(8,128)(2,1)} %param.10) | copy-start | bytes 2359300
  11.9 17.9 %collective-permute-start.2 = (bf16[384,512]{1,0:T(8,128)(2,1)S(1)}, bf16[384,512]{1,0:T(8,128)(2,1)S(1)}, u32[]{:S(2)}, u32[]{:S(2)}) collective-permute-start(bf16[384,512]{1,0:T(8,128)(2,1)S(1)} %shard_map.119), channel_id=1, source_target_pairs={{0,1},{1,0},{2,3},{3,2},{4,5},{5,4},{6,7},{7,6},{8,9},{9,8},{10,11... | collective-permute-start | bytes 1179656 | tf_op jit(solution)/shard_map/ppermute | solution.py:475
  30.4 8.1 %copy-start.4 = (bf16[1,512,1024]{2,1,0:T(8,128)(2,1)S(1)}, bf16[1,512,1024]{2,1,0:T(8,128)(2,1)}, u32[]{:S(2)}) copy-start(bf16[1,512,1024]{2,1,0:T(8,128)(2,1)} %param.9) | copy-start | bytes 3145732
  30.4 18.8 %collective-permute-start.6 = (bf16[384,1024]{1,0:T(8,128)(2,1)S(1)}, bf16[384,1024]{1,0:T(8,128)(2,1)S(1)}, u32[]{:S(2)}, u32[]{:S(2)}) collective-permute-start(bf16[384,1024]{1,0:T(8,128)(2,1)S(1)} %shard_map.121), channel_id=1, source_target_pairs={{0,1},{1,0},{2,3},{3,2},{4,5},{5,4},{6,7},{7,6},{8,9},{9,8},{10,11... | collective-permute-start | bytes 2359304 | tf_op jit(solution)/shard_map/ppermute | solution.py:475
  33.8 7.1 %copy-start.1 = (bf16[1,384,4096]{2,1,0:T(8,128)(2,1)S(1)}, bf16[1,384,4096]{2,1,0:T(8,128)(2,1)}, u32[]{:S(2)}) copy-start(bf16[1,384,4096]{2,1,0:T(8,128)(2,1)} %param.8) | copy-start | bytes 9437188
  33.8 17.5 %collective-permute-start.4 = (bf16[512,512]{1,0:T(8,128)(2,1)S(1)}, bf16[512,512]{1,0:T(8,128)(2,1)S(1)}, u32[]{:S(2)}, u32[]{:S(2)}) collective-permute-start(bf16[512,512]{1,0:T(8,128)(2,1)S(1)} %get-tuple-element.41), channel_id=1, source_target_pairs={{2,4},{3,5},{4,2},{5,3},{10,12},{11,13},{12,10},{13,11},{18,20},{1... | collective-permute-start | bytes 1572872 | tf_op jit(solution)/shard_map/ppermute | solution.py:461
  34.6 16.7 %collective-permute-start.5 = (bf16[512,512]{1,0:T(8,128)(2,1)S(1)}, bf16[512,512]{1,0:T(8,128)(2,1)S(1)}, u32[]{:S(2)}, u32[]{:S(2)}) collective-permute-start(bf16[512,512]{1,0:T(8,128)(2,1)S(1)} %get-tuple-element.42.refs_7_), channel_id=1, source_target_pairs={{0,2},{1,3},{2,0},{3,1},{4,6},{5,7},{6,4},{7,5},{8,10},{9,11},{10,... | collective-permute-start | bytes 1572872 | tf_op jit(solution)/shard_map/ppermute | solution.py:461
  42.5 15.5 %collective-permute-start.8 = (bf16[512,512]{1,0:T(8,128)(2,1)S(1)}, bf16[512,512]{1,0:T(8,128)(2,1)S(1)}, u32[]{:S(2)}, u32[]{:S(2)}) collective-permute-start(bf16[512,512]{1,0:T(8,128)(2,1)S(1)} %get-tuple-element.45), channel_id=1, source_target_pairs={{2,4},{3,5},{4,2},{5,3},{10,12},{11,13},{12,10},{13,11},{18,20},{1... | collective-permute-start | bytes 1572872 | tf_op jit(solution)/shard_map/ppermute | solution.py:461
  43.2 19.4 %collective-permute-start.9 = (bf16[512,512]{1,0:T(8,128)(2,1)S(1)}, bf16[512,512]{1,0:T(8,128)(2,1)S(1)}, u32[]{:S(2)}, u32[]{:S(2)}) collective-permute-start(bf16[512,512]{1,0:T(8,128)(2,1)S(1)} %get-tuple-element.43.refs_8_), channel_id=1, source_target_pairs={{0,2},{1,3},{2,0},{3,1},{4,6},{5,7},{6,4},{7,5},{8,10},{9,11},{10,... | collective-permute-start | bytes 1572872 | tf_op jit(solution)/shard_map/ppermute | solution.py:461
  49.8 23.7 %collective-permute-start.11 = (bf16[384,1024]{1,0:T(8,128)(2,1)S(1)}, bf16[384,1024]{1,0:T(8,128)(2,1)S(1)}, u32[]{:S(2)}, u32[]{:S(2)}) collective-permute-start(bf16[384,1024]{1,0:T(8,128)(2,1)S(1)} %shard_map.129), channel_id=1, source_target_pairs={{0,1},{1,0},{2,3},{3,2},{4,5},{5,4},{6,7},{7,6},{8,9},{9,8},{10,11... | collective-permute-start | bytes 2359304 | tf_op jit(solution)/shard_map/ppermute | solution.py:496
  52.8 23.7 %collective-permute-start.15 = (bf16[512,512]{1,0:T(8,128)(2,1)S(1)}, bf16[512,512]{1,0:T(8,128)(2,1)S(1)}, u32[]{:S(2)}, u32[]{:S(2)}) collective-permute-start(bf16[512,512]{1,0:T(8,128)(2,1)S(1)} %get-tuple-element.66), channel_id=1, source_target_pairs={{2,4},{3,5},{4,2},{5,3},{10,12},{11,13},{12,10},{13,11},{18,20},{1... | collective-permute-start | bytes 1572872 | tf_op jit(solution)/shard_map/ppermute | solution.py:461
  53.5 23.0 %collective-permute-start.7 = (bf16[512,512]{1,0:T(8,128)(2,1)S(1)}, bf16[512,512]{1,0:T(8,128)(2,1)S(1)}, u32[]{:S(2)}, u32[]{:S(2)}) collective-permute-start(bf16[512,512]{1,0:T(8,128)(2,1)S(1)} %get-tuple-element.44.refs_8_), channel_id=1, source_target_pairs={{0,2},{1,3},{2,0},{3,1},{4,6},{5,7},{6,4},{7,5},{8,10},{9,11},{10,... | collective-permute-start | bytes 1572872 | tf_op jit(solution)/shard_map/ppermute | solution.py:461
  64.0 22.2 %collective-permute-start.14 = (bf16[512,512]{1,0:T(8,128)(2,1)S(1)}, bf16[512,512]{1,0:T(8,128)(2,1)S(1)}, u32[]{:S(2)}, u32[]{:S(2)}) collective-permute-start(bf16[512,512]{1,0:T(8,128)(2,1)S(1)} %get-tuple-element.65), channel_id=1, source_target_pairs={{2,4},{3,5},{4,2},{5,3},{10,12},{11,13},{12,10},{13,11},{18,20},{1... | collective-permute-start | bytes 1572872 | tf_op jit(solution)/shard_map/ppermute | solution.py:461
  64.7 21.6 %collective-permute-start.10 = (bf16[512,512]{1,0:T(8,128)(2,1)S(1)}, bf16[512,512]{1,0:T(8,128)(2,1)S(1)}, u32[]{:S(2)}, u32[]{:S(2)}) collective-permute-start(bf16[512,512]{1,0:T(8,128)(2,1)S(1)} %get-tuple-element.46.refs_9_), channel_id=1, source_target_pairs={{0,2},{1,3},{2,0},{3,1},{4,6},{5,7},{6,4},{7,5},{8,10},{9,11},{10,... | collective-permute-start | bytes 1572872 | tf_op jit(solution)/shard_map/ppermute | solution.py:461
  74.1 26.7 %collective-permute-start.13 = (bf16[384,1024]{1,0:T(8,128)(2,1)S(1)}, bf16[384,1024]{1,0:T(8,128)(2,1)S(1)}, u32[]{:S(2)}, u32[]{:S(2)}) collective-permute-start(bf16[384,1024]{1,0:T(8,128)(2,1)S(1)} %shard_map.132), channel_id=1, source_target_pairs={{0,1},{1,0},{2,3},{3,2},{4,5},{5,4},{6,7},{7,6},{8,9},{9,8},{10,11... | collective-permute-start | bytes 2359304 | tf_op jit(solution)/shard_map/ppermute | solution.py:496
  78.0 16.5 %collective-permute-start.19 = (bf16[512,512]{1,0:T(8,128)(2,1)S(1)}, bf16[512,512]{1,0:T(8,128)(2,1)S(1)}, u32[]{:S(2)}, u32[]{:S(2)}) collective-permute-start(bf16[512,512]{1,0:T(8,128)(2,1)S(1)} %get-tuple-element.70), channel_id=1, source_target_pairs={{2,4},{3,5},{4,2},{5,3},{10,12},{11,13},{12,10},{13,11},{18,20},{1... | collective-permute-start | bytes 1572872 | tf_op jit(solution)/shard_map/ppermute | solution.py:461
  78.7 17.5 %collective-permute-start.18 = (bf16[512,512]{1,0:T(8,128)(2,1)S(1)}, bf16[512,512]{1,0:T(8,128)(2,1)S(1)}, u32[]{:S(2)}, u32[]{:S(2)}) collective-permute-start(bf16[512,512]{1,0:T(8,128)(2,1)S(1)} %get-tuple-element.67.refs_9_), channel_id=1, source_target_pairs={{0,2},{1,3},{2,0},{3,1},{4,6},{5,7},{6,4},{7,5},{8,10},{9,11},{10,... | collective-permute-start | bytes 1572872 | tf_op jit(solution)/shard_map/ppermute | solution.py:461
  87.8 17.3 %collective-permute-start.16 = (bf16[512,512]{1,0:T(8,128)(2,1)S(1)}, bf16[512,512]{1,0:T(8,128)(2,1)S(1)}, u32[]{:S(2)}, u32[]{:S(2)}) collective-permute-start(bf16[512,512]{1,0:T(8,128)(2,1)S(1)} %get-tuple-element.68), channel_id=1, source_target_pairs={{0,2},{1,3},{2,0},{3,1},{4,6},{5,7},{6,4},{7,5},{8,10},{9,11},{10,... | collective-permute-start | bytes 1572872 | tf_op jit(solution)/shard_map/ppermute | solution.py:461
  89.4 15.8 %collective-permute-start.17 = (bf16[512,512]{1,0:T(8,128)(2,1)S(1)}, bf16[512,512]{1,0:T(8,128)(2,1)S(1)}, u32[]{:S(2)}, u32[]{:S(2)}) collective-permute-start(bf16[512,512]{1,0:T(8,128)(2,1)S(1)} %get-tuple-element.69), channel_id=1, source_target_pairs={{2,4},{3,5},{4,2},{5,3},{10,12},{11,13},{12,10},{13,11},{18,20},{1... | collective-permute-start | bytes 1572872 | tf_op jit(solution)/shard_map/ppermute | solution.py:461
  92.6 3.7 %copy-start.5 = (f32[1,512,1024]{2,1,0:T(8,128)S(1)}, f32[1,512,1024]{2,1,0:T(8,128)}, u32[]{:S(2)}) copy-start(f32[1,512,1024]{2,1,0:T(8,128)} %param.11) | copy-start | bytes 6291460
  92.6 3.7 %copy-start.6 = (f32[1,512,1024]{2,1,0:T(8,128)S(1)}, f32[1,512,1024]{2,1,0:T(8,128)}, u32[]{:S(2)}) copy-start(f32[1,512,1024]{2,1,0:T(8,128)} %param.12) | copy-start | bytes 6291460
  94.5 27.2 %collective-permute-start.12 = (bf16[384,1536]{1,0:T(8,128)(2,1)S(1)}, bf16[384,1536]{1,0:T(8,128)(2,1)S(1)}, u32[]{:S(2)}, u32[]{:S(2)}) collective-permute-start(bf16[384,1536]{1,0:T(8,128)(2,1)S(1)} %get-tuple-element.58.refs_0_.refs_3_), channel_id=1, source_target_pairs={{0,1},{1,0},{2,3},{3,2},{4,5},{5,4},{6,7},{7,6},{8,9},{9,8},{10,11... | collective-permute-start | bytes 3538952 | tf_op jit(solution)/shard_map/ppermute | solution.py:521
  99.3 12.3 %collective-permute-start.24 = (bf16[512,512]{1,0:T(8,128)(2,1)S(1)}, bf16[512,512]{1,0:T(8,128)(2,1)S(1)}, u32[]{:S(2)}, u32[]{:S(2)}) collective-permute-start(bf16[512,512]{1,0:T(8,128)(2,1)S(1)} %get-tuple-element.74.stepped_ref), channel_id=1, source_target_pairs={{0,16},{8,24},{16,0},{24,8},{1,17},{9,25},{17,1},{25,9},{2,18},{10... | collective-permute-start | bytes 1572872 | tf_op jit(solution)/shard_map/ppermute | solution.py:436
  105.2 1.9 %copy-start.2 = (bf16[384,4096]{1,0:T(8,128)(2,1)S(1)}, bf16[384,4096]{1,0:T(8,128)(2,1)}, u32[]{:S(2)}) copy-start(bf16[384,4096]{1,0:T(8,128)(2,1)} %shard_map.133.refs_3_.refs_2_) | copy-start | bytes 9437188
  110.1 11.6 %collective-permute-start.21 = (bf16[512,512]{1,0:T(8,128)(2,1)S(1)}, bf16[512,512]{1,0:T(8,128)(2,1)S(1)}, u32[]{:S(2)}, u32[]{:S(2)}) collective-permute-start(bf16[512,512]{1,0:T(8,128)(2,1)S(1)} %get-tuple-element.73.stepped_ref), channel_id=1, source_target_pairs={{0,16},{8,24},{16,0},{24,8},{1,17},{9,25},{17,1},{25,9},{2,18},{10... | collective-permute-start | bytes 1572872 | tf_op jit(solution)/shard_map/ppermute | solution.py:436
  111.6 11.8 %collective-permute-start.23 = (bf16[512,512]{1,0:T(8,128)(2,1)S(1)}, bf16[512,512]{1,0:T(8,128)(2,1)S(1)}, u32[]{:S(2)}, u32[]{:S(2)}) collective-permute-start(bf16[512,512]{1,0:T(8,128)(2,1)S(1)} %get-tuple-element.74.stepped_ref), channel_id=1, source_target_pairs={{0,8},{8,0},{16,24},{24,16},{1,9},{9,1},{17,25},{25,17},{2,10},{10... | collective-permute-start | bytes 1572872 | tf_op jit(solution)/shard_map/ppermute | solution.py:438
  111.6 11.8 %collective-permute-start.25 = (bf16[512,512]{1,0:T(8,128)(2,1)S(1)}, bf16[512,512]{1,0:T(8,128)(2,1)S(1)}, u32[]{:S(2)}, u32[]{:S(2)}) collective-permute-start(bf16[512,512]{1,0:T(8,128)(2,1)S(1)} %collective-permute-done.24.refs_1_), channel_id=1, source_target_pairs={{0,8},{8,0},{16,24},{24,16},{1,9},{9,1},{17,25},{25,17},{2,10},{10... | collective-permute-start | bytes 1572872 | tf_op jit(solution)/shard_map/ppermute | solution.py:438
  112.1 12.8 %collective-permute-start.20 = (bf16[512,512]{1,0:T(8,128)(2,1)S(1)}, bf16[512,512]{1,0:T(8,128)(2,1)S(1)}, u32[]{:S(2)}, u32[]{:S(2)}) collective-permute-start(bf16[512,512]{1,0:T(8,128)(2,1)S(1)} %get-tuple-element.73.stepped_ref), channel_id=1, source_target_pairs={{0,8},{8,0},{16,24},{24,16},{1,9},{9,1},{17,25},{25,17},{2,10},{10... | collective-permute-start | bytes 1572872 | tf_op jit(solution)/shard_map/ppermute | solution.py:438
  121.7 3.3 %collective-permute-start.22 = (bf16[512,512]{1,0:T(8,128)(2,1)S(1)}, bf16[512,512]{1,0:T(8,128)(2,1)S(1)}, u32[]{:S(2)}, u32[]{:S(2)}) collective-permute-start(bf16[512,512]{1,0:T(8,128)(2,1)S(1)} %collective-permute-done.21.refs_1_), channel_id=1, source_target_pairs={{0,8},{8,0},{16,24},{24,16},{1,9},{9,1},{17,25},{25,17},{2,10},{10... | collective-permute-start | bytes 1572872 | tf_op jit(solution)/shard_map/ppermute | solution.py:438
  (4 other events, 6.9 us)

commit v8 on v7

--- a/solution.py
+++ b/solution.py
@@ -313,21 +313,23 @@
     )
 
 
-def place(plan, row, xg, arrived, first, sums=None):
+def place(plan, row, xg, arrived, first, sums=None, after=()):
     count = len(arrived)
     tokens, width = arrived[0].shape
     table = [plan[f"theirs{first + j}"] for j in range(count)]
 
     def kernel(row_ref, *refs):
         g = pl.program_id(0)
-        out_ref = refs[-1] if sums is None else refs[-2]
+        out_ref = refs[-2]
         for j in range(count):
 
             @pl.when(g == j)
             def _():
                 out_ref[...] = refs[j][...]
 
-        if sums is not None:
+        if sums is None:
+            refs[-1][...] = jnp.zeros_like(refs[-1])
+        else:
             total = refs[count][...] + refs[count + 1][...].astype(jnp.float32)
             refs[-1][...] = total.astype(jnp.bfloat16)
 
@@ -339,7 +341,10 @@
 
     ins = [view.operand() for view in arrived]
     outs = [(struct(xg.shape, xg.dtype), pl.BlockSpec((tokens, width), column))]
-    if sums is not None:
+    if sums is None:
+        tile = struct((8, 128), jnp.float32)
+        outs.append((tile, whole(tile)))
+    else:
         own, other = sums
         kv_block = pl.BlockSpec((tokens // count, own.shape[1]), lambda g, row: (g, 0))
         assert other.start == 0
@@ -349,7 +354,7 @@
     return call(
         kernel,
         row,
-        ins + [(xg, HBM)],
+        ins + [(xg, HBM)] + [(a, ANY) for a in after],
         outs,
         grid=(count,),
         aliases=aliases,
@@ -381,7 +386,7 @@
     if kept is not None:
         aliases = {1 + len(ins): 0, 2 + len(ins): 1}
         ins += [(a, HBM) for a in kept]
-    ins += [(a, ANY) for a in after]
+    ins += after
     return call(
         kernel,
         row,
@@ -408,11 +413,14 @@
 
             @pl.when((partner_ref[0] == j + 1) | (count == 1))
             def _():
-                refs[-1][...] = (
+                refs[-2][...] = (
                     (1.0 - mix) * stepped_ref[...].astype(jnp.float32)
                     + mix * refs[j][...].astype(jnp.float32)
                 ).astype(jnp.bfloat16)
 
+        refs[-1][...] = jnp.zeros_like(refs[-1])
+
+    tile = struct((8, 128), jnp.float32)
     local = pl.BlockSpec((size, columns), lambda g, *scalars: (g, 0))
     part = pl.BlockSpec((size, columns), lambda g, *scalars: (g, h))
     ins = [(a, local) for a in (stepped, *others)]
@@ -423,10 +431,13 @@
         kernel,
         scalars,
         ins,
-        [(struct((rows, width), jnp.bfloat16), part)],
+        [
+            (struct((rows, width), jnp.bfloat16), part),
+            (tile, pl.BlockSpec(tile.shape, lambda g, *scalars: (0, 0))),
+        ],
         grid=(steps,),
         aliases={} if kept is None else {count + 4: 0},
-    )[0]
+    )
 
 
 def partner_rows(stepped, partner, replica, n_rep):
@@ -503,15 +514,18 @@
     bufs = {}
     for s in range(2, depth + 1):
         if s == depth:
-            for j in range(1, depth - 1):
+            for j in range(2, depth - 1):
                 xg = shard_step(j, xg)
             send_parts(parts[1:], [], [parcel])
             grad = own_gradient(plan, row, act, pieces[depth - 1], cot, cot_oth)
             sums = values(plan, row, list(range(depth - 1)), shards, act, pieces, None)
         for h in range(CHUNKS):
             after = list(bufs.values())[:1]
-            if s == depth:
-                after.append(grad if h == 0 else sums[0])
+            if s == 3 and h == 0:
+                xg = shard_step(1, xg)
+                after.append(parts[1].array)
+            if s == depth and h == CHUNKS - 1:
+                after.append(sums[0])
             bufs = relay(
                 plan, row, s, got[s - 1, h], act, pieces[: s - 1], part(cot, h), cot_oth[h], after
             )
@@ -524,19 +538,19 @@
     moments, averaged, placed = None, None, None
     for h in range(CHUNKS):
         last = h == CHUNKS - 1
-        after = [] if h == 0 else [placed]
+        after = [] if h == 0 else [(tile, ANY)]
         *moments, stepped = adam(
-            row, h, got[depth, h], grad, weights, first, second, moments, after + [parcel]
+            row, h, got[depth, h], grad, weights, first, second, moments, after + [(parcel, ANY)]
         )
         if placed is None:
-            placed = place(plan, row, xg, arrived, 0)[0]
+            placed, tile = place(plan, row, xg, arrived, 0)
         others = partner_rows(stepped, partner, row[plan["replica"]], n_rep)
         if last:
             views = [View(final, columns, rows)]
             kv_views = (kv_own, View(final, 0, columns))
-            x_grad, kv_out = place(plan, row, placed, views, depth - 1, kv_views)
-        averaged = average(
-            plan, scalars, h, stepped, others, averaged, columns, [kv_out] if last else [final]
+            x_grad, kv_out = place(plan, row, placed, views, depth - 1, kv_views, [tile])
+        averaged, tile = average(
+            plan, scalars, h, stepped, others, averaged, columns, [kv_out] if last else []
         )
     return (
         kv_out[None],

time: 127 us -> 167 us (1.31)
  waiting for transfers between devices: 39 us -> 80.3 us
    ppermute x2, waiting for transfers between devices: 0.01 us -> 19.1 us  [send_parts(): parcel = swap(pack(plan, row, rows, views, act, turns, after))]
    ppermute x14, waiting for transfers between devices: 7.61 us -> 24.1 us  [exchange(): lax.ppermute(bufs[name], 'fsdp', links[name])]
    ppermute x2, waiting for transfers between devices: 9.55 us -> 15 us  [partner_rows(): far = lax.ppermute(stepped, 'rep', [(r, r ^ 2) for r in range(4)])]
    ppermute x14, starting transfers between devices: 28.1 us -> 30.4 us  [exchange(): lax.ppermute(bufs[name], 'fsdp', links[name])]
    unnamed x20 -> x18, local copies, waits for them, and re-layouts: 3.82 us -> 3.34 us
  transfers between devices with their start and end apart: 26 -> 26, of which waited for: 6 -> 9; matrix products, arithmetic and copies ran while one was open for 1% -> 0% of each run, Pallas kernels for 32% -> 23%
where the time goes in v8:
time: 167 us; the launch traced here: 166 us
  waiting for transfers between devices  80.3 us (48%)
  Pallas kernels  42 us (25%)
  starting transfers between devices  38.9 us (23%)
  local copies, waits for them, and re-layouts  4.03 us (2%)
    pallas_call x23, Pallas kernels, call(): pl.pallas_call(kernel, grid_spec=pltpu.PrefetchScalarGridSpec(num_scalar_...  42 us
    ppermute x14, starting transfers between devices, exchange(): lax.ppermute(bufs[name], 'fsdp', links[name])  30.4 us
    ppermute x14, waiting for transfers between devices, exchange(): lax.ppermute(bufs[name], 'fsdp', links[name])  24.1 us
    ppermute x2, waiting for transfers between devices, send(): return swap(pack(plan, row, rows, [], act, turns, after))  22.1 us
    ppermute x2, waiting for transfers between devices, send_parts(): parcel = swap(pack(plan, row, rows, views, act, turns, after))  19.1 us
    ppermute x2, waiting for transfers between devices, partner_rows(): far = lax.ppermute(stepped, 'rep', [(r, r ^ 2) for r in range(4)])  15 us
  transfers between devices with their start and end apart: 26, of which 9 were waited for; matrix products, arithmetic and copies ran while one was open for 0% of the time, Pallas kernels for 23%

profile of v8, /device:TPU:0, one launch (start us, length us, event | category | flops | bytes accessed | tf_op | source)
XLA Modules:
  0.0 166.2 jit_solution(1810133143520203463)
XLA Ops:
  1.4 5.8 %collective-permute-start = (bf16[512,1024]{1,0:T(8,128)(2,1)}, bf16[512,1024]{1,0:T(8,128)(2,1)S(1)}, u32[]{:S(2)}, u32[]{:S(2)}) collective-permute-start(bf16[512,1024]{1,0:T(8,128)(2,1)} %bitcast.46), channel_id=1, source_target_pairs={{0,2},{1,3},{2,0},{3,1},{4,6},{5,7},{6,4},{7,5},{8,10},{9,11},{10,... | collective-permute-start | bytes 3145736 | tf_op jit(solution)/shard_map/ppermute | solution.py:472
  9.4 1.9 %copy-done = bf16[1,384,4096]{2,1,0:T(8,128)(2,1)S(1)} copy-done((bf16[1,384,4096]{2,1,0:T(8,128)(2,1)S(1)}, bf16[1,384,4096]{2,1,0:T(8,128)(2,1)}, u32[]{:S(2)}) %copy-start) | copy-done | bytes 3145752
  12.5 22.1 %collective-permute-done.2.refs_4_.refs_3_.refs_6_.refs_2_ = bf16[384,512]{1,0:T(8,128)(2,1)S(1)} collective-permute-done((bf16[384,512]{1,0:T(8,128)(2,1)S(1)}, bf16[384,512]{1,0:T(8,128)(2,1)S(1)}, u32[]{:S(2)}, u32[]{:S(2)}) %collective-permute-start.2) | collective-permute-done | bytes 393248 | tf_op jit(solution)/shard_map/ppermute | solution.py:486
  35.2 1.6 collective-permute-start.6
  36.8 1.5 shard_map.120
  40.4 1.5 shard_map.122
  42.6 2.2 %collective-permute-start.9 = (bf16[512,512]{1,0:T(8,128)(2,1)S(1)}, bf16[512,512]{1,0:T(8,128)(2,1)S(1)}, u32[]{:S(2)}, u32[]{:S(2)}) collective-permute-start(bf16[512,512]{1,0:T(8,128)(2,1)S(1)} %get-tuple-element.47.refs_8_), channel_id=1, source_target_pairs={{0,2},{1,3},{2,0},{3,1},{4,6},{5,7},{6,4},{7,5},{8,10},{9,11},{10,... | collective-permute-start | bytes 1572872 | tf_op jit(solution)/shard_map/ppermute | solution.py:472
  44.8 2.4 %shard_map.123 = (bf16[384,4096]{1,0:T(8,128)(2,1)}, bf16[384,512]{1,0:T(8,128)(2,1)S(1)}, bf16[512,1024]{1,0:T(8,128)(2,1)S(1)}) custom-call(s32[40]{0:T(128)S(1)} %dynamic-slice_bitcast_fusion.row_ref, bf16[512,1024]{1,0:T(8,128)(2,1)S(1)} %bitcast.47, ...), custom_call_target="tpu_custom_call" | custom-call | tf_op jit(solution)/shard_map/pallas_call | solution.py:86
  47.2 2.4 %shard_map.124 = (bf16[384,4096]{1,0:T(8,128)(2,1)}, bf16[384,512]{1,0:T(8,128)(2,1)S(1)}, bf16[512,1024]{1,0:T(8,128)(2,1)S(1)}) custom-call(s32[40]{0:T(128)S(1)} %dynamic-slice_bitcast_fusion.row_ref, bf16[512,1024]{1,0:T(8,128)(2,1)S(1)} %collective-permute-done.refs_1_.refs_0_, ...), custom_call_target="tpu_custom_call", output_to_operand_aliasing={{0}: (6, {})} | custom-call | tf_op jit(solution)/shard_map/pallas_call | solution.py:86
  49.7 4.2 %collective-permute-done.5.refs_1_.refs_0_ = bf16[512,512]{1,0:T(8,128)(2,1)S(1)} collective-permute-done((bf16[512,512]{1,0:T(8,128)(2,1)S(1)}, bf16[512,512]{1,0:T(8,128)(2,1)S(1)}, u32[]{:S(2)}, u32[]{:S(2)}) %collective-permute-start.5) | collective-permute-done | bytes 524320 | tf_op jit(solution)/shard_map/ppermute | solution.py:472
  56.1 4.2 %collective-permute-start.7 = (bf16[512,512]{1,0:T(8,128)(2,1)S(1)}, bf16[512,512]{1,0:T(8,128)(2,1)S(1)}, u32[]{:S(2)}, u32[]{:S(2)}) collective-permute-start(bf16[512,512]{1,0:T(8,128)(2,1)S(1)} %get-tuple-element.50.refs_8_), channel_id=1, source_target_pairs={{0,2},{1,3},{2,0},{3,1},{4,6},{5,7},{6,4},{7,5},{8,10},{9,11},{10,... | collective-permute-start | bytes 1572872 | tf_op jit(solution)/shard_map/ppermute | solution.py:472
  61.5 3.7 %collective-permute-done.9.refs_1_ = bf16[512,512]{1,0:T(8,128)(2,1)S(1)} collective-permute-done((bf16[512,512]{1,0:T(8,128)(2,1)S(1)}, bf16[512,512]{1,0:T(8,128)(2,1)S(1)}, u32[]{:S(2)}, u32[]{:S(2)}) %collective-permute-start.9) | collective-permute-done | bytes 524320 | tf_op jit(solution)/shard_map/ppermute | solution.py:472
  68.0 8.4 %collective-permute-done.7.refs_1_ = bf16[512,512]{1,0:T(8,128)(2,1)S(1)} collective-permute-done((bf16[512,512]{1,0:T(8,128)(2,1)S(1)}, bf16[512,512]{1,0:T(8,128)(2,1)S(1)}, u32[]{:S(2)}, u32[]{:S(2)}) %collective-permute-start.7) | collective-permute-done | bytes 524320 | tf_op jit(solution)/shard_map/ppermute | solution.py:472
  78.6 4.9 %collective-permute-start.15 = (bf16[512,512]{1,0:T(8,128)(2,1)S(1)}, bf16[512,512]{1,0:T(8,128)(2,1)S(1)}, u32[]{:S(2)}, u32[]{:S(2)}) collective-permute-start(bf16[512,512]{1,0:T(8,128)(2,1)S(1)} %get-tuple-element.69.refs_9_), channel_id=1, source_target_pairs={{0,2},{1,3},{2,0},{3,1},{4,6},{5,7},{6,4},{7,5},{8,10},{9,11},{10,... | collective-permute-start | bytes 1572872 | tf_op jit(solution)/shard_map/ppermute | solution.py:472
  83.5 2.5 %shard_map.127 = (bf16[384,4096]{1,0:T(8,128)(2,1)}, bf16[384,512]{1,0:T(8,128)(2,1)S(1)}, bf16[512,1024]{1,0:T(8,128)(2,1)S(1)}) custom-call(s32[40]{0:T(128)S(1)} %dynamic-slice_bitcast_fusion.row_ref, bf16[512,512]{1,0:T(8,128)(2,1)S(1)} %collective-permute-done.5.refs_1_.refs_0_, ...), custom_call_target="tpu_custom_call", output_to_operand_aliasing={{0}: (8, {})} | custom-call | tf_op jit(solution)/shard_map/pallas_call | solution.py:86
  86.0 1.6 collective-permute-done.10.refs_2_.refs_1_
  87.6 2.7 %shard_map.128 = (bf16[384,4096]{1,0:T(8,128)(2,1)}, bf16[384,512]{1,0:T(8,128)(2,1)S(1)}, bf16[512,1024]{1,0:T(8,128)(2,1)S(1)}) custom-call(s32[40]{0:T(128)S(1)} %dynamic-slice_bitcast_fusion.row_ref, bf16[512,1024]{1,0:T(8,128)(2,1)S(1)} %collective-permute-done.refs_1_.refs_0_, ...), custom_call_target="tpu_custom_call", output_to_operand_aliasing={{0}: (7, {})} | custom-call | tf_op jit(solution)/shard_map/pallas_call | solution.py:86
  90.4 1.8 %shard_map.135.grad_ref = f32[512,1024]{1,0:T(8,128)S(1)} custom-call(s32[40]{0:T(128)S(1)} %dynamic-slice_bitcast_fusion.row_ref, bf16[384,4096]{1,0:T(8,128)(2,1)S(1)} %bitcast.26, bf16[384,1024]{1,0:T(8,128)(2,1)S(1)} %collective-permute-done.11.refs_9_.refs_5_.refs_2_.refs_0_.piece_ref, bf16[384,1024]{1,0:T(8,128)(2,1)S(1)} %bitcast.43, ...), custom_call_target="tpu_custom_call" | custom-call | tf_op jit(solution)/shard_map/pallas_call | solution.py:86
  92.2 3.7 %shard_map.130 = (f32[384,1024]{1,0:T(8,128)S(1)}, f32[384,1024]{1,0:T(8,128)S(1)}) custom-call(s32[40]{0:T(128)S(1)} %dynamic-slice_bitcast_fusion.row_ref, bf16[512,1024]{1,0:T(8,128)(2,1)S(1)} %get-tuple-element.57.refs_0_, bf16[512,1024]{1,0:T(8,128)(2,1)S(1)} %get-tuple-element.58.refs_1_, bf16[512,1024]{1,0:T(8,128)(2,1)S(1)} %get-tuple-element.59.refs_2_, ...), custom_call_target="tpu_custom_call" | custom-call | tf_op jit(solution)/shard_map/pallas_call | solution.py:86
  96.0 1.9 %shard_map.131 = (f32[384,1024]{1,0:T(8,128)S(1)}, bf16[384,1536]{1,0:T(8,128)(2,1)S(1)}) custom-call(s32[40]{0:T(128)S(1)} %dynamic-slice_bitcast_fusion.row_ref, bf16[512,1024]{1,0:T(8,128)(2,1)S(1)} %get-tuple-element.55.refs_0_, bf16[384,4096]{1,0:T(8,128)(2,1)S(1)} %bitcast.30, ...), custom_call_target="tpu_custom_call" | custom-call | tf_op jit(solution)/shard_map/pallas_call | solution.py:86
  98.2 3.1 %shard_map.136 = (f32[512,1024]{1,0:T(8,128)}, f32[512,1024]{1,0:T(8,128)}, bf16[512,512]{1,0:T(8,128)(2,1)S(1)}) custom-call(s32[40]{0:T(128)S(1)} %dynamic-slice_bitcast_fusion.row_ref, bf16[512,512]{1,0:T(8,128)(2,1)S(1)} %collective-permute-done.15.up_ref, bf16[512,512]{1,0:T(8,128)(2,1)S(1)} %collective-permute-done.16.dn_ref, ...), custom_call_target="tpu_custom_call" | custom-call | tf_op jit(solution)/shard_map/pallas_call | solution.py:86
  103.6 6.8 %collective-permute-done.18.refs_1_ = bf16[512,512]{1,0:T(8,128)(2,1)S(1)} collective-permute-done((bf16[512,512]{1,0:T(8,128)(2,1)S(1)}, bf16[512,512]{1,0:T(8,128)(2,1)S(1)}, u32[]{:S(2)}, u32[]{:S(2)}) %collective-permute-start.18) | collective-permute-done | bytes 524320 | tf_op jit(solution)/shard_map/ppermute | solution.py:447
  111.9 5.6 %collective-permute-start.21 = (bf16[512,512]{1,0:T(8,128)(2,1)S(1)}, bf16[512,512]{1,0:T(8,128)(2,1)S(1)}, u32[]{:S(2)}, u32[]{:S(2)}) collective-permute-start(bf16[512,512]{1,0:T(8,128)(2,1)S(1)} %get-tuple-element.76), channel_id=1, source_target_pairs={{0,2},{1,3},{2,0},{3,1},{4,6},{5,7},{6,4},{7,5},{8,10},{9,11},{10,... | collective-permute-start | bytes 1572872 | tf_op jit(solution)/shard_map/ppermute | solution.py:472
  118.8 1.5 shard_map.137
  120.3 6.2 %collective-permute-done.21.up_ref = bf16[512,512]{1,0:T(8,128)(2,1)S(1)} collective-permute-done((bf16[512,512]{1,0:T(8,128)(2,1)S(1)}, bf16[512,512]{1,0:T(8,128)(2,1)S(1)}, u32[]{:S(2)}, u32[]{:S(2)}) %collective-permute-start.21) | collective-permute-done | bytes 524320 | tf_op jit(solution)/shard_map/ppermute | solution.py:472
  126.5 3.1 %shard_map.140 = (f32[512,1024]{1,0:T(8,128)}, f32[512,1024]{1,0:T(8,128)}, bf16[512,512]{1,0:T(8,128)(2,1)S(1)}) custom-call(s32[40]{0:T(128)S(1)} %dynamic-slice_bitcast_fusion.row_ref, bf16[512,512]{1,0:T(8,128)(2,1)S(1)} %collective-permute-done.21.up_ref, ...), custom_call_target="tpu_custom_call", output_to_operand_aliasing={{0}: (7, {}), {1}: (8, {})} | custom-call | tf_op jit(solution)/shard_map/pallas_call | solution.py:86
  129.6 1.5 collective-permute-start.24
  132.3 8.2 %collective-permute-done.24.refs_1_ = bf16[512,512]{1,0:T(8,128)(2,1)S(1)} collective-permute-done((bf16[512,512]{1,0:T(8,128)(2,1)S(1)}, bf16[512,512]{1,0:T(8,128)(2,1)S(1)}, u32[]{:S(2)}, u32[]{:S(2)}) %collective-permute-start.24) | collective-permute-done | bytes 524320 | tf_op jit(solution)/shard_map/ppermute | solution.py:447
  140.6 19.1 %collective-permute-done.13.refs_1_.refs_2_ = bf16[384,1024]{1,0:T(8,128)(2,1)S(1)} collective-permute-done((bf16[384,1024]{1,0:T(8,128)(2,1)S(1)}, bf16[384,1024]{1,0:T(8,128)(2,1)S(1)}, u32[]{:S(2)}, u32[]{:S(2)}) %collective-permute-start.13) | collective-permute-done | bytes 786464 | tf_op jit(solution)/shard_map/ppermute | solution.py:507
  159.7 2.2 %shard_map.133 = (bf16[384,4096]{1,0:T(8,128)(2,1)}, f32[8,128]{1,0:T(8,128)}) custom-call(s32[40]{0:T(128)S(1)} %dynamic-slice_bitcast_fusion.row_ref, bf16[384,1024]{1,0:T(8,128)(2,1)S(1)} %collective-permute-done.11.refs_9_.refs_5_.refs_2_.refs_0_.piece_ref, ...), custom_call_target="tpu_custom_call", output_to_operand_aliasing={{0}: (4, {})} | custom-call | tf_op jit(solution)/shard_map/pallas_call | solution.py:86
  161.9 1.7 %shard_map.138 = (bf16[384,4096]{1,0:T(8,128)(2,1)}, bf16[384,1024]{1,0:T(8,128)(2,1)}) custom-call(s32[40]{0:T(128)S(1)} %dynamic-slice_bitcast_fusion.row_ref, bf16[384,1536]{1,0:T(8,128)(2,1)S(1)} %collective-permute-done.12.refs_0_.refs_2_, f32[384,1024]{1,0:T(8,128)S(1)} %get-tuple-element.64.refs_1_, ...), custom_call_target="tpu_custom_call", output_to_operand_aliasing={{0}: (4, {})} | custom-call | tf_op jit(solution)/shard_map/pallas_call | solution.py:86
  164.7 1.5 shard_map.141
  (62 shorter events, 23.7 us)
Async XLA Ops:
  0.6 36.1 %collective-permute-start.1 = (bf16[512,1024]{1,0:T(8,128)(2,1)}, bf16[512,1024]{1,0:T(8,128)(2,1)S(1)}, u32[]{:S(2)}, u32[]{:S(2)}) collective-permute-start(bf16[512,1024]{1,0:T(8,128)(2,1)} %bitcast.45), channel_id=1, source_target_pairs={{2,4},{3,5},{4,2},{5,3},{10,12},{11,13},{12,10},{13,11},{18,20},{1... | collective-permute-start | bytes 3145736 | tf_op jit(solution)/shard_map/ppermute | solution.py:472
  1.4 35.4 %collective-permute-start = (bf16[512,1024]{1,0:T(8,128)(2,1)}, bf16[512,1024]{1,0:T(8,128)(2,1)S(1)}, u32[]{:S(2)}, u32[]{:S(2)}) collective-permute-start(bf16[512,1024]{1,0:T(8,128)(2,1)} %bitcast.46), channel_id=1, source_target_pairs={{0,2},{1,3},{2,0},{3,1},{4,6},{5,7},{6,4},{7,5},{8,10},{9,11},{10,... | collective-permute-start | bytes 3145736 | tf_op jit(solution)/shard_map/ppermute | solution.py:472
  7.2 27.4 %collective-permute-start.3 = (bf16[384,1024]{1,0:T(8,128)(2,1)}, bf16[384,1024]{1,0:T(8,128)(2,1)S(1)}, u32[]{:S(2)}, u32[]{:S(2)}) collective-permute-start(bf16[384,1024]{1,0:T(8,128)(2,1)} %bitcast.33), channel_id=1, source_target_pairs={{0,1},{1,0},{2,3},{3,2},{4,5},{5,4},{6,7},{7,6},{8,9},{9,8},{10,11... | collective-permute-start | bytes 2359304 | tf_op jit(solution)/shard_map/ppermute | solution.py:488
  11.9 24.9 %copy-start.2 = (bf16[1,384,1024]{2,1,0:T(8,128)(2,1)S(1)}, bf16[1,384,1024]{2,1,0:T(8,128)(2,1)}, u32[]{:S(2)}) copy-start(bf16[1,384,1024]{2,1,0:T(8,128)(2,1)} %param.10) | copy-start | bytes 2359300
  11.9 22.7 %collective-permute-start.2 = (bf16[384,512]{1,0:T(8,128)(2,1)S(1)}, bf16[384,512]{1,0:T(8,128)(2,1)S(1)}, u32[]{:S(2)}, u32[]{:S(2)}) collective-permute-start(bf16[384,512]{1,0:T(8,128)(2,1)S(1)} %shard_map.119), channel_id=1, source_target_pairs={{0,1},{1,0},{2,3},{3,2},{4,5},{5,4},{6,7},{7,6},{8,9},{9,8},{10,11... | collective-permute-start | bytes 1179656 | tf_op jit(solution)/shard_map/ppermute | solution.py:486
  35.2 18.8 %collective-permute-start.6 = (bf16[384,1024]{1,0:T(8,128)(2,1)S(1)}, bf16[384,1024]{1,0:T(8,128)(2,1)S(1)}, u32[]{:S(2)}, u32[]{:S(2)}) collective-permute-start(bf16[384,1024]{1,0:T(8,128)(2,1)S(1)} %shard_map.121), channel_id=1, source_target_pairs={{0,1},{1,0},{2,3},{3,2},{4,5},{5,4},{6,7},{7,6},{8,9},{9,8},{10,11... | collective-permute-start | bytes 2359304 | tf_op jit(solution)/shard_map/ppermute | solution.py:486
  38.3 11.4 %collective-permute-start.4 = (bf16[512,512]{1,0:T(8,128)(2,1)S(1)}, bf16[512,512]{1,0:T(8,128)(2,1)S(1)}, u32[]{:S(2)}, u32[]{:S(2)}) collective-permute-start(bf16[512,512]{1,0:T(8,128)(2,1)S(1)} %get-tuple-element.45), channel_id=1, source_target_pairs={{2,4},{3,5},{4,2},{5,3},{10,12},{11,13},{12,10},{13,11},{18,20},{1... | collective-permute-start | bytes 1572872 | tf_op jit(solution)/shard_map/ppermute | solution.py:472
  39.0 5.8 %copy-start.3 = (bf16[1,512,1024]{2,1,0:T(8,128)(2,1)S(1)}, bf16[1,512,1024]{2,1,0:T(8,128)(2,1)}, u32[]{:S(2)}) copy-start(bf16[1,512,1024]{2,1,0:T(8,128)(2,1)} %param.9) | copy-start | bytes 3145732
  39.0 14.9 %collective-permute-start.5 = (bf16[512,512]{1,0:T(8,128)(2,1)S(1)}, bf16[512,512]{1,0:T(8,128)(2,1)S(1)}, u32[]{:S(2)}, u32[]{:S(2)}) collective-permute-start(bf16[512,512]{1,0:T(8,128)(2,1)S(1)} %get-tuple-element.46.refs_7_), channel_id=1, source_target_pairs={{0,2},{1,3},{2,0},{3,1},{4,6},{5,7},{6,4},{7,5},{8,10},{9,11},{10,... | collective-permute-start | bytes 1572872 | tf_op jit(solution)/shard_map/ppermute | solution.py:472
  41.9 19.6 %collective-permute-start.8 = (bf16[512,512]{1,0:T(8,128)(2,1)S(1)}, bf16[512,512]{1,0:T(8,128)(2,1)S(1)}, u32[]{:S(2)}, u32[]{:S(2)}) collective-permute-start(bf16[512,512]{1,0:T(8,128)(2,1)S(1)} %get-tuple-element.51), channel_id=1, source_target_pairs={{2,4},{3,5},{4,2},{5,3},{10,12},{11,13},{12,10},{13,11},{18,20},{1... | collective-permute-start | bytes 1572872 | tf_op jit(solution)/shard_map/ppermute | solution.py:472
  42.6 22.6 %collective-permute-start.9 = (bf16[512,512]{1,0:T(8,128)(2,1)S(1)}, bf16[512,512]{1,0:T(8,128)(2,1)S(1)}, u32[]{:S(2)}, u32[]{:S(2)}) collective-permute-start(bf16[512,512]{1,0:T(8,128)(2,1)S(1)} %get-tuple-element.47.refs_8_), channel_id=1, source_target_pairs={{0,2},{1,3},{2,0},{3,1},{4,6},{5,7},{6,4},{7,5},{8,10},{9,11},{10,... | collective-permute-start | bytes 1572872 | tf_op jit(solution)/shard_map/ppermute | solution.py:472
  47.2 6.7 %copy-start.1 = (bf16[1,384,4096]{2,1,0:T(8,128)(2,1)S(1)}, bf16[1,384,4096]{2,1,0:T(8,128)(2,1)}, u32[]{:S(2)}) copy-start(bf16[1,384,4096]{2,1,0:T(8,128)(2,1)} %param.8) | copy-start | bytes 9437188
  55.4 12.6 %collective-permute-start.14 = (bf16[512,512]{1,0:T(8,128)(2,1)S(1)}, bf16[512,512]{1,0:T(8,128)(2,1)S(1)}, u32[]{:S(2)}, u32[]{:S(2)}) collective-permute-start(bf16[512,512]{1,0:T(8,128)(2,1)S(1)} %get-tuple-element.68), channel_id=1, source_target_pairs={{2,4},{3,5},{4,2},{5,3},{10,12},{11,13},{12,10},{13,11},{18,20},{1... | collective-permute-start | bytes 1572872 | tf_op jit(solution)/shard_map/ppermute | solution.py:472
  56.1 20.3 %collective-permute-start.7 = (bf16[512,512]{1,0:T(8,128)(2,1)S(1)}, bf16[512,512]{1,0:T(8,128)(2,1)S(1)}, u32[]{:S(2)}, u32[]{:S(2)}) collective-permute-start(bf16[512,512]{1,0:T(8,128)(2,1)S(1)} %get-tuple-element.50.refs_8_), channel_id=1, source_target_pairs={{0,2},{1,3},{2,0},{3,1},{4,6},{5,7},{6,4},{7,5},{8,10},{9,11},{10,... | collective-permute-start | bytes 1572872 | tf_op jit(solution)/shard_map/ppermute | solution.py:472
  60.9 29.5 %collective-permute-start.11 = (bf16[384,1024]{1,0:T(8,128)(2,1)S(1)}, bf16[384,1024]{1,0:T(8,128)(2,1)S(1)}, u32[]{:S(2)}, u32[]{:S(2)}) collective-permute-start(bf16[384,1024]{1,0:T(8,128)(2,1)S(1)} %shard_map.129), channel_id=1, source_target_pairs={{0,1},{1,0},{2,3},{3,2},{4,5},{5,4},{6,7},{7,6},{8,9},{9,8},{10,11... | collective-permute-start | bytes 2359304 | tf_op jit(solution)/shard_map/ppermute | solution.py:507
  66.7 21.0 %collective-permute-start.10 = (bf16[512,512]{1,0:T(8,128)(2,1)S(1)}, bf16[512,512]{1,0:T(8,128)(2,1)S(1)}, u32[]{:S(2)}, u32[]{:S(2)}) collective-permute-start(bf16[512,512]{1,0:T(8,128)(2,1)S(1)} %get-tuple-element.52.refs_9_), channel_id=1, source_target_pairs={{0,2},{1,3},{2,0},{3,1},{4,6},{5,7},{6,4},{7,5},{8,10},{9,11},{10,... | collective-permute-start | bytes 1572872 | tf_op jit(solution)/shard_map/ppermute | solution.py:472
  77.9 19.9 %collective-permute-start.16 = (bf16[512,512]{1,0:T(8,128)(2,1)S(1)}, bf16[512,512]{1,0:T(8,128)(2,1)S(1)}, u32[]{:S(2)}, u32[]{:S(2)}) collective-permute-start(bf16[512,512]{1,0:T(8,128)(2,1)S(1)} %get-tuple-element.70), channel_id=1, source_target_pairs={{2,4},{3,5},{4,2},{5,3},{10,12},{11,13},{12,10},{13,11},{18,20},{1... | collective-permute-start | bytes 1572872 | tf_op jit(solution)/shard_map/ppermute | solution.py:472
  78.6 19.2 %collective-permute-start.15 = (bf16[512,512]{1,0:T(8,128)(2,1)S(1)}, bf16[512,512]{1,0:T(8,128)(2,1)S(1)}, u32[]{:S(2)}, u32[]{:S(2)}) collective-permute-start(bf16[512,512]{1,0:T(8,128)(2,1)S(1)} %get-tuple-element.69.refs_9_), channel_id=1, source_target_pairs={{0,2},{1,3},{2,0},{3,1},{4,6},{5,7},{6,4},{7,5},{8,10},{9,11},{10,... | collective-permute-start | bytes 1572872 | tf_op jit(solution)/shard_map/ppermute | solution.py:472
  95.9 2.2 %copy-start.5 = (f32[1,512,1024]{2,1,0:T(8,128)S(1)}, f32[1,512,1024]{2,1,0:T(8,128)}, u32[]{:S(2)}) copy-start(f32[1,512,1024]{2,1,0:T(8,128)} %param.12) | copy-start | bytes 6291460
  101.2 9.2 %collective-permute-start.18 = (bf16[512,512]{1,0:T(8,128)(2,1)S(1)}, bf16[512,512]{1,0:T(8,128)(2,1)S(1)}, u32[]{:S(2)}, u32[]{:S(2)}) collective-permute-start(bf16[512,512]{1,0:T(8,128)(2,1)S(1)} %get-tuple-element.71.stepped_ref), channel_id=1, source_target_pairs={{0,16},{8,24},{16,0},{24,8},{1,17},{9,25},{17,1},{25,9},{2,18},{10... | collective-permute-start | bytes 1572872 | tf_op jit(solution)/shard_map/ppermute | solution.py:447
  102.7 16.0 %copy-start.7 = (s32[4]{0:T(128)S(1)}, s32[4]{0:T(128)}, u32[]{:S(2)}) copy-start(s32[4]{0:T(128)} %numerator_ref.3) | copy-start | bytes 52
  102.7 16.1 %copy-start.8 = (s32[4]{0:T(128)S(1)}, s32[4]{0:T(128)}, u32[]{:S(2)}) copy-start(s32[4]{0:T(128)} %partner_ref.3) | copy-start | bytes 52
  102.7 7.7 %collective-permute-start.20 = (bf16[512,512]{1,0:T(8,128)(2,1)S(1)}, bf16[512,512]{1,0:T(8,128)(2,1)S(1)}, u32[]{:S(2)}, u32[]{:S(2)}) collective-permute-start(bf16[512,512]{1,0:T(8,128)(2,1)S(1)} %get-tuple-element.75), channel_id=1, source_target_pairs={{2,4},{3,5},{4,2},{5,3},{10,12},{11,13},{12,10},{13,11},{18,20},{1... | collective-permute-start | bytes 1572872 | tf_op jit(solution)/shard_map/ppermute | solution.py:472
  103.5 15.2 %collective-permute-start.17 = (bf16[512,512]{1,0:T(8,128)(2,1)S(1)}, bf16[512,512]{1,0:T(8,128)(2,1)S(1)}, u32[]{:S(2)}, u32[]{:S(2)}) collective-permute-start(bf16[512,512]{1,0:T(8,128)(2,1)S(1)} %get-tuple-element.71.stepped_ref), channel_id=1, source_target_pairs={{0,8},{8,0},{16,24},{24,16},{1,9},{9,1},{17,25},{25,17},{2,10},{10... | collective-permute-start | bytes 1572872 | tf_op jit(solution)/shard_map/ppermute | solution.py:449
  110.4 8.4 %collective-permute-start.19 = (bf16[512,512]{1,0:T(8,128)(2,1)S(1)}, bf16[512,512]{1,0:T(8,128)(2,1)S(1)}, u32[]{:S(2)}, u32[]{:S(2)}) collective-permute-start(bf16[512,512]{1,0:T(8,128)(2,1)S(1)} %collective-permute-done.18.refs_1_), channel_id=1, source_target_pairs={{0,8},{8,0},{16,24},{24,16},{1,9},{9,1},{17,25},{25,17},{2,10},{10... | collective-permute-start | bytes 1572872 | tf_op jit(solution)/shard_map/ppermute | solution.py:449
  111.9 14.6 %collective-permute-start.21 = (bf16[512,512]{1,0:T(8,128)(2,1)S(1)}, bf16[512,512]{1,0:T(8,128)(2,1)S(1)}, u32[]{:S(2)}, u32[]{:S(2)}) collective-permute-start(bf16[512,512]{1,0:T(8,128)(2,1)S(1)} %get-tuple-element.76), channel_id=1, source_target_pairs={{0,2},{1,3},{2,0},{3,1},{4,6},{5,7},{6,4},{7,5},{8,10},{9,11},{10,... | collective-permute-start | bytes 1572872 | tf_op jit(solution)/shard_map/ppermute | solution.py:472
  117.5 9.1 %collective-permute-start.22 = (bf16[512,512]{1,0:T(8,128)(2,1)S(1)}, bf16[512,512]{1,0:T(8,128)(2,1)S(1)}, u32[]{:S(2)}, u32[]{:S(2)}) collective-permute-start(bf16[512,512]{1,0:T(8,128)(2,1)S(1)} %get-tuple-element.77), channel_id=1, source_target_pairs={{2,4},{3,5},{4,2},{5,3},{10,12},{11,13},{12,10},{13,11},{18,20},{1... | collective-permute-start | bytes 1572872 | tf_op jit(solution)/shard_map/ppermute | solution.py:472
  118.2 43.7 %collective-permute-start.12 = (bf16[384,1536]{1,0:T(8,128)(2,1)S(1)}, bf16[384,1536]{1,0:T(8,128)(2,1)S(1)}, u32[]{:S(2)}, u32[]{:S(2)}) collective-permute-start(bf16[384,1536]{1,0:T(8,128)(2,1)S(1)} %get-tuple-element.63.refs_0_.refs_3_), channel_id=1, source_target_pairs={{0,1},{1,0},{2,3},{3,2},{4,5},{5,4},{6,7},{7,6},{8,9},{9,8},{10,11... | collective-permute-start | bytes 3538952 | tf_op jit(solution)/shard_map/ppermute | solution.py:535
  129.6 10.9 %collective-permute-start.24 = (bf16[512,512]{1,0:T(8,128)(2,1)S(1)}, bf16[512,512]{1,0:T(8,128)(2,1)S(1)}, u32[]{:S(2)}, u32[]{:S(2)}) collective-permute-start(bf16[512,512]{1,0:T(8,128)(2,1)S(1)} %get-tuple-element.80.stepped_ref), channel_id=1, source_target_pairs={{0,16},{8,24},{16,0},{24,8},{1,17},{9,25},{17,1},{25,9},{2,18},{10... | collective-permute-start | bytes 1572872 | tf_op jit(solution)/shard_map/ppermute | solution.py:447
  131.7 27.9 %collective-permute-start.13 = (bf16[384,1024]{1,0:T(8,128)(2,1)S(1)}, bf16[384,1024]{1,0:T(8,128)(2,1)S(1)}, u32[]{:S(2)}, u32[]{:S(2)}) collective-permute-start(bf16[384,1024]{1,0:T(8,128)(2,1)S(1)} %shard_map.132), channel_id=1, source_target_pairs={{0,1},{1,0},{2,3},{3,2},{4,5},{5,4},{6,7},{7,6},{8,9},{9,8},{10,11... | collective-permute-start | bytes 2359304 | tf_op jit(solution)/shard_map/ppermute | solution.py:507
  132.3 31.2 %collective-permute-start.23 = (bf16[512,512]{1,0:T(8,128)(2,1)S(1)}, bf16[512,512]{1,0:T(8,128)(2,1)S(1)}, u32[]{:S(2)}, u32[]{:S(2)}) collective-permute-start(bf16[512,512]{1,0:T(8,128)(2,1)S(1)} %get-tuple-element.80.stepped_ref), channel_id=1, source_target_pairs={{0,8},{8,0},{16,24},{24,16},{1,9},{9,1},{17,25},{25,17},{2,10},{10... | collective-permute-start | bytes 1572872 | tf_op jit(solution)/shard_map/ppermute | solution.py:449
  140.6 23.0 %collective-permute-start.25 = (bf16[512,512]{1,0:T(8,128)(2,1)S(1)}, bf16[512,512]{1,0:T(8,128)(2,1)S(1)}, u32[]{:S(2)}, u32[]{:S(2)}) collective-permute-start(bf16[512,512]{1,0:T(8,128)(2,1)S(1)} %collective-permute-done.24.refs_1_), channel_id=1, source_target_pairs={{0,8},{8,0},{16,24},{24,16},{1,9},{9,1},{17,25},{25,17},{2,10},{10... | collective-permute-start | bytes 1572872 | tf_op jit(solution)/shard_map/ppermute | solution.py:449
  (3 other events, 5.0 us)

commit v9 on v8

--- a/solution.py
+++ b/solution.py
@@ -538,12 +538,12 @@
     moments, averaged, placed = None, None, None
     for h in range(CHUNKS):
         last = h == CHUNKS - 1
-        after = [] if h == 0 else [(tile, ANY)]
+        after = [] if h == 0 else [(placed_tile, ANY)]
         *moments, stepped = adam(
             row, h, got[depth, h], grad, weights, first, second, moments, after + [(parcel, ANY)]
         )
         if placed is None:
-            placed, tile = place(plan, row, xg, arrived, 0)
+            placed, placed_tile = place(plan, row, xg, arrived, 0)
         others = partner_rows(stepped, partner, row[plan["replica"]], n_rep)
         if last:
             views = [View(final, columns, rows)]

time: 167 us -> 128 us (0.77)
  waiting for transfers between devices: 80.3 us -> 41.9 us
    ppermute x2, waiting for transfers between devices: 19.1 us -> 0.01 us  [send_parts(): parcel = swap(pack(plan, row, rows, views, act, turns, after))]
    ppermute x14, waiting for transfers between devices: 24.1 us -> 5.75 us  [exchange(): lax.ppermute(bufs[name], 'fsdp', links[name])]
    ppermute x2, waiting for transfers between devices: 15 us -> 12.6 us  [partner_rows(): far = lax.ppermute(stepped, 'rep', [(r, r ^ 2) for r in range(4)])]
    ppermute x14, starting transfers between devices: 30.4 us -> 28.3 us  [exchange(): lax.ppermute(bufs[name], 'fsdp', links[name])]
  transfers between devices with their start and end apart: 26 -> 26, of which waited for: 9 -> 7; matrix products, arithmetic and copies ran while one was open for 0% -> 1% of each run, Pallas kernels for 23% -> 32%
where the time goes in v9:
time: 128 us
  Pallas kernels  42.1 us (33%)
  waiting for transfers between devices  41.9 us (33%)
  starting transfers between devices  38.9 us (30%)
  local copies, waits for them, and re-layouts  3.76 us (3%)
    pallas_call x23, Pallas kernels, call(): pl.pallas_call(kernel, grid_spec=pltpu.PrefetchScalarGridSpec(num_scalar_...  42.1 us
    ppermute x14, starting transfers between devices, exchange(): lax.ppermute(bufs[name], 'fsdp', links[name])  28.3 us
    ppermute x2, waiting for transfers between devices, send(): return swap(pack(plan, row, rows, [], act, turns, after))  23.5 us
    ppermute x2, waiting for transfers between devices, partner_rows(): far = lax.ppermute(stepped, 'rep', [(r, r ^ 2) for r in range(4)])  12.6 us
    ppermute x14, waiting for transfers between devices, exchange(): lax.ppermute(bufs[name], 'fsdp', links[name])  5.75 us
    unnamed x18, local copies, waits for them, and re-layouts  3.06 us
    ppermute x1, starting transfers between devices, per_device(): parcel = swap(cot)  3 us
  transfers between devices with their start and end apart: 26, of which 7 were waited for; matrix products, arithmetic and copies ran while one was open for 1% of the time, Pallas kernels for 32%

profile of v9, /device:TPU:0, one launch (start us, length us, event | category | flops | bytes accessed | tf_op | source)
XLA Modules:
  0.0 127.6 jit_solution(17008516136290283394)
XLA Ops:
  0.6 3.0 %collective-permute-start.3 = (bf16[384,1024]{1,0:T(8,128)(2,1)}, bf16[384,1024]{1,0:T(8,128)(2,1)S(1)}, u32[]{:S(2)}, u32[]{:S(2)}) collective-permute-start(bf16[384,1024]{1,0:T(8,128)(2,1)} %bitcast.33), channel_id=1, source_target_pairs={{0,1},{1,0},{2,3},{3,2},{4,5},{5,4},{6,7},{7,6},{8,9},{9,8},{10,11... | collective-permute-start | bytes 2359304 | tf_op jit(solution)/shard_map/ppermute | solution.py:488
  3.6 1.6 %collective-permute-start = (bf16[512,1024]{1,0:T(8,128)(2,1)}, bf16[512,1024]{1,0:T(8,128)(2,1)S(1)}, u32[]{:S(2)}, u32[]{:S(2)}) collective-permute-start(bf16[512,1024]{1,0:T(8,128)(2,1)} %bitcast.45), channel_id=1, source_target_pairs={{0,2},{1,3},{2,0},{3,1},{4,6},{5,7},{6,4},{7,5},{8,10},{9,11},{10,... | collective-permute-start | bytes 3145736 | tf_op jit(solution)/shard_map/ppermute | solution.py:472
  6.6 1.9 %copy-done = bf16[1,384,4096]{2,1,0:T(8,128)(2,1)S(1)} copy-done((bf16[1,384,4096]{2,1,0:T(8,128)(2,1)S(1)}, bf16[1,384,4096]{2,1,0:T(8,128)(2,1)}, u32[]{:S(2)}) %copy-start) | copy-done | bytes 3145752
  9.7 20.1 %collective-permute-done.2.refs_4_.refs_3_.refs_6_.refs_2_ = bf16[384,512]{1,0:T(8,128)(2,1)S(1)} collective-permute-done((bf16[384,512]{1,0:T(8,128)(2,1)S(1)}, bf16[384,512]{1,0:T(8,128)(2,1)S(1)}, u32[]{:S(2)}, u32[]{:S(2)}) %collective-permute-start.2) | collective-permute-done | bytes 393248 | tf_op jit(solution)/shard_map/ppermute | solution.py:486
  30.4 1.8 %collective-permute-start.6 = (bf16[384,1024]{1,0:T(8,128)(2,1)S(1)}, bf16[384,1024]{1,0:T(8,128)(2,1)S(1)}, u32[]{:S(2)}, u32[]{:S(2)}) collective-permute-start(bf16[384,1024]{1,0:T(8,128)(2,1)S(1)} %shard_map.121), channel_id=1, source_target_pairs={{0,1},{1,0},{2,3},{3,2},{4,5},{5,4},{6,7},{7,6},{8,9},{9,8},{10,11... | collective-permute-start | bytes 2359304 | tf_op jit(solution)/shard_map/ppermute | solution.py:486
  32.3 1.5 %shard_map.120 = (bf16[512,512]{1,0:T(8,128)(2,1)S(1)}, bf16[512,512]{1,0:T(8,128)(2,1)S(1)}) custom-call(s32[40]{0:T(128)S(1)} %dynamic-slice_bitcast_fusion.row_ref, bf16[512,1024]{1,0:T(8,128)(2,1)S(1)} %collective-permute-done.1.refs_0_.refs_1_, bf16[512,1024]{1,0:T(8,128)(2,1)S(1)} %collective-permute-done.refs_1_.refs_0_, ...), custom_call_target="tpu_custom_call" | custom-call | tf_op jit(solution)/shard_map/pallas_call | solution.py:86
  35.6 2.4 %shard_map.123 = (bf16[384,4096]{1,0:T(8,128)(2,1)}, bf16[384,512]{1,0:T(8,128)(2,1)S(1)}, bf16[512,1024]{1,0:T(8,128)(2,1)S(1)}) custom-call(s32[40]{0:T(128)S(1)} %dynamic-slice_bitcast_fusion.row_ref, bf16[512,1024]{1,0:T(8,128)(2,1)S(1)} %bitcast.47, ...), custom_call_target="tpu_custom_call" | custom-call | tf_op jit(solution)/shard_map/pallas_call | solution.py:86
  38.0 1.5 %shard_map.122 = (bf16[512,512]{1,0:T(8,128)(2,1)S(1)}, bf16[512,512]{1,0:T(8,128)(2,1)S(1)}) custom-call(s32[40]{0:T(128)S(1)} %dynamic-slice_bitcast_fusion.row_ref, bf16[512,1024]{1,0:T(8,128)(2,1)S(1)} %collective-permute-done.1.refs_0_.refs_1_, bf16[512,1024]{1,0:T(8,128)(2,1)S(1)} %collective-permute-done.refs_1_.refs_0_, ...), custom_call_target="tpu_custom_call" | custom-call | tf_op jit(solution)/shard_map/pallas_call | solution.py:86
  40.3 5.5 %collective-permute-start.9 = (bf16[512,512]{1,0:T(8,128)(2,1)S(1)}, bf16[512,512]{1,0:T(8,128)(2,1)S(1)}, u32[]{:S(2)}, u32[]{:S(2)}) collective-permute-start(bf16[512,512]{1,0:T(8,128)(2,1)S(1)} %get-tuple-element.48.refs_8_), channel_id=1, source_target_pairs={{0,2},{1,3},{2,0},{3,1},{4,6},{5,7},{6,4},{7,5},{8,10},{9,11},{10,... | collective-permute-start | bytes 1572872 | tf_op jit(solution)/shard_map/ppermute | solution.py:472
  45.8 3.4 %collective-permute-done.6.refs_5_.refs_2_.refs_7_.refs_8_.refs_3_.refs_4_.refs_6_ = bf16[384,1024]{1,0:T(8,128)(2,1)S(1)} collective-permute-done((bf16[384,1024]{1,0:T(8,128)(2,1)S(1)}, bf16[384,1024]{1,0:T(8,128)(2,1)S(1)}, u32[]{:S(2)}, u32[]{:S(2)}) %collective-permute-start.6) | collective-permute-done | bytes 786464 | tf_op jit(solution)/shard_map/ppermute | solution.py:486
  51.3 2.4 %shard_map.124 = (bf16[384,4096]{1,0:T(8,128)(2,1)}, bf16[384,512]{1,0:T(8,128)(2,1)S(1)}, bf16[512,1024]{1,0:T(8,128)(2,1)S(1)}) custom-call(s32[40]{0:T(128)S(1)} %dynamic-slice_bitcast_fusion.row_ref, bf16[512,1024]{1,0:T(8,128)(2,1)S(1)} %collective-permute-done.refs_1_.refs_0_, ...), custom_call_target="tpu_custom_call", output_to_operand_aliasing={{0}: (6, {})} | custom-call | tf_op jit(solution)/shard_map/pallas_call | solution.py:86
  56.0 4.4 %collective-permute-start.7 = (bf16[512,512]{1,0:T(8,128)(2,1)S(1)}, bf16[512,512]{1,0:T(8,128)(2,1)S(1)}, u32[]{:S(2)}, u32[]{:S(2)}) collective-permute-start(bf16[512,512]{1,0:T(8,128)(2,1)S(1)} %get-tuple-element.51.refs_8_), channel_id=1, source_target_pairs={{0,2},{1,3},{2,0},{3,1},{4,6},{5,7},{6,4},{7,5},{8,10},{9,11},{10,... | collective-permute-start | bytes 1572872 | tf_op jit(solution)/shard_map/ppermute | solution.py:472
  61.9 4.2 %collective-permute-start.10 = (bf16[512,512]{1,0:T(8,128)(2,1)S(1)}, bf16[512,512]{1,0:T(8,128)(2,1)S(1)}, u32[]{:S(2)}, u32[]{:S(2)}) collective-permute-start(bf16[512,512]{1,0:T(8,128)(2,1)S(1)} %get-tuple-element.53.refs_9_), channel_id=1, source_target_pairs={{0,2},{1,3},{2,0},{3,1},{4,6},{5,7},{6,4},{7,5},{8,10},{9,11},{10,... | collective-permute-start | bytes 1572872 | tf_op jit(solution)/shard_map/ppermute | solution.py:472
  66.8 2.5 %shard_map.127 = (bf16[384,4096]{1,0:T(8,128)(2,1)}, bf16[384,512]{1,0:T(8,128)(2,1)S(1)}, bf16[512,1024]{1,0:T(8,128)(2,1)S(1)}) custom-call(s32[40]{0:T(128)S(1)} %dynamic-slice_bitcast_fusion.row_ref, bf16[512,512]{1,0:T(8,128)(2,1)S(1)} %collective-permute-done.5.refs_1_.refs_0_, ...), custom_call_target="tpu_custom_call", output_to_operand_aliasing={{0}: (8, {})} | custom-call | tf_op jit(solution)/shard_map/pallas_call | solution.py:86
  70.6 2.7 %collective-permute-done.7.refs_1_ = bf16[512,512]{1,0:T(8,128)(2,1)S(1)} collective-permute-done((bf16[512,512]{1,0:T(8,128)(2,1)S(1)}, bf16[512,512]{1,0:T(8,128)(2,1)S(1)}, u32[]{:S(2)}, u32[]{:S(2)}) %collective-permute-start.7) | collective-permute-done | bytes 524320 | tf_op jit(solution)/shard_map/ppermute | solution.py:472
  74.8 3.3 %collective-permute-start.15 = (bf16[512,512]{1,0:T(8,128)(2,1)S(1)}, bf16[512,512]{1,0:T(8,128)(2,1)S(1)}, u32[]{:S(2)}, u32[]{:S(2)}) collective-permute-start(bf16[512,512]{1,0:T(8,128)(2,1)S(1)} %get-tuple-element.70.refs_9_), channel_id=1, source_target_pairs={{0,2},{1,3},{2,0},{3,1},{4,6},{5,7},{6,4},{7,5},{8,10},{9,11},{10,... | collective-permute-start | bytes 1572872 | tf_op jit(solution)/shard_map/ppermute | solution.py:472
  78.8 3.9 %shard_map.130 = (f32[384,1024]{1,0:T(8,128)S(1)}, f32[384,1024]{1,0:T(8,128)S(1)}) custom-call(s32[40]{0:T(128)S(1)} %dynamic-slice_bitcast_fusion.row_ref, bf16[512,1024]{1,0:T(8,128)(2,1)S(1)} %get-tuple-element.58.refs_0_, bf16[512,1024]{1,0:T(8,128)(2,1)S(1)} %get-tuple-element.59.refs_1_, bf16[512,1024]{1,0:T(8,128)(2,1)S(1)} %get-tuple-element.60.refs_2_, ...), custom_call_target="tpu_custom_call" | custom-call | tf_op jit(solution)/shard_map/pallas_call | solution.py:86
  82.7 1.8 %collective-permute-done.10.refs_2_.refs_1_ = bf16[512,512]{1,0:T(8,128)(2,1)S(1)} collective-permute-done((bf16[512,512]{1,0:T(8,128)(2,1)S(1)}, bf16[512,512]{1,0:T(8,128)(2,1)S(1)}, u32[]{:S(2)}, u32[]{:S(2)}) %collective-permute-start.10) | collective-permute-done | bytes 524320 | tf_op jit(solution)/shard_map/ppermute | solution.py:472
  84.5 1.5 %shard_map.139 = (bf16[512,512]{1,0:T(8,128)(2,1)S(1)}, bf16[512,512]{1,0:T(8,128)(2,1)S(1)}) custom-call(s32[40]{0:T(128)S(1)} %dynamic-slice_bitcast_fusion.row_ref, bf16[512,512]{1,0:T(8,128)(2,1)S(1)} %collective-permute-done.20.refs_0_, bf16[512,512]{1,0:T(8,128)(2,1)S(1)} %collective-permute-done.10.refs_2_.refs_1_, bf16[384,4096]{1,0:T(8,128)(2,1)S(1)} %bitcast.29, ...), custom_call_target="tpu_custom_call" | custom-call | tf_op jit(solution)/shard_map/pallas_call | solution.py:86
  86.0 3.3 %collective-permute-start.21 = (bf16[512,512]{1,0:T(8,128)(2,1)S(1)}, bf16[512,512]{1,0:T(8,128)(2,1)S(1)}, u32[]{:S(2)}, u32[]{:S(2)}) collective-permute-start(bf16[512,512]{1,0:T(8,128)(2,1)S(1)} %get-tuple-element.77), channel_id=1, source_target_pairs={{0,2},{1,3},{2,0},{3,1},{4,6},{5,7},{6,4},{7,5},{8,10},{9,11},{10,... | collective-permute-start | bytes 1572872 | tf_op jit(solution)/shard_map/ppermute | solution.py:472
  90.0 2.5 %shard_map.128 = (bf16[384,4096]{1,0:T(8,128)(2,1)}, bf16[384,512]{1,0:T(8,128)(2,1)S(1)}, bf16[512,1024]{1,0:T(8,128)(2,1)S(1)}) custom-call(s32[40]{0:T(128)S(1)} %dynamic-slice_bitcast_fusion.row_ref, bf16[512,1024]{1,0:T(8,128)(2,1)S(1)} %collective-permute-done.refs_1_.refs_0_, ...), custom_call_target="tpu_custom_call", output_to_operand_aliasing={{0}: (7, {})} | custom-call | tf_op jit(solution)/shard_map/pallas_call | solution.py:86
  92.6 1.9 %shard_map.131 = (f32[384,1024]{1,0:T(8,128)S(1)}, bf16[384,1536]{1,0:T(8,128)(2,1)S(1)}) custom-call(s32[40]{0:T(128)S(1)} %dynamic-slice_bitcast_fusion.row_ref, bf16[512,1024]{1,0:T(8,128)(2,1)S(1)} %get-tuple-element.56.refs_0_, bf16[384,4096]{1,0:T(8,128)(2,1)S(1)} %bitcast.31, ...), custom_call_target="tpu_custom_call" | custom-call | tf_op jit(solution)/shard_map/pallas_call | solution.py:86
  96.3 1.8 %shard_map.135.grad_ref = f32[512,1024]{1,0:T(8,128)S(1)} custom-call(s32[40]{0:T(128)S(1)} %dynamic-slice_bitcast_fusion.row_ref, bf16[384,4096]{1,0:T(8,128)(2,1)S(1)} %bitcast.32, bf16[384,1024]{1,0:T(8,128)(2,1)S(1)} %collective-permute-done.11.refs_9_.refs_5_.refs_2_.refs_0_.piece_ref, bf16[384,1024]{1,0:T(8,128)(2,1)S(1)} %bitcast.44, ...), custom_call_target="tpu_custom_call" | custom-call | tf_op jit(solution)/shard_map/pallas_call | solution.py:86
  98.1 3.1 %shard_map.136 = (f32[512,1024]{1,0:T(8,128)}, f32[512,1024]{1,0:T(8,128)}, bf16[512,512]{1,0:T(8,128)(2,1)S(1)}) custom-call(s32[40]{0:T(128)S(1)} %dynamic-slice_bitcast_fusion.row_ref, bf16[512,512]{1,0:T(8,128)(2,1)S(1)} %collective-permute-done.15.up_ref, bf16[512,512]{1,0:T(8,128)(2,1)S(1)} %collective-permute-done.16.dn_ref, ...), custom_call_target="tpu_custom_call" | custom-call | tf_op jit(solution)/shard_map/pallas_call | solution.py:86
  101.2 1.5 %collective-permute-start.18 = (bf16[512,512]{1,0:T(8,128)(2,1)S(1)}, bf16[512,512]{1,0:T(8,128)(2,1)S(1)}, u32[]{:S(2)}, u32[]{:S(2)}) collective-permute-start(bf16[512,512]{1,0:T(8,128)(2,1)S(1)} %get-tuple-element.72.stepped_ref), channel_id=1, source_target_pairs={{0,16},{8,24},{16,0},{24,8},{1,17},{9,25},{17,1},{25,9},{2,18},{10... | collective-permute-start | bytes 1572872 | tf_op jit(solution)/shard_map/ppermute | solution.py:447
  102.7 2.2 %shard_map.133 = (bf16[384,4096]{1,0:T(8,128)(2,1)}, f32[8,128]{1,0:T(8,128)S(1)}) custom-call(s32[40]{0:T(128)S(1)} %dynamic-slice_bitcast_fusion.row_ref, bf16[384,1024]{1,0:T(8,128)(2,1)S(1)} %collective-permute-done.11.refs_9_.refs_5_.refs_2_.refs_0_.piece_ref, ...), custom_call_target="tpu_custom_call", output_to_operand_aliasing={{0}: (4, {})} | custom-call | tf_op jit(solution)/shard_map/pallas_call | solution.py:86
  104.9 3.1 %shard_map.140 = (f32[512,1024]{1,0:T(8,128)}, f32[512,1024]{1,0:T(8,128)}, bf16[512,512]{1,0:T(8,128)(2,1)S(1)}) custom-call(s32[40]{0:T(128)S(1)} %dynamic-slice_bitcast_fusion.row_ref, bf16[512,512]{1,0:T(8,128)(2,1)S(1)} %collective-permute-done.21.up_ref, ...), custom_call_target="tpu_custom_call", output_to_operand_aliasing={{0}: (7, {}), {1}: (8, {})} | custom-call | tf_op jit(solution)/shard_map/pallas_call | solution.py:86
  108.5 6.0 %collective-permute-done.18.refs_1_ = bf16[512,512]{1,0:T(8,128)(2,1)S(1)} collective-permute-done((bf16[512,512]{1,0:T(8,128)(2,1)S(1)}, bf16[512,512]{1,0:T(8,128)(2,1)S(1)}, u32[]{:S(2)}, u32[]{:S(2)}) %collective-permute-start.18) | collective-permute-done | bytes 524320 | tf_op jit(solution)/shard_map/ppermute | solution.py:447
  115.0 6.6 %collective-permute-done.24.refs_1_ = bf16[512,512]{1,0:T(8,128)(2,1)S(1)} collective-permute-done((bf16[512,512]{1,0:T(8,128)(2,1)S(1)}, bf16[512,512]{1,0:T(8,128)(2,1)S(1)}, u32[]{:S(2)}, u32[]{:S(2)}) %collective-permute-start.24) | collective-permute-done | bytes 524320 | tf_op jit(solution)/shard_map/ppermute | solution.py:447
  121.6 1.5 %shard_map.137 = (bf16[512,1024]{1,0:T(8,128)(2,1)}, f32[8,128]{1,0:T(8,128)S(1)}) custom-call(s32[40]{0:T(128)S(1)} %dynamic-slice_bitcast_fusion.row_ref, s32[4]{0:T(128)S(1)} %copy-done.7, s32[4]{0:T(128)S(1)} %copy-done.8, bf16[512,512]{1,0:T(8,128)(2,1)S(1)} %get-tuple-element.72.stepped_ref, bf16[512,512]{1,0:T(8,128)(2,1)S(1)} %collective-permute-done.17.refs_0_, ...), custom_call_target="tpu_custom_call" | custom-call | tf_op jit(solution)/shard_map/pallas_call | solution.py:86
  123.2 1.7 %shard_map.138 = (bf16[384,4096]{1,0:T(8,128)(2,1)}, bf16[384,1024]{1,0:T(8,128)(2,1)}) custom-call(s32[40]{0:T(128)S(1)} %dynamic-slice_bitcast_fusion.row_ref, bf16[384,1536]{1,0:T(8,128)(2,1)S(1)} %collective-permute-done.12.refs_0_.refs_2_, f32[384,1024]{1,0:T(8,128)S(1)} %get-tuple-element.65.refs_1_, ...), custom_call_target="tpu_custom_call", output_to_operand_aliasing={{0}: (4, {})} | custom-call | tf_op jit(solution)/shard_map/pallas_call | solution.py:86
  126.0 1.5 %shard_map.141 = (bf16[512,1024]{1,0:T(8,128)(2,1)}, f32[8,128]{1,0:T(8,128)}) custom-call(s32[40]{0:T(128)S(1)} %dynamic-slice_bitcast_fusion.row_ref, s32[4]{0:T(128)S(1)} %copy-done.7, s32[4]{0:T(128)S(1)} %copy-done.8, bf16[512,512]{1,0:T(8,128)(2,1)S(1)} %get-tuple-element.82.stepped_ref, ...), custom_call_target="tpu_custom_call", output_to_operand_aliasing={{0}: (7, {})} | custom-call | tf_op jit(solution)/shard_map/pallas_call | solution.py:86
  (62 shorter events, 20.1 us)
Async XLA Ops:
  0.6 29.2 %collective-permute-start.3 = (bf16[384,1024]{1,0:T(8,128)(2,1)}, bf16[384,1024]{1,0:T(8,128)(2,1)S(1)}, u32[]{:S(2)}, u32[]{:S(2)}) collective-permute-start(bf16[384,1024]{1,0:T(8,128)(2,1)} %bitcast.33), channel_id=1, source_target_pairs={{0,1},{1,0},{2,3},{3,2},{4,5},{5,4},{6,7},{7,6},{8,9},{9,8},{10,11... | collective-permute-start | bytes 2359304 | tf_op jit(solution)/shard_map/ppermute | solution.py:488
  3.6 28.6 %collective-permute-start = (bf16[512,1024]{1,0:T(8,128)(2,1)}, bf16[512,1024]{1,0:T(8,128)(2,1)S(1)}, u32[]{:S(2)}, u32[]{:S(2)}) collective-permute-start(bf16[512,1024]{1,0:T(8,128)(2,1)} %bitcast.45), channel_id=1, source_target_pairs={{0,2},{1,3},{2,0},{3,1},{4,6},{5,7},{6,4},{7,5},{8,10},{9,11},{10,... | collective-permute-start | bytes 3145736 | tf_op jit(solution)/shard_map/ppermute | solution.py:472
  5.2 27.0 %collective-permute-start.1 = (bf16[512,1024]{1,0:T(8,128)(2,1)}, bf16[512,1024]{1,0:T(8,128)(2,1)S(1)}, u32[]{:S(2)}, u32[]{:S(2)}) collective-permute-start(bf16[512,1024]{1,0:T(8,128)(2,1)} %bitcast.46), channel_id=1, source_target_pairs={{2,4},{3,5},{4,2},{5,3},{10,12},{11,13},{12,10},{13,11},{18,20},{1... | collective-permute-start | bytes 3145736 | tf_op jit(solution)/shard_map/ppermute | solution.py:472
  9.1 23.1 %copy-start.2 = (bf16[1,384,1024]{2,1,0:T(8,128)(2,1)S(1)}, bf16[1,384,1024]{2,1,0:T(8,128)(2,1)}, u32[]{:S(2)}) copy-start(bf16[1,384,1024]{2,1,0:T(8,128)(2,1)} %param.10) | copy-start | bytes 2359300
  9.1 20.7 %collective-permute-start.2 = (bf16[384,512]{1,0:T(8,128)(2,1)S(1)}, bf16[384,512]{1,0:T(8,128)(2,1)S(1)}, u32[]{:S(2)}, u32[]{:S(2)}) collective-permute-start(bf16[384,512]{1,0:T(8,128)(2,1)S(1)} %shard_map.119), channel_id=1, source_target_pairs={{0,1},{1,0},{2,3},{3,2},{4,5},{5,4},{6,7},{7,6},{8,9},{9,8},{10,11... | collective-permute-start | bytes 1179656 | tf_op jit(solution)/shard_map/ppermute | solution.py:486
  30.4 5.1 %copy-start.3 = (bf16[1,512,1024]{2,1,0:T(8,128)(2,1)S(1)}, bf16[1,512,1024]{2,1,0:T(8,128)(2,1)}, u32[]{:S(2)}) copy-start(bf16[1,512,1024]{2,1,0:T(8,128)(2,1)} %param.9) | copy-start | bytes 3145732
  30.4 18.8 %collective-permute-start.6 = (bf16[384,1024]{1,0:T(8,128)(2,1)S(1)}, bf16[384,1024]{1,0:T(8,128)(2,1)S(1)}, u32[]{:S(2)}, u32[]{:S(2)}) collective-permute-start(bf16[384,1024]{1,0:T(8,128)(2,1)S(1)} %shard_map.121), channel_id=1, source_target_pairs={{0,1},{1,0},{2,3},{3,2},{4,5},{5,4},{6,7},{7,6},{8,9},{9,8},{10,11... | collective-permute-start | bytes 2359304 | tf_op jit(solution)/shard_map/ppermute | solution.py:486
  33.8 4.2 %copy-start.1 = (bf16[1,384,4096]{2,1,0:T(8,128)(2,1)S(1)}, bf16[1,384,4096]{2,1,0:T(8,128)(2,1)}, u32[]{:S(2)}) copy-start(bf16[1,384,4096]{2,1,0:T(8,128)(2,1)} %param.8) | copy-start | bytes 9437188
  33.8 20.0 %collective-permute-start.5 = (bf16[512,512]{1,0:T(8,128)(2,1)S(1)}, bf16[512,512]{1,0:T(8,128)(2,1)S(1)}, u32[]{:S(2)}, u32[]{:S(2)}) collective-permute-start(bf16[512,512]{1,0:T(8,128)(2,1)S(1)} %get-tuple-element.47.refs_7_), channel_id=1, source_target_pairs={{0,2},{1,3},{2,0},{3,1},{4,6},{5,7},{6,4},{7,5},{8,10},{9,11},{10,... | collective-permute-start | bytes 1572872 | tf_op jit(solution)/shard_map/ppermute | solution.py:472
  34.7 19.1 %collective-permute-start.4 = (bf16[512,512]{1,0:T(8,128)(2,1)S(1)}, bf16[512,512]{1,0:T(8,128)(2,1)S(1)}, u32[]{:S(2)}, u32[]{:S(2)}) collective-permute-start(bf16[512,512]{1,0:T(8,128)(2,1)S(1)} %get-tuple-element.46), channel_id=1, source_target_pairs={{2,4},{3,5},{4,2},{5,3},{10,12},{11,13},{12,10},{13,11},{18,20},{1... | collective-permute-start | bytes 1572872 | tf_op jit(solution)/shard_map/ppermute | solution.py:472
  39.6 20.9 %collective-permute-start.8 = (bf16[512,512]{1,0:T(8,128)(2,1)S(1)}, bf16[512,512]{1,0:T(8,128)(2,1)S(1)}, u32[]{:S(2)}, u32[]{:S(2)}) collective-permute-start(bf16[512,512]{1,0:T(8,128)(2,1)S(1)} %get-tuple-element.52), channel_id=1, source_target_pairs={{2,4},{3,5},{4,2},{5,3},{10,12},{11,13},{12,10},{13,11},{18,20},{1... | collective-permute-start | bytes 1572872 | tf_op jit(solution)/shard_map/ppermute | solution.py:472
  40.3 20.2 %collective-permute-start.9 = (bf16[512,512]{1,0:T(8,128)(2,1)S(1)}, bf16[512,512]{1,0:T(8,128)(2,1)S(1)}, u32[]{:S(2)}, u32[]{:S(2)}) collective-permute-start(bf16[512,512]{1,0:T(8,128)(2,1)S(1)} %get-tuple-element.48.refs_8_), channel_id=1, source_target_pairs={{0,2},{1,3},{2,0},{3,1},{4,6},{5,7},{6,4},{7,5},{8,10},{9,11},{10,... | collective-permute-start | bytes 1572872 | tf_op jit(solution)/shard_map/ppermute | solution.py:472
  49.8 19.5 %collective-permute-start.11 = (bf16[384,1024]{1,0:T(8,128)(2,1)S(1)}, bf16[384,1024]{1,0:T(8,128)(2,1)S(1)}, u32[]{:S(2)}, u32[]{:S(2)}) collective-permute-start(bf16[384,1024]{1,0:T(8,128)(2,1)S(1)} %shard_map.129), channel_id=1, source_target_pairs={{0,1},{1,0},{2,3},{3,2},{4,5},{5,4},{6,7},{7,6},{8,9},{9,8},{10,11... | collective-permute-start | bytes 2359304 | tf_op jit(solution)/shard_map/ppermute | solution.py:507
  55.3 15.3 %collective-permute-start.14 = (bf16[512,512]{1,0:T(8,128)(2,1)S(1)}, bf16[512,512]{1,0:T(8,128)(2,1)S(1)}, u32[]{:S(2)}, u32[]{:S(2)}) collective-permute-start(bf16[512,512]{1,0:T(8,128)(2,1)S(1)} %get-tuple-element.69), channel_id=1, source_target_pairs={{2,4},{3,5},{4,2},{5,3},{10,12},{11,13},{12,10},{13,11},{18,20},{1... | collective-permute-start | bytes 1572872 | tf_op jit(solution)/shard_map/ppermute | solution.py:472
  56.0 17.3 %collective-permute-start.7 = (bf16[512,512]{1,0:T(8,128)(2,1)S(1)}, bf16[512,512]{1,0:T(8,128)(2,1)S(1)}, u32[]{:S(2)}, u32[]{:S(2)}) collective-permute-start(bf16[512,512]{1,0:T(8,128)(2,1)S(1)} %get-tuple-element.51.refs_8_), channel_id=1, source_target_pairs={{0,2},{1,3},{2,0},{3,1},{4,6},{5,7},{6,4},{7,5},{8,10},{9,11},{10,... | collective-permute-start | bytes 1572872 | tf_op jit(solution)/shard_map/ppermute | solution.py:472
  61.9 22.6 %collective-permute-start.10 = (bf16[512,512]{1,0:T(8,128)(2,1)S(1)}, bf16[512,512]{1,0:T(8,128)(2,1)S(1)}, u32[]{:S(2)}, u32[]{:S(2)}) collective-permute-start(bf16[512,512]{1,0:T(8,128)(2,1)S(1)} %get-tuple-element.53.refs_9_), channel_id=1, source_target_pairs={{0,2},{1,3},{2,0},{3,1},{4,6},{5,7},{6,4},{7,5},{8,10},{9,11},{10,... | collective-permute-start | bytes 1572872 | tf_op jit(solution)/shard_map/ppermute | solution.py:472
  66.1 18.4 %collective-permute-start.20 = (bf16[512,512]{1,0:T(8,128)(2,1)S(1)}, bf16[512,512]{1,0:T(8,128)(2,1)S(1)}, u32[]{:S(2)}, u32[]{:S(2)}) collective-permute-start(bf16[512,512]{1,0:T(8,128)(2,1)S(1)} %get-tuple-element.76), channel_id=1, source_target_pairs={{2,4},{3,5},{4,2},{5,3},{10,12},{11,13},{12,10},{13,11},{18,20},{1... | collective-permute-start | bytes 1572872 | tf_op jit(solution)/shard_map/ppermute | solution.py:472
  70.0 32.7 %collective-permute-start.13 = (bf16[384,1024]{1,0:T(8,128)(2,1)S(1)}, bf16[384,1024]{1,0:T(8,128)(2,1)S(1)}, u32[]{:S(2)}, u32[]{:S(2)}) collective-permute-start(bf16[384,1024]{1,0:T(8,128)(2,1)S(1)} %shard_map.132), channel_id=1, source_target_pairs={{0,1},{1,0},{2,3},{3,2},{4,5},{5,4},{6,7},{7,6},{8,9},{9,8},{10,11... | collective-permute-start | bytes 2359304 | tf_op jit(solution)/shard_map/ppermute | solution.py:507
  74.8 21.0 %collective-permute-start.15 = (bf16[512,512]{1,0:T(8,128)(2,1)S(1)}, bf16[512,512]{1,0:T(8,128)(2,1)S(1)}, u32[]{:S(2)}, u32[]{:S(2)}) collective-permute-start(bf16[512,512]{1,0:T(8,128)(2,1)S(1)} %get-tuple-element.70.refs_9_), channel_id=1, source_target_pairs={{0,2},{1,3},{2,0},{3,1},{4,6},{5,7},{6,4},{7,5},{8,10},{9,11},{10,... | collective-permute-start | bytes 1572872 | tf_op jit(solution)/shard_map/ppermute | solution.py:472
  78.1 20.0 %collective-permute-start.16 = (bf16[512,512]{1,0:T(8,128)(2,1)S(1)}, bf16[512,512]{1,0:T(8,128)(2,1)S(1)}, u32[]{:S(2)}, u32[]{:S(2)}) collective-permute-start(bf16[512,512]{1,0:T(8,128)(2,1)S(1)} %get-tuple-element.71), channel_id=1, source_target_pairs={{2,4},{3,5},{4,2},{5,3},{10,12},{11,13},{12,10},{13,11},{18,20},{1... | collective-permute-start | bytes 1572872 | tf_op jit(solution)/shard_map/ppermute | solution.py:472
  86.0 18.9 %collective-permute-start.21 = (bf16[512,512]{1,0:T(8,128)(2,1)S(1)}, bf16[512,512]{1,0:T(8,128)(2,1)S(1)}, u32[]{:S(2)}, u32[]{:S(2)}) collective-permute-start(bf16[512,512]{1,0:T(8,128)(2,1)S(1)} %get-tuple-element.77), channel_id=1, source_target_pairs={{0,2},{1,3},{2,0},{3,1},{4,6},{5,7},{6,4},{7,5},{8,10},{9,11},{10,... | collective-permute-start | bytes 1572872 | tf_op jit(solution)/shard_map/ppermute | solution.py:472
  89.3 15.6 %collective-permute-start.22 = (bf16[512,512]{1,0:T(8,128)(2,1)S(1)}, bf16[512,512]{1,0:T(8,128)(2,1)S(1)}, u32[]{:S(2)}, u32[]{:S(2)}) collective-permute-start(bf16[512,512]{1,0:T(8,128)(2,1)S(1)} %get-tuple-element.78), channel_id=1, source_target_pairs={{2,4},{3,5},{4,2},{5,3},{10,12},{11,13},{12,10},{13,11},{18,20},{1... | collective-permute-start | bytes 1572872 | tf_op jit(solution)/shard_map/ppermute | solution.py:472
  95.7 2.4 %copy-start.5 = (f32[1,512,1024]{2,1,0:T(8,128)S(1)}, f32[1,512,1024]{2,1,0:T(8,128)}, u32[]{:S(2)}) copy-start(f32[1,512,1024]{2,1,0:T(8,128)} %param.12) | copy-start | bytes 6291460
  95.7 27.4 %collective-permute-start.12 = (bf16[384,1536]{1,0:T(8,128)(2,1)S(1)}, bf16[384,1536]{1,0:T(8,128)(2,1)S(1)}, u32[]{:S(2)}, u32[]{:S(2)}) collective-permute-start(bf16[384,1536]{1,0:T(8,128)(2,1)S(1)} %get-tuple-element.64.refs_0_.refs_3_), channel_id=1, source_target_pairs={{0,1},{1,0},{2,3},{3,2},{4,5},{5,4},{6,7},{7,6},{8,9},{9,8},{10,11... | collective-permute-start | bytes 3538952 | tf_op jit(solution)/shard_map/ppermute | solution.py:535
  101.2 13.3 %collective-permute-start.18 = (bf16[512,512]{1,0:T(8,128)(2,1)S(1)}, bf16[512,512]{1,0:T(8,128)(2,1)S(1)}, u32[]{:S(2)}, u32[]{:S(2)}) collective-permute-start(bf16[512,512]{1,0:T(8,128)(2,1)S(1)} %get-tuple-element.72.stepped_ref), channel_id=1, source_target_pairs={{0,16},{8,24},{16,0},{24,8},{1,17},{9,25},{17,1},{25,9},{2,18},{10... | collective-permute-start | bytes 1572872 | tf_op jit(solution)/shard_map/ppermute | solution.py:447
  104.9 16.7 %copy-start.7 = (s32[4]{0:T(128)S(1)}, s32[4]{0:T(128)}, u32[]{:S(2)}) copy-start(s32[4]{0:T(128)} %numerator_ref.3) | copy-start | bytes 52
  104.9 16.7 %copy-start.8 = (s32[4]{0:T(128)S(1)}, s32[4]{0:T(128)}, u32[]{:S(2)}) copy-start(s32[4]{0:T(128)} %partner_ref.3) | copy-start | bytes 52
  108.0 13.6 %collective-permute-start.24 = (bf16[512,512]{1,0:T(8,128)(2,1)S(1)}, bf16[512,512]{1,0:T(8,128)(2,1)S(1)}, u32[]{:S(2)}, u32[]{:S(2)}) collective-permute-start(bf16[512,512]{1,0:T(8,128)(2,1)S(1)} %get-tuple-element.82.stepped_ref), channel_id=1, source_target_pairs={{0,16},{8,24},{16,0},{24,8},{1,17},{9,25},{17,1},{25,9},{2,18},{10... | collective-permute-start | bytes 1572872 | tf_op jit(solution)/shard_map/ppermute | solution.py:447
  108.5 13.1 %collective-permute-start.17 = (bf16[512,512]{1,0:T(8,128)(2,1)S(1)}, bf16[512,512]{1,0:T(8,128)(2,1)S(1)}, u32[]{:S(2)}, u32[]{:S(2)}) collective-permute-start(bf16[512,512]{1,0:T(8,128)(2,1)S(1)} %get-tuple-element.72.stepped_ref), channel_id=1, source_target_pairs={{0,8},{8,0},{16,24},{24,16},{1,9},{9,1},{17,25},{25,17},{2,10},{10... | collective-permute-start | bytes 1572872 | tf_op jit(solution)/shard_map/ppermute | solution.py:449
  114.5 7.1 %collective-permute-start.19 = (bf16[512,512]{1,0:T(8,128)(2,1)S(1)}, bf16[512,512]{1,0:T(8,128)(2,1)S(1)}, u32[]{:S(2)}, u32[]{:S(2)}) collective-permute-start(bf16[512,512]{1,0:T(8,128)(2,1)S(1)} %collective-permute-done.18.refs_1_), channel_id=1, source_target_pairs={{0,8},{8,0},{16,24},{24,16},{1,9},{9,1},{17,25},{25,17},{2,10},{10... | collective-permute-start | bytes 1572872 | tf_op jit(solution)/shard_map/ppermute | solution.py:449
  114.5 10.4 %collective-permute-start.23 = (bf16[512,512]{1,0:T(8,128)(2,1)S(1)}, bf16[512,512]{1,0:T(8,128)(2,1)S(1)}, u32[]{:S(2)}, u32[]{:S(2)}) collective-permute-start(bf16[512,512]{1,0:T(8,128)(2,1)S(1)} %get-tuple-element.82.stepped_ref), channel_id=1, source_target_pairs={{0,8},{8,0},{16,24},{24,16},{1,9},{9,1},{17,25},{25,17},{2,10},{10... | collective-permute-start | bytes 1572872 | tf_op jit(solution)/shard_map/ppermute | solution.py:449
  121.6 3.3 %collective-permute-start.25 = (bf16[512,512]{1,0:T(8,128)(2,1)S(1)}, bf16[512,512]{1,0:T(8,128)(2,1)S(1)}, u32[]{:S(2)}, u32[]{:S(2)}) collective-permute-start(bf16[512,512]{1,0:T(8,128)(2,1)S(1)} %collective-permute-done.24.refs_1_), channel_id=1, source_target_pairs={{0,8},{8,0},{16,24},{24,16},{1,9},{9,1},{17,25},{25,17},{2,10},{10... | collective-permute-start | bytes 1572872 | tf_op jit(solution)/shard_map/ppermute | solution.py:449
  (3 other events, 5.4 us)

commit v10 on v7

--- a/solution.py
+++ b/solution.py
@@ -320,13 +320,14 @@
 
     def kernel(row_ref, *refs):
         g = pl.program_id(0)
-        out_ref = refs[-1] if sums is None else refs[-2]
+        out_ref, tile_ref = refs[-2:] if sums is None else refs[-3:-1]
         for j in range(count):
 
             @pl.when(g == j)
             def _():
                 out_ref[...] = refs[j][...]
 
+        tile_ref[...] = jnp.zeros_like(tile_ref)
         if sums is not None:
             total = refs[count][...] + refs[count + 1][...].astype(jnp.float32)
             refs[-1][...] = total.astype(jnp.bfloat16)
@@ -339,6 +340,8 @@
 
     ins = [view.operand() for view in arrived]
     outs = [(struct(xg.shape, xg.dtype), pl.BlockSpec((tokens, width), column))]
+    tile = struct((8, 128), jnp.float32)
+    outs.append((tile, whole(tile)))
     if sums is not None:
         own, other = sums
         kv_block = pl.BlockSpec((tokens // count, own.shape[1]), lambda g, row: (g, 0))
@@ -381,7 +384,7 @@
     if kept is not None:
         aliases = {1 + len(ins): 0, 2 + len(ins): 1}
         ins += [(a, HBM) for a in kept]
-    ins += [(a, ANY) for a in after]
+    ins += after
     return call(
         kernel,
         row,
@@ -396,36 +399,34 @@
     )
 
 
-def average(plan, scalars, h, stepped, others, kept, width, after=()):
-    rows, columns = stepped.shape
-    steps = 2 if rows % 32 == 0 else 1
+def average(plan, scalars, stepped, others, after):
+    rows, columns = stepped[0].shape
+    chunks, count = len(stepped), len(others[0])
+    steps = 4 if rows % 64 == 0 else 1
     size = rows // steps
-    count = len(others)
-
-    def kernel(row_ref, numerator_ref, partner_ref, stepped_ref, *refs):
+
+    def kernel(row_ref, numerator_ref, partner_ref, *refs):
         mix = numerator_ref[row_ref[plan["replica"]]].astype(jnp.float32) / mix_denom
         for j in range(count):
 
             @pl.when((partner_ref[0] == j + 1) | (count == 1))
             def _():
-                refs[-1][...] = (
-                    (1.0 - mix) * stepped_ref[...].astype(jnp.float32)
-                    + mix * refs[j][...].astype(jnp.float32)
-                ).astype(jnp.bfloat16)
+                for h in range(chunks):
+                    own, other = refs[h * (count + 1)], refs[h * (count + 1) + 1 + j]
+                    refs[-1][:, h * columns : (h + 1) * columns] = (
+                        (1.0 - mix) * own[...].astype(jnp.float32)
+                        + mix * other[...].astype(jnp.float32)
+                    ).astype(jnp.bfloat16)
 
     local = pl.BlockSpec((size, columns), lambda g, *scalars: (g, 0))
-    part = pl.BlockSpec((size, columns), lambda g, *scalars: (g, h))
-    ins = [(a, local) for a in (stepped, *others)]
-    if kept is not None:
-        ins.append((kept, HBM))
-    ins += [(a, ANY) for a in after]
+    full = pl.BlockSpec((size, chunks * columns), lambda g, *scalars: (g, 0))
+    ins = [(a, local) for h in range(chunks) for a in (stepped[h], *others[h])]
     return call(
         kernel,
         scalars,
-        ins,
-        [(struct((rows, width), jnp.bfloat16), part)],
+        ins + [(a, ANY) for a in after],
+        [(struct((rows, chunks * columns), jnp.bfloat16), full)],
         grid=(steps,),
-        aliases={} if kept is None else {count + 4: 0},
     )[0]
 
 
@@ -503,41 +504,43 @@
     bufs = {}
     for s in range(2, depth + 1):
         if s == depth:
-            for j in range(1, depth - 1):
+            for j in range(2, depth - 1):
                 xg = shard_step(j, xg)
             send_parts(parts[1:], [], [parcel])
             grad = own_gradient(plan, row, act, pieces[depth - 1], cot, cot_oth)
             sums = values(plan, row, list(range(depth - 1)), shards, act, pieces, None)
         for h in range(CHUNKS):
             after = list(bufs.values())[:1]
-            if s == depth:
-                after.append(grad if h == 0 else sums[0])
+            if s == 3 and h == 0:
+                xg = shard_step(1, xg)
+                after.append(parts[1].array)
+            if s == depth and h == CHUNKS - 1:
+                xg = shard_step(depth - 1, xg)
+                kv_own, parcel = values(
+                    plan, row, [depth - 1], shards[-1:], act, pieces, sums, parts[-1]
+                )
+                final = swap(parcel)
+                after += [sums[0], grad]
             bufs = relay(
                 plan, row, s, got[s - 1, h], act, pieces[: s - 1], part(cot, h), cot_oth[h], after
             )
             got[s, h] = {link: part(array, 0) for link, array in exchange(bufs).items()}
-    xg = shard_step(depth - 1, xg)
-    kv_own, parcel = values(plan, row, [depth - 1], shards[-1:], act, pieces, sums, parts[-1])
-    final = swap(parcel)
-
     scalars = (row, mix_numerator, partner)
-    moments, averaged, placed = None, None, None
+    moments, placed = None, None
+    stepped, others = [], []
     for h in range(CHUNKS):
-        last = h == CHUNKS - 1
-        after = [] if h == 0 else [placed]
-        *moments, stepped = adam(
-            row, h, got[depth, h], grad, weights, first, second, moments, after + [parcel]
+        after = [] if h == 0 else [(placed_tile, ANY)]
+        *moments, rows_now = adam(
+            row, h, got[depth, h], grad, weights, first, second, moments, after
         )
         if placed is None:
-            placed = place(plan, row, xg, arrived, 0)[0]
-        others = partner_rows(stepped, partner, row[plan["replica"]], n_rep)
-        if last:
-            views = [View(final, columns, rows)]
-            kv_views = (kv_own, View(final, 0, columns))
-            x_grad, kv_out = place(plan, row, placed, views, depth - 1, kv_views)
-        averaged = average(
-            plan, scalars, h, stepped, others, averaged, columns, [kv_out] if last else [final]
-        )
+            placed, placed_tile = place(plan, row, xg, arrived, 0)
+        stepped.append(rows_now)
+        others.append(partner_rows(rows_now, partner, row[plan["replica"]], n_rep))
+    views = [View(final, columns, rows)]
+    kv_views = (kv_own, View(final, 0, columns))
+    x_grad, tile, kv_out = place(plan, row, placed, views, depth - 1, kv_views)
+    averaged = average(plan, scalars, stepped, others, [tile])
     return (
         kv_out[None],
         x_grad[None],

time: 127 us -> 125 us (0.984)
  local copies, waits for them, and re-layouts: 4.52 us -> 2.62 us
    unnamed x20 -> x16, local copies, waits for them, and re-layouts: 3.82 us -> 1.93 us
    pallas_call x23 -> x22, Pallas kernels: 42 us -> 41.3 us  [call(): pl.pallas_call(kernel, grid_spec=pltpu.PrefetchScalarGridSpec(num_scalar_...]
  transfers between devices with their start and end apart: 26 -> 26, of which waited for: 6 -> 8; matrix products, arithmetic and copies ran while one was open for 1% -> 1% of each run, Pallas kernels for 32% -> 31%
where the time goes in v10:
time: 125 us
  Pallas kernels  41.3 us (33%)
  starting transfers between devices  40.4 us (32%)
  waiting for transfers between devices  39.4 us (32%)
  local copies, waits for them, and re-layouts  2.62 us (2%)
    pallas_call x22, Pallas kernels, call(): pl.pallas_call(kernel, grid_spec=pltpu.PrefetchScalarGridSpec(num_scalar_...  41.3 us
    ppermute x14, starting transfers between devices, exchange(): lax.ppermute(bufs[name], 'fsdp', links[name])  28.7 us
    ppermute x2, waiting for transfers between devices, send(): return swap(pack(plan, row, rows, [], act, turns, after))  21.8 us
    ppermute x2, waiting for transfers between devices, partner_rows(): far = lax.ppermute(stepped, 'rep', [(r, r ^ 2) for r in range(4)])  10.1 us
    ppermute x14, waiting for transfers between devices, exchange(): lax.ppermute(bufs[name], 'fsdp', links[name])  7.23 us
    ppermute x2, starting transfers between devices, partner_rows(): far = lax.ppermute(stepped, 'rep', [(r, r ^ 2) for r in range(4)])  3.04 us
    ppermute x1, starting transfers between devices, per_device(): parcel = swap(cot)  3 us
  transfers between devices with their start and end apart: 26, of which 8 were waited for; matrix products, arithmetic and copies ran while one was open for 1% of the time, Pallas kernels for 31%

profile of v10, /device:TPU:0, one launch (start us, length us, event | category | flops | bytes accessed | tf_op | source)
XLA Modules:
  0.0 124.6 jit_solution(6340069602969780657)
XLA Ops:
  0.6 3.0 %collective-permute-start.3 = (bf16[384,1024]{1,0:T(8,128)(2,1)}, bf16[384,1024]{1,0:T(8,128)(2,1)S(1)}, u32[]{:S(2)}, u32[]{:S(2)}) collective-permute-start(bf16[384,1024]{1,0:T(8,128)(2,1)} %bitcast.33), channel_id=1, source_target_pairs={{0,1},{1,0},{2,3},{3,2},{4,5},{5,4},{6,7},{7,6},{8,9},{9,8},{10,11... | collective-permute-start | bytes 2359304 | tf_op jit(solution)/shard_map/ppermute | solution.py:478
  4.4 4.4 %collective-permute-start = (bf16[512,1024]{1,0:T(8,128)(2,1)}, bf16[512,1024]{1,0:T(8,128)(2,1)S(1)}, u32[]{:S(2)}, u32[]{:S(2)}) collective-permute-start(bf16[512,1024]{1,0:T(8,128)(2,1)} %bitcast.46), channel_id=1, source_target_pairs={{0,2},{1,3},{2,0},{3,1},{4,6},{5,7},{6,4},{7,5},{8,10},{9,11},{10,... | collective-permute-start | bytes 3145736 | tf_op jit(solution)/shard_map/ppermute | solution.py:462
  9.5 1.9 %copy-done = bf16[1,384,4096]{2,1,0:T(8,128)(2,1)S(1)} copy-done((bf16[1,384,4096]{2,1,0:T(8,128)(2,1)S(1)}, bf16[1,384,4096]{2,1,0:T(8,128)(2,1)}, u32[]{:S(2)}) %copy-start) | copy-done | bytes 3145752
  12.5 17.3 %collective-permute-done.2.refs_4_.refs_3_.refs_6_.refs_2_ = bf16[384,512]{1,0:T(8,128)(2,1)S(1)} collective-permute-done((bf16[384,512]{1,0:T(8,128)(2,1)S(1)}, bf16[384,512]{1,0:T(8,128)(2,1)S(1)}, u32[]{:S(2)}, u32[]{:S(2)}) %collective-permute-start.2) | collective-permute-done | bytes 393248 | tf_op jit(solution)/shard_map/ppermute | solution.py:476
  30.4 1.8 %collective-permute-start.6 = (bf16[384,1024]{1,0:T(8,128)(2,1)S(1)}, bf16[384,1024]{1,0:T(8,128)(2,1)S(1)}, u32[]{:S(2)}, u32[]{:S(2)}) collective-permute-start(bf16[384,1024]{1,0:T(8,128)(2,1)S(1)} %shard_map.121), channel_id=1, source_target_pairs={{0,1},{1,0},{2,3},{3,2},{4,5},{5,4},{6,7},{7,6},{8,9},{9,8},{10,11... | collective-permute-start | bytes 2359304 | tf_op jit(solution)/shard_map/ppermute | solution.py:476
  32.3 1.5 %shard_map.120 = (bf16[512,512]{1,0:T(8,128)(2,1)S(1)}, bf16[512,512]{1,0:T(8,128)(2,1)S(1)}) custom-call(s32[40]{0:T(128)S(1)} %dynamic-slice_bitcast_fusion.row_ref, bf16[512,1024]{1,0:T(8,128)(2,1)S(1)} %collective-permute-done.1.refs_0_.refs_1_, bf16[512,1024]{1,0:T(8,128)(2,1)S(1)} %collective-permute-done.refs_1_.refs_0_, ...), custom_call_target="tpu_custom_call" | custom-call | tf_op jit(solution)/shard_map/pallas_call | solution.py:86
  34.6 3.8 %collective-permute-start.5 = (bf16[512,512]{1,0:T(8,128)(2,1)S(1)}, bf16[512,512]{1,0:T(8,128)(2,1)S(1)}, u32[]{:S(2)}, u32[]{:S(2)}) collective-permute-start(bf16[512,512]{1,0:T(8,128)(2,1)S(1)} %get-tuple-element.45.refs_7_), channel_id=1, source_target_pairs={{0,2},{1,3},{2,0},{3,1},{4,6},{5,7},{6,4},{7,5},{8,10},{9,11},{10,... | collective-permute-start | bytes 1572872 | tf_op jit(solution)/shard_map/ppermute | solution.py:462
  38.5 2.4 %shard_map.123 = (bf16[384,4096]{1,0:T(8,128)(2,1)}, bf16[384,512]{1,0:T(8,128)(2,1)S(1)}, bf16[512,1024]{1,0:T(8,128)(2,1)S(1)}) custom-call(s32[40]{0:T(128)S(1)} %dynamic-slice_bitcast_fusion.row_ref, bf16[512,1024]{1,0:T(8,128)(2,1)S(1)} %bitcast.47, ...), custom_call_target="tpu_custom_call" | custom-call | tf_op jit(solution)/shard_map/pallas_call | solution.py:86
  40.9 1.5 %shard_map.122 = (bf16[512,512]{1,0:T(8,128)(2,1)S(1)}, bf16[512,512]{1,0:T(8,128)(2,1)S(1)}) custom-call(s32[40]{0:T(128)S(1)} %dynamic-slice_bitcast_fusion.row_ref, bf16[512,1024]{1,0:T(8,128)(2,1)S(1)} %collective-permute-done.1.refs_0_.refs_1_, bf16[512,1024]{1,0:T(8,128)(2,1)S(1)} %collective-permute-done.refs_1_.refs_0_, ...), custom_call_target="tpu_custom_call" | custom-call | tf_op jit(solution)/shard_map/pallas_call | solution.py:86
  43.2 1.5 %collective-permute-start.9 = (bf16[512,512]{1,0:T(8,128)(2,1)S(1)}, bf16[512,512]{1,0:T(8,128)(2,1)S(1)}, u32[]{:S(2)}, u32[]{:S(2)}) collective-permute-start(bf16[512,512]{1,0:T(8,128)(2,1)S(1)} %get-tuple-element.46.refs_8_), channel_id=1, source_target_pairs={{0,2},{1,3},{2,0},{3,1},{4,6},{5,7},{6,4},{7,5},{8,10},{9,11},{10,... | collective-permute-start | bytes 1572872 | tf_op jit(solution)/shard_map/ppermute | solution.py:462
  44.7 4.5 %collective-permute-done.6.refs_5_.refs_2_.refs_7_.refs_8_.refs_3_.refs_4_.refs_6_ = bf16[384,1024]{1,0:T(8,128)(2,1)S(1)} collective-permute-done((bf16[384,1024]{1,0:T(8,128)(2,1)S(1)}, bf16[384,1024]{1,0:T(8,128)(2,1)S(1)}, u32[]{:S(2)}, u32[]{:S(2)}) %collective-permute-start.6) | collective-permute-done | bytes 786464 | tf_op jit(solution)/shard_map/ppermute | solution.py:476
  51.3 2.4 %shard_map.124 = (bf16[384,4096]{1,0:T(8,128)(2,1)}, bf16[384,512]{1,0:T(8,128)(2,1)S(1)}, bf16[512,1024]{1,0:T(8,128)(2,1)S(1)}) custom-call(s32[40]{0:T(128)S(1)} %dynamic-slice_bitcast_fusion.row_ref, bf16[512,1024]{1,0:T(8,128)(2,1)S(1)} %collective-permute-done.refs_1_.refs_0_, ...), custom_call_target="tpu_custom_call", output_to_operand_aliasing={{0}: (6, {})} | custom-call | tf_op jit(solution)/shard_map/pallas_call | solution.py:86
  56.0 4.4 %collective-permute-start.7 = (bf16[512,512]{1,0:T(8,128)(2,1)S(1)}, bf16[512,512]{1,0:T(8,128)(2,1)S(1)}, u32[]{:S(2)}, u32[]{:S(2)}) collective-permute-start(bf16[512,512]{1,0:T(8,128)(2,1)S(1)} %get-tuple-element.49.refs_8_), channel_id=1, source_target_pairs={{0,2},{1,3},{2,0},{3,1},{4,6},{5,7},{6,4},{7,5},{8,10},{9,11},{10,... | collective-permute-start | bytes 1572872 | tf_op jit(solution)/shard_map/ppermute | solution.py:462
  63.8 3.5 %collective-permute-start.10 = (bf16[512,512]{1,0:T(8,128)(2,1)S(1)}, bf16[512,512]{1,0:T(8,128)(2,1)S(1)}, u32[]{:S(2)}, u32[]{:S(2)}) collective-permute-start(bf16[512,512]{1,0:T(8,128)(2,1)S(1)} %get-tuple-element.51.refs_9_), channel_id=1, source_target_pairs={{0,2},{1,3},{2,0},{3,1},{4,6},{5,7},{6,4},{7,5},{8,10},{9,11},{10,... | collective-permute-start | bytes 1572872 | tf_op jit(solution)/shard_map/ppermute | solution.py:462
  67.3 2.5 %shard_map.127 = (bf16[384,4096]{1,0:T(8,128)(2,1)}, bf16[384,512]{1,0:T(8,128)(2,1)S(1)}, bf16[512,1024]{1,0:T(8,128)(2,1)S(1)}) custom-call(s32[40]{0:T(128)S(1)} %dynamic-slice_bitcast_fusion.row_ref, bf16[512,512]{1,0:T(8,128)(2,1)S(1)} %collective-permute-done.5.refs_1_.refs_0_, ...), custom_call_target="tpu_custom_call", output_to_operand_aliasing={{0}: (8, {})} | custom-call | tf_op jit(solution)/shard_map/pallas_call | solution.py:86
  71.0 2.3 %collective-permute-done.7.refs_1_ = bf16[512,512]{1,0:T(8,128)(2,1)S(1)} collective-permute-done((bf16[512,512]{1,0:T(8,128)(2,1)S(1)}, bf16[512,512]{1,0:T(8,128)(2,1)S(1)}, u32[]{:S(2)}, u32[]{:S(2)}) %collective-permute-start.7) | collective-permute-done | bytes 524320 | tf_op jit(solution)/shard_map/ppermute | solution.py:462
  75.5 4.5 %collective-permute-start.15 = (bf16[512,512]{1,0:T(8,128)(2,1)S(1)}, bf16[512,512]{1,0:T(8,128)(2,1)S(1)}, u32[]{:S(2)}, u32[]{:S(2)}) collective-permute-start(bf16[512,512]{1,0:T(8,128)(2,1)S(1)} %get-tuple-element.70.refs_9_), channel_id=1, source_target_pairs={{0,2},{1,3},{2,0},{3,1},{4,6},{5,7},{6,4},{7,5},{8,10},{9,11},{10,... | collective-permute-start | bytes 1572872 | tf_op jit(solution)/shard_map/ppermute | solution.py:462
  79.9 1.8 %shard_map.136.grad_ref.refs_11_ = f32[512,1024]{1,0:T(8,128)S(1)} custom-call(s32[40]{0:T(128)S(1)} %dynamic-slice_bitcast_fusion.row_ref, bf16[384,4096]{1,0:T(8,128)(2,1)S(1)} %bitcast.26, bf16[384,1024]{1,0:T(8,128)(2,1)S(1)} %collective-permute-done.11.refs_9_.refs_5_.refs_2_.refs_0_.piece_ref, bf16[384,1024]{1,0:T(8,128)(2,1)S(1)} %bitcast.42, ...), custom_call_target="tpu_custom_call" | custom-call | tf_op jit(solution)/shard_map/pallas_call | solution.py:86
  81.8 3.9 %shard_map.130 = (f32[384,1024]{1,0:T(8,128)S(1)}, f32[384,1024]{1,0:T(8,128)S(1)}) custom-call(s32[40]{0:T(128)S(1)} %dynamic-slice_bitcast_fusion.row_ref, bf16[512,1024]{1,0:T(8,128)(2,1)S(1)} %get-tuple-element.56.refs_0_, bf16[512,1024]{1,0:T(8,128)(2,1)S(1)} %get-tuple-element.57.refs_1_, bf16[512,1024]{1,0:T(8,128)(2,1)S(1)} %get-tuple-element.58.refs_2_, ...), custom_call_target="tpu_custom_call" | custom-call | tf_op jit(solution)/shard_map/pallas_call | solution.py:86
  85.7 1.5 %shard_map.138 = (bf16[512,512]{1,0:T(8,128)(2,1)S(1)}, bf16[512,512]{1,0:T(8,128)(2,1)S(1)}) custom-call(s32[40]{0:T(128)S(1)} %dynamic-slice_bitcast_fusion.row_ref, bf16[512,512]{1,0:T(8,128)(2,1)S(1)} %collective-permute-done.20.refs_0_, bf16[512,512]{1,0:T(8,128)(2,1)S(1)} %collective-permute-done.10.refs_2_.refs_1_, bf16[384,4096]{1,0:T(8,128)(2,1)S(1)} %bitcast.30, ...), custom_call_target="tpu_custom_call" | custom-call | tf_op jit(solution)/shard_map/pallas_call | solution.py:86
  87.2 1.6 %collective-permute-start.21 = (bf16[512,512]{1,0:T(8,128)(2,1)S(1)}, bf16[512,512]{1,0:T(8,128)(2,1)S(1)}, u32[]{:S(2)}, u32[]{:S(2)}) collective-permute-start(bf16[512,512]{1,0:T(8,128)(2,1)S(1)} %get-tuple-element.74), channel_id=1, source_target_pairs={{0,2},{1,3},{2,0},{3,1},{4,6},{5,7},{6,4},{7,5},{8,10},{9,11},{10,... | collective-permute-start | bytes 1572872 | tf_op jit(solution)/shard_map/ppermute | solution.py:462
  89.5 2.5 %shard_map.128 = (bf16[384,4096]{1,0:T(8,128)(2,1)}, bf16[384,512]{1,0:T(8,128)(2,1)S(1)}, bf16[512,1024]{1,0:T(8,128)(2,1)S(1)}) custom-call(s32[40]{0:T(128)S(1)} %dynamic-slice_bitcast_fusion.row_ref, bf16[512,1024]{1,0:T(8,128)(2,1)S(1)} %collective-permute-done.refs_1_.refs_0_, ...), custom_call_target="tpu_custom_call", output_to_operand_aliasing={{0}: (7, {})} | custom-call | tf_op jit(solution)/shard_map/pallas_call | solution.py:86
  92.1 1.9 %shard_map.131 = (f32[384,1024]{1,0:T(8,128)S(1)}, bf16[384,1536]{1,0:T(8,128)(2,1)S(1)}) custom-call(s32[40]{0:T(128)S(1)} %dynamic-slice_bitcast_fusion.row_ref, bf16[512,1024]{1,0:T(8,128)(2,1)S(1)} %get-tuple-element.54.refs_0_, bf16[384,4096]{1,0:T(8,128)(2,1)S(1)} %bitcast.32, ...), custom_call_target="tpu_custom_call" | custom-call | tf_op jit(solution)/shard_map/pallas_call | solution.py:86
  95.7 3.1 %shard_map.137 = (f32[512,1024]{1,0:T(8,128)}, f32[512,1024]{1,0:T(8,128)}, bf16[512,512]{1,0:T(8,128)(2,1)S(1)}) custom-call(s32[40]{0:T(128)S(1)} %dynamic-slice_bitcast_fusion.row_ref, bf16[512,512]{1,0:T(8,128)(2,1)S(1)} %collective-permute-done.15.up_ref, bf16[512,512]{1,0:T(8,128)(2,1)S(1)} %collective-permute-done.16.dn_ref, ...), custom_call_target="tpu_custom_call" | custom-call | tf_op jit(solution)/shard_map/pallas_call | solution.py:86
  98.8 1.5 %collective-permute-start.18 = (bf16[512,512]{1,0:T(8,128)(2,1)S(1)}, bf16[512,512]{1,0:T(8,128)(2,1)S(1)}, u32[]{:S(2)}, u32[]{:S(2)}) collective-permute-start(bf16[512,512]{1,0:T(8,128)(2,1)S(1)} %get-tuple-element.72.refs_0_), channel_id=1, source_target_pairs={{0,16},{8,24},{16,0},{24,8},{1,17},{9,25},{17,1},{25,9},{2,18},{10... | collective-permute-start | bytes 1572872 | tf_op jit(solution)/shard_map/ppermute | solution.py:437
  100.3 2.2 %shard_map.133 = (bf16[384,4096]{1,0:T(8,128)(2,1)}, f32[8,128]{1,0:T(8,128)S(1)}) custom-call(s32[40]{0:T(128)S(1)} %dynamic-slice_bitcast_fusion.row_ref, bf16[384,1024]{1,0:T(8,128)(2,1)S(1)} %collective-permute-done.11.refs_9_.refs_5_.refs_2_.refs_0_.piece_ref, ...), custom_call_target="tpu_custom_call", output_to_operand_aliasing={{0}: (4, {})} | custom-call | tf_op jit(solution)/shard_map/pallas_call | solution.py:86
  102.5 2.6 %collective-permute-done.21.up_ref = bf16[512,512]{1,0:T(8,128)(2,1)S(1)} collective-permute-done((bf16[512,512]{1,0:T(8,128)(2,1)S(1)}, bf16[512,512]{1,0:T(8,128)(2,1)S(1)}, u32[]{:S(2)}, u32[]{:S(2)}) %collective-permute-start.21) | collective-permute-done | bytes 524320 | tf_op jit(solution)/shard_map/ppermute | solution.py:462
  105.2 3.1 %shard_map.139 = (f32[512,1024]{1,0:T(8,128)}, f32[512,1024]{1,0:T(8,128)}, bf16[512,512]{1,0:T(8,128)(2,1)S(1)}) custom-call(s32[40]{0:T(128)S(1)} %dynamic-slice_bitcast_fusion.row_ref, bf16[512,512]{1,0:T(8,128)(2,1)S(1)} %collective-permute-done.21.up_ref, ...), custom_call_target="tpu_custom_call", output_to_operand_aliasing={{0}: (7, {}), {1}: (8, {})} | custom-call | tf_op jit(solution)/shard_map/pallas_call | solution.py:86
  108.2 1.5 %collective-permute-start.24 = (bf16[512,512]{1,0:T(8,128)(2,1)S(1)}, bf16[512,512]{1,0:T(8,128)(2,1)S(1)}, u32[]{:S(2)}, u32[]{:S(2)}) collective-permute-start(bf16[512,512]{1,0:T(8,128)(2,1)S(1)} %get-tuple-element.79.refs_4_), channel_id=1, source_target_pairs={{0,16},{8,24},{16,0},{24,8},{1,17},{9,25},{17,1},{25,9},{2,18},{10... | collective-permute-start | bytes 1572872 | tf_op jit(solution)/shard_map/ppermute | solution.py:437
  110.2 10.1 %collective-permute-done.24.refs_6_ = bf16[512,512]{1,0:T(8,128)(2,1)S(1)} collective-permute-done((bf16[512,512]{1,0:T(8,128)(2,1)S(1)}, bf16[512,512]{1,0:T(8,128)(2,1)S(1)}, u32[]{:S(2)}, u32[]{:S(2)}) %collective-permute-start.24) | collective-permute-done | bytes 524320 | tf_op jit(solution)/shard_map/ppermute | solution.py:437
  120.4 1.7 %shard_map.134 = (bf16[384,4096]{1,0:T(8,128)(2,1)}, f32[8,128]{1,0:T(8,128)S(1)}, bf16[384,1024]{1,0:T(8,128)(2,1)}) custom-call(s32[40]{0:T(128)S(1)} %dynamic-slice_bitcast_fusion.row_ref, bf16[384,1536]{1,0:T(8,128)(2,1)S(1)} %collective-permute-done.12.refs_0_.refs_2_, ...), custom_call_target="tpu_custom_call", output_to_operand_aliasing={{0}: (4, {})} | custom-call | tf_op jit(solution)/shard_map/pallas_call | solution.py:86
  122.3 2.4 %shard_map.140 = bf16[512,1024]{1,0:T(8,128)(2,1)} custom-call(s32[40]{0:T(128)S(1)} %dynamic-slice_bitcast_fusion.row_ref, s32[4]{0:T(128)S(1)} %copy-done.6, s32[4]{0:T(128)S(1)} %copy-done.7, bf16[512,512]{1,0:T(8,128)(2,1)S(1)} %get-tuple-element.72.refs_0_, bf16[512,512]{1,0:T(8,128)(2,1)S(1)} %collective-permute-done.17.refs_1_, ...), custom_call_target="tpu_custom_call" | custom-call | tf_op jit(solution)/shard_map/pallas_call | solution.py:86
  (59 shorter events, 18.9 us)
Async XLA Ops:
  0.6 29.2 %collective-permute-start.3 = (bf16[384,1024]{1,0:T(8,128)(2,1)}, bf16[384,1024]{1,0:T(8,128)(2,1)S(1)}, u32[]{:S(2)}, u32[]{:S(2)}) collective-permute-start(bf16[384,1024]{1,0:T(8,128)(2,1)} %bitcast.33), channel_id=1, source_target_pairs={{0,1},{1,0},{2,3},{3,2},{4,5},{5,4},{6,7},{7,6},{8,9},{9,8},{10,11... | collective-permute-start | bytes 2359304 | tf_op jit(solution)/shard_map/ppermute | solution.py:478
  3.6 28.6 %collective-permute-start.1 = (bf16[512,1024]{1,0:T(8,128)(2,1)}, bf16[512,1024]{1,0:T(8,128)(2,1)S(1)}, u32[]{:S(2)}, u32[]{:S(2)}) collective-permute-start(bf16[512,1024]{1,0:T(8,128)(2,1)} %bitcast.45), channel_id=1, source_target_pairs={{2,4},{3,5},{4,2},{5,3},{10,12},{11,13},{12,10},{13,11},{18,20},{1... | collective-permute-start | bytes 3145736 | tf_op jit(solution)/shard_map/ppermute | solution.py:462
  4.4 27.9 %collective-permute-start = (bf16[512,1024]{1,0:T(8,128)(2,1)}, bf16[512,1024]{1,0:T(8,128)(2,1)S(1)}, u32[]{:S(2)}, u32[]{:S(2)}) collective-permute-start(bf16[512,1024]{1,0:T(8,128)(2,1)} %bitcast.46), channel_id=1, source_target_pairs={{0,2},{1,3},{2,0},{3,1},{4,6},{5,7},{6,4},{7,5},{8,10},{9,11},{10,... | collective-permute-start | bytes 3145736 | tf_op jit(solution)/shard_map/ppermute | solution.py:462
  11.9 20.3 %copy-start.2 = (bf16[1,384,1024]{2,1,0:T(8,128)(2,1)S(1)}, bf16[1,384,1024]{2,1,0:T(8,128)(2,1)}, u32[]{:S(2)}) copy-start(bf16[1,384,1024]{2,1,0:T(8,128)(2,1)} %param.10) | copy-start | bytes 2359300
  11.9 17.9 %collective-permute-start.2 = (bf16[384,512]{1,0:T(8,128)(2,1)S(1)}, bf16[384,512]{1,0:T(8,128)(2,1)S(1)}, u32[]{:S(2)}, u32[]{:S(2)}) collective-permute-start(bf16[384,512]{1,0:T(8,128)(2,1)S(1)} %shard_map.119), channel_id=1, source_target_pairs={{0,1},{1,0},{2,3},{3,2},{4,5},{5,4},{6,7},{7,6},{8,9},{9,8},{10,11... | collective-permute-start | bytes 1179656 | tf_op jit(solution)/shard_map/ppermute | solution.py:476
  30.4 8.1 %copy-start.3 = (bf16[1,512,1024]{2,1,0:T(8,128)(2,1)S(1)}, bf16[1,512,1024]{2,1,0:T(8,128)(2,1)}, u32[]{:S(2)}) copy-start(bf16[1,512,1024]{2,1,0:T(8,128)(2,1)} %param.9) | copy-start | bytes 3145732
  30.4 18.8 %collective-permute-start.6 = (bf16[384,1024]{1,0:T(8,128)(2,1)S(1)}, bf16[384,1024]{1,0:T(8,128)(2,1)S(1)}, u32[]{:S(2)}, u32[]{:S(2)}) collective-permute-start(bf16[384,1024]{1,0:T(8,128)(2,1)S(1)} %shard_map.121), channel_id=1, source_target_pairs={{0,1},{1,0},{2,3},{3,2},{4,5},{5,4},{6,7},{7,6},{8,9},{9,8},{10,11... | collective-permute-start | bytes 2359304 | tf_op jit(solution)/shard_map/ppermute | solution.py:476
  33.8 7.1 %copy-start.1 = (bf16[1,384,4096]{2,1,0:T(8,128)(2,1)S(1)}, bf16[1,384,4096]{2,1,0:T(8,128)(2,1)}, u32[]{:S(2)}) copy-start(bf16[1,384,4096]{2,1,0:T(8,128)(2,1)} %param.8) | copy-start | bytes 9437188
  33.8 20.0 %collective-permute-start.4 = (bf16[512,512]{1,0:T(8,128)(2,1)S(1)}, bf16[512,512]{1,0:T(8,128)(2,1)S(1)}, u32[]{:S(2)}, u32[]{:S(2)}) collective-permute-start(bf16[512,512]{1,0:T(8,128)(2,1)S(1)} %get-tuple-element.44), channel_id=1, source_target_pairs={{2,4},{3,5},{4,2},{5,3},{10,12},{11,13},{12,10},{13,11},{18,20},{1... | collective-permute-start | bytes 1572872 | tf_op jit(solution)/shard_map/ppermute | solution.py:462
  34.6 19.1 %collective-permute-start.5 = (bf16[512,512]{1,0:T(8,128)(2,1)S(1)}, bf16[512,512]{1,0:T(8,128)(2,1)S(1)}, u32[]{:S(2)}, u32[]{:S(2)}) collective-permute-start(bf16[512,512]{1,0:T(8,128)(2,1)S(1)} %get-tuple-element.45.refs_7_), channel_id=1, source_target_pairs={{0,2},{1,3},{2,0},{3,1},{4,6},{5,7},{6,4},{7,5},{8,10},{9,11},{10,... | collective-permute-start | bytes 1572872 | tf_op jit(solution)/shard_map/ppermute | solution.py:462
  42.5 17.9 %collective-permute-start.8 = (bf16[512,512]{1,0:T(8,128)(2,1)S(1)}, bf16[512,512]{1,0:T(8,128)(2,1)S(1)}, u32[]{:S(2)}, u32[]{:S(2)}) collective-permute-start(bf16[512,512]{1,0:T(8,128)(2,1)S(1)} %get-tuple-element.50), channel_id=1, source_target_pairs={{2,4},{3,5},{4,2},{5,3},{10,12},{11,13},{12,10},{13,11},{18,20},{1... | collective-permute-start | bytes 1572872 | tf_op jit(solution)/shard_map/ppermute | solution.py:462
  43.2 18.4 %collective-permute-start.9 = (bf16[512,512]{1,0:T(8,128)(2,1)S(1)}, bf16[512,512]{1,0:T(8,128)(2,1)S(1)}, u32[]{:S(2)}, u32[]{:S(2)}) collective-permute-start(bf16[512,512]{1,0:T(8,128)(2,1)S(1)} %get-tuple-element.46.refs_8_), channel_id=1, source_target_pairs={{0,2},{1,3},{2,0},{3,1},{4,6},{5,7},{6,4},{7,5},{8,10},{9,11},{10,... | collective-permute-start | bytes 1572872 | tf_op jit(solution)/shard_map/ppermute | solution.py:462
  49.8 20.0 %collective-permute-start.11 = (bf16[384,1024]{1,0:T(8,128)(2,1)S(1)}, bf16[384,1024]{1,0:T(8,128)(2,1)S(1)}, u32[]{:S(2)}, u32[]{:S(2)}) collective-permute-start(bf16[384,1024]{1,0:T(8,128)(2,1)S(1)} %shard_map.129), channel_id=1, source_target_pairs={{0,1},{1,0},{2,3},{3,2},{4,5},{5,4},{6,7},{7,6},{8,9},{9,8},{10,11... | collective-permute-start | bytes 2359304 | tf_op jit(solution)/shard_map/ppermute | solution.py:497
  55.3 15.7 %collective-permute-start.14 = (bf16[512,512]{1,0:T(8,128)(2,1)S(1)}, bf16[512,512]{1,0:T(8,128)(2,1)S(1)}, u32[]{:S(2)}, u32[]{:S(2)}) collective-permute-start(bf16[512,512]{1,0:T(8,128)(2,1)S(1)} %get-tuple-element.69), channel_id=1, source_target_pairs={{2,4},{3,5},{4,2},{5,3},{10,12},{11,13},{12,10},{13,11},{18,20},{1... | collective-permute-start | bytes 1572872 | tf_op jit(solution)/shard_map/ppermute | solution.py:462
  56.0 17.3 %collective-permute-start.7 = (bf16[512,512]{1,0:T(8,128)(2,1)S(1)}, bf16[512,512]{1,0:T(8,128)(2,1)S(1)}, u32[]{:S(2)}, u32[]{:S(2)}) collective-permute-start(bf16[512,512]{1,0:T(8,128)(2,1)S(1)} %get-tuple-element.49.refs_8_), channel_id=1, source_target_pairs={{0,2},{1,3},{2,0},{3,1},{4,6},{5,7},{6,4},{7,5},{8,10},{9,11},{10,... | collective-permute-start | bytes 1572872 | tf_op jit(solution)/shard_map/ppermute | solution.py:462
  63.1 22.6 %collective-permute-start.20 = (bf16[512,512]{1,0:T(8,128)(2,1)S(1)}, bf16[512,512]{1,0:T(8,128)(2,1)S(1)}, u32[]{:S(2)}, u32[]{:S(2)}) collective-permute-start(bf16[512,512]{1,0:T(8,128)(2,1)S(1)} %get-tuple-element.73), channel_id=1, source_target_pairs={{2,4},{3,5},{4,2},{5,3},{10,12},{11,13},{12,10},{13,11},{18,20},{1... | collective-permute-start | bytes 1572872 | tf_op jit(solution)/shard_map/ppermute | solution.py:462
  63.8 21.9 %collective-permute-start.10 = (bf16[512,512]{1,0:T(8,128)(2,1)S(1)}, bf16[512,512]{1,0:T(8,128)(2,1)S(1)}, u32[]{:S(2)}, u32[]{:S(2)}) collective-permute-start(bf16[512,512]{1,0:T(8,128)(2,1)S(1)} %get-tuple-element.51.refs_9_), channel_id=1, source_target_pairs={{0,2},{1,3},{2,0},{3,1},{4,6},{5,7},{6,4},{7,5},{8,10},{9,11},{10,... | collective-permute-start | bytes 1572872 | tf_op jit(solution)/shard_map/ppermute | solution.py:462
  70.4 29.9 %collective-permute-start.13 = (bf16[384,1024]{1,0:T(8,128)(2,1)S(1)}, bf16[384,1024]{1,0:T(8,128)(2,1)S(1)}, u32[]{:S(2)}, u32[]{:S(2)}) collective-permute-start(bf16[384,1024]{1,0:T(8,128)(2,1)S(1)} %shard_map.132), channel_id=1, source_target_pairs={{0,1},{1,0},{2,3},{3,2},{4,5},{5,4},{6,7},{7,6},{8,9},{9,8},{10,11... | collective-permute-start | bytes 2359304 | tf_op jit(solution)/shard_map/ppermute | solution.py:497
  74.8 19.2 %collective-permute-start.16 = (bf16[512,512]{1,0:T(8,128)(2,1)S(1)}, bf16[512,512]{1,0:T(8,128)(2,1)S(1)}, u32[]{:S(2)}, u32[]{:S(2)}) collective-permute-start(bf16[512,512]{1,0:T(8,128)(2,1)S(1)} %get-tuple-element.71), channel_id=1, source_target_pairs={{2,4},{3,5},{4,2},{5,3},{10,12},{11,13},{12,10},{13,11},{18,20},{1... | collective-permute-start | bytes 1572872 | tf_op jit(solution)/shard_map/ppermute | solution.py:462
  75.5 20.3 %collective-permute-start.15 = (bf16[512,512]{1,0:T(8,128)(2,1)S(1)}, bf16[512,512]{1,0:T(8,128)(2,1)S(1)}, u32[]{:S(2)}, u32[]{:S(2)}) collective-permute-start(bf16[512,512]{1,0:T(8,128)(2,1)S(1)} %get-tuple-element.70.refs_9_), channel_id=1, source_target_pairs={{0,2},{1,3},{2,0},{3,1},{4,6},{5,7},{6,4},{7,5},{8,10},{9,11},{10,... | collective-permute-start | bytes 1572872 | tf_op jit(solution)/shard_map/ppermute | solution.py:462
  87.2 17.9 %collective-permute-start.21 = (bf16[512,512]{1,0:T(8,128)(2,1)S(1)}, bf16[512,512]{1,0:T(8,128)(2,1)S(1)}, u32[]{:S(2)}, u32[]{:S(2)}) collective-permute-start(bf16[512,512]{1,0:T(8,128)(2,1)S(1)} %get-tuple-element.74), channel_id=1, source_target_pairs={{0,2},{1,3},{2,0},{3,1},{4,6},{5,7},{6,4},{7,5},{8,10},{9,11},{10,... | collective-permute-start | bytes 1572872 | tf_op jit(solution)/shard_map/ppermute | solution.py:462
  88.8 16.3 %collective-permute-start.22 = (bf16[512,512]{1,0:T(8,128)(2,1)S(1)}, bf16[512,512]{1,0:T(8,128)(2,1)S(1)}, u32[]{:S(2)}, u32[]{:S(2)}) collective-permute-start(bf16[512,512]{1,0:T(8,128)(2,1)S(1)} %get-tuple-element.75), channel_id=1, source_target_pairs={{2,4},{3,5},{4,2},{5,3},{10,12},{11,13},{12,10},{13,11},{18,20},{1... | collective-permute-start | bytes 1572872 | tf_op jit(solution)/shard_map/ppermute | solution.py:462
  92.1 3.7 %copy-start.4 = (f32[1,512,1024]{2,1,0:T(8,128)S(1)}, f32[1,512,1024]{2,1,0:T(8,128)}, u32[]{:S(2)}) copy-start(f32[1,512,1024]{2,1,0:T(8,128)} %param.11) | copy-start | bytes 6291460
  92.1 3.7 %copy-start.5 = (f32[1,512,1024]{2,1,0:T(8,128)S(1)}, f32[1,512,1024]{2,1,0:T(8,128)}, u32[]{:S(2)}) copy-start(f32[1,512,1024]{2,1,0:T(8,128)} %param.12) | copy-start | bytes 6291460
  94.0 26.3 %collective-permute-start.12 = (bf16[384,1536]{1,0:T(8,128)(2,1)S(1)}, bf16[384,1536]{1,0:T(8,128)(2,1)S(1)}, u32[]{:S(2)}, u32[]{:S(2)}) collective-permute-start(bf16[384,1536]{1,0:T(8,128)(2,1)S(1)} %get-tuple-element.62), channel_id=1, source_target_pairs={{0,1},{1,0},{2,3},{3,2},{4,5},{5,4},{6,7},{7,6},{8,9},{9,8},{10,11... | collective-permute-start | bytes 3538952 | tf_op jit(solution)/shard_map/ppermute | solution.py:522
  98.8 11.5 %collective-permute-start.18 = (bf16[512,512]{1,0:T(8,128)(2,1)S(1)}, bf16[512,512]{1,0:T(8,128)(2,1)S(1)}, u32[]{:S(2)}, u32[]{:S(2)}) collective-permute-start(bf16[512,512]{1,0:T(8,128)(2,1)S(1)} %get-tuple-element.72.refs_0_), channel_id=1, source_target_pairs={{0,16},{8,24},{16,0},{24,8},{1,17},{9,25},{17,1},{25,9},{2,18},{10... | collective-permute-start | bytes 1572872 | tf_op jit(solution)/shard_map/ppermute | solution.py:437
  108.2 12.1 %collective-permute-start.24 = (bf16[512,512]{1,0:T(8,128)(2,1)S(1)}, bf16[512,512]{1,0:T(8,128)(2,1)S(1)}, u32[]{:S(2)}, u32[]{:S(2)}) collective-permute-start(bf16[512,512]{1,0:T(8,128)(2,1)S(1)} %get-tuple-element.79.refs_4_), channel_id=1, source_target_pairs={{0,16},{8,24},{16,0},{24,8},{1,17},{9,25},{17,1},{25,9},{2,18},{10... | collective-permute-start | bytes 1572872 | tf_op jit(solution)/shard_map/ppermute | solution.py:437
  109.7 12.3 %collective-permute-start.17 = (bf16[512,512]{1,0:T(8,128)(2,1)S(1)}, bf16[512,512]{1,0:T(8,128)(2,1)S(1)}, u32[]{:S(2)}, u32[]{:S(2)}) collective-permute-start(bf16[512,512]{1,0:T(8,128)(2,1)S(1)} %get-tuple-element.72.refs_0_), channel_id=1, source_target_pairs={{0,8},{8,0},{16,24},{24,16},{1,9},{9,1},{17,25},{25,17},{2,10},{10... | collective-permute-start | bytes 1572872 | tf_op jit(solution)/shard_map/ppermute | solution.py:439
  109.7 12.3 %collective-permute-start.23 = (bf16[512,512]{1,0:T(8,128)(2,1)S(1)}, bf16[512,512]{1,0:T(8,128)(2,1)S(1)}, u32[]{:S(2)}, u32[]{:S(2)}) collective-permute-start(bf16[512,512]{1,0:T(8,128)(2,1)S(1)} %get-tuple-element.79.refs_4_), channel_id=1, source_target_pairs={{0,8},{8,0},{16,24},{24,16},{1,9},{9,1},{17,25},{25,17},{2,10},{10... | collective-permute-start | bytes 1572872 | tf_op jit(solution)/shard_map/ppermute | solution.py:439
  110.2 11.8 %collective-permute-start.19 = (bf16[512,512]{1,0:T(8,128)(2,1)S(1)}, bf16[512,512]{1,0:T(8,128)(2,1)S(1)}, u32[]{:S(2)}, u32[]{:S(2)}) collective-permute-start(bf16[512,512]{1,0:T(8,128)(2,1)S(1)} %collective-permute-done.18.refs_2_), channel_id=1, source_target_pairs={{0,8},{8,0},{16,24},{24,16},{1,9},{9,1},{17,25},{25,17},{2,10},{10... | collective-permute-start | bytes 1572872 | tf_op jit(solution)/shard_map/ppermute | solution.py:439
  120.3 1.9 %collective-permute-start.25 = (bf16[512,512]{1,0:T(8,128)(2,1)S(1)}, bf16[512,512]{1,0:T(8,128)(2,1)S(1)}, u32[]{:S(2)}, u32[]{:S(2)}) collective-permute-start(bf16[512,512]{1,0:T(8,128)(2,1)S(1)} %collective-permute-done.24.refs_6_), channel_id=1, source_target_pairs={{0,8},{8,0},{16,24},{24,16},{1,9},{9,1},{17,25},{25,17},{2,10},{10... | collective-permute-start | bytes 1572872 | tf_op jit(solution)/shard_map/ppermute | solution.py:439
  120.3 1.9 %copy-start.6 = (s32[4]{0:T(128)S(1)}, s32[4]{0:T(128)}, u32[]{:S(2)}) copy-start(s32[4]{0:T(128)} %numerator_ref.1) | copy-start | bytes 52
  (2 other events, 3.8 us)

commit v11 on v10

--- a/solution.py
+++ b/solution.py
@@ -371,7 +371,8 @@
         moment_a = beta_one * a_ref[...] + (1.0 - beta_one) * gradient
         moment_b = beta_two * b_ref[...] + (1.0 - beta_two) * gradient * gradient
         old = w_ref[...].astype(jnp.float32)
-        update = moment_a / corr_one / (jnp.sqrt(moment_b / corr_two) + adam_eps) + weight_decay * old
+        update = moment_a * (1.0 / corr_one) / (jnp.sqrt(moment_b * (1.0 / corr_two)) + adam_eps)
+        update = update + weight_decay * old
         a_out[...] = moment_a
         b_out[...] = moment_b
         stepped[...] = (old - learn_rate * update).astype(jnp.bfloat16)
@@ -420,7 +421,19 @@
 
     local = pl.BlockSpec((size, columns), lambda g, *scalars: (g, 0))
     full = pl.BlockSpec((size, chunks * columns), lambda g, *scalars: (g, 0))
-    ins = [(a, local) for h in range(chunks) for a in (stepped[h], *others[h])]
+    chosen = [
+        pl.BlockSpec(
+            (size, columns),
+            lambda g, row, numerator, partner, j=j: (
+                jnp.where((partner[0] == j + 1) | (count == 1), g, 0),
+                0,
+            ),
+        )
+        for j in range(count)
+    ]
+    ins = []
+    for h in range(chunks):
+        ins += [(stepped[h], local), *zip(others[h], chosen)]
     return call(
         kernel,
         scalars,

time: 125 us -> 125 us (level)
  no operation moved by 1% of the time
where the time goes in v11:
time: 125 us
  Pallas kernels  41.3 us (33%)
  starting transfers between devices  40.4 us (32%)
  waiting for transfers between devices  39.4 us (32%)
  local copies, waits for them, and re-layouts  2.62 us (2%)
    pallas_call x22, Pallas kernels, call(): pl.pallas_call(kernel, grid_spec=pltpu.PrefetchScalarGridSpec(num_scalar_...  41.3 us
    ppermute x14, starting transfers between devices, exchange(): lax.ppermute(bufs[name], 'fsdp', links[name])  28.7 us
    ppermute x2, waiting for transfers between devices, send(): return swap(pack(plan, row, rows, [], act, turns, after))  21.8 us
    ppermute x2, waiting for transfers between devices, partner_rows(): far = lax.ppermute(stepped, 'rep', [(r, r ^ 2) for r in range(4)])  10.1 us
    ppermute x14, waiting for transfers between devices, exchange(): lax.ppermute(bufs[name], 'fsdp', links[name])  7.23 us
    ppermute x2, starting transfers between devices, partner_rows(): far = lax.ppermute(stepped, 'rep', [(r, r ^ 2) for r in range(4)])  3.04 us
    ppermute x1, starting transfers between devices, per_device(): parcel = swap(cot)  3 us
  transfers between devices with their start and end apart: 26, of which 8 were waited for; matrix products, arithmetic and copies ran while one was open for 1% of the time, Pallas kernels for 31%

profile of v11, /device:TPU:0, one launch (start us, length us, event | category | flops | bytes accessed | tf_op | source)
XLA Modules:
  0.0 124.6 jit_solution(12906425089393546170)
XLA Ops:
  0.6 3.0 %collective-permute-start.3 = (bf16[384,1024]{1,0:T(8,128)(2,1)}, bf16[384,1024]{1,0:T(8,128)(2,1)S(1)}, u32[]{:S(2)}, u32[]{:S(2)}) collective-permute-start(bf16[384,1024]{1,0:T(8,128)(2,1)} %bitcast.33), channel_id=1, source_target_pairs={{0,1},{1,0},{2,3},{3,2},{4,5},{5,4},{6,7},{7,6},{8,9},{9,8},{10,11... | collective-permute-start | bytes 2359304 | tf_op jit(solution)/shard_map/ppermute | solution.py:491
  4.4 4.4 %collective-permute-start = (bf16[512,1024]{1,0:T(8,128)(2,1)}, bf16[512,1024]{1,0:T(8,128)(2,1)S(1)}, u32[]{:S(2)}, u32[]{:S(2)}) collective-permute-start(bf16[512,1024]{1,0:T(8,128)(2,1)} %bitcast.46), channel_id=1, source_target_pairs={{0,2},{1,3},{2,0},{3,1},{4,6},{5,7},{6,4},{7,5},{8,10},{9,11},{10,... | collective-permute-start | bytes 3145736 | tf_op jit(solution)/shard_map/ppermute | solution.py:475
  9.5 1.9 %copy-done = bf16[1,384,4096]{2,1,0:T(8,128)(2,1)S(1)} copy-done((bf16[1,384,4096]{2,1,0:T(8,128)(2,1)S(1)}, bf16[1,384,4096]{2,1,0:T(8,128)(2,1)}, u32[]{:S(2)}) %copy-start) | copy-done | bytes 3145752
  12.5 17.3 %collective-permute-done.2.refs_4_.refs_3_.refs_6_.refs_2_ = bf16[384,512]{1,0:T(8,128)(2,1)S(1)} collective-permute-done((bf16[384,512]{1,0:T(8,128)(2,1)S(1)}, bf16[384,512]{1,0:T(8,128)(2,1)S(1)}, u32[]{:S(2)}, u32[]{:S(2)}) %collective-permute-start.2) | collective-permute-done | bytes 393248 | tf_op jit(solution)/shard_map/ppermute | solution.py:489
  30.4 1.8 %collective-permute-start.6 = (bf16[384,1024]{1,0:T(8,128)(2,1)S(1)}, bf16[384,1024]{1,0:T(8,128)(2,1)S(1)}, u32[]{:S(2)}, u32[]{:S(2)}) collective-permute-start(bf16[384,1024]{1,0:T(8,128)(2,1)S(1)} %shard_map.121), channel_id=1, source_target_pairs={{0,1},{1,0},{2,3},{3,2},{4,5},{5,4},{6,7},{7,6},{8,9},{9,8},{10,11... | collective-permute-start | bytes 2359304 | tf_op jit(solution)/shard_map/ppermute | solution.py:489
  32.3 1.5 %shard_map.120 = (bf16[512,512]{1,0:T(8,128)(2,1)S(1)}, bf16[512,512]{1,0:T(8,128)(2,1)S(1)}) custom-call(s32[40]{0:T(128)S(1)} %dynamic-slice_bitcast_fusion.row_ref, bf16[512,1024]{1,0:T(8,128)(2,1)S(1)} %collective-permute-done.1.refs_0_.refs_1_, bf16[512,1024]{1,0:T(8,128)(2,1)S(1)} %collective-permute-done.refs_1_.refs_0_, ...), custom_call_target="tpu_custom_call" | custom-call | tf_op jit(solution)/shard_map/pallas_call | solution.py:86
  34.6 3.8 %collective-permute-start.5 = (bf16[512,512]{1,0:T(8,128)(2,1)S(1)}, bf16[512,512]{1,0:T(8,128)(2,1)S(1)}, u32[]{:S(2)}, u32[]{:S(2)}) collective-permute-start(bf16[512,512]{1,0:T(8,128)(2,1)S(1)} %get-tuple-element.45.refs_7_), channel_id=1, source_target_pairs={{0,2},{1,3},{2,0},{3,1},{4,6},{5,7},{6,4},{7,5},{8,10},{9,11},{10,... | collective-permute-start | bytes 1572872 | tf_op jit(solution)/shard_map/ppermute | solution.py:475
  38.5 2.4 %shard_map.123 = (bf16[384,4096]{1,0:T(8,128)(2,1)}, bf16[384,512]{1,0:T(8,128)(2,1)S(1)}, bf16[512,1024]{1,0:T(8,128)(2,1)S(1)}) custom-call(s32[40]{0:T(128)S(1)} %dynamic-slice_bitcast_fusion.row_ref, bf16[512,1024]{1,0:T(8,128)(2,1)S(1)} %bitcast.47, ...), custom_call_target="tpu_custom_call" | custom-call | tf_op jit(solution)/shard_map/pallas_call | solution.py:86
  40.9 1.5 %shard_map.122 = (bf16[512,512]{1,0:T(8,128)(2,1)S(1)}, bf16[512,512]{1,0:T(8,128)(2,1)S(1)}) custom-call(s32[40]{0:T(128)S(1)} %dynamic-slice_bitcast_fusion.row_ref, bf16[512,1024]{1,0:T(8,128)(2,1)S(1)} %collective-permute-done.1.refs_0_.refs_1_, bf16[512,1024]{1,0:T(8,128)(2,1)S(1)} %collective-permute-done.refs_1_.refs_0_, ...), custom_call_target="tpu_custom_call" | custom-call | tf_op jit(solution)/shard_map/pallas_call | solution.py:86
  43.2 1.5 %collective-permute-start.9 = (bf16[512,512]{1,0:T(8,128)(2,1)S(1)}, bf16[512,512]{1,0:T(8,128)(2,1)S(1)}, u32[]{:S(2)}, u32[]{:S(2)}) collective-permute-start(bf16[512,512]{1,0:T(8,128)(2,1)S(1)} %get-tuple-element.46.refs_8_), channel_id=1, source_target_pairs={{0,2},{1,3},{2,0},{3,1},{4,6},{5,7},{6,4},{7,5},{8,10},{9,11},{10,... | collective-permute-start | bytes 1572872 | tf_op jit(solution)/shard_map/ppermute | solution.py:475
  44.7 4.5 %collective-permute-done.6.refs_5_.refs_2_.refs_7_.refs_8_.refs_3_.refs_4_.refs_6_ = bf16[384,1024]{1,0:T(8,128)(2,1)S(1)} collective-permute-done((bf16[384,1024]{1,0:T(8,128)(2,1)S(1)}, bf16[384,1024]{1,0:T(8,128)(2,1)S(1)}, u32[]{:S(2)}, u32[]{:S(2)}) %collective-permute-start.6) | collective-permute-done | bytes 786464 | tf_op jit(solution)/shard_map/ppermute | solution.py:489
  51.3 2.4 %shard_map.124 = (bf16[384,4096]{1,0:T(8,128)(2,1)}, bf16[384,512]{1,0:T(8,128)(2,1)S(1)}, bf16[512,1024]{1,0:T(8,128)(2,1)S(1)}) custom-call(s32[40]{0:T(128)S(1)} %dynamic-slice_bitcast_fusion.row_ref, bf16[512,1024]{1,0:T(8,128)(2,1)S(1)} %collective-permute-done.refs_1_.refs_0_, ...), custom_call_target="tpu_custom_call", output_to_operand_aliasing={{0}: (6, {})} | custom-call | tf_op jit(solution)/shard_map/pallas_call | solution.py:86
  56.0 4.4 %collective-permute-start.7 = (bf16[512,512]{1,0:T(8,128)(2,1)S(1)}, bf16[512,512]{1,0:T(8,128)(2,1)S(1)}, u32[]{:S(2)}, u32[]{:S(2)}) collective-permute-start(bf16[512,512]{1,0:T(8,128)(2,1)S(1)} %get-tuple-element.49.refs_8_), channel_id=1, source_target_pairs={{0,2},{1,3},{2,0},{3,1},{4,6},{5,7},{6,4},{7,5},{8,10},{9,11},{10,... | collective-permute-start | bytes 1572872 | tf_op jit(solution)/shard_map/ppermute | solution.py:475
  63.8 3.5 %collective-permute-start.10 = (bf16[512,512]{1,0:T(8,128)(2,1)S(1)}, bf16[512,512]{1,0:T(8,128)(2,1)S(1)}, u32[]{:S(2)}, u32[]{:S(2)}) collective-permute-start(bf16[512,512]{1,0:T(8,128)(2,1)S(1)} %get-tuple-element.51.refs_9_), channel_id=1, source_target_pairs={{0,2},{1,3},{2,0},{3,1},{4,6},{5,7},{6,4},{7,5},{8,10},{9,11},{10,... | collective-permute-start | bytes 1572872 | tf_op jit(solution)/shard_map/ppermute | solution.py:475
  67.3 2.5 %shard_map.127 = (bf16[384,4096]{1,0:T(8,128)(2,1)}, bf16[384,512]{1,0:T(8,128)(2,1)S(1)}, bf16[512,1024]{1,0:T(8,128)(2,1)S(1)}) custom-call(s32[40]{0:T(128)S(1)} %dynamic-slice_bitcast_fusion.row_ref, bf16[512,512]{1,0:T(8,128)(2,1)S(1)} %collective-permute-done.5.refs_1_.refs_0_, ...), custom_call_target="tpu_custom_call", output_to_operand_aliasing={{0}: (8, {})} | custom-call | tf_op jit(solution)/shard_map/pallas_call | solution.py:86
  71.0 2.3 %collective-permute-done.7.refs_1_ = bf16[512,512]{1,0:T(8,128)(2,1)S(1)} collective-permute-done((bf16[512,512]{1,0:T(8,128)(2,1)S(1)}, bf16[512,512]{1,0:T(8,128)(2,1)S(1)}, u32[]{:S(2)}, u32[]{:S(2)}) %collective-permute-start.7) | collective-permute-done | bytes 524320 | tf_op jit(solution)/shard_map/ppermute | solution.py:475
  75.5 4.5 %collective-permute-start.15 = (bf16[512,512]{1,0:T(8,128)(2,1)S(1)}, bf16[512,512]{1,0:T(8,128)(2,1)S(1)}, u32[]{:S(2)}, u32[]{:S(2)}) collective-permute-start(bf16[512,512]{1,0:T(8,128)(2,1)S(1)} %get-tuple-element.70.refs_9_), channel_id=1, source_target_pairs={{0,2},{1,3},{2,0},{3,1},{4,6},{5,7},{6,4},{7,5},{8,10},{9,11},{10,... | collective-permute-start | bytes 1572872 | tf_op jit(solution)/shard_map/ppermute | solution.py:475
  79.9 1.8 %shard_map.136.grad_ref.refs_11_ = f32[512,1024]{1,0:T(8,128)S(1)} custom-call(s32[40]{0:T(128)S(1)} %dynamic-slice_bitcast_fusion.row_ref, bf16[384,4096]{1,0:T(8,128)(2,1)S(1)} %bitcast.26, bf16[384,1024]{1,0:T(8,128)(2,1)S(1)} %collective-permute-done.11.refs_9_.refs_5_.refs_2_.refs_0_.piece_ref, bf16[384,1024]{1,0:T(8,128)(2,1)S(1)} %bitcast.42, ...), custom_call_target="tpu_custom_call" | custom-call | tf_op jit(solution)/shard_map/pallas_call | solution.py:86
  81.8 3.9 %shard_map.130 = (f32[384,1024]{1,0:T(8,128)S(1)}, f32[384,1024]{1,0:T(8,128)S(1)}) custom-call(s32[40]{0:T(128)S(1)} %dynamic-slice_bitcast_fusion.row_ref, bf16[512,1024]{1,0:T(8,128)(2,1)S(1)} %get-tuple-element.56.refs_0_, bf16[512,1024]{1,0:T(8,128)(2,1)S(1)} %get-tuple-element.57.refs_1_, bf16[512,1024]{1,0:T(8,128)(2,1)S(1)} %get-tuple-element.58.refs_2_, ...), custom_call_target="tpu_custom_call" | custom-call | tf_op jit(solution)/shard_map/pallas_call | solution.py:86
  85.7 1.5 %shard_map.138 = (bf16[512,512]{1,0:T(8,128)(2,1)S(1)}, bf16[512,512]{1,0:T(8,128)(2,1)S(1)}) custom-call(s32[40]{0:T(128)S(1)} %dynamic-slice_bitcast_fusion.row_ref, bf16[512,512]{1,0:T(8,128)(2,1)S(1)} %collective-permute-done.20.refs_0_, bf16[512,512]{1,0:T(8,128)(2,1)S(1)} %collective-permute-done.10.refs_2_.refs_1_, bf16[384,4096]{1,0:T(8,128)(2,1)S(1)} %bitcast.30, ...), custom_call_target="tpu_custom_call" | custom-call | tf_op jit(solution)/shard_map/pallas_call | solution.py:86
  87.2 1.6 %collective-permute-start.21 = (bf16[512,512]{1,0:T(8,128)(2,1)S(1)}, bf16[512,512]{1,0:T(8,128)(2,1)S(1)}, u32[]{:S(2)}, u32[]{:S(2)}) collective-permute-start(bf16[512,512]{1,0:T(8,128)(2,1)S(1)} %get-tuple-element.74), channel_id=1, source_target_pairs={{0,2},{1,3},{2,0},{3,1},{4,6},{5,7},{6,4},{7,5},{8,10},{9,11},{10,... | collective-permute-start | bytes 1572872 | tf_op jit(solution)/shard_map/ppermute | solution.py:475
  89.5 2.5 %shard_map.128 = (bf16[384,4096]{1,0:T(8,128)(2,1)}, bf16[384,512]{1,0:T(8,128)(2,1)S(1)}, bf16[512,1024]{1,0:T(8,128)(2,1)S(1)}) custom-call(s32[40]{0:T(128)S(1)} %dynamic-slice_bitcast_fusion.row_ref, bf16[512,1024]{1,0:T(8,128)(2,1)S(1)} %collective-permute-done.refs_1_.refs_0_, ...), custom_call_target="tpu_custom_call", output_to_operand_aliasing={{0}: (7, {})} | custom-call | tf_op jit(solution)/shard_map/pallas_call | solution.py:86
  92.1 1.9 %shard_map.131 = (f32[384,1024]{1,0:T(8,128)S(1)}, bf16[384,1536]{1,0:T(8,128)(2,1)S(1)}) custom-call(s32[40]{0:T(128)S(1)} %dynamic-slice_bitcast_fusion.row_ref, bf16[512,1024]{1,0:T(8,128)(2,1)S(1)} %get-tuple-element.54.refs_0_, bf16[384,4096]{1,0:T(8,128)(2,1)S(1)} %bitcast.32, ...), custom_call_target="tpu_custom_call" | custom-call | tf_op jit(solution)/shard_map/pallas_call | solution.py:86
  95.7 3.1 %shard_map.137 = (f32[512,1024]{1,0:T(8,128)}, f32[512,1024]{1,0:T(8,128)}, bf16[512,512]{1,0:T(8,128)(2,1)S(1)}) custom-call(s32[40]{0:T(128)S(1)} %dynamic-slice_bitcast_fusion.row_ref, bf16[512,512]{1,0:T(8,128)(2,1)S(1)} %collective-permute-done.15.up_ref, bf16[512,512]{1,0:T(8,128)(2,1)S(1)} %collective-permute-done.16.dn_ref, ...), custom_call_target="tpu_custom_call" | custom-call | tf_op jit(solution)/shard_map/pallas_call | solution.py:86
  98.8 1.5 %collective-permute-start.18 = (bf16[512,512]{1,0:T(8,128)(2,1)S(1)}, bf16[512,512]{1,0:T(8,128)(2,1)S(1)}, u32[]{:S(2)}, u32[]{:S(2)}) collective-permute-start(bf16[512,512]{1,0:T(8,128)(2,1)S(1)} %get-tuple-element.72.refs_0_), channel_id=1, source_target_pairs={{0,16},{8,24},{16,0},{24,8},{1,17},{9,25},{17,1},{25,9},{2,18},{10... | collective-permute-start | bytes 1572872 | tf_op jit(solution)/shard_map/ppermute | solution.py:450
  100.3 2.2 %shard_map.133 = (bf16[384,4096]{1,0:T(8,128)(2,1)}, f32[8,128]{1,0:T(8,128)S(1)}) custom-call(s32[40]{0:T(128)S(1)} %dynamic-slice_bitcast_fusion.row_ref, bf16[384,1024]{1,0:T(8,128)(2,1)S(1)} %collective-permute-done.11.refs_9_.refs_5_.refs_2_.refs_0_.piece_ref, ...), custom_call_target="tpu_custom_call", output_to_operand_aliasing={{0}: (4, {})} | custom-call | tf_op jit(solution)/shard_map/pallas_call | solution.py:86
  102.5 2.6 %collective-permute-done.21.up_ref = bf16[512,512]{1,0:T(8,128)(2,1)S(1)} collective-permute-done((bf16[512,512]{1,0:T(8,128)(2,1)S(1)}, bf16[512,512]{1,0:T(8,128)(2,1)S(1)}, u32[]{:S(2)}, u32[]{:S(2)}) %collective-permute-start.21) | collective-permute-done | bytes 524320 | tf_op jit(solution)/shard_map/ppermute | solution.py:475
  105.2 3.1 %shard_map.139 = (f32[512,1024]{1,0:T(8,128)}, f32[512,1024]{1,0:T(8,128)}, bf16[512,512]{1,0:T(8,128)(2,1)S(1)}) custom-call(s32[40]{0:T(128)S(1)} %dynamic-slice_bitcast_fusion.row_ref, bf16[512,512]{1,0:T(8,128)(2,1)S(1)} %collective-permute-done.21.up_ref, ...), custom_call_target="tpu_custom_call", output_to_operand_aliasing={{0}: (7, {}), {1}: (8, {})} | custom-call | tf_op jit(solution)/shard_map/pallas_call | solution.py:86
  108.2 1.5 %collective-permute-start.24 = (bf16[512,512]{1,0:T(8,128)(2,1)S(1)}, bf16[512,512]{1,0:T(8,128)(2,1)S(1)}, u32[]{:S(2)}, u32[]{:S(2)}) collective-permute-start(bf16[512,512]{1,0:T(8,128)(2,1)S(1)} %get-tuple-element.79.refs_4_), channel_id=1, source_target_pairs={{0,16},{8,24},{16,0},{24,8},{1,17},{9,25},{17,1},{25,9},{2,18},{10... | collective-permute-start | bytes 1572872 | tf_op jit(solution)/shard_map/ppermute | solution.py:450
  110.2 10.1 %collective-permute-done.24.refs_6_ = bf16[512,512]{1,0:T(8,128)(2,1)S(1)} collective-permute-done((bf16[512,512]{1,0:T(8,128)(2,1)S(1)}, bf16[512,512]{1,0:T(8,128)(2,1)S(1)}, u32[]{:S(2)}, u32[]{:S(2)}) %collective-permute-start.24) | collective-permute-done | bytes 524320 | tf_op jit(solution)/shard_map/ppermute | solution.py:450
  120.4 1.7 %shard_map.134 = (bf16[384,4096]{1,0:T(8,128)(2,1)}, f32[8,128]{1,0:T(8,128)S(1)}, bf16[384,1024]{1,0:T(8,128)(2,1)}) custom-call(s32[40]{0:T(128)S(1)} %dynamic-slice_bitcast_fusion.row_ref, bf16[384,1536]{1,0:T(8,128)(2,1)S(1)} %collective-permute-done.12.refs_0_.refs_2_, ...), custom_call_target="tpu_custom_call", output_to_operand_aliasing={{0}: (4, {})} | custom-call | tf_op jit(solution)/shard_map/pallas_call | solution.py:86
  122.3 2.4 %shard_map.140 = bf16[512,1024]{1,0:T(8,128)(2,1)} custom-call(s32[40]{0:T(128)S(1)} %dynamic-slice_bitcast_fusion.row_ref, s32[4]{0:T(128)S(1)} %copy-done.6, s32[4]{0:T(128)S(1)} %copy-done.7, bf16[512,512]{1,0:T(8,128)(2,1)S(1)} %get-tuple-element.72.refs_0_, bf16[512,512]{1,0:T(8,128)(2,1)S(1)} %collective-permute-done.17.refs_1_, ...), custom_call_target="tpu_custom_call" | custom-call | tf_op jit(solution)/shard_map/pallas_call | solution.py:86
  (59 shorter events, 18.9 us)
Async XLA Ops:
  0.6 29.2 %collective-permute-start.3 = (bf16[384,1024]{1,0:T(8,128)(2,1)}, bf16[384,1024]{1,0:T(8,128)(2,1)S(1)}, u32[]{:S(2)}, u32[]{:S(2)}) collective-permute-start(bf16[384,1024]{1,0:T(8,128)(2,1)} %bitcast.33), channel_id=1, source_target_pairs={{0,1},{1,0},{2,3},{3,2},{4,5},{5,4},{6,7},{7,6},{8,9},{9,8},{10,11... | collective-permute-start | bytes 2359304 | tf_op jit(solution)/shard_map/ppermute | solution.py:491
  3.6 28.6 %collective-permute-start.1 = (bf16[512,1024]{1,0:T(8,128)(2,1)}, bf16[512,1024]{1,0:T(8,128)(2,1)S(1)}, u32[]{:S(2)}, u32[]{:S(2)}) collective-permute-start(bf16[512,1024]{1,0:T(8,128)(2,1)} %bitcast.45), channel_id=1, source_target_pairs={{2,4},{3,5},{4,2},{5,3},{10,12},{11,13},{12,10},{13,11},{18,20},{1... | collective-permute-start | bytes 3145736 | tf_op jit(solution)/shard_map/ppermute | solution.py:475
  4.4 27.9 %collective-permute-start = (bf16[512,1024]{1,0:T(8,128)(2,1)}, bf16[512,1024]{1,0:T(8,128)(2,1)S(1)}, u32[]{:S(2)}, u32[]{:S(2)}) collective-permute-start(bf16[512,1024]{1,0:T(8,128)(2,1)} %bitcast.46), channel_id=1, source_target_pairs={{0,2},{1,3},{2,0},{3,1},{4,6},{5,7},{6,4},{7,5},{8,10},{9,11},{10,... | collective-permute-start | bytes 3145736 | tf_op jit(solution)/shard_map/ppermute | solution.py:475
  11.9 20.3 %copy-start.2 = (bf16[1,384,1024]{2,1,0:T(8,128)(2,1)S(1)}, bf16[1,384,1024]{2,1,0:T(8,128)(2,1)}, u32[]{:S(2)}) copy-start(bf16[1,384,1024]{2,1,0:T(8,128)(2,1)} %param.10) | copy-start | bytes 2359300
  11.9 17.9 %collective-permute-start.2 = (bf16[384,512]{1,0:T(8,128)(2,1)S(1)}, bf16[384,512]{1,0:T(8,128)(2,1)S(1)}, u32[]{:S(2)}, u32[]{:S(2)}) collective-permute-start(bf16[384,512]{1,0:T(8,128)(2,1)S(1)} %shard_map.119), channel_id=1, source_target_pairs={{0,1},{1,0},{2,3},{3,2},{4,5},{5,4},{6,7},{7,6},{8,9},{9,8},{10,11... | collective-permute-start | bytes 1179656 | tf_op jit(solution)/shard_map/ppermute | solution.py:489
  30.4 8.1 %copy-start.3 = (bf16[1,512,1024]{2,1,0:T(8,128)(2,1)S(1)}, bf16[1,512,1024]{2,1,0:T(8,128)(2,1)}, u32[]{:S(2)}) copy-start(bf16[1,512,1024]{2,1,0:T(8,128)(2,1)} %param.9) | copy-start | bytes 3145732
  30.4 18.8 %collective-permute-start.6 = (bf16[384,1024]{1,0:T(8,128)(2,1)S(1)}, bf16[384,1024]{1,0:T(8,128)(2,1)S(1)}, u32[]{:S(2)}, u32[]{:S(2)}) collective-permute-start(bf16[384,1024]{1,0:T(8,128)(2,1)S(1)} %shard_map.121), channel_id=1, source_target_pairs={{0,1},{1,0},{2,3},{3,2},{4,5},{5,4},{6,7},{7,6},{8,9},{9,8},{10,11... | collective-permute-start | bytes 2359304 | tf_op jit(solution)/shard_map/ppermute | solution.py:489
  33.8 7.1 %copy-start.1 = (bf16[1,384,4096]{2,1,0:T(8,128)(2,1)S(1)}, bf16[1,384,4096]{2,1,0:T(8,128)(2,1)}, u32[]{:S(2)}) copy-start(bf16[1,384,4096]{2,1,0:T(8,128)(2,1)} %param.8) | copy-start | bytes 9437188
  33.8 20.0 %collective-permute-start.4 = (bf16[512,512]{1,0:T(8,128)(2,1)S(1)}, bf16[512,512]{1,0:T(8,128)(2,1)S(1)}, u32[]{:S(2)}, u32[]{:S(2)}) collective-permute-start(bf16[512,512]{1,0:T(8,128)(2,1)S(1)} %get-tuple-element.44), channel_id=1, source_target_pairs={{2,4},{3,5},{4,2},{5,3},{10,12},{11,13},{12,10},{13,11},{18,20},{1... | collective-permute-start | bytes 1572872 | tf_op jit(solution)/shard_map/ppermute | solution.py:475
  34.6 19.1 %collective-permute-start.5 = (bf16[512,512]{1,0:T(8,128)(2,1)S(1)}, bf16[512,512]{1,0:T(8,128)(2,1)S(1)}, u32[]{:S(2)}, u32[]{:S(2)}) collective-permute-start(bf16[512,512]{1,0:T(8,128)(2,1)S(1)} %get-tuple-element.45.refs_7_), channel_id=1, source_target_pairs={{0,2},{1,3},{2,0},{3,1},{4,6},{5,7},{6,4},{7,5},{8,10},{9,11},{10,... | collective-permute-start | bytes 1572872 | tf_op jit(solution)/shard_map/ppermute | solution.py:475
  42.5 17.9 %collective-permute-start.8 = (bf16[512,512]{1,0:T(8,128)(2,1)S(1)}, bf16[512,512]{1,0:T(8,128)(2,1)S(1)}, u32[]{:S(2)}, u32[]{:S(2)}) collective-permute-start(bf16[512,512]{1,0:T(8,128)(2,1)S(1)} %get-tuple-element.50), channel_id=1, source_target_pairs={{2,4},{3,5},{4,2},{5,3},{10,12},{11,13},{12,10},{13,11},{18,20},{1... | collective-permute-start | bytes 1572872 | tf_op jit(solution)/shard_map/ppermute | solution.py:475
  43.2 18.4 %collective-permute-start.9 = (bf16[512,512]{1,0:T(8,128)(2,1)S(1)}, bf16[512,512]{1,0:T(8,128)(2,1)S(1)}, u32[]{:S(2)}, u32[]{:S(2)}) collective-permute-start(bf16[512,512]{1,0:T(8,128)(2,1)S(1)} %get-tuple-element.46.refs_8_), channel_id=1, source_target_pairs={{0,2},{1,3},{2,0},{3,1},{4,6},{5,7},{6,4},{7,5},{8,10},{9,11},{10,... | collective-permute-start | bytes 1572872 | tf_op jit(solution)/shard_map/ppermute | solution.py:475
  49.8 20.0 %collective-permute-start.11 = (bf16[384,1024]{1,0:T(8,128)(2,1)S(1)}, bf16[384,1024]{1,0:T(8,128)(2,1)S(1)}, u32[]{:S(2)}, u32[]{:S(2)}) collective-permute-start(bf16[384,1024]{1,0:T(8,128)(2,1)S(1)} %shard_map.129), channel_id=1, source_target_pairs={{0,1},{1,0},{2,3},{3,2},{4,5},{5,4},{6,7},{7,6},{8,9},{9,8},{10,11... | collective-permute-start | bytes 2359304 | tf_op jit(solution)/shard_map/ppermute | solution.py:510
  55.3 15.7 %collective-permute-start.14 = (bf16[512,512]{1,0:T(8,128)(2,1)S(1)}, bf16[512,512]{1,0:T(8,128)(2,1)S(1)}, u32[]{:S(2)}, u32[]{:S(2)}) collective-permute-start(bf16[512,512]{1,0:T(8,128)(2,1)S(1)} %get-tuple-element.69), channel_id=1, source_target_pairs={{2,4},{3,5},{4,2},{5,3},{10,12},{11,13},{12,10},{13,11},{18,20},{1... | collective-permute-start | bytes 1572872 | tf_op jit(solution)/shard_map/ppermute | solution.py:475
  56.0 17.3 %collective-permute-start.7 = (bf16[512,512]{1,0:T(8,128)(2,1)S(1)}, bf16[512,512]{1,0:T(8,128)(2,1)S(1)}, u32[]{:S(2)}, u32[]{:S(2)}) collective-permute-start(bf16[512,512]{1,0:T(8,128)(2,1)S(1)} %get-tuple-element.49.refs_8_), channel_id=1, source_target_pairs={{0,2},{1,3},{2,0},{3,1},{4,6},{5,7},{6,4},{7,5},{8,10},{9,11},{10,... | collective-permute-start | bytes 1572872 | tf_op jit(solution)/shard_map/ppermute | solution.py:475
  63.1 22.6 %collective-permute-start.20 = (bf16[512,512]{1,0:T(8,128)(2,1)S(1)}, bf16[512,512]{1,0:T(8,128)(2,1)S(1)}, u32[]{:S(2)}, u32[]{:S(2)}) collective-permute-start(bf16[512,512]{1,0:T(8,128)(2,1)S(1)} %get-tuple-element.73), channel_id=1, source_target_pairs={{2,4},{3,5},{4,2},{5,3},{10,12},{11,13},{12,10},{13,11},{18,20},{1... | collective-permute-start | bytes 1572872 | tf_op jit(solution)/shard_map/ppermute | solution.py:475
  63.8 21.9 %collective-permute-start.10 = (bf16[512,512]{1,0:T(8,128)(2,1)S(1)}, bf16[512,512]{1,0:T(8,128)(2,1)S(1)}, u32[]{:S(2)}, u32[]{:S(2)}) collective-permute-start(bf16[512,512]{1,0:T(8,128)(2,1)S(1)} %get-tuple-element.51.refs_9_), channel_id=1, source_target_pairs={{0,2},{1,3},{2,0},{3,1},{4,6},{5,7},{6,4},{7,5},{8,10},{9,11},{10,... | collective-permute-start | bytes 1572872 | tf_op jit(solution)/shard_map/ppermute | solution.py:475
  70.4 29.9 %collective-permute-start.13 = (bf16[384,1024]{1,0:T(8,128)(2,1)S(1)}, bf16[384,1024]{1,0:T(8,128)(2,1)S(1)}, u32[]{:S(2)}, u32[]{:S(2)}) collective-permute-start(bf16[384,1024]{1,0:T(8,128)(2,1)S(1)} %shard_map.132), channel_id=1, source_target_pairs={{0,1},{1,0},{2,3},{3,2},{4,5},{5,4},{6,7},{7,6},{8,9},{9,8},{10,11... | collective-permute-start | bytes 2359304 | tf_op jit(solution)/shard_map/ppermute | solution.py:510
  74.8 19.2 %collective-permute-start.16 = (bf16[512,512]{1,0:T(8,128)(2,1)S(1)}, bf16[512,512]{1,0:T(8,128)(2,1)S(1)}, u32[]{:S(2)}, u32[]{:S(2)}) collective-permute-start(bf16[512,512]{1,0:T(8,128)(2,1)S(1)} %get-tuple-element.71), channel_id=1, source_target_pairs={{2,4},{3,5},{4,2},{5,3},{10,12},{11,13},{12,10},{13,11},{18,20},{1... | collective-permute-start | bytes 1572872 | tf_op jit(solution)/shard_map/ppermute | solution.py:475
  75.5 20.3 %collective-permute-start.15 = (bf16[512,512]{1,0:T(8,128)(2,1)S(1)}, bf16[512,512]{1,0:T(8,128)(2,1)S(1)}, u32[]{:S(2)}, u32[]{:S(2)}) collective-permute-start(bf16[512,512]{1,0:T(8,128)(2,1)S(1)} %get-tuple-element.70.refs_9_), channel_id=1, source_target_pairs={{0,2},{1,3},{2,0},{3,1},{4,6},{5,7},{6,4},{7,5},{8,10},{9,11},{10,... | collective-permute-start | bytes 1572872 | tf_op jit(solution)/shard_map/ppermute | solution.py:475
  87.2 17.9 %collective-permute-start.21 = (bf16[512,512]{1,0:T(8,128)(2,1)S(1)}, bf16[512,512]{1,0:T(8,128)(2,1)S(1)}, u32[]{:S(2)}, u32[]{:S(2)}) collective-permute-start(bf16[512,512]{1,0:T(8,128)(2,1)S(1)} %get-tuple-element.74), channel_id=1, source_target_pairs={{0,2},{1,3},{2,0},{3,1},{4,6},{5,7},{6,4},{7,5},{8,10},{9,11},{10,... | collective-permute-start | bytes 1572872 | tf_op jit(solution)/shard_map/ppermute | solution.py:475
  88.8 16.3 %collective-permute-start.22 = (bf16[512,512]{1,0:T(8,128)(2,1)S(1)}, bf16[512,512]{1,0:T(8,128)(2,1)S(1)}, u32[]{:S(2)}, u32[]{:S(2)}) collective-permute-start(bf16[512,512]{1,0:T(8,128)(2,1)S(1)} %get-tuple-element.75), channel_id=1, source_target_pairs={{2,4},{3,5},{4,2},{5,3},{10,12},{11,13},{12,10},{13,11},{18,20},{1... | collective-permute-start | bytes 1572872 | tf_op jit(solution)/shard_map/ppermute | solution.py:475
  92.1 3.7 %copy-start.4 = (f32[1,512,1024]{2,1,0:T(8,128)S(1)}, f32[1,512,1024]{2,1,0:T(8,128)}, u32[]{:S(2)}) copy-start(f32[1,512,1024]{2,1,0:T(8,128)} %param.11) | copy-start | bytes 6291460
  92.1 3.7 %copy-start.5 = (f32[1,512,1024]{2,1,0:T(8,128)S(1)}, f32[1,512,1024]{2,1,0:T(8,128)}, u32[]{:S(2)}) copy-start(f32[1,512,1024]{2,1,0:T(8,128)} %param.12) | copy-start | bytes 6291460
  94.0 26.3 %collective-permute-start.12 = (bf16[384,1536]{1,0:T(8,128)(2,1)S(1)}, bf16[384,1536]{1,0:T(8,128)(2,1)S(1)}, u32[]{:S(2)}, u32[]{:S(2)}) collective-permute-start(bf16[384,1536]{1,0:T(8,128)(2,1)S(1)} %get-tuple-element.62), channel_id=1, source_target_pairs={{0,1},{1,0},{2,3},{3,2},{4,5},{5,4},{6,7},{7,6},{8,9},{9,8},{10,11... | collective-permute-start | bytes 3538952 | tf_op jit(solution)/shard_map/ppermute | solution.py:535
  98.8 11.5 %collective-permute-start.18 = (bf16[512,512]{1,0:T(8,128)(2,1)S(1)}, bf16[512,512]{1,0:T(8,128)(2,1)S(1)}, u32[]{:S(2)}, u32[]{:S(2)}) collective-permute-start(bf16[512,512]{1,0:T(8,128)(2,1)S(1)} %get-tuple-element.72.refs_0_), channel_id=1, source_target_pairs={{0,16},{8,24},{16,0},{24,8},{1,17},{9,25},{17,1},{25,9},{2,18},{10... | collective-permute-start | bytes 1572872 | tf_op jit(solution)/shard_map/ppermute | solution.py:450
  108.2 12.1 %collective-permute-start.24 = (bf16[512,512]{1,0:T(8,128)(2,1)S(1)}, bf16[512,512]{1,0:T(8,128)(2,1)S(1)}, u32[]{:S(2)}, u32[]{:S(2)}) collective-permute-start(bf16[512,512]{1,0:T(8,128)(2,1)S(1)} %get-tuple-element.79.refs_4_), channel_id=1, source_target_pairs={{0,16},{8,24},{16,0},{24,8},{1,17},{9,25},{17,1},{25,9},{2,18},{10... | collective-permute-start | bytes 1572872 | tf_op jit(solution)/shard_map/ppermute | solution.py:450
  109.7 12.3 %collective-permute-start.17 = (bf16[512,512]{1,0:T(8,128)(2,1)S(1)}, bf16[512,512]{1,0:T(8,128)(2,1)S(1)}, u32[]{:S(2)}, u32[]{:S(2)}) collective-permute-start(bf16[512,512]{1,0:T(8,128)(2,1)S(1)} %get-tuple-element.72.refs_0_), channel_id=1, source_target_pairs={{0,8},{8,0},{16,24},{24,16},{1,9},{9,1},{17,25},{25,17},{2,10},{10... | collective-permute-start | bytes 1572872 | tf_op jit(solution)/shard_map/ppermute | solution.py:452
  109.7 12.3 %collective-permute-start.23 = (bf16[512,512]{1,0:T(8,128)(2,1)S(1)}, bf16[512,512]{1,0:T(8,128)(2,1)S(1)}, u32[]{:S(2)}, u32[]{:S(2)}) collective-permute-start(bf16[512,512]{1,0:T(8,128)(2,1)S(1)} %get-tuple-element.79.refs_4_), channel_id=1, source_target_pairs={{0,8},{8,0},{16,24},{24,16},{1,9},{9,1},{17,25},{25,17},{2,10},{10... | collective-permute-start | bytes 1572872 | tf_op jit(solution)/shard_map/ppermute | solution.py:452
  110.2 11.8 %collective-permute-start.19 = (bf16[512,512]{1,0:T(8,128)(2,1)S(1)}, bf16[512,512]{1,0:T(8,128)(2,1)S(1)}, u32[]{:S(2)}, u32[]{:S(2)}) collective-permute-start(bf16[512,512]{1,0:T(8,128)(2,1)S(1)} %collective-permute-done.18.refs_2_), channel_id=1, source_target_pairs={{0,8},{8,0},{16,24},{24,16},{1,9},{9,1},{17,25},{25,17},{2,10},{10... | collective-permute-start | bytes 1572872 | tf_op jit(solution)/shard_map/ppermute | solution.py:452
  120.3 1.9 %collective-permute-start.25 = (bf16[512,512]{1,0:T(8,128)(2,1)S(1)}, bf16[512,512]{1,0:T(8,128)(2,1)S(1)}, u32[]{:S(2)}, u32[]{:S(2)}) collective-permute-start(bf16[512,512]{1,0:T(8,128)(2,1)S(1)} %collective-permute-done.24.refs_6_), channel_id=1, source_target_pairs={{0,8},{8,0},{16,24},{24,16},{1,9},{9,1},{17,25},{25,17},{2,10},{10... | collective-permute-start | bytes 1572872 | tf_op jit(solution)/shard_map/ppermute | solution.py:452
  120.3 1.9 %copy-start.6 = (s32[4]{0:T(128)S(1)}, s32[4]{0:T(128)}, u32[]{:S(2)}) copy-start(s32[4]{0:T(128)} %numerator_ref.1) | copy-start | bytes 52
  (2 other events, 3.8 us)

commit v12 on v11

--- a/solution.py
+++ b/solution.py
@@ -313,24 +313,20 @@
     )
 
 
-def place(plan, row, xg, arrived, first, sums=None):
+def place(plan, row, xg, arrived):
     count = len(arrived)
     tokens, width = arrived[0].shape
-    table = [plan[f"theirs{first + j}"] for j in range(count)]
+    table = [plan[f"theirs{j}"] for j in range(count)]
 
     def kernel(row_ref, *refs):
         g = pl.program_id(0)
-        out_ref, tile_ref = refs[-2:] if sums is None else refs[-3:-1]
+        out_ref, tile_ref = refs[-2:]
+        tile_ref[...] = jnp.zeros_like(tile_ref)
         for j in range(count):
 
             @pl.when(g == j)
             def _():
                 out_ref[...] = refs[j][...]
-
-        tile_ref[...] = jnp.zeros_like(tile_ref)
-        if sums is not None:
-            total = refs[count][...] + refs[count + 1][...].astype(jnp.float32)
-            refs[-1][...] = total.astype(jnp.bfloat16)
 
     def column(g, row):
         at = row[table[0]]
@@ -338,24 +334,18 @@
             at = jnp.where(g == j, row[table[j]], at)
         return (0, at)
 
+    tile = struct((8, 128), jnp.float32)
     ins = [view.operand() for view in arrived]
-    outs = [(struct(xg.shape, xg.dtype), pl.BlockSpec((tokens, width), column))]
-    tile = struct((8, 128), jnp.float32)
-    outs.append((tile, whole(tile)))
-    if sums is not None:
-        own, other = sums
-        kv_block = pl.BlockSpec((tokens // count, own.shape[1]), lambda g, row: (g, 0))
-        assert other.start == 0
-        ins += [(own, kv_block), (other.array, kv_block)]
-        outs.append((struct(own.shape, jnp.bfloat16), kv_block))
-    aliases = {1 + len(ins): 0}
     return call(
         kernel,
         row,
         ins + [(xg, HBM)],
-        outs,
+        [
+            (struct(xg.shape, xg.dtype), pl.BlockSpec((tokens, width), column)),
+            (tile, whole(tile)),
+        ],
         grid=(count,),
-        aliases=aliases,
+        aliases={1 + len(ins): 0},
     )
 
 
@@ -400,27 +390,34 @@
     )
 
 
-def average(plan, scalars, stepped, others, after):
+def finish(plan, scalars, stepped, others, xg, piece, sums):
     rows, columns = stepped[0].shape
+    tokens, width = piece.shape
+    own, other = sums
     chunks, count = len(stepped), len(others[0])
-    steps = 4 if rows % 64 == 0 else 1
-    size = rows // steps
+    steps = 4 if rows % 64 == 0 and tokens % 64 == 0 else 1
+    size, part = rows // steps, tokens // steps
 
     def kernel(row_ref, numerator_ref, partner_ref, *refs):
+        piece_ref, own_ref, other_ref = refs[-7:-4]
+        averaged_ref, xg_ref, kv_ref = refs[-3:]
         mix = numerator_ref[row_ref[plan["replica"]]].astype(jnp.float32) / mix_denom
+        xg_ref[...] = piece_ref[...]
+        kv_ref[...] = (own_ref[...] + other_ref[...].astype(jnp.float32)).astype(jnp.bfloat16)
         for j in range(count):
 
             @pl.when((partner_ref[0] == j + 1) | (count == 1))
             def _():
                 for h in range(chunks):
-                    own, other = refs[h * (count + 1)], refs[h * (count + 1) + 1 + j]
-                    refs[-1][:, h * columns : (h + 1) * columns] = (
-                        (1.0 - mix) * own[...].astype(jnp.float32)
-                        + mix * other[...].astype(jnp.float32)
+                    mine, theirs = refs[h * (count + 1)], refs[h * (count + 1) + 1 + j]
+                    averaged_ref[:, h * columns : (h + 1) * columns] = (
+                        (1.0 - mix) * mine[...].astype(jnp.float32)
+                        + mix * theirs[...].astype(jnp.float32)
                     ).astype(jnp.bfloat16)
 
-    local = pl.BlockSpec((size, columns), lambda g, *scalars: (g, 0))
-    full = pl.BlockSpec((size, chunks * columns), lambda g, *scalars: (g, 0))
+    def lines(shape, at=0):
+        return pl.BlockSpec(shape, lambda g, *scalars: (g, at))
+
     chosen = [
         pl.BlockSpec(
             (size, columns),
@@ -431,16 +428,31 @@
         )
         for j in range(count)
     ]
+    theirs = plan[f"theirs{plan.depth - 1}"]
     ins = []
     for h in range(chunks):
-        ins += [(stepped[h], local), *zip(others[h], chosen)]
+        ins += [(stepped[h], lines((size, columns))), *zip(others[h], chosen)]
+    ins += [
+        (piece.array, lines((part, width), piece.start // width)),
+        (own, lines((part, own.shape[1]))),
+        (other.array, lines((part, other.count), other.start // other.count)),
+        (xg, HBM),
+    ]
     return call(
         kernel,
         scalars,
-        ins + [(a, ANY) for a in after],
-        [(struct((rows, chunks * columns), jnp.bfloat16), full)],
+        ins,
+        [
+            (struct((rows, chunks * columns), jnp.bfloat16), lines((size, chunks * columns))),
+            (
+                struct(xg.shape, xg.dtype),
+                pl.BlockSpec((part, width), lambda g, row, *scalars: (g, row[theirs])),
+            ),
+            (struct(own.shape, jnp.bfloat16), lines((part, own.shape[1]))),
+        ],
         grid=(steps,),
-    )[0]
+        aliases={len(scalars) + len(ins) - 1: 1},
+    )
 
 
 def partner_rows(stepped, partner, replica, n_rep):
@@ -547,13 +559,18 @@
             row, h, got[depth, h], grad, weights, first, second, moments, after
         )
         if placed is None:
-            placed, placed_tile = place(plan, row, xg, arrived, 0)
+            placed, placed_tile = place(plan, row, xg, arrived)
         stepped.append(rows_now)
         others.append(partner_rows(rows_now, partner, row[plan["replica"]], n_rep))
-    views = [View(final, columns, rows)]
-    kv_views = (kv_own, View(final, 0, columns))
-    x_grad, tile, kv_out = place(plan, row, placed, views, depth - 1, kv_views)
-    averaged = average(plan, scalars, stepped, others, [tile])
+    averaged, x_grad, kv_out = finish(
+        plan,
+        scalars,
+        stepped,
+        others,
+        placed,
+        View(final, columns, rows),
+        (kv_own, View(final, 0, columns)),
+    )
     return (
         kv_out[None],
         x_grad[None],

time: 125 us -> 128 us (1.024)
  waiting for transfers between devices: 39.4 us -> 43 us
  Pallas kernels: 41.3 us -> 40 us
    ppermute x14, waiting for transfers between devices: 7.23 us -> 9.02 us  [exchange(): lax.ppermute(bufs[name], 'fsdp', links[name])]
    ppermute x2, waiting for transfers between devices: 0.2 us -> 1.88 us  [partner_rows(): lax.ppermute(far, 'rep', core)]
    pallas_call x22 -> x21, Pallas kernels: 41.3 us -> 40 us  [call(): pl.pallas_call(kernel, grid_spec=pltpu.PrefetchScalarGridSpec(num_scalar_...]
  transfers between devices with their start and end apart: 26 -> 26, of which waited for: 8 -> 9; matrix products, arithmetic and copies ran while one was open for 1% -> 1% of each run, Pallas kernels for 31% -> 29%
where the time goes in v12:
time: 128 us; the launch traced here: 127 us
  waiting for transfers between devices  43 us (34%)
  starting transfers between devices  40.3 us (31%)
  Pallas kernels  40 us (31%)
  local copies, waits for them, and re-layouts  3.16 us (2%)
    pallas_call x21, Pallas kernels, call(): pl.pallas_call(kernel, grid_spec=pltpu.PrefetchScalarGridSpec(num_scalar_...  40 us
    ppermute x14, starting transfers between devices, exchange(): lax.ppermute(bufs[name], 'fsdp', links[name])  27.9 us
    ppermute x2, waiting for transfers between devices, send(): return swap(pack(plan, row, rows, [], act, turns, after))  22.3 us
    ppermute x2, waiting for transfers between devices, partner_rows(): far = lax.ppermute(stepped, 'rep', [(r, r ^ 2) for r in range(4)])  9.82 us
    ppermute x14, waiting for transfers between devices, exchange(): lax.ppermute(bufs[name], 'fsdp', links[name])  9.02 us
    ppermute x2, starting transfers between devices, partner_rows(): far = lax.ppermute(stepped, 'rep', [(r, r ^ 2) for r in range(4)])  3.04 us
    ppermute x1, starting transfers between devices, per_device(): parcel = swap(cot)  3 us
    ppermute x2, starting transfers between devices, send_parts(): parcel = swap(pack(plan, row, rows, views, act, turns, after))  2.72 us
  transfers between devices with their start and end apart: 26, of which 9 were waited for; matrix products, arithmetic and copies ran while one was open for 1% of the time, Pallas kernels for 29%

profile of v12, /device:TPU:0, one launch (start us, length us, event | category | flops | bytes accessed | tf_op | source)
XLA Modules:
  0.0 127.4 jit_solution(15866015128528900142)
XLA Ops:
  0.6 3.0 %collective-permute-start.3 = (bf16[384,1024]{1,0:T(8,128)(2,1)}, bf16[384,1024]{1,0:T(8,128)(2,1)S(1)}, u32[]{:S(2)}, u32[]{:S(2)}) collective-permute-start(bf16[384,1024]{1,0:T(8,128)(2,1)} %bitcast.33), channel_id=1, source_target_pairs={{0,1},{1,0},{2,3},{3,2},{4,5},{5,4},{6,7},{7,6},{8,9},{9,8},{10,11... | collective-permute-start | bytes 2359304 | tf_op jit(solution)/shard_map/ppermute | solution.py:503
  4.3 1.9 %copy-done = bf16[1,384,4096]{2,1,0:T(8,128)(2,1)S(1)} copy-done((bf16[1,384,4096]{2,1,0:T(8,128)(2,1)S(1)}, bf16[1,384,4096]{2,1,0:T(8,128)(2,1)}, u32[]{:S(2)}) %copy-start) | copy-done | bytes 3145752
  7.4 1.6 %collective-permute-start.1 = (bf16[512,1024]{1,0:T(8,128)(2,1)S(1)}, bf16[512,1024]{1,0:T(8,128)(2,1)S(1)}, u32[]{:S(2)}, u32[]{:S(2)}) collective-permute-start(bf16[512,1024]{1,0:T(8,128)(2,1)S(1)} %bitcast.45), channel_id=1, source_target_pairs={{0,2},{1,3},{2,0},{3,1},{4,6},{5,7},{6,4},{7,5},{8,10},{9,11},{10,... | collective-permute-start | bytes 3145736 | tf_op jit(solution)/shard_map/ppermute | solution.py:487
  9.7 20.1 %collective-permute-done.2.refs_4_.refs_3_.refs_6_.refs_2_ = bf16[384,512]{1,0:T(8,128)(2,1)S(1)} collective-permute-done((bf16[384,512]{1,0:T(8,128)(2,1)S(1)}, bf16[384,512]{1,0:T(8,128)(2,1)S(1)}, u32[]{:S(2)}, u32[]{:S(2)}) %collective-permute-start.2) | collective-permute-done | bytes 393248 | tf_op jit(solution)/shard_map/ppermute | solution.py:501
  30.4 1.8 %collective-permute-start.6 = (bf16[384,1024]{1,0:T(8,128)(2,1)S(1)}, bf16[384,1024]{1,0:T(8,128)(2,1)S(1)}, u32[]{:S(2)}, u32[]{:S(2)}) collective-permute-start(bf16[384,1024]{1,0:T(8,128)(2,1)S(1)} %shard_map.121), channel_id=1, source_target_pairs={{0,1},{1,0},{2,3},{3,2},{4,5},{5,4},{6,7},{7,6},{8,9},{9,8},{10,11... | collective-permute-start | bytes 2359304 | tf_op jit(solution)/shard_map/ppermute | solution.py:501
  32.2 1.5 %shard_map.120 = (bf16[512,512]{1,0:T(8,128)(2,1)S(1)}, bf16[512,512]{1,0:T(8,128)(2,1)S(1)}) custom-call(s32[40]{0:T(128)S(1)} %dynamic-slice_bitcast_fusion.row_ref, bf16[512,1024]{1,0:T(8,128)(2,1)S(1)} %collective-permute-done.refs_0_.refs_1_, bf16[512,1024]{1,0:T(8,128)(2,1)S(1)} %collective-permute-done.1.refs_1_.refs_0_, ...), custom_call_target="tpu_custom_call" | custom-call | tf_op jit(solution)/shard_map/pallas_call | solution.py:86
  34.6 6.8 %collective-permute-start.5 = (bf16[512,512]{1,0:T(8,128)(2,1)S(1)}, bf16[512,512]{1,0:T(8,128)(2,1)S(1)}, u32[]{:S(2)}, u32[]{:S(2)}) collective-permute-start(bf16[512,512]{1,0:T(8,128)(2,1)S(1)} %get-tuple-element.45.refs_7_), channel_id=1, source_target_pairs={{0,2},{1,3},{2,0},{3,1},{4,6},{5,7},{6,4},{7,5},{8,10},{9,11},{10,... | collective-permute-start | bytes 1572872 | tf_op jit(solution)/shard_map/ppermute | solution.py:487
  41.5 2.4 %shard_map.123 = (bf16[384,4096]{1,0:T(8,128)(2,1)}, bf16[384,512]{1,0:T(8,128)(2,1)S(1)}, bf16[512,1024]{1,0:T(8,128)(2,1)S(1)}) custom-call(s32[40]{0:T(128)S(1)} %dynamic-slice_bitcast_fusion.row_ref, bf16[512,1024]{1,0:T(8,128)(2,1)S(1)} %bitcast.47, ...), custom_call_target="tpu_custom_call" | custom-call | tf_op jit(solution)/shard_map/pallas_call | solution.py:86
  43.9 1.5 %shard_map.122 = (bf16[512,512]{1,0:T(8,128)(2,1)S(1)}, bf16[512,512]{1,0:T(8,128)(2,1)S(1)}) custom-call(s32[40]{0:T(128)S(1)} %dynamic-slice_bitcast_fusion.row_ref, bf16[512,1024]{1,0:T(8,128)(2,1)S(1)} %collective-permute-done.refs_0_.refs_1_, bf16[512,1024]{1,0:T(8,128)(2,1)S(1)} %collective-permute-done.1.refs_1_.refs_0_, ...), custom_call_target="tpu_custom_call" | custom-call | tf_op jit(solution)/shard_map/pallas_call | solution.py:86
  47.0 2.2 %collective-permute-done.6.refs_5_.refs_6_.refs_2_.refs_7_.refs_8_.refs_3_.refs_4_ = bf16[384,1024]{1,0:T(8,128)(2,1)S(1)} collective-permute-done((bf16[384,1024]{1,0:T(8,128)(2,1)S(1)}, bf16[384,1024]{1,0:T(8,128)(2,1)S(1)}, u32[]{:S(2)}, u32[]{:S(2)}) %collective-permute-start.6) | collective-permute-done | bytes 786464 | tf_op jit(solution)/shard_map/ppermute | solution.py:501
  51.3 2.4 %shard_map.124 = (bf16[384,4096]{1,0:T(8,128)(2,1)}, bf16[384,512]{1,0:T(8,128)(2,1)S(1)}, bf16[512,1024]{1,0:T(8,128)(2,1)S(1)}) custom-call(s32[40]{0:T(128)S(1)} %dynamic-slice_bitcast_fusion.row_ref, bf16[512,1024]{1,0:T(8,128)(2,1)S(1)} %collective-permute-done.1.refs_1_.refs_0_, ...), custom_call_target="tpu_custom_call", output_to_operand_aliasing={{0}: (6, {})} | custom-call | tf_op jit(solution)/shard_map/pallas_call | solution.py:86
  56.5 3.9 %collective-permute-start.8 = (bf16[512,512]{1,0:T(8,128)(2,1)S(1)}, bf16[512,512]{1,0:T(8,128)(2,1)S(1)}, u32[]{:S(2)}, u32[]{:S(2)}) collective-permute-start(bf16[512,512]{1,0:T(8,128)(2,1)S(1)} %get-tuple-element.50.refs_8_), channel_id=1, source_target_pairs={{0,2},{1,3},{2,0},{3,1},{4,6},{5,7},{6,4},{7,5},{8,10},{9,11},{10,... | collective-permute-start | bytes 1572872 | tf_op jit(solution)/shard_map/ppermute | solution.py:487
  60.4 5.1 %collective-permute-done.10.refs_1_ = bf16[512,512]{1,0:T(8,128)(2,1)S(1)} collective-permute-done((bf16[512,512]{1,0:T(8,128)(2,1)S(1)}, bf16[512,512]{1,0:T(8,128)(2,1)S(1)}, u32[]{:S(2)}, u32[]{:S(2)}) %collective-permute-start.10) | collective-permute-done | bytes 524320 | tf_op jit(solution)/shard_map/ppermute | solution.py:487
  67.7 3.6 %collective-permute-start.18 = (bf16[512,512]{1,0:T(8,128)(2,1)S(1)}, bf16[512,512]{1,0:T(8,128)(2,1)S(1)}, u32[]{:S(2)}, u32[]{:S(2)}) collective-permute-start(bf16[512,512]{1,0:T(8,128)(2,1)S(1)} %get-tuple-element.52.refs_9_), channel_id=1, source_target_pairs={{0,2},{1,3},{2,0},{3,1},{4,6},{5,7},{6,4},{7,5},{8,10},{9,11},{10,... | collective-permute-start | bytes 1572872 | tf_op jit(solution)/shard_map/ppermute | solution.py:487
  71.3 2.5 %shard_map.131 = (bf16[384,4096]{1,0:T(8,128)(2,1)}, bf16[384,512]{1,0:T(8,128)(2,1)S(1)}, bf16[512,1024]{1,0:T(8,128)(2,1)S(1)}) custom-call(s32[40]{0:T(128)S(1)} %dynamic-slice_bitcast_fusion.row_ref, bf16[512,512]{1,0:T(8,128)(2,1)S(1)} %collective-permute-done.5.refs_1_.refs_0_, ...), custom_call_target="tpu_custom_call", output_to_operand_aliasing={{0}: (8, {})} | custom-call | tf_op jit(solution)/shard_map/pallas_call | solution.py:86
  76.8 1.5 %shard_map.127 = (bf16[512,512]{1,0:T(8,128)(2,1)S(1)}, bf16[512,512]{1,0:T(8,128)(2,1)S(1)}) custom-call(s32[40]{0:T(128)S(1)} %dynamic-slice_bitcast_fusion.row_ref, bf16[512,512]{1,0:T(8,128)(2,1)S(1)} %collective-permute-done.7.refs_0_, bf16[512,512]{1,0:T(8,128)(2,1)S(1)} %collective-permute-done.8.refs_1_, bf16[384,4096]{1,0:T(8,128)(2,1)S(1)} %bitcast.24, ...), custom_call_target="tpu_custom_call" | custom-call | tf_op jit(solution)/shard_map/pallas_call | solution.py:86
  79.0 4.3 %collective-permute-start.11 = (bf16[512,512]{1,0:T(8,128)(2,1)S(1)}, bf16[512,512]{1,0:T(8,128)(2,1)S(1)}, u32[]{:S(2)}, u32[]{:S(2)}) collective-permute-start(bf16[512,512]{1,0:T(8,128)(2,1)S(1)} %get-tuple-element.53.refs_9_), channel_id=1, source_target_pairs={{0,2},{1,3},{2,0},{3,1},{4,6},{5,7},{6,4},{7,5},{8,10},{9,11},{10,... | collective-permute-start | bytes 1572872 | tf_op jit(solution)/shard_map/ppermute | solution.py:487
  83.3 1.8 %shard_map.129.grad_ref.refs_11_ = f32[512,1024]{1,0:T(8,128)S(1)} custom-call(s32[40]{0:T(128)S(1)} %dynamic-slice_bitcast_fusion.row_ref, bf16[384,4096]{1,0:T(8,128)(2,1)S(1)} %bitcast.26, bf16[384,1024]{1,0:T(8,128)(2,1)S(1)} %collective-permute-done.13.piece_ref.refs_9_.refs_2_.refs_0_.refs_5_, bf16[384,1024]{1,0:T(8,128)(2,1)S(1)} %bitcast.42, ...), custom_call_target="tpu_custom_call" | custom-call | tf_op jit(solution)/shard_map/pallas_call | solution.py:86
  85.1 3.9 %shard_map.132 = (f32[384,1024]{1,0:T(8,128)S(1)}, f32[384,1024]{1,0:T(8,128)S(1)}) custom-call(s32[40]{0:T(128)S(1)} %dynamic-slice_bitcast_fusion.row_ref, bf16[512,1024]{1,0:T(8,128)(2,1)S(1)} %get-tuple-element.58.refs_0_, bf16[512,1024]{1,0:T(8,128)(2,1)S(1)} %get-tuple-element.59.refs_1_, bf16[512,1024]{1,0:T(8,128)(2,1)S(1)} %get-tuple-element.61.refs_2_, ...), custom_call_target="tpu_custom_call" | custom-call | tf_op jit(solution)/shard_map/pallas_call | solution.py:86
  89.1 1.5 %shard_map.133 = (bf16[512,512]{1,0:T(8,128)(2,1)S(1)}, bf16[512,512]{1,0:T(8,128)(2,1)S(1)}) custom-call(s32[40]{0:T(128)S(1)} %dynamic-slice_bitcast_fusion.row_ref, bf16[512,512]{1,0:T(8,128)(2,1)S(1)} %collective-permute-done.17.refs_0_, bf16[512,512]{1,0:T(8,128)(2,1)S(1)} %collective-permute-done.18.refs_1_.refs_2_, bf16[384,4096]{1,0:T(8,128)(2,1)S(1)} %bitcast.30, ...), custom_call_target="tpu_custom_call" | custom-call | tf_op jit(solution)/shard_map/pallas_call | solution.py:86
  90.6 1.7 %collective-permute-start.19 = (bf16[512,512]{1,0:T(8,128)(2,1)S(1)}, bf16[512,512]{1,0:T(8,128)(2,1)S(1)}, u32[]{:S(2)}, u32[]{:S(2)}) collective-permute-start(bf16[512,512]{1,0:T(8,128)(2,1)S(1)} %get-tuple-element.63), channel_id=1, source_target_pairs={{0,2},{1,3},{2,0},{3,1},{4,6},{5,7},{6,4},{7,5},{8,10},{9,11},{10,... | collective-permute-start | bytes 1572872 | tf_op jit(solution)/shard_map/ppermute | solution.py:487
  93.0 2.5 %shard_map.135 = (bf16[384,4096]{1,0:T(8,128)(2,1)}, bf16[384,512]{1,0:T(8,128)(2,1)S(1)}, bf16[512,1024]{1,0:T(8,128)(2,1)S(1)}) custom-call(s32[40]{0:T(128)S(1)} %dynamic-slice_bitcast_fusion.row_ref, bf16[512,1024]{1,0:T(8,128)(2,1)S(1)} %collective-permute-done.1.refs_1_.refs_0_, ...), custom_call_target="tpu_custom_call", output_to_operand_aliasing={{0}: (7, {})} | custom-call | tf_op jit(solution)/shard_map/pallas_call | solution.py:86
  95.6 1.9 %shard_map.138 = (f32[384,1024]{1,0:T(8,128)S(1)}, bf16[384,1536]{1,0:T(8,128)(2,1)S(1)}) custom-call(s32[40]{0:T(128)S(1)} %dynamic-slice_bitcast_fusion.row_ref, bf16[512,1024]{1,0:T(8,128)(2,1)S(1)} %get-tuple-element.72.refs_0_, bf16[384,4096]{1,0:T(8,128)(2,1)S(1)} %bitcast.32, ...), custom_call_target="tpu_custom_call" | custom-call | tf_op jit(solution)/shard_map/pallas_call | solution.py:86
  99.2 3.1 %shard_map.130 = (f32[512,1024]{1,0:T(8,128)}, f32[512,1024]{1,0:T(8,128)}, bf16[512,512]{1,0:T(8,128)(2,1)S(1)}) custom-call(s32[40]{0:T(128)S(1)} %dynamic-slice_bitcast_fusion.row_ref, bf16[512,512]{1,0:T(8,128)(2,1)S(1)} %collective-permute-done.11.up_ref, bf16[512,512]{1,0:T(8,128)(2,1)S(1)} %collective-permute-done.12.dn_ref, ...), custom_call_target="tpu_custom_call" | custom-call | tf_op jit(solution)/shard_map/pallas_call | solution.py:86
  102.3 1.5 %collective-permute-start.15 = (bf16[512,512]{1,0:T(8,128)(2,1)S(1)}, bf16[512,512]{1,0:T(8,128)(2,1)S(1)}, u32[]{:S(2)}, u32[]{:S(2)}) collective-permute-start(bf16[512,512]{1,0:T(8,128)(2,1)S(1)} %get-tuple-element.56.refs_0_), channel_id=1, source_target_pairs={{0,16},{8,24},{16,0},{24,8},{1,17},{9,25},{17,1},{25,9},{2,18},{10... | collective-permute-start | bytes 1572872 | tf_op jit(solution)/shard_map/ppermute | solution.py:462
  103.8 2.2 %shard_map.136 = (bf16[384,4096]{1,0:T(8,128)(2,1)}, f32[8,128]{1,0:T(8,128)S(1)}) custom-call(s32[40]{0:T(128)S(1)} %dynamic-slice_bitcast_fusion.row_ref, bf16[384,1024]{1,0:T(8,128)(2,1)S(1)} %collective-permute-done.13.piece_ref.refs_9_.refs_2_.refs_0_.refs_5_, ...), custom_call_target="tpu_custom_call", output_to_operand_aliasing={{0}: (4, {})} | custom-call | tf_op jit(solution)/shard_map/pallas_call | solution.py:86
  106.0 1.8 %collective-permute-done.19.up_ref = bf16[512,512]{1,0:T(8,128)(2,1)S(1)} collective-permute-done((bf16[512,512]{1,0:T(8,128)(2,1)S(1)}, bf16[512,512]{1,0:T(8,128)(2,1)S(1)}, u32[]{:S(2)}, u32[]{:S(2)}) %collective-permute-start.19) | collective-permute-done | bytes 524320 | tf_op jit(solution)/shard_map/ppermute | solution.py:487
  107.8 3.1 %shard_map.137 = (f32[512,1024]{1,0:T(8,128)}, f32[512,1024]{1,0:T(8,128)}, bf16[512,512]{1,0:T(8,128)(2,1)S(1)}) custom-call(s32[40]{0:T(128)S(1)} %dynamic-slice_bitcast_fusion.row_ref, bf16[512,512]{1,0:T(8,128)(2,1)S(1)} %collective-permute-done.19.up_ref, ...), custom_call_target="tpu_custom_call", output_to_operand_aliasing={{0}: (7, {}), {1}: (8, {})} | custom-call | tf_op jit(solution)/shard_map/pallas_call | solution.py:86
  110.9 1.5 %collective-permute-start.23 = (bf16[512,512]{1,0:T(8,128)(2,1)S(1)}, bf16[512,512]{1,0:T(8,128)(2,1)S(1)}, u32[]{:S(2)}, u32[]{:S(2)}) collective-permute-start(bf16[512,512]{1,0:T(8,128)(2,1)S(1)} %get-tuple-element.71.refs_4_), channel_id=1, source_target_pairs={{0,16},{8,24},{16,0},{24,8},{1,17},{9,25},{17,1},{25,9},{2,18},{10... | collective-permute-start | bytes 1572872 | tf_op jit(solution)/shard_map/ppermute | solution.py:462
  112.9 9.8 %collective-permute-done.23.refs_6_ = bf16[512,512]{1,0:T(8,128)(2,1)S(1)} collective-permute-done((bf16[512,512]{1,0:T(8,128)(2,1)S(1)}, bf16[512,512]{1,0:T(8,128)(2,1)S(1)}, u32[]{:S(2)}, u32[]{:S(2)}) %collective-permute-start.23) | collective-permute-done | bytes 524320 | tf_op jit(solution)/shard_map/ppermute | solution.py:462
  122.8 1.9 %collective-permute-done.24.refs_7_ = bf16[512,512]{1,0:T(8,128)(2,1)S(1)} collective-permute-done((bf16[512,512]{1,0:T(8,128)(2,1)S(1)}, bf16[512,512]{1,0:T(8,128)(2,1)S(1)}, u32[]{:S(2)}, u32[]{:S(2)}) %collective-permute-start.24) | collective-permute-done | bytes 524320 | tf_op jit(solution)/shard_map/ppermute | solution.py:464
  124.6 2.8 %shard_map.139 = (bf16[512,1024]{1,0:T(8,128)(2,1)}, bf16[384,4096]{1,0:T(8,128)(2,1)}, bf16[384,1024]{1,0:T(8,128)(2,1)}) custom-call(s32[40]{0:T(128)S(1)} %dynamic-slice_bitcast_fusion.row_ref, s32[4]{0:T(128)S(1)} %copy-done.6, s32[4]{0:T(128)S(1)} %copy-done.7, ...), custom_call_target="tpu_custom_call", output_to_operand_aliasing={{1}: (14, {})} | custom-call | tf_op jit(solution)/shard_map/pallas_call | solution.py:86
  (58 shorter events, 19.2 us)
Async XLA Ops:
  0.6 29.2 %collective-permute-start.3 = (bf16[384,1024]{1,0:T(8,128)(2,1)}, bf16[384,1024]{1,0:T(8,128)(2,1)S(1)}, u32[]{:S(2)}, u32[]{:S(2)}) collective-permute-start(bf16[384,1024]{1,0:T(8,128)(2,1)} %bitcast.33), channel_id=1, source_target_pairs={{0,1},{1,0},{2,3},{3,2},{4,5},{5,4},{6,7},{7,6},{8,9},{9,8},{10,11... | collective-permute-start | bytes 2359304 | tf_op jit(solution)/shard_map/ppermute | solution.py:503
  6.8 23.0 %collective-permute-start.2 = (bf16[384,512]{1,0:T(8,128)(2,1)S(1)}, bf16[384,512]{1,0:T(8,128)(2,1)S(1)}, u32[]{:S(2)}, u32[]{:S(2)}) collective-permute-start(bf16[384,512]{1,0:T(8,128)(2,1)S(1)} %shard_map.119), channel_id=1, source_target_pairs={{0,1},{1,0},{2,3},{3,2},{4,5},{5,4},{6,7},{7,6},{8,9},{9,8},{10,11... | collective-permute-start | bytes 1179656 | tf_op jit(solution)/shard_map/ppermute | solution.py:501
  7.4 24.8 %copy-start.2 = (bf16[1,384,1024]{2,1,0:T(8,128)(2,1)S(1)}, bf16[1,384,1024]{2,1,0:T(8,128)(2,1)}, u32[]{:S(2)}) copy-start(bf16[1,384,1024]{2,1,0:T(8,128)(2,1)} %param.10) | copy-start | bytes 2359300
  7.4 24.8 %collective-permute-start.1 = (bf16[512,1024]{1,0:T(8,128)(2,1)S(1)}, bf16[512,1024]{1,0:T(8,128)(2,1)S(1)}, u32[]{:S(2)}, u32[]{:S(2)}) collective-permute-start(bf16[512,1024]{1,0:T(8,128)(2,1)S(1)} %bitcast.45), channel_id=1, source_target_pairs={{0,2},{1,3},{2,0},{3,1},{4,6},{5,7},{6,4},{7,5},{8,10},{9,11},{10,... | collective-permute-start | bytes 3145736 | tf_op jit(solution)/shard_map/ppermute | solution.py:487
  9.0 23.2 %collective-permute-start = (bf16[512,1024]{1,0:T(8,128)(2,1)S(1)}, bf16[512,1024]{1,0:T(8,128)(2,1)S(1)}, u32[]{:S(2)}, u32[]{:S(2)}) collective-permute-start(bf16[512,1024]{1,0:T(8,128)(2,1)S(1)} %bitcast.46), channel_id=1, source_target_pairs={{2,4},{3,5},{4,2},{5,3},{10,12},{11,13},{12,10},{13,11},{18,20},{1... | collective-permute-start | bytes 3145736 | tf_op jit(solution)/shard_map/ppermute | solution.py:487
  30.4 18.8 %collective-permute-start.6 = (bf16[384,1024]{1,0:T(8,128)(2,1)S(1)}, bf16[384,1024]{1,0:T(8,128)(2,1)S(1)}, u32[]{:S(2)}, u32[]{:S(2)}) collective-permute-start(bf16[384,1024]{1,0:T(8,128)(2,1)S(1)} %shard_map.121), channel_id=1, source_target_pairs={{0,1},{1,0},{2,3},{3,2},{4,5},{5,4},{6,7},{7,6},{8,9},{9,8},{10,11... | collective-permute-start | bytes 2359304 | tf_op jit(solution)/shard_map/ppermute | solution.py:501
  33.8 10.1 %copy-start.1 = (bf16[1,384,4096]{2,1,0:T(8,128)(2,1)S(1)}, bf16[1,384,4096]{2,1,0:T(8,128)(2,1)}, u32[]{:S(2)}) copy-start(bf16[1,384,4096]{2,1,0:T(8,128)(2,1)} %param.8) | copy-start | bytes 9437188
  33.8 20.0 %collective-permute-start.4 = (bf16[512,512]{1,0:T(8,128)(2,1)S(1)}, bf16[512,512]{1,0:T(8,128)(2,1)S(1)}, u32[]{:S(2)}, u32[]{:S(2)}) collective-permute-start(bf16[512,512]{1,0:T(8,128)(2,1)S(1)} %get-tuple-element.44), channel_id=1, source_target_pairs={{2,4},{3,5},{4,2},{5,3},{10,12},{11,13},{12,10},{13,11},{18,20},{1... | collective-permute-start | bytes 1572872 | tf_op jit(solution)/shard_map/ppermute | solution.py:487
  34.6 19.7 %collective-permute-start.5 = (bf16[512,512]{1,0:T(8,128)(2,1)S(1)}, bf16[512,512]{1,0:T(8,128)(2,1)S(1)}, u32[]{:S(2)}, u32[]{:S(2)}) collective-permute-start(bf16[512,512]{1,0:T(8,128)(2,1)S(1)} %get-tuple-element.45.refs_7_), channel_id=1, source_target_pairs={{0,2},{1,3},{2,0},{3,1},{4,6},{5,7},{6,4},{7,5},{8,10},{9,11},{10,... | collective-permute-start | bytes 1572872 | tf_op jit(solution)/shard_map/ppermute | solution.py:487
  45.4 15.0 %collective-permute-start.9 = (bf16[512,512]{1,0:T(8,128)(2,1)S(1)}, bf16[512,512]{1,0:T(8,128)(2,1)S(1)}, u32[]{:S(2)}, u32[]{:S(2)}) collective-permute-start(bf16[512,512]{1,0:T(8,128)(2,1)S(1)} %get-tuple-element.51), channel_id=1, source_target_pairs={{2,4},{3,5},{4,2},{5,3},{10,12},{11,13},{12,10},{13,11},{18,20},{1... | collective-permute-start | bytes 1572872 | tf_op jit(solution)/shard_map/ppermute | solution.py:487
  46.1 19.4 %collective-permute-start.10 = (bf16[512,512]{1,0:T(8,128)(2,1)S(1)}, bf16[512,512]{1,0:T(8,128)(2,1)S(1)}, u32[]{:S(2)}, u32[]{:S(2)}) collective-permute-start(bf16[512,512]{1,0:T(8,128)(2,1)S(1)} %get-tuple-element.46.refs_8_), channel_id=1, source_target_pairs={{0,2},{1,3},{2,0},{3,1},{4,6},{5,7},{6,4},{7,5},{8,10},{9,11},{10,... | collective-permute-start | bytes 1572872 | tf_op jit(solution)/shard_map/ppermute | solution.py:487
  49.8 24.0 %collective-permute-start.13 = (bf16[384,1024]{1,0:T(8,128)(2,1)S(1)}, bf16[384,1024]{1,0:T(8,128)(2,1)S(1)}, u32[]{:S(2)}, u32[]{:S(2)}) collective-permute-start(bf16[384,1024]{1,0:T(8,128)(2,1)S(1)} %shard_map.128), channel_id=1, source_target_pairs={{0,1},{1,0},{2,3},{3,2},{4,5},{5,4},{6,7},{7,6},{8,9},{9,8},{10,11... | collective-permute-start | bytes 2359304 | tf_op jit(solution)/shard_map/ppermute | solution.py:522
  55.8 19.9 %collective-permute-start.7 = (bf16[512,512]{1,0:T(8,128)(2,1)S(1)}, bf16[512,512]{1,0:T(8,128)(2,1)S(1)}, u32[]{:S(2)}, u32[]{:S(2)}) collective-permute-start(bf16[512,512]{1,0:T(8,128)(2,1)S(1)} %get-tuple-element.49), channel_id=1, source_target_pairs={{2,4},{3,5},{4,2},{5,3},{10,12},{11,13},{12,10},{13,11},{18,20},{1... | collective-permute-start | bytes 1572872 | tf_op jit(solution)/shard_map/ppermute | solution.py:487
  56.5 20.3 %collective-permute-start.8 = (bf16[512,512]{1,0:T(8,128)(2,1)S(1)}, bf16[512,512]{1,0:T(8,128)(2,1)S(1)}, u32[]{:S(2)}, u32[]{:S(2)}) collective-permute-start(bf16[512,512]{1,0:T(8,128)(2,1)S(1)} %get-tuple-element.50.refs_8_), channel_id=1, source_target_pairs={{0,2},{1,3},{2,0},{3,1},{4,6},{5,7},{6,4},{7,5},{8,10},{9,11},{10,... | collective-permute-start | bytes 1572872 | tf_op jit(solution)/shard_map/ppermute | solution.py:487
  67.0 22.0 %collective-permute-start.17 = (bf16[512,512]{1,0:T(8,128)(2,1)S(1)}, bf16[512,512]{1,0:T(8,128)(2,1)S(1)}, u32[]{:S(2)}, u32[]{:S(2)}) collective-permute-start(bf16[512,512]{1,0:T(8,128)(2,1)S(1)} %get-tuple-element.57), channel_id=1, source_target_pairs={{2,4},{3,5},{4,2},{5,3},{10,12},{11,13},{12,10},{13,11},{18,20},{1... | collective-permute-start | bytes 1572872 | tf_op jit(solution)/shard_map/ppermute | solution.py:487
  67.7 21.3 %collective-permute-start.18 = (bf16[512,512]{1,0:T(8,128)(2,1)S(1)}, bf16[512,512]{1,0:T(8,128)(2,1)S(1)}, u32[]{:S(2)}, u32[]{:S(2)}) collective-permute-start(bf16[512,512]{1,0:T(8,128)(2,1)S(1)} %get-tuple-element.52.refs_9_), channel_id=1, source_target_pairs={{0,2},{1,3},{2,0},{3,1},{4,6},{5,7},{6,4},{7,5},{8,10},{9,11},{10,... | collective-permute-start | bytes 1572872 | tf_op jit(solution)/shard_map/ppermute | solution.py:487
  74.5 29.4 %collective-permute-start.21 = (bf16[384,1024]{1,0:T(8,128)(2,1)S(1)}, bf16[384,1024]{1,0:T(8,128)(2,1)S(1)}, u32[]{:S(2)}, u32[]{:S(2)}) collective-permute-start(bf16[384,1024]{1,0:T(8,128)(2,1)S(1)} %shard_map.134), channel_id=1, source_target_pairs={{0,1},{1,0},{2,3},{3,2},{4,5},{5,4},{6,7},{7,6},{8,9},{9,8},{10,11... | collective-permute-start | bytes 2359304 | tf_op jit(solution)/shard_map/ppermute | solution.py:522
  78.3 19.2 %collective-permute-start.12 = (bf16[512,512]{1,0:T(8,128)(2,1)S(1)}, bf16[512,512]{1,0:T(8,128)(2,1)S(1)}, u32[]{:S(2)}, u32[]{:S(2)}) collective-permute-start(bf16[512,512]{1,0:T(8,128)(2,1)S(1)} %get-tuple-element.54), channel_id=1, source_target_pairs={{2,4},{3,5},{4,2},{5,3},{10,12},{11,13},{12,10},{13,11},{18,20},{1... | collective-permute-start | bytes 1572872 | tf_op jit(solution)/shard_map/ppermute | solution.py:487
  79.0 20.3 %collective-permute-start.11 = (bf16[512,512]{1,0:T(8,128)(2,1)S(1)}, bf16[512,512]{1,0:T(8,128)(2,1)S(1)}, u32[]{:S(2)}, u32[]{:S(2)}) collective-permute-start(bf16[512,512]{1,0:T(8,128)(2,1)S(1)} %get-tuple-element.53.refs_9_), channel_id=1, source_target_pairs={{0,2},{1,3},{2,0},{3,1},{4,6},{5,7},{6,4},{7,5},{8,10},{9,11},{10,... | collective-permute-start | bytes 1572872 | tf_op jit(solution)/shard_map/ppermute | solution.py:487
  90.6 17.2 %collective-permute-start.19 = (bf16[512,512]{1,0:T(8,128)(2,1)S(1)}, bf16[512,512]{1,0:T(8,128)(2,1)S(1)}, u32[]{:S(2)}, u32[]{:S(2)}) collective-permute-start(bf16[512,512]{1,0:T(8,128)(2,1)S(1)} %get-tuple-element.63), channel_id=1, source_target_pairs={{0,2},{1,3},{2,0},{3,1},{4,6},{5,7},{6,4},{7,5},{8,10},{9,11},{10,... | collective-permute-start | bytes 1572872 | tf_op jit(solution)/shard_map/ppermute | solution.py:487
  92.3 15.5 %collective-permute-start.20 = (bf16[512,512]{1,0:T(8,128)(2,1)S(1)}, bf16[512,512]{1,0:T(8,128)(2,1)S(1)}, u32[]{:S(2)}, u32[]{:S(2)}) collective-permute-start(bf16[512,512]{1,0:T(8,128)(2,1)S(1)} %get-tuple-element.64), channel_id=1, source_target_pairs={{2,4},{3,5},{4,2},{5,3},{10,12},{11,13},{12,10},{13,11},{18,20},{1... | collective-permute-start | bytes 1572872 | tf_op jit(solution)/shard_map/ppermute | solution.py:487
  95.6 3.7 %copy-start.4 = (f32[1,512,1024]{2,1,0:T(8,128)S(1)}, f32[1,512,1024]{2,1,0:T(8,128)}, u32[]{:S(2)}) copy-start(f32[1,512,1024]{2,1,0:T(8,128)} %param.11) | copy-start | bytes 6291460
  95.6 3.7 %copy-start.5 = (f32[1,512,1024]{2,1,0:T(8,128)S(1)}, f32[1,512,1024]{2,1,0:T(8,128)}, u32[]{:S(2)}) copy-start(f32[1,512,1024]{2,1,0:T(8,128)} %param.12) | copy-start | bytes 6291460
  97.5 25.2 %collective-permute-start.25 = (bf16[384,1536]{1,0:T(8,128)(2,1)S(1)}, bf16[384,1536]{1,0:T(8,128)(2,1)S(1)}, u32[]{:S(2)}, u32[]{:S(2)}) collective-permute-start(bf16[384,1536]{1,0:T(8,128)(2,1)S(1)} %get-tuple-element.75), channel_id=1, source_target_pairs={{0,1},{1,0},{2,3},{3,2},{4,5},{5,4},{6,7},{7,6},{8,9},{9,8},{10,11... | collective-permute-start | bytes 3538952 | tf_op jit(solution)/shard_map/ppermute | solution.py:547
  102.3 10.6 %collective-permute-start.15 = (bf16[512,512]{1,0:T(8,128)(2,1)S(1)}, bf16[512,512]{1,0:T(8,128)(2,1)S(1)}, u32[]{:S(2)}, u32[]{:S(2)}) collective-permute-start(bf16[512,512]{1,0:T(8,128)(2,1)S(1)} %get-tuple-element.56.refs_0_), channel_id=1, source_target_pairs={{0,16},{8,24},{16,0},{24,8},{1,17},{9,25},{17,1},{25,9},{2,18},{10... | collective-permute-start | bytes 1572872 | tf_op jit(solution)/shard_map/ppermute | solution.py:462
  107.8 16.8 %copy-start.6 = (s32[4]{0:T(128)S(1)}, s32[4]{0:T(128)}, u32[]{:S(2)}) copy-start(s32[4]{0:T(128)} %numerator_ref.1) | copy-start | bytes 52
  107.8 16.8 %copy-start.7 = (s32[4]{0:T(128)S(1)}, s32[4]{0:T(128)}, u32[]{:S(2)}) copy-start(s32[4]{0:T(128)} %partner_ref.1) | copy-start | bytes 52
  110.9 11.9 %collective-permute-start.23 = (bf16[512,512]{1,0:T(8,128)(2,1)S(1)}, bf16[512,512]{1,0:T(8,128)(2,1)S(1)}, u32[]{:S(2)}, u32[]{:S(2)}) collective-permute-start(bf16[512,512]{1,0:T(8,128)(2,1)S(1)} %get-tuple-element.71.refs_4_), channel_id=1, source_target_pairs={{0,16},{8,24},{16,0},{24,8},{1,17},{9,25},{17,1},{25,9},{2,18},{10... | collective-permute-start | bytes 1572872 | tf_op jit(solution)/shard_map/ppermute | solution.py:462
  112.4 10.3 %collective-permute-start.14 = (bf16[512,512]{1,0:T(8,128)(2,1)S(1)}, bf16[512,512]{1,0:T(8,128)(2,1)S(1)}, u32[]{:S(2)}, u32[]{:S(2)}) collective-permute-start(bf16[512,512]{1,0:T(8,128)(2,1)S(1)} %get-tuple-element.56.refs_0_), channel_id=1, source_target_pairs={{0,8},{8,0},{16,24},{24,16},{1,9},{9,1},{17,25},{25,17},{2,10},{10... | collective-permute-start | bytes 1572872 | tf_op jit(solution)/shard_map/ppermute | solution.py:464
  112.4 10.4 %collective-permute-start.22 = (bf16[512,512]{1,0:T(8,128)(2,1)S(1)}, bf16[512,512]{1,0:T(8,128)(2,1)S(1)}, u32[]{:S(2)}, u32[]{:S(2)}) collective-permute-start(bf16[512,512]{1,0:T(8,128)(2,1)S(1)} %get-tuple-element.71.refs_4_), channel_id=1, source_target_pairs={{0,8},{8,0},{16,24},{24,16},{1,9},{9,1},{17,25},{25,17},{2,10},{10... | collective-permute-start | bytes 1572872 | tf_op jit(solution)/shard_map/ppermute | solution.py:464
  112.9 9.9 %collective-permute-start.16 = (bf16[512,512]{1,0:T(8,128)(2,1)S(1)}, bf16[512,512]{1,0:T(8,128)(2,1)S(1)}, u32[]{:S(2)}, u32[]{:S(2)}) collective-permute-start(bf16[512,512]{1,0:T(8,128)(2,1)S(1)} %collective-permute-done.15.refs_2_), channel_id=1, source_target_pairs={{0,8},{8,0},{16,24},{24,16},{1,9},{9,1},{17,25},{25,17},{2,10},{10... | collective-permute-start | bytes 1572872 | tf_op jit(solution)/shard_map/ppermute | solution.py:464
  122.7 1.9 %collective-permute-start.24 = (bf16[512,512]{1,0:T(8,128)(2,1)S(1)}, bf16[512,512]{1,0:T(8,128)(2,1)S(1)}, u32[]{:S(2)}, u32[]{:S(2)}) collective-permute-start(bf16[512,512]{1,0:T(8,128)(2,1)S(1)} %collective-permute-done.23.refs_6_), channel_id=1, source_target_pairs={{0,8},{8,0},{16,24},{24,16},{1,9},{9,1},{17,25},{25,17},{2,10},{10... | collective-permute-start | bytes 1572872 | tf_op jit(solution)/shard_map/ppermute | solution.py:464
  (2 other events, 3.1 us)

commit v13 on v11

--- a/solution.py
+++ b/solution.py
@@ -362,7 +362,7 @@
 def adam(row, h, got, grad, weights, first, second, kept, after=()):
     rows, columns = got["a"].shape
     assert got["a"].start == 0
-    steps = 4 if rows % 64 == 0 else 1
+    steps = 2 if rows % 32 == 0 else 1
     size = rows // steps
 
     def kernel(row_ref, up_ref, dn_ref, grad_ref, w_ref, a_ref, b_ref, *refs):
@@ -403,7 +403,7 @@
 def average(plan, scalars, stepped, others, after):
     rows, columns = stepped[0].shape
     chunks, count = len(stepped), len(others[0])
-    steps = 4 if rows % 64 == 0 else 1
+    steps = 2 if rows % 32 == 0 else 1
     size = rows // steps
 
     def kernel(row_ref, numerator_ref, partner_ref, *refs):

time: 125 us -> 124 us (level)
  no operation moved by 1% of the time
where the time goes in v13:
time: 124 us
  starting transfers between devices  40.4 us (33%)
  Pallas kernels  40.4 us (33%)
  waiting for transfers between devices  39.6 us (32%)
  local copies, waits for them, and re-layouts  2.62 us (2%)
    pallas_call x22, Pallas kernels, call(): pl.pallas_call(kernel, grid_spec=pltpu.PrefetchScalarGridSpec(num_scalar_...  40.4 us
    ppermute x14, starting transfers between devices, exchange(): lax.ppermute(bufs[name], 'fsdp', links[name])  28.7 us
    ppermute x2, waiting for transfers between devices, send(): return swap(pack(plan, row, rows, [], act, turns, after))  21.8 us
    ppermute x2, waiting for transfers between devices, partner_rows(): far = lax.ppermute(stepped, 'rep', [(r, r ^ 2) for r in range(4)])  10.1 us
    ppermute x14, waiting for transfers between devices, exchange(): lax.ppermute(bufs[name], 'fsdp', links[name])  7.43 us
    ppermute x2, starting transfers between devices, partner_rows(): far = lax.ppermute(stepped, 'rep', [(r, r ^ 2) for r in range(4)])  3.04 us
    ppermute x1, starting transfers between devices, per_device(): parcel = swap(cot)  3 us
  transfers between devices with their start and end apart: 26, of which 8 were waited for; matrix products, arithmetic and copies ran while one was open for 1% of the time, Pallas kernels for 31%

profile of v13, /device:TPU:0, one launch (start us, length us, event | category | flops | bytes accessed | tf_op | source)
XLA Modules:
  0.0 123.9 jit_solution(5797816954144942110)
XLA Ops:
  0.6 3.0 %collective-permute-start.3 = (bf16[384,1024]{1,0:T(8,128)(2,1)}, bf16[384,1024]{1,0:T(8,128)(2,1)S(1)}, u32[]{:S(2)}, u32[]{:S(2)}) collective-permute-start(bf16[384,1024]{1,0:T(8,128)(2,1)} %bitcast.33), channel_id=1, source_target_pairs={{0,1},{1,0},{2,3},{3,2},{4,5},{5,4},{6,7},{7,6},{8,9},{9,8},{10,11... | collective-permute-start | bytes 2359304 | tf_op jit(solution)/shard_map/ppermute | solution.py:491
  4.4 4.4 %collective-permute-start = (bf16[512,1024]{1,0:T(8,128)(2,1)}, bf16[512,1024]{1,0:T(8,128)(2,1)S(1)}, u32[]{:S(2)}, u32[]{:S(2)}) collective-permute-start(bf16[512,1024]{1,0:T(8,128)(2,1)} %bitcast.46), channel_id=1, source_target_pairs={{0,2},{1,3},{2,0},{3,1},{4,6},{5,7},{6,4},{7,5},{8,10},{9,11},{10,... | collective-permute-start | bytes 3145736 | tf_op jit(solution)/shard_map/ppermute | solution.py:475
  9.5 1.9 %copy-done = bf16[1,384,4096]{2,1,0:T(8,128)(2,1)S(1)} copy-done((bf16[1,384,4096]{2,1,0:T(8,128)(2,1)S(1)}, bf16[1,384,4096]{2,1,0:T(8,128)(2,1)}, u32[]{:S(2)}) %copy-start) | copy-done | bytes 3145752
  12.5 17.3 %collective-permute-done.2.refs_4_.refs_3_.refs_6_.refs_2_ = bf16[384,512]{1,0:T(8,128)(2,1)S(1)} collective-permute-done((bf16[384,512]{1,0:T(8,128)(2,1)S(1)}, bf16[384,512]{1,0:T(8,128)(2,1)S(1)}, u32[]{:S(2)}, u32[]{:S(2)}) %collective-permute-start.2) | collective-permute-done | bytes 393248 | tf_op jit(solution)/shard_map/ppermute | solution.py:489
  30.4 1.8 %collective-permute-start.6 = (bf16[384,1024]{1,0:T(8,128)(2,1)S(1)}, bf16[384,1024]{1,0:T(8,128)(2,1)S(1)}, u32[]{:S(2)}, u32[]{:S(2)}) collective-permute-start(bf16[384,1024]{1,0:T(8,128)(2,1)S(1)} %shard_map.121), channel_id=1, source_target_pairs={{0,1},{1,0},{2,3},{3,2},{4,5},{5,4},{6,7},{7,6},{8,9},{9,8},{10,11... | collective-permute-start | bytes 2359304 | tf_op jit(solution)/shard_map/ppermute | solution.py:489
  32.3 1.5 %shard_map.120 = (bf16[512,512]{1,0:T(8,128)(2,1)S(1)}, bf16[512,512]{1,0:T(8,128)(2,1)S(1)}) custom-call(s32[40]{0:T(128)S(1)} %dynamic-slice_bitcast_fusion.row_ref, bf16[512,1024]{1,0:T(8,128)(2,1)S(1)} %collective-permute-done.1.refs_0_.refs_1_, bf16[512,1024]{1,0:T(8,128)(2,1)S(1)} %collective-permute-done.refs_1_.refs_0_, ...), custom_call_target="tpu_custom_call" | custom-call | tf_op jit(solution)/shard_map/pallas_call | solution.py:86
  34.6 3.8 %collective-permute-start.5 = (bf16[512,512]{1,0:T(8,128)(2,1)S(1)}, bf16[512,512]{1,0:T(8,128)(2,1)S(1)}, u32[]{:S(2)}, u32[]{:S(2)}) collective-permute-start(bf16[512,512]{1,0:T(8,128)(2,1)S(1)} %get-tuple-element.45.refs_7_), channel_id=1, source_target_pairs={{0,2},{1,3},{2,0},{3,1},{4,6},{5,7},{6,4},{7,5},{8,10},{9,11},{10,... | collective-permute-start | bytes 1572872 | tf_op jit(solution)/shard_map/ppermute | solution.py:475
  38.5 2.4 %shard_map.123 = (bf16[384,4096]{1,0:T(8,128)(2,1)}, bf16[384,512]{1,0:T(8,128)(2,1)S(1)}, bf16[512,1024]{1,0:T(8,128)(2,1)S(1)}) custom-call(s32[40]{0:T(128)S(1)} %dynamic-slice_bitcast_fusion.row_ref, bf16[512,1024]{1,0:T(8,128)(2,1)S(1)} %bitcast.47, ...), custom_call_target="tpu_custom_call" | custom-call | tf_op jit(solution)/shard_map/pallas_call | solution.py:86
  40.9 1.5 %shard_map.122 = (bf16[512,512]{1,0:T(8,128)(2,1)S(1)}, bf16[512,512]{1,0:T(8,128)(2,1)S(1)}) custom-call(s32[40]{0:T(128)S(1)} %dynamic-slice_bitcast_fusion.row_ref, bf16[512,1024]{1,0:T(8,128)(2,1)S(1)} %collective-permute-done.1.refs_0_.refs_1_, bf16[512,1024]{1,0:T(8,128)(2,1)S(1)} %collective-permute-done.refs_1_.refs_0_, ...), custom_call_target="tpu_custom_call" | custom-call | tf_op jit(solution)/shard_map/pallas_call | solution.py:86
  43.2 1.5 %collective-permute-start.9 = (bf16[512,512]{1,0:T(8,128)(2,1)S(1)}, bf16[512,512]{1,0:T(8,128)(2,1)S(1)}, u32[]{:S(2)}, u32[]{:S(2)}) collective-permute-start(bf16[512,512]{1,0:T(8,128)(2,1)S(1)} %get-tuple-element.46.refs_8_), channel_id=1, source_target_pairs={{0,2},{1,3},{2,0},{3,1},{4,6},{5,7},{6,4},{7,5},{8,10},{9,11},{10,... | collective-permute-start | bytes 1572872 | tf_op jit(solution)/shard_map/ppermute | solution.py:475
  44.7 4.5 %collective-permute-done.6.refs_5_.refs_2_.refs_7_.refs_8_.refs_3_.refs_4_.refs_6_ = bf16[384,1024]{1,0:T(8,128)(2,1)S(1)} collective-permute-done((bf16[384,1024]{1,0:T(8,128)(2,1)S(1)}, bf16[384,1024]{1,0:T(8,128)(2,1)S(1)}, u32[]{:S(2)}, u32[]{:S(2)}) %collective-permute-start.6) | collective-permute-done | bytes 786464 | tf_op jit(solution)/shard_map/ppermute | solution.py:489
  51.3 2.4 %shard_map.124 = (bf16[384,4096]{1,0:T(8,128)(2,1)}, bf16[384,512]{1,0:T(8,128)(2,1)S(1)}, bf16[512,1024]{1,0:T(8,128)(2,1)S(1)}) custom-call(s32[40]{0:T(128)S(1)} %dynamic-slice_bitcast_fusion.row_ref, bf16[512,1024]{1,0:T(8,128)(2,1)S(1)} %collective-permute-done.refs_1_.refs_0_, ...), custom_call_target="tpu_custom_call", output_to_operand_aliasing={{0}: (6, {})} | custom-call | tf_op jit(solution)/shard_map/pallas_call | solution.py:86
  56.0 4.4 %collective-permute-start.7 = (bf16[512,512]{1,0:T(8,128)(2,1)S(1)}, bf16[512,512]{1,0:T(8,128)(2,1)S(1)}, u32[]{:S(2)}, u32[]{:S(2)}) collective-permute-start(bf16[512,512]{1,0:T(8,128)(2,1)S(1)} %get-tuple-element.49.refs_8_), channel_id=1, source_target_pairs={{0,2},{1,3},{2,0},{3,1},{4,6},{5,7},{6,4},{7,5},{8,10},{9,11},{10,... | collective-permute-start | bytes 1572872 | tf_op jit(solution)/shard_map/ppermute | solution.py:475
  63.8 3.5 %collective-permute-start.10 = (bf16[512,512]{1,0:T(8,128)(2,1)S(1)}, bf16[512,512]{1,0:T(8,128)(2,1)S(1)}, u32[]{:S(2)}, u32[]{:S(2)}) collective-permute-start(bf16[512,512]{1,0:T(8,128)(2,1)S(1)} %get-tuple-element.51.refs_9_), channel_id=1, source_target_pairs={{0,2},{1,3},{2,0},{3,1},{4,6},{5,7},{6,4},{7,5},{8,10},{9,11},{10,... | collective-permute-start | bytes 1572872 | tf_op jit(solution)/shard_map/ppermute | solution.py:475
  67.3 2.5 %shard_map.127 = (bf16[384,4096]{1,0:T(8,128)(2,1)}, bf16[384,512]{1,0:T(8,128)(2,1)S(1)}, bf16[512,1024]{1,0:T(8,128)(2,1)S(1)}) custom-call(s32[40]{0:T(128)S(1)} %dynamic-slice_bitcast_fusion.row_ref, bf16[512,512]{1,0:T(8,128)(2,1)S(1)} %collective-permute-done.5.refs_1_.refs_0_, ...), custom_call_target="tpu_custom_call", output_to_operand_aliasing={{0}: (8, {})} | custom-call | tf_op jit(solution)/shard_map/pallas_call | solution.py:86
  71.0 2.3 %collective-permute-done.7.refs_1_ = bf16[512,512]{1,0:T(8,128)(2,1)S(1)} collective-permute-done((bf16[512,512]{1,0:T(8,128)(2,1)S(1)}, bf16[512,512]{1,0:T(8,128)(2,1)S(1)}, u32[]{:S(2)}, u32[]{:S(2)}) %collective-permute-start.7) | collective-permute-done | bytes 524320 | tf_op jit(solution)/shard_map/ppermute | solution.py:475
  75.5 4.5 %collective-permute-start.15 = (bf16[512,512]{1,0:T(8,128)(2,1)S(1)}, bf16[512,512]{1,0:T(8,128)(2,1)S(1)}, u32[]{:S(2)}, u32[]{:S(2)}) collective-permute-start(bf16[512,512]{1,0:T(8,128)(2,1)S(1)} %get-tuple-element.70.refs_9_), channel_id=1, source_target_pairs={{0,2},{1,3},{2,0},{3,1},{4,6},{5,7},{6,4},{7,5},{8,10},{9,11},{10,... | collective-permute-start | bytes 1572872 | tf_op jit(solution)/shard_map/ppermute | solution.py:475
  79.9 1.8 %shard_map.136.grad_ref.refs_11_ = f32[512,1024]{1,0:T(8,128)S(1)} custom-call(s32[40]{0:T(128)S(1)} %dynamic-slice_bitcast_fusion.row_ref, bf16[384,4096]{1,0:T(8,128)(2,1)S(1)} %bitcast.26, bf16[384,1024]{1,0:T(8,128)(2,1)S(1)} %collective-permute-done.11.refs_9_.refs_5_.refs_2_.refs_0_.piece_ref, bf16[384,1024]{1,0:T(8,128)(2,1)S(1)} %bitcast.42, ...), custom_call_target="tpu_custom_call" | custom-call | tf_op jit(solution)/shard_map/pallas_call | solution.py:86
  81.8 3.9 %shard_map.130 = (f32[384,1024]{1,0:T(8,128)S(1)}, f32[384,1024]{1,0:T(8,128)S(1)}) custom-call(s32[40]{0:T(128)S(1)} %dynamic-slice_bitcast_fusion.row_ref, bf16[512,1024]{1,0:T(8,128)(2,1)S(1)} %get-tuple-element.56.refs_0_, bf16[512,1024]{1,0:T(8,128)(2,1)S(1)} %get-tuple-element.57.refs_1_, bf16[512,1024]{1,0:T(8,128)(2,1)S(1)} %get-tuple-element.58.refs_2_, ...), custom_call_target="tpu_custom_call" | custom-call | tf_op jit(solution)/shard_map/pallas_call | solution.py:86
  85.7 1.5 %shard_map.138 = (bf16[512,512]{1,0:T(8,128)(2,1)S(1)}, bf16[512,512]{1,0:T(8,128)(2,1)S(1)}) custom-call(s32[40]{0:T(128)S(1)} %dynamic-slice_bitcast_fusion.row_ref, bf16[512,512]{1,0:T(8,128)(2,1)S(1)} %collective-permute-done.20.refs_0_, bf16[512,512]{1,0:T(8,128)(2,1)S(1)} %collective-permute-done.10.refs_2_.refs_1_, bf16[384,4096]{1,0:T(8,128)(2,1)S(1)} %bitcast.30, ...), custom_call_target="tpu_custom_call" | custom-call | tf_op jit(solution)/shard_map/pallas_call | solution.py:86
  87.2 1.6 %collective-permute-start.21 = (bf16[512,512]{1,0:T(8,128)(2,1)S(1)}, bf16[512,512]{1,0:T(8,128)(2,1)S(1)}, u32[]{:S(2)}, u32[]{:S(2)}) collective-permute-start(bf16[512,512]{1,0:T(8,128)(2,1)S(1)} %get-tuple-element.74), channel_id=1, source_target_pairs={{0,2},{1,3},{2,0},{3,1},{4,6},{5,7},{6,4},{7,5},{8,10},{9,11},{10,... | collective-permute-start | bytes 1572872 | tf_op jit(solution)/shard_map/ppermute | solution.py:475
  89.5 2.5 %shard_map.128 = (bf16[384,4096]{1,0:T(8,128)(2,1)}, bf16[384,512]{1,0:T(8,128)(2,1)S(1)}, bf16[512,1024]{1,0:T(8,128)(2,1)S(1)}) custom-call(s32[40]{0:T(128)S(1)} %dynamic-slice_bitcast_fusion.row_ref, bf16[512,1024]{1,0:T(8,128)(2,1)S(1)} %collective-permute-done.refs_1_.refs_0_, ...), custom_call_target="tpu_custom_call", output_to_operand_aliasing={{0}: (7, {})} | custom-call | tf_op jit(solution)/shard_map/pallas_call | solution.py:86
  92.1 1.9 %shard_map.131 = (f32[384,1024]{1,0:T(8,128)S(1)}, bf16[384,1536]{1,0:T(8,128)(2,1)S(1)}) custom-call(s32[40]{0:T(128)S(1)} %dynamic-slice_bitcast_fusion.row_ref, bf16[512,1024]{1,0:T(8,128)(2,1)S(1)} %get-tuple-element.54.refs_0_, bf16[384,4096]{1,0:T(8,128)(2,1)S(1)} %bitcast.32, ...), custom_call_target="tpu_custom_call" | custom-call | tf_op jit(solution)/shard_map/pallas_call | solution.py:86
  95.7 2.9 %shard_map.137 = (f32[512,1024]{1,0:T(8,128)}, f32[512,1024]{1,0:T(8,128)}, bf16[512,512]{1,0:T(8,128)(2,1)S(1)}) custom-call(s32[40]{0:T(128)S(1)} %dynamic-slice_bitcast_fusion.row_ref, bf16[512,512]{1,0:T(8,128)(2,1)S(1)} %collective-permute-done.15.up_ref, bf16[512,512]{1,0:T(8,128)(2,1)S(1)} %collective-permute-done.16.dn_ref, ...), custom_call_target="tpu_custom_call" | custom-call | tf_op jit(solution)/shard_map/pallas_call | solution.py:86
  98.6 1.5 %collective-permute-start.18 = (bf16[512,512]{1,0:T(8,128)(2,1)S(1)}, bf16[512,512]{1,0:T(8,128)(2,1)S(1)}, u32[]{:S(2)}, u32[]{:S(2)}) collective-permute-start(bf16[512,512]{1,0:T(8,128)(2,1)S(1)} %get-tuple-element.72.refs_0_), channel_id=1, source_target_pairs={{0,16},{8,24},{16,0},{24,8},{1,17},{9,25},{17,1},{25,9},{2,18},{10... | collective-permute-start | bytes 1572872 | tf_op jit(solution)/shard_map/ppermute | solution.py:450
  100.1 2.2 %shard_map.133 = (bf16[384,4096]{1,0:T(8,128)(2,1)}, f32[8,128]{1,0:T(8,128)S(1)}) custom-call(s32[40]{0:T(128)S(1)} %dynamic-slice_bitcast_fusion.row_ref, bf16[384,1024]{1,0:T(8,128)(2,1)S(1)} %collective-permute-done.11.refs_9_.refs_5_.refs_2_.refs_0_.piece_ref, ...), custom_call_target="tpu_custom_call", output_to_operand_aliasing={{0}: (4, {})} | custom-call | tf_op jit(solution)/shard_map/pallas_call | solution.py:86
  102.3 2.8 %collective-permute-done.21.up_ref = bf16[512,512]{1,0:T(8,128)(2,1)S(1)} collective-permute-done((bf16[512,512]{1,0:T(8,128)(2,1)S(1)}, bf16[512,512]{1,0:T(8,128)(2,1)S(1)}, u32[]{:S(2)}, u32[]{:S(2)}) %collective-permute-start.21) | collective-permute-done | bytes 524320 | tf_op jit(solution)/shard_map/ppermute | solution.py:475
  105.2 2.9 %shard_map.139 = (f32[512,1024]{1,0:T(8,128)}, f32[512,1024]{1,0:T(8,128)}, bf16[512,512]{1,0:T(8,128)(2,1)S(1)}) custom-call(s32[40]{0:T(128)S(1)} %dynamic-slice_bitcast_fusion.row_ref, bf16[512,512]{1,0:T(8,128)(2,1)S(1)} %collective-permute-done.21.up_ref, ...), custom_call_target="tpu_custom_call", output_to_operand_aliasing={{0}: (7, {}), {1}: (8, {})} | custom-call | tf_op jit(solution)/shard_map/pallas_call | solution.py:86
  108.0 1.5 %collective-permute-start.24 = (bf16[512,512]{1,0:T(8,128)(2,1)S(1)}, bf16[512,512]{1,0:T(8,128)(2,1)S(1)}, u32[]{:S(2)}, u32[]{:S(2)}) collective-permute-start(bf16[512,512]{1,0:T(8,128)(2,1)S(1)} %get-tuple-element.79.refs_4_), channel_id=1, source_target_pairs={{0,16},{8,24},{16,0},{24,8},{1,17},{9,25},{17,1},{25,9},{2,18},{10... | collective-permute-start | bytes 1572872 | tf_op jit(solution)/shard_map/ppermute | solution.py:450
  110.0 10.1 %collective-permute-done.24.refs_6_ = bf16[512,512]{1,0:T(8,128)(2,1)S(1)} collective-permute-done((bf16[512,512]{1,0:T(8,128)(2,1)S(1)}, bf16[512,512]{1,0:T(8,128)(2,1)S(1)}, u32[]{:S(2)}, u32[]{:S(2)}) %collective-permute-start.24) | collective-permute-done | bytes 524320 | tf_op jit(solution)/shard_map/ppermute | solution.py:450
  120.2 1.7 %shard_map.134 = (bf16[384,4096]{1,0:T(8,128)(2,1)}, f32[8,128]{1,0:T(8,128)S(1)}, bf16[384,1024]{1,0:T(8,128)(2,1)}) custom-call(s32[40]{0:T(128)S(1)} %dynamic-slice_bitcast_fusion.row_ref, bf16[384,1536]{1,0:T(8,128)(2,1)S(1)} %collective-permute-done.12.refs_0_.refs_2_, ...), custom_call_target="tpu_custom_call", output_to_operand_aliasing={{0}: (4, {})} | custom-call | tf_op jit(solution)/shard_map/pallas_call | solution.py:86
  122.1 1.8 %shard_map.140 = bf16[512,1024]{1,0:T(8,128)(2,1)} custom-call(s32[40]{0:T(128)S(1)} %dynamic-slice_bitcast_fusion.row_ref, s32[4]{0:T(128)S(1)} %copy-done.6, s32[4]{0:T(128)S(1)} %copy-done.7, bf16[512,512]{1,0:T(8,128)(2,1)S(1)} %get-tuple-element.72.refs_0_, bf16[512,512]{1,0:T(8,128)(2,1)S(1)} %collective-permute-done.17.refs_1_, ...), custom_call_target="tpu_custom_call" | custom-call | tf_op jit(solution)/shard_map/pallas_call | solution.py:86
  (59 shorter events, 18.9 us)
Async XLA Ops:
  0.6 29.2 %collective-permute-start.3 = (bf16[384,1024]{1,0:T(8,128)(2,1)}, bf16[384,1024]{1,0:T(8,128)(2,1)S(1)}, u32[]{:S(2)}, u32[]{:S(2)}) collective-permute-start(bf16[384,1024]{1,0:T(8,128)(2,1)} %bitcast.33), channel_id=1, source_target_pairs={{0,1},{1,0},{2,3},{3,2},{4,5},{5,4},{6,7},{7,6},{8,9},{9,8},{10,11... | collective-permute-start | bytes 2359304 | tf_op jit(solution)/shard_map/ppermute | solution.py:491
  3.6 28.6 %collective-permute-start.1 = (bf16[512,1024]{1,0:T(8,128)(2,1)}, bf16[512,1024]{1,0:T(8,128)(2,1)S(1)}, u32[]{:S(2)}, u32[]{:S(2)}) collective-permute-start(bf16[512,1024]{1,0:T(8,128)(2,1)} %bitcast.45), channel_id=1, source_target_pairs={{2,4},{3,5},{4,2},{5,3},{10,12},{11,13},{12,10},{13,11},{18,20},{1... | collective-permute-start | bytes 3145736 | tf_op jit(solution)/shard_map/ppermute | solution.py:475
  4.4 27.9 %collective-permute-start = (bf16[512,1024]{1,0:T(8,128)(2,1)}, bf16[512,1024]{1,0:T(8,128)(2,1)S(1)}, u32[]{:S(2)}, u32[]{:S(2)}) collective-permute-start(bf16[512,1024]{1,0:T(8,128)(2,1)} %bitcast.46), channel_id=1, source_target_pairs={{0,2},{1,3},{2,0},{3,1},{4,6},{5,7},{6,4},{7,5},{8,10},{9,11},{10,... | collective-permute-start | bytes 3145736 | tf_op jit(solution)/shard_map/ppermute | solution.py:475
  11.9 20.3 %copy-start.2 = (bf16[1,384,1024]{2,1,0:T(8,128)(2,1)S(1)}, bf16[1,384,1024]{2,1,0:T(8,128)(2,1)}, u32[]{:S(2)}) copy-start(bf16[1,384,1024]{2,1,0:T(8,128)(2,1)} %param.10) | copy-start | bytes 2359300
  11.9 17.9 %collective-permute-start.2 = (bf16[384,512]{1,0:T(8,128)(2,1)S(1)}, bf16[384,512]{1,0:T(8,128)(2,1)S(1)}, u32[]{:S(2)}, u32[]{:S(2)}) collective-permute-start(bf16[384,512]{1,0:T(8,128)(2,1)S(1)} %shard_map.119), channel_id=1, source_target_pairs={{0,1},{1,0},{2,3},{3,2},{4,5},{5,4},{6,7},{7,6},{8,9},{9,8},{10,11... | collective-permute-start | bytes 1179656 | tf_op jit(solution)/shard_map/ppermute | solution.py:489
  30.4 8.1 %copy-start.3 = (bf16[1,512,1024]{2,1,0:T(8,128)(2,1)S(1)}, bf16[1,512,1024]{2,1,0:T(8,128)(2,1)}, u32[]{:S(2)}) copy-start(bf16[1,512,1024]{2,1,0:T(8,128)(2,1)} %param.9) | copy-start | bytes 3145732
  30.4 18.8 %collective-permute-start.6 = (bf16[384,1024]{1,0:T(8,128)(2,1)S(1)}, bf16[384,1024]{1,0:T(8,128)(2,1)S(1)}, u32[]{:S(2)}, u32[]{:S(2)}) collective-permute-start(bf16[384,1024]{1,0:T(8,128)(2,1)S(1)} %shard_map.121), channel_id=1, source_target_pairs={{0,1},{1,0},{2,3},{3,2},{4,5},{5,4},{6,7},{7,6},{8,9},{9,8},{10,11... | collective-permute-start | bytes 2359304 | tf_op jit(solution)/shard_map/ppermute | solution.py:489
  33.8 7.1 %copy-start.1 = (bf16[1,384,4096]{2,1,0:T(8,128)(2,1)S(1)}, bf16[1,384,4096]{2,1,0:T(8,128)(2,1)}, u32[]{:S(2)}) copy-start(bf16[1,384,4096]{2,1,0:T(8,128)(2,1)} %param.8) | copy-start | bytes 9437188
  33.8 20.0 %collective-permute-start.4 = (bf16[512,512]{1,0:T(8,128)(2,1)S(1)}, bf16[512,512]{1,0:T(8,128)(2,1)S(1)}, u32[]{:S(2)}, u32[]{:S(2)}) collective-permute-start(bf16[512,512]{1,0:T(8,128)(2,1)S(1)} %get-tuple-element.44), channel_id=1, source_target_pairs={{2,4},{3,5},{4,2},{5,3},{10,12},{11,13},{12,10},{13,11},{18,20},{1... | collective-permute-start | bytes 1572872 | tf_op jit(solution)/shard_map/ppermute | solution.py:475
  34.6 19.1 %collective-permute-start.5 = (bf16[512,512]{1,0:T(8,128)(2,1)S(1)}, bf16[512,512]{1,0:T(8,128)(2,1)S(1)}, u32[]{:S(2)}, u32[]{:S(2)}) collective-permute-start(bf16[512,512]{1,0:T(8,128)(2,1)S(1)} %get-tuple-element.45.refs_7_), channel_id=1, source_target_pairs={{0,2},{1,3},{2,0},{3,1},{4,6},{5,7},{6,4},{7,5},{8,10},{9,11},{10,... | collective-permute-start | bytes 1572872 | tf_op jit(solution)/shard_map/ppermute | solution.py:475
  42.5 17.9 %collective-permute-start.8 = (bf16[512,512]{1,0:T(8,128)(2,1)S(1)}, bf16[512,512]{1,0:T(8,128)(2,1)S(1)}, u32[]{:S(2)}, u32[]{:S(2)}) collective-permute-start(bf16[512,512]{1,0:T(8,128)(2,1)S(1)} %get-tuple-element.50), channel_id=1, source_target_pairs={{2,4},{3,5},{4,2},{5,3},{10,12},{11,13},{12,10},{13,11},{18,20},{1... | collective-permute-start | bytes 1572872 | tf_op jit(solution)/shard_map/ppermute | solution.py:475
  43.2 18.4 %collective-permute-start.9 = (bf16[512,512]{1,0:T(8,128)(2,1)S(1)}, bf16[512,512]{1,0:T(8,128)(2,1)S(1)}, u32[]{:S(2)}, u32[]{:S(2)}) collective-permute-start(bf16[512,512]{1,0:T(8,128)(2,1)S(1)} %get-tuple-element.46.refs_8_), channel_id=1, source_target_pairs={{0,2},{1,3},{2,0},{3,1},{4,6},{5,7},{6,4},{7,5},{8,10},{9,11},{10,... | collective-permute-start | bytes 1572872 | tf_op jit(solution)/shard_map/ppermute | solution.py:475
  49.8 20.0 %collective-permute-start.11 = (bf16[384,1024]{1,0:T(8,128)(2,1)S(1)}, bf16[384,1024]{1,0:T(8,128)(2,1)S(1)}, u32[]{:S(2)}, u32[]{:S(2)}) collective-permute-start(bf16[384,1024]{1,0:T(8,128)(2,1)S(1)} %shard_map.129), channel_id=1, source_target_pairs={{0,1},{1,0},{2,3},{3,2},{4,5},{5,4},{6,7},{7,6},{8,9},{9,8},{10,11... | collective-permute-start | bytes 2359304 | tf_op jit(solution)/shard_map/ppermute | solution.py:510
  55.3 15.7 %collective-permute-start.14 = (bf16[512,512]{1,0:T(8,128)(2,1)S(1)}, bf16[512,512]{1,0:T(8,128)(2,1)S(1)}, u32[]{:S(2)}, u32[]{:S(2)}) collective-permute-start(bf16[512,512]{1,0:T(8,128)(2,1)S(1)} %get-tuple-element.69), channel_id=1, source_target_pairs={{2,4},{3,5},{4,2},{5,3},{10,12},{11,13},{12,10},{13,11},{18,20},{1... | collective-permute-start | bytes 1572872 | tf_op jit(solution)/shard_map/ppermute | solution.py:475
  56.0 17.3 %collective-permute-start.7 = (bf16[512,512]{1,0:T(8,128)(2,1)S(1)}, bf16[512,512]{1,0:T(8,128)(2,1)S(1)}, u32[]{:S(2)}, u32[]{:S(2)}) collective-permute-start(bf16[512,512]{1,0:T(8,128)(2,1)S(1)} %get-tuple-element.49.refs_8_), channel_id=1, source_target_pairs={{0,2},{1,3},{2,0},{3,1},{4,6},{5,7},{6,4},{7,5},{8,10},{9,11},{10,... | collective-permute-start | bytes 1572872 | tf_op jit(solution)/shard_map/ppermute | solution.py:475
  63.1 22.6 %collective-permute-start.20 = (bf16[512,512]{1,0:T(8,128)(2,1)S(1)}, bf16[512,512]{1,0:T(8,128)(2,1)S(1)}, u32[]{:S(2)}, u32[]{:S(2)}) collective-permute-start(bf16[512,512]{1,0:T(8,128)(2,1)S(1)} %get-tuple-element.73), channel_id=1, source_target_pairs={{2,4},{3,5},{4,2},{5,3},{10,12},{11,13},{12,10},{13,11},{18,20},{1... | collective-permute-start | bytes 1572872 | tf_op jit(solution)/shard_map/ppermute | solution.py:475
  63.8 21.9 %collective-permute-start.10 = (bf16[512,512]{1,0:T(8,128)(2,1)S(1)}, bf16[512,512]{1,0:T(8,128)(2,1)S(1)}, u32[]{:S(2)}, u32[]{:S(2)}) collective-permute-start(bf16[512,512]{1,0:T(8,128)(2,1)S(1)} %get-tuple-element.51.refs_9_), channel_id=1, source_target_pairs={{0,2},{1,3},{2,0},{3,1},{4,6},{5,7},{6,4},{7,5},{8,10},{9,11},{10,... | collective-permute-start | bytes 1572872 | tf_op jit(solution)/shard_map/ppermute | solution.py:475
  70.4 29.7 %collective-permute-start.13 = (bf16[384,1024]{1,0:T(8,128)(2,1)S(1)}, bf16[384,1024]{1,0:T(8,128)(2,1)S(1)}, u32[]{:S(2)}, u32[]{:S(2)}) collective-permute-start(bf16[384,1024]{1,0:T(8,128)(2,1)S(1)} %shard_map.132), channel_id=1, source_target_pairs={{0,1},{1,0},{2,3},{3,2},{4,5},{5,4},{6,7},{7,6},{8,9},{9,8},{10,11... | collective-permute-start | bytes 2359304 | tf_op jit(solution)/shard_map/ppermute | solution.py:510
  74.8 19.2 %collective-permute-start.16 = (bf16[512,512]{1,0:T(8,128)(2,1)S(1)}, bf16[512,512]{1,0:T(8,128)(2,1)S(1)}, u32[]{:S(2)}, u32[]{:S(2)}) collective-permute-start(bf16[512,512]{1,0:T(8,128)(2,1)S(1)} %get-tuple-element.71), channel_id=1, source_target_pairs={{2,4},{3,5},{4,2},{5,3},{10,12},{11,13},{12,10},{13,11},{18,20},{1... | collective-permute-start | bytes 1572872 | tf_op jit(solution)/shard_map/ppermute | solution.py:475
  75.5 20.3 %collective-permute-start.15 = (bf16[512,512]{1,0:T(8,128)(2,1)S(1)}, bf16[512,512]{1,0:T(8,128)(2,1)S(1)}, u32[]{:S(2)}, u32[]{:S(2)}) collective-permute-start(bf16[512,512]{1,0:T(8,128)(2,1)S(1)} %get-tuple-element.70.refs_9_), channel_id=1, source_target_pairs={{0,2},{1,3},{2,0},{3,1},{4,6},{5,7},{6,4},{7,5},{8,10},{9,11},{10,... | collective-permute-start | bytes 1572872 | tf_op jit(solution)/shard_map/ppermute | solution.py:475
  87.2 17.9 %collective-permute-start.21 = (bf16[512,512]{1,0:T(8,128)(2,1)S(1)}, bf16[512,512]{1,0:T(8,128)(2,1)S(1)}, u32[]{:S(2)}, u32[]{:S(2)}) collective-permute-start(bf16[512,512]{1,0:T(8,128)(2,1)S(1)} %get-tuple-element.74), channel_id=1, source_target_pairs={{0,2},{1,3},{2,0},{3,1},{4,6},{5,7},{6,4},{7,5},{8,10},{9,11},{10,... | collective-permute-start | bytes 1572872 | tf_op jit(solution)/shard_map/ppermute | solution.py:475
  88.8 16.3 %collective-permute-start.22 = (bf16[512,512]{1,0:T(8,128)(2,1)S(1)}, bf16[512,512]{1,0:T(8,128)(2,1)S(1)}, u32[]{:S(2)}, u32[]{:S(2)}) collective-permute-start(bf16[512,512]{1,0:T(8,128)(2,1)S(1)} %get-tuple-element.75), channel_id=1, source_target_pairs={{2,4},{3,5},{4,2},{5,3},{10,12},{11,13},{12,10},{13,11},{18,20},{1... | collective-permute-start | bytes 1572872 | tf_op jit(solution)/shard_map/ppermute | solution.py:475
  92.1 3.7 %copy-start.4 = (f32[1,512,1024]{2,1,0:T(8,128)S(1)}, f32[1,512,1024]{2,1,0:T(8,128)}, u32[]{:S(2)}) copy-start(f32[1,512,1024]{2,1,0:T(8,128)} %param.11) | copy-start | bytes 6291460
  92.1 3.7 %copy-start.5 = (f32[1,512,1024]{2,1,0:T(8,128)S(1)}, f32[1,512,1024]{2,1,0:T(8,128)}, u32[]{:S(2)}) copy-start(f32[1,512,1024]{2,1,0:T(8,128)} %param.12) | copy-start | bytes 6291460
  94.0 26.1 %collective-permute-start.12 = (bf16[384,1536]{1,0:T(8,128)(2,1)S(1)}, bf16[384,1536]{1,0:T(8,128)(2,1)S(1)}, u32[]{:S(2)}, u32[]{:S(2)}) collective-permute-start(bf16[384,1536]{1,0:T(8,128)(2,1)S(1)} %get-tuple-element.62), channel_id=1, source_target_pairs={{0,1},{1,0},{2,3},{3,2},{4,5},{5,4},{6,7},{7,6},{8,9},{9,8},{10,11... | collective-permute-start | bytes 3538952 | tf_op jit(solution)/shard_map/ppermute | solution.py:535
  98.6 11.5 %collective-permute-start.18 = (bf16[512,512]{1,0:T(8,128)(2,1)S(1)}, bf16[512,512]{1,0:T(8,128)(2,1)S(1)}, u32[]{:S(2)}, u32[]{:S(2)}) collective-permute-start(bf16[512,512]{1,0:T(8,128)(2,1)S(1)} %get-tuple-element.72.refs_0_), channel_id=1, source_target_pairs={{0,16},{8,24},{16,0},{24,8},{1,17},{9,25},{17,1},{25,9},{2,18},{10... | collective-permute-start | bytes 1572872 | tf_op jit(solution)/shard_map/ppermute | solution.py:450
  108.0 12.1 %collective-permute-start.24 = (bf16[512,512]{1,0:T(8,128)(2,1)S(1)}, bf16[512,512]{1,0:T(8,128)(2,1)S(1)}, u32[]{:S(2)}, u32[]{:S(2)}) collective-permute-start(bf16[512,512]{1,0:T(8,128)(2,1)S(1)} %get-tuple-element.79.refs_4_), channel_id=1, source_target_pairs={{0,16},{8,24},{16,0},{24,8},{1,17},{9,25},{17,1},{25,9},{2,18},{10... | collective-permute-start | bytes 1572872 | tf_op jit(solution)/shard_map/ppermute | solution.py:450
  109.5 12.3 %collective-permute-start.17 = (bf16[512,512]{1,0:T(8,128)(2,1)S(1)}, bf16[512,512]{1,0:T(8,128)(2,1)S(1)}, u32[]{:S(2)}, u32[]{:S(2)}) collective-permute-start(bf16[512,512]{1,0:T(8,128)(2,1)S(1)} %get-tuple-element.72.refs_0_), channel_id=1, source_target_pairs={{0,8},{8,0},{16,24},{24,16},{1,9},{9,1},{17,25},{25,17},{2,10},{10... | collective-permute-start | bytes 1572872 | tf_op jit(solution)/shard_map/ppermute | solution.py:452
  109.5 12.3 %collective-permute-start.23 = (bf16[512,512]{1,0:T(8,128)(2,1)S(1)}, bf16[512,512]{1,0:T(8,128)(2,1)S(1)}, u32[]{:S(2)}, u32[]{:S(2)}) collective-permute-start(bf16[512,512]{1,0:T(8,128)(2,1)S(1)} %get-tuple-element.79.refs_4_), channel_id=1, source_target_pairs={{0,8},{8,0},{16,24},{24,16},{1,9},{9,1},{17,25},{25,17},{2,10},{10... | collective-permute-start | bytes 1572872 | tf_op jit(solution)/shard_map/ppermute | solution.py:452
  110.0 11.8 %collective-permute-start.19 = (bf16[512,512]{1,0:T(8,128)(2,1)S(1)}, bf16[512,512]{1,0:T(8,128)(2,1)S(1)}, u32[]{:S(2)}, u32[]{:S(2)}) collective-permute-start(bf16[512,512]{1,0:T(8,128)(2,1)S(1)} %collective-permute-done.18.refs_2_), channel_id=1, source_target_pairs={{0,8},{8,0},{16,24},{24,16},{1,9},{9,1},{17,25},{25,17},{2,10},{10... | collective-permute-start | bytes 1572872 | tf_op jit(solution)/shard_map/ppermute | solution.py:452
  120.1 1.9 %collective-permute-start.25 = (bf16[512,512]{1,0:T(8,128)(2,1)S(1)}, bf16[512,512]{1,0:T(8,128)(2,1)S(1)}, u32[]{:S(2)}, u32[]{:S(2)}) collective-permute-start(bf16[512,512]{1,0:T(8,128)(2,1)S(1)} %collective-permute-done.24.refs_6_), channel_id=1, source_target_pairs={{0,8},{8,0},{16,24},{24,16},{1,9},{9,1},{17,25},{25,17},{2,10},{10... | collective-permute-start | bytes 1572872 | tf_op jit(solution)/shard_map/ppermute | solution.py:452
  120.1 1.9 %copy-start.6 = (s32[4]{0:T(128)S(1)}, s32[4]{0:T(128)}, u32[]{:S(2)}) copy-start(s32[4]{0:T(128)} %numerator_ref.1) | copy-start | bytes 52
  (2 other events, 3.8 us)

commit v14 on v13

--- a/solution.py
+++ b/solution.py
@@ -403,8 +403,7 @@
 def average(plan, scalars, stepped, others, after):
     rows, columns = stepped[0].shape
     chunks, count = len(stepped), len(others[0])
-    steps = 2 if rows % 32 == 0 else 1
-    size = rows // steps
+    size = rows
 
     def kernel(row_ref, numerator_ref, partner_ref, *refs):
         mix = numerator_ref[row_ref[plan["replica"]]].astype(jnp.float32) / mix_denom
@@ -439,7 +438,7 @@
         scalars,
         ins + [(a, ANY) for a in after],
         [(struct((rows, chunks * columns), jnp.bfloat16), full)],
-        grid=(steps,),
+        vmem=24,
     )[0]
 
 

time: 124 us -> 124 us (level)
  no operation moved by 1% of the time
where the time goes in v14:
time: 124 us
  Pallas kernels  40.5 us (33%)
  starting transfers between devices  40.4 us (33%)
  waiting for transfers between devices  39.6 us (32%)
  local copies, waits for them, and re-layouts  2.62 us (2%)
    pallas_call x22, Pallas kernels, call(): pl.pallas_call(kernel, grid_spec=pltpu.PrefetchScalarGridSpec(num_scalar_...  40.5 us
    ppermute x14, starting transfers between devices, exchange(): lax.ppermute(bufs[name], 'fsdp', links[name])  28.7 us
    ppermute x2, waiting for transfers between devices, send(): return swap(pack(plan, row, rows, [], act, turns, after))  21.8 us
    ppermute x2, waiting for transfers between devices, partner_rows(): far = lax.ppermute(stepped, 'rep', [(r, r ^ 2) for r in range(4)])  10.1 us
    ppermute x14, waiting for transfers between devices, exchange(): lax.ppermute(bufs[name], 'fsdp', links[name])  7.43 us
    ppermute x2, starting transfers between devices, partner_rows(): far = lax.ppermute(stepped, 'rep', [(r, r ^ 2) for r in range(4)])  3.04 us
    ppermute x1, starting transfers between devices, per_device(): parcel = swap(cot)  3 us
  transfers between devices with their start and end apart: 26, of which 8 were waited for; matrix products, arithmetic and copies ran while one was open for 1% of the time, Pallas kernels for 31%

profile of v14, /device:TPU:0, one launch (start us, length us, event | category | flops | bytes accessed | tf_op | source)
XLA Modules:
  0.0 124.0 jit_solution(3316424609439615606)
XLA Ops:
  0.6 3.0 %collective-permute-start.3 = (bf16[384,1024]{1,0:T(8,128)(2,1)}, bf16[384,1024]{1,0:T(8,128)(2,1)S(1)}, u32[]{:S(2)}, u32[]{:S(2)}) collective-permute-start(bf16[384,1024]{1,0:T(8,128)(2,1)} %bitcast.33), channel_id=1, source_target_pairs={{0,1},{1,0},{2,3},{3,2},{4,5},{5,4},{6,7},{7,6},{8,9},{9,8},{10,11... | collective-permute-start | bytes 2359304 | tf_op jit(solution)/shard_map/ppermute | solution.py:490
  4.4 4.4 %collective-permute-start = (bf16[512,1024]{1,0:T(8,128)(2,1)}, bf16[512,1024]{1,0:T(8,128)(2,1)S(1)}, u32[]{:S(2)}, u32[]{:S(2)}) collective-permute-start(bf16[512,1024]{1,0:T(8,128)(2,1)} %bitcast.46), channel_id=1, source_target_pairs={{0,2},{1,3},{2,0},{3,1},{4,6},{5,7},{6,4},{7,5},{8,10},{9,11},{10,... | collective-permute-start | bytes 3145736 | tf_op jit(solution)/shard_map/ppermute | solution.py:474
  9.5 1.9 %copy-done = bf16[1,384,4096]{2,1,0:T(8,128)(2,1)S(1)} copy-done((bf16[1,384,4096]{2,1,0:T(8,128)(2,1)S(1)}, bf16[1,384,4096]{2,1,0:T(8,128)(2,1)}, u32[]{:S(2)}) %copy-start) | copy-done | bytes 3145752
  12.5 17.3 %collective-permute-done.2.refs_4_.refs_3_.refs_6_.refs_2_ = bf16[384,512]{1,0:T(8,128)(2,1)S(1)} collective-permute-done((bf16[384,512]{1,0:T(8,128)(2,1)S(1)}, bf16[384,512]{1,0:T(8,128)(2,1)S(1)}, u32[]{:S(2)}, u32[]{:S(2)}) %collective-permute-start.2) | collective-permute-done | bytes 393248 | tf_op jit(solution)/shard_map/ppermute | solution.py:488
  30.4 1.8 %collective-permute-start.6 = (bf16[384,1024]{1,0:T(8,128)(2,1)S(1)}, bf16[384,1024]{1,0:T(8,128)(2,1)S(1)}, u32[]{:S(2)}, u32[]{:S(2)}) collective-permute-start(bf16[384,1024]{1,0:T(8,128)(2,1)S(1)} %shard_map.121), channel_id=1, source_target_pairs={{0,1},{1,0},{2,3},{3,2},{4,5},{5,4},{6,7},{7,6},{8,9},{9,8},{10,11... | collective-permute-start | bytes 2359304 | tf_op jit(solution)/shard_map/ppermute | solution.py:488
  32.3 1.5 %shard_map.120 = (bf16[512,512]{1,0:T(8,128)(2,1)S(1)}, bf16[512,512]{1,0:T(8,128)(2,1)S(1)}) custom-call(s32[40]{0:T(128)S(1)} %dynamic-slice_bitcast_fusion.row_ref, bf16[512,1024]{1,0:T(8,128)(2,1)S(1)} %collective-permute-done.1.refs_0_.refs_1_, bf16[512,1024]{1,0:T(8,128)(2,1)S(1)} %collective-permute-done.refs_1_.refs_0_, ...), custom_call_target="tpu_custom_call" | custom-call | tf_op jit(solution)/shard_map/pallas_call | solution.py:86
  34.6 3.8 %collective-permute-start.5 = (bf16[512,512]{1,0:T(8,128)(2,1)S(1)}, bf16[512,512]{1,0:T(8,128)(2,1)S(1)}, u32[]{:S(2)}, u32[]{:S(2)}) collective-permute-start(bf16[512,512]{1,0:T(8,128)(2,1)S(1)} %get-tuple-element.45.refs_7_), channel_id=1, source_target_pairs={{0,2},{1,3},{2,0},{3,1},{4,6},{5,7},{6,4},{7,5},{8,10},{9,11},{10,... | collective-permute-start | bytes 1572872 | tf_op jit(solution)/shard_map/ppermute | solution.py:474
  38.5 2.4 %shard_map.123 = (bf16[384,4096]{1,0:T(8,128)(2,1)}, bf16[384,512]{1,0:T(8,128)(2,1)S(1)}, bf16[512,1024]{1,0:T(8,128)(2,1)S(1)}) custom-call(s32[40]{0:T(128)S(1)} %dynamic-slice_bitcast_fusion.row_ref, bf16[512,1024]{1,0:T(8,128)(2,1)S(1)} %bitcast.47, ...), custom_call_target="tpu_custom_call" | custom-call | tf_op jit(solution)/shard_map/pallas_call | solution.py:86
  40.9 1.5 %shard_map.122 = (bf16[512,512]{1,0:T(8,128)(2,1)S(1)}, bf16[512,512]{1,0:T(8,128)(2,1)S(1)}) custom-call(s32[40]{0:T(128)S(1)} %dynamic-slice_bitcast_fusion.row_ref, bf16[512,1024]{1,0:T(8,128)(2,1)S(1)} %collective-permute-done.1.refs_0_.refs_1_, bf16[512,1024]{1,0:T(8,128)(2,1)S(1)} %collective-permute-done.refs_1_.refs_0_, ...), custom_call_target="tpu_custom_call" | custom-call | tf_op jit(solution)/shard_map/pallas_call | solution.py:86
  43.2 1.5 %collective-permute-start.9 = (bf16[512,512]{1,0:T(8,128)(2,1)S(1)}, bf16[512,512]{1,0:T(8,128)(2,1)S(1)}, u32[]{:S(2)}, u32[]{:S(2)}) collective-permute-start(bf16[512,512]{1,0:T(8,128)(2,1)S(1)} %get-tuple-element.46.refs_8_), channel_id=1, source_target_pairs={{0,2},{1,3},{2,0},{3,1},{4,6},{5,7},{6,4},{7,5},{8,10},{9,11},{10,... | collective-permute-start | bytes 1572872 | tf_op jit(solution)/shard_map/ppermute | solution.py:474
  44.7 4.5 %collective-permute-done.6.refs_5_.refs_2_.refs_7_.refs_8_.refs_3_.refs_4_.refs_6_ = bf16[384,1024]{1,0:T(8,128)(2,1)S(1)} collective-permute-done((bf16[384,1024]{1,0:T(8,128)(2,1)S(1)}, bf16[384,1024]{1,0:T(8,128)(2,1)S(1)}, u32[]{:S(2)}, u32[]{:S(2)}) %collective-permute-start.6) | collective-permute-done | bytes 786464 | tf_op jit(solution)/shard_map/ppermute | solution.py:488
  51.3 2.4 %shard_map.124 = (bf16[384,4096]{1,0:T(8,128)(2,1)}, bf16[384,512]{1,0:T(8,128)(2,1)S(1)}, bf16[512,1024]{1,0:T(8,128)(2,1)S(1)}) custom-call(s32[40]{0:T(128)S(1)} %dynamic-slice_bitcast_fusion.row_ref, bf16[512,1024]{1,0:T(8,128)(2,1)S(1)} %collective-permute-done.refs_1_.refs_0_, ...), custom_call_target="tpu_custom_call", output_to_operand_aliasing={{0}: (6, {})} | custom-call | tf_op jit(solution)/shard_map/pallas_call | solution.py:86
  56.0 4.4 %collective-permute-start.7 = (bf16[512,512]{1,0:T(8,128)(2,1)S(1)}, bf16[512,512]{1,0:T(8,128)(2,1)S(1)}, u32[]{:S(2)}, u32[]{:S(2)}) collective-permute-start(bf16[512,512]{1,0:T(8,128)(2,1)S(1)} %get-tuple-element.49.refs_8_), channel_id=1, source_target_pairs={{0,2},{1,3},{2,0},{3,1},{4,6},{5,7},{6,4},{7,5},{8,10},{9,11},{10,... | collective-permute-start | bytes 1572872 | tf_op jit(solution)/shard_map/ppermute | solution.py:474
  63.8 3.5 %collective-permute-start.10 = (bf16[512,512]{1,0:T(8,128)(2,1)S(1)}, bf16[512,512]{1,0:T(8,128)(2,1)S(1)}, u32[]{:S(2)}, u32[]{:S(2)}) collective-permute-start(bf16[512,512]{1,0:T(8,128)(2,1)S(1)} %get-tuple-element.51.refs_9_), channel_id=1, source_target_pairs={{0,2},{1,3},{2,0},{3,1},{4,6},{5,7},{6,4},{7,5},{8,10},{9,11},{10,... | collective-permute-start | bytes 1572872 | tf_op jit(solution)/shard_map/ppermute | solution.py:474
  67.3 2.5 %shard_map.127 = (bf16[384,4096]{1,0:T(8,128)(2,1)}, bf16[384,512]{1,0:T(8,128)(2,1)S(1)}, bf16[512,1024]{1,0:T(8,128)(2,1)S(1)}) custom-call(s32[40]{0:T(128)S(1)} %dynamic-slice_bitcast_fusion.row_ref, bf16[512,512]{1,0:T(8,128)(2,1)S(1)} %collective-permute-done.5.refs_1_.refs_0_, ...), custom_call_target="tpu_custom_call", output_to_operand_aliasing={{0}: (8, {})} | custom-call | tf_op jit(solution)/shard_map/pallas_call | solution.py:86
  71.0 2.3 %collective-permute-done.7.refs_1_ = bf16[512,512]{1,0:T(8,128)(2,1)S(1)} collective-permute-done((bf16[512,512]{1,0:T(8,128)(2,1)S(1)}, bf16[512,512]{1,0:T(8,128)(2,1)S(1)}, u32[]{:S(2)}, u32[]{:S(2)}) %collective-permute-start.7) | collective-permute-done | bytes 524320 | tf_op jit(solution)/shard_map/ppermute | solution.py:474
  75.5 4.5 %collective-permute-start.15 = (bf16[512,512]{1,0:T(8,128)(2,1)S(1)}, bf16[512,512]{1,0:T(8,128)(2,1)S(1)}, u32[]{:S(2)}, u32[]{:S(2)}) collective-permute-start(bf16[512,512]{1,0:T(8,128)(2,1)S(1)} %get-tuple-element.70.refs_9_), channel_id=1, source_target_pairs={{0,2},{1,3},{2,0},{3,1},{4,6},{5,7},{6,4},{7,5},{8,10},{9,11},{10,... | collective-permute-start | bytes 1572872 | tf_op jit(solution)/shard_map/ppermute | solution.py:474
  79.9 1.8 %shard_map.136.grad_ref.refs_11_ = f32[512,1024]{1,0:T(8,128)S(1)} custom-call(s32[40]{0:T(128)S(1)} %dynamic-slice_bitcast_fusion.row_ref, bf16[384,4096]{1,0:T(8,128)(2,1)S(1)} %bitcast.26, bf16[384,1024]{1,0:T(8,128)(2,1)S(1)} %collective-permute-done.11.refs_9_.refs_5_.refs_2_.refs_0_.piece_ref, bf16[384,1024]{1,0:T(8,128)(2,1)S(1)} %bitcast.42, ...), custom_call_target="tpu_custom_call" | custom-call | tf_op jit(solution)/shard_map/pallas_call | solution.py:86
  81.8 3.9 %shard_map.130 = (f32[384,1024]{1,0:T(8,128)S(1)}, f32[384,1024]{1,0:T(8,128)S(1)}) custom-call(s32[40]{0:T(128)S(1)} %dynamic-slice_bitcast_fusion.row_ref, bf16[512,1024]{1,0:T(8,128)(2,1)S(1)} %get-tuple-element.56.refs_0_, bf16[512,1024]{1,0:T(8,128)(2,1)S(1)} %get-tuple-element.57.refs_1_, bf16[512,1024]{1,0:T(8,128)(2,1)S(1)} %get-tuple-element.58.refs_2_, ...), custom_call_target="tpu_custom_call" | custom-call | tf_op jit(solution)/shard_map/pallas_call | solution.py:86
  85.7 1.5 %shard_map.138 = (bf16[512,512]{1,0:T(8,128)(2,1)S(1)}, bf16[512,512]{1,0:T(8,128)(2,1)S(1)}) custom-call(s32[40]{0:T(128)S(1)} %dynamic-slice_bitcast_fusion.row_ref, bf16[512,512]{1,0:T(8,128)(2,1)S(1)} %collective-permute-done.20.refs_0_, bf16[512,512]{1,0:T(8,128)(2,1)S(1)} %collective-permute-done.10.refs_2_.refs_1_, bf16[384,4096]{1,0:T(8,128)(2,1)S(1)} %bitcast.30, ...), custom_call_target="tpu_custom_call" | custom-call | tf_op jit(solution)/shard_map/pallas_call | solution.py:86
  87.2 1.6 %collective-permute-start.21 = (bf16[512,512]{1,0:T(8,128)(2,1)S(1)}, bf16[512,512]{1,0:T(8,128)(2,1)S(1)}, u32[]{:S(2)}, u32[]{:S(2)}) collective-permute-start(bf16[512,512]{1,0:T(8,128)(2,1)S(1)} %get-tuple-element.74), channel_id=1, source_target_pairs={{0,2},{1,3},{2,0},{3,1},{4,6},{5,7},{6,4},{7,5},{8,10},{9,11},{10,... | collective-permute-start | bytes 1572872 | tf_op jit(solution)/shard_map/ppermute | solution.py:474
  89.5 2.5 %shard_map.128 = (bf16[384,4096]{1,0:T(8,128)(2,1)}, bf16[384,512]{1,0:T(8,128)(2,1)S(1)}, bf16[512,1024]{1,0:T(8,128)(2,1)S(1)}) custom-call(s32[40]{0:T(128)S(1)} %dynamic-slice_bitcast_fusion.row_ref, bf16[512,1024]{1,0:T(8,128)(2,1)S(1)} %collective-permute-done.refs_1_.refs_0_, ...), custom_call_target="tpu_custom_call", output_to_operand_aliasing={{0}: (7, {})} | custom-call | tf_op jit(solution)/shard_map/pallas_call | solution.py:86
  92.1 1.9 %shard_map.131 = (f32[384,1024]{1,0:T(8,128)S(1)}, bf16[384,1536]{1,0:T(8,128)(2,1)S(1)}) custom-call(s32[40]{0:T(128)S(1)} %dynamic-slice_bitcast_fusion.row_ref, bf16[512,1024]{1,0:T(8,128)(2,1)S(1)} %get-tuple-element.54.refs_0_, bf16[384,4096]{1,0:T(8,128)(2,1)S(1)} %bitcast.32, ...), custom_call_target="tpu_custom_call" | custom-call | tf_op jit(solution)/shard_map/pallas_call | solution.py:86
  95.7 2.9 %shard_map.137 = (f32[512,1024]{1,0:T(8,128)}, f32[512,1024]{1,0:T(8,128)}, bf16[512,512]{1,0:T(8,128)(2,1)S(1)}) custom-call(s32[40]{0:T(128)S(1)} %dynamic-slice_bitcast_fusion.row_ref, bf16[512,512]{1,0:T(8,128)(2,1)S(1)} %collective-permute-done.15.up_ref, bf16[512,512]{1,0:T(8,128)(2,1)S(1)} %collective-permute-done.16.dn_ref, ...), custom_call_target="tpu_custom_call" | custom-call | tf_op jit(solution)/shard_map/pallas_call | solution.py:86
  98.6 1.5 %collective-permute-start.18 = (bf16[512,512]{1,0:T(8,128)(2,1)S(1)}, bf16[512,512]{1,0:T(8,128)(2,1)S(1)}, u32[]{:S(2)}, u32[]{:S(2)}) collective-permute-start(bf16[512,512]{1,0:T(8,128)(2,1)S(1)} %get-tuple-element.72.refs_0_), channel_id=1, source_target_pairs={{0,16},{8,24},{16,0},{24,8},{1,17},{9,25},{17,1},{25,9},{2,18},{10... | collective-permute-start | bytes 1572872 | tf_op jit(solution)/shard_map/ppermute | solution.py:449
  100.1 2.2 %shard_map.133 = (bf16[384,4096]{1,0:T(8,128)(2,1)}, f32[8,128]{1,0:T(8,128)S(1)}) custom-call(s32[40]{0:T(128)S(1)} %dynamic-slice_bitcast_fusion.row_ref, bf16[384,1024]{1,0:T(8,128)(2,1)S(1)} %collective-permute-done.11.refs_9_.refs_5_.refs_2_.refs_0_.piece_ref, ...), custom_call_target="tpu_custom_call", output_to_operand_aliasing={{0}: (4, {})} | custom-call | tf_op jit(solution)/shard_map/pallas_call | solution.py:86
  102.3 2.8 %collective-permute-done.21.up_ref = bf16[512,512]{1,0:T(8,128)(2,1)S(1)} collective-permute-done((bf16[512,512]{1,0:T(8,128)(2,1)S(1)}, bf16[512,512]{1,0:T(8,128)(2,1)S(1)}, u32[]{:S(2)}, u32[]{:S(2)}) %collective-permute-start.21) | collective-permute-done | bytes 524320 | tf_op jit(solution)/shard_map/ppermute | solution.py:474
  105.2 2.9 %shard_map.139 = (f32[512,1024]{1,0:T(8,128)}, f32[512,1024]{1,0:T(8,128)}, bf16[512,512]{1,0:T(8,128)(2,1)S(1)}) custom-call(s32[40]{0:T(128)S(1)} %dynamic-slice_bitcast_fusion.row_ref, bf16[512,512]{1,0:T(8,128)(2,1)S(1)} %collective-permute-done.21.up_ref, ...), custom_call_target="tpu_custom_call", output_to_operand_aliasing={{0}: (7, {}), {1}: (8, {})} | custom-call | tf_op jit(solution)/shard_map/pallas_call | solution.py:86
  108.0 1.5 %collective-permute-start.24 = (bf16[512,512]{1,0:T(8,128)(2,1)S(1)}, bf16[512,512]{1,0:T(8,128)(2,1)S(1)}, u32[]{:S(2)}, u32[]{:S(2)}) collective-permute-start(bf16[512,512]{1,0:T(8,128)(2,1)S(1)} %get-tuple-element.79.refs_4_), channel_id=1, source_target_pairs={{0,16},{8,24},{16,0},{24,8},{1,17},{9,25},{17,1},{25,9},{2,18},{10... | collective-permute-start | bytes 1572872 | tf_op jit(solution)/shard_map/ppermute | solution.py:449
  110.0 10.1 %collective-permute-done.24.refs_6_ = bf16[512,512]{1,0:T(8,128)(2,1)S(1)} collective-permute-done((bf16[512,512]{1,0:T(8,128)(2,1)S(1)}, bf16[512,512]{1,0:T(8,128)(2,1)S(1)}, u32[]{:S(2)}, u32[]{:S(2)}) %collective-permute-start.24) | collective-permute-done | bytes 524320 | tf_op jit(solution)/shard_map/ppermute | solution.py:449
  120.2 1.7 %shard_map.134 = (bf16[384,4096]{1,0:T(8,128)(2,1)}, f32[8,128]{1,0:T(8,128)S(1)}, bf16[384,1024]{1,0:T(8,128)(2,1)}) custom-call(s32[40]{0:T(128)S(1)} %dynamic-slice_bitcast_fusion.row_ref, bf16[384,1536]{1,0:T(8,128)(2,1)S(1)} %collective-permute-done.12.refs_0_.refs_2_, ...), custom_call_target="tpu_custom_call", output_to_operand_aliasing={{0}: (4, {})} | custom-call | tf_op jit(solution)/shard_map/pallas_call | solution.py:86
  122.1 1.9 %shard_map.140 = bf16[512,1024]{1,0:T(8,128)(2,1)} custom-call(s32[40]{0:T(128)S(1)} %dynamic-slice_bitcast_fusion.row_ref, s32[4]{0:T(128)S(1)} %copy-done.6, s32[4]{0:T(128)S(1)} %copy-done.7, bf16[512,512]{1,0:T(8,128)(2,1)S(1)} %get-tuple-element.72.refs_0_, bf16[512,512]{1,0:T(8,128)(2,1)S(1)} %collective-permute-done.17.refs_1_, ...), custom_call_target="tpu_custom_call" | custom-call | tf_op jit(solution)/shard_map/pallas_call | solution.py:86
  (59 shorter events, 18.9 us)
Async XLA Ops:
  0.6 29.2 %collective-permute-start.3 = (bf16[384,1024]{1,0:T(8,128)(2,1)}, bf16[384,1024]{1,0:T(8,128)(2,1)S(1)}, u32[]{:S(2)}, u32[]{:S(2)}) collective-permute-start(bf16[384,1024]{1,0:T(8,128)(2,1)} %bitcast.33), channel_id=1, source_target_pairs={{0,1},{1,0},{2,3},{3,2},{4,5},{5,4},{6,7},{7,6},{8,9},{9,8},{10,11... | collective-permute-start | bytes 2359304 | tf_op jit(solution)/shard_map/ppermute | solution.py:490
  3.6 28.6 %collective-permute-start.1 = (bf16[512,1024]{1,0:T(8,128)(2,1)}, bf16[512,1024]{1,0:T(8,128)(2,1)S(1)}, u32[]{:S(2)}, u32[]{:S(2)}) collective-permute-start(bf16[512,1024]{1,0:T(8,128)(2,1)} %bitcast.45), channel_id=1, source_target_pairs={{2,4},{3,5},{4,2},{5,3},{10,12},{11,13},{12,10},{13,11},{18,20},{1... | collective-permute-start | bytes 3145736 | tf_op jit(solution)/shard_map/ppermute | solution.py:474
  4.4 27.9 %collective-permute-start = (bf16[512,1024]{1,0:T(8,128)(2,1)}, bf16[512,1024]{1,0:T(8,128)(2,1)S(1)}, u32[]{:S(2)}, u32[]{:S(2)}) collective-permute-start(bf16[512,1024]{1,0:T(8,128)(2,1)} %bitcast.46), channel_id=1, source_target_pairs={{0,2},{1,3},{2,0},{3,1},{4,6},{5,7},{6,4},{7,5},{8,10},{9,11},{10,... | collective-permute-start | bytes 3145736 | tf_op jit(solution)/shard_map/ppermute | solution.py:474
  11.9 20.3 %copy-start.2 = (bf16[1,384,1024]{2,1,0:T(8,128)(2,1)S(1)}, bf16[1,384,1024]{2,1,0:T(8,128)(2,1)}, u32[]{:S(2)}) copy-start(bf16[1,384,1024]{2,1,0:T(8,128)(2,1)} %param.10) | copy-start | bytes 2359300
  11.9 17.9 %collective-permute-start.2 = (bf16[384,512]{1,0:T(8,128)(2,1)S(1)}, bf16[384,512]{1,0:T(8,128)(2,1)S(1)}, u32[]{:S(2)}, u32[]{:S(2)}) collective-permute-start(bf16[384,512]{1,0:T(8,128)(2,1)S(1)} %shard_map.119), channel_id=1, source_target_pairs={{0,1},{1,0},{2,3},{3,2},{4,5},{5,4},{6,7},{7,6},{8,9},{9,8},{10,11... | collective-permute-start | bytes 1179656 | tf_op jit(solution)/shard_map/ppermute | solution.py:488
  30.4 8.1 %copy-start.3 = (bf16[1,512,1024]{2,1,0:T(8,128)(2,1)S(1)}, bf16[1,512,1024]{2,1,0:T(8,128)(2,1)}, u32[]{:S(2)}) copy-start(bf16[1,512,1024]{2,1,0:T(8,128)(2,1)} %param.9) | copy-start | bytes 3145732
  30.4 18.8 %collective-permute-start.6 = (bf16[384,1024]{1,0:T(8,128)(2,1)S(1)}, bf16[384,1024]{1,0:T(8,128)(2,1)S(1)}, u32[]{:S(2)}, u32[]{:S(2)}) collective-permute-start(bf16[384,1024]{1,0:T(8,128)(2,1)S(1)} %shard_map.121), channel_id=1, source_target_pairs={{0,1},{1,0},{2,3},{3,2},{4,5},{5,4},{6,7},{7,6},{8,9},{9,8},{10,11... | collective-permute-start | bytes 2359304 | tf_op jit(solution)/shard_map/ppermute | solution.py:488
  33.8 7.1 %copy-start.1 = (bf16[1,384,4096]{2,1,0:T(8,128)(2,1)S(1)}, bf16[1,384,4096]{2,1,0:T(8,128)(2,1)}, u32[]{:S(2)}) copy-start(bf16[1,384,4096]{2,1,0:T(8,128)(2,1)} %param.8) | copy-start | bytes 9437188
  33.8 20.0 %collective-permute-start.4 = (bf16[512,512]{1,0:T(8,128)(2,1)S(1)}, bf16[512,512]{1,0:T(8,128)(2,1)S(1)}, u32[]{:S(2)}, u32[]{:S(2)}) collective-permute-start(bf16[512,512]{1,0:T(8,128)(2,1)S(1)} %get-tuple-element.44), channel_id=1, source_target_pairs={{2,4},{3,5},{4,2},{5,3},{10,12},{11,13},{12,10},{13,11},{18,20},{1... | collective-permute-start | bytes 1572872 | tf_op jit(solution)/shard_map/ppermute | solution.py:474
  34.6 19.1 %collective-permute-start.5 = (bf16[512,512]{1,0:T(8,128)(2,1)S(1)}, bf16[512,512]{1,0:T(8,128)(2,1)S(1)}, u32[]{:S(2)}, u32[]{:S(2)}) collective-permute-start(bf16[512,512]{1,0:T(8,128)(2,1)S(1)} %get-tuple-element.45.refs_7_), channel_id=1, source_target_pairs={{0,2},{1,3},{2,0},{3,1},{4,6},{5,7},{6,4},{7,5},{8,10},{9,11},{10,... | collective-permute-start | bytes 1572872 | tf_op jit(solution)/shard_map/ppermute | solution.py:474
  42.5 17.9 %collective-permute-start.8 = (bf16[512,512]{1,0:T(8,128)(2,1)S(1)}, bf16[512,512]{1,0:T(8,128)(2,1)S(1)}, u32[]{:S(2)}, u32[]{:S(2)}) collective-permute-start(bf16[512,512]{1,0:T(8,128)(2,1)S(1)} %get-tuple-element.50), channel_id=1, source_target_pairs={{2,4},{3,5},{4,2},{5,3},{10,12},{11,13},{12,10},{13,11},{18,20},{1... | collective-permute-start | bytes 1572872 | tf_op jit(solution)/shard_map/ppermute | solution.py:474
  43.2 18.4 %collective-permute-start.9 = (bf16[512,512]{1,0:T(8,128)(2,1)S(1)}, bf16[512,512]{1,0:T(8,128)(2,1)S(1)}, u32[]{:S(2)}, u32[]{:S(2)}) collective-permute-start(bf16[512,512]{1,0:T(8,128)(2,1)S(1)} %get-tuple-element.46.refs_8_), channel_id=1, source_target_pairs={{0,2},{1,3},{2,0},{3,1},{4,6},{5,7},{6,4},{7,5},{8,10},{9,11},{10,... | collective-permute-start | bytes 1572872 | tf_op jit(solution)/shard_map/ppermute | solution.py:474
  49.8 20.0 %collective-permute-start.11 = (bf16[384,1024]{1,0:T(8,128)(2,1)S(1)}, bf16[384,1024]{1,0:T(8,128)(2,1)S(1)}, u32[]{:S(2)}, u32[]{:S(2)}) collective-permute-start(bf16[384,1024]{1,0:T(8,128)(2,1)S(1)} %shard_map.129), channel_id=1, source_target_pairs={{0,1},{1,0},{2,3},{3,2},{4,5},{5,4},{6,7},{7,6},{8,9},{9,8},{10,11... | collective-permute-start | bytes 2359304 | tf_op jit(solution)/shard_map/ppermute | solution.py:509
  55.3 15.7 %collective-permute-start.14 = (bf16[512,512]{1,0:T(8,128)(2,1)S(1)}, bf16[512,512]{1,0:T(8,128)(2,1)S(1)}, u32[]{:S(2)}, u32[]{:S(2)}) collective-permute-start(bf16[512,512]{1,0:T(8,128)(2,1)S(1)} %get-tuple-element.69), channel_id=1, source_target_pairs={{2,4},{3,5},{4,2},{5,3},{10,12},{11,13},{12,10},{13,11},{18,20},{1... | collective-permute-start | bytes 1572872 | tf_op jit(solution)/shard_map/ppermute | solution.py:474
  56.0 17.3 %collective-permute-start.7 = (bf16[512,512]{1,0:T(8,128)(2,1)S(1)}, bf16[512,512]{1,0:T(8,128)(2,1)S(1)}, u32[]{:S(2)}, u32[]{:S(2)}) collective-permute-start(bf16[512,512]{1,0:T(8,128)(2,1)S(1)} %get-tuple-element.49.refs_8_), channel_id=1, source_target_pairs={{0,2},{1,3},{2,0},{3,1},{4,6},{5,7},{6,4},{7,5},{8,10},{9,11},{10,... | collective-permute-start | bytes 1572872 | tf_op jit(solution)/shard_map/ppermute | solution.py:474
  63.1 22.6 %collective-permute-start.20 = (bf16[512,512]{1,0:T(8,128)(2,1)S(1)}, bf16[512,512]{1,0:T(8,128)(2,1)S(1)}, u32[]{:S(2)}, u32[]{:S(2)}) collective-permute-start(bf16[512,512]{1,0:T(8,128)(2,1)S(1)} %get-tuple-element.73), channel_id=1, source_target_pairs={{2,4},{3,5},{4,2},{5,3},{10,12},{11,13},{12,10},{13,11},{18,20},{1... | collective-permute-start | bytes 1572872 | tf_op jit(solution)/shard_map/ppermute | solution.py:474
  63.8 21.9 %collective-permute-start.10 = (bf16[512,512]{1,0:T(8,128)(2,1)S(1)}, bf16[512,512]{1,0:T(8,128)(2,1)S(1)}, u32[]{:S(2)}, u32[]{:S(2)}) collective-permute-start(bf16[512,512]{1,0:T(8,128)(2,1)S(1)} %get-tuple-element.51.refs_9_), channel_id=1, source_target_pairs={{0,2},{1,3},{2,0},{3,1},{4,6},{5,7},{6,4},{7,5},{8,10},{9,11},{10,... | collective-permute-start | bytes 1572872 | tf_op jit(solution)/shard_map/ppermute | solution.py:474
  70.4 29.7 %collective-permute-start.13 = (bf16[384,1024]{1,0:T(8,128)(2,1)S(1)}, bf16[384,1024]{1,0:T(8,128)(2,1)S(1)}, u32[]{:S(2)}, u32[]{:S(2)}) collective-permute-start(bf16[384,1024]{1,0:T(8,128)(2,1)S(1)} %shard_map.132), channel_id=1, source_target_pairs={{0,1},{1,0},{2,3},{3,2},{4,5},{5,4},{6,7},{7,6},{8,9},{9,8},{10,11... | collective-permute-start | bytes 2359304 | tf_op jit(solution)/shard_map/ppermute | solution.py:509
  74.8 19.2 %collective-permute-start.16 = (bf16[512,512]{1,0:T(8,128)(2,1)S(1)}, bf16[512,512]{1,0:T(8,128)(2,1)S(1)}, u32[]{:S(2)}, u32[]{:S(2)}) collective-permute-start(bf16[512,512]{1,0:T(8,128)(2,1)S(1)} %get-tuple-element.71), channel_id=1, source_target_pairs={{2,4},{3,5},{4,2},{5,3},{10,12},{11,13},{12,10},{13,11},{18,20},{1... | collective-permute-start | bytes 1572872 | tf_op jit(solution)/shard_map/ppermute | solution.py:474
  75.5 20.3 %collective-permute-start.15 = (bf16[512,512]{1,0:T(8,128)(2,1)S(1)}, bf16[512,512]{1,0:T(8,128)(2,1)S(1)}, u32[]{:S(2)}, u32[]{:S(2)}) collective-permute-start(bf16[512,512]{1,0:T(8,128)(2,1)S(1)} %get-tuple-element.70.refs_9_), channel_id=1, source_target_pairs={{0,2},{1,3},{2,0},{3,1},{4,6},{5,7},{6,4},{7,5},{8,10},{9,11},{10,... | collective-permute-start | bytes 1572872 | tf_op jit(solution)/shard_map/ppermute | solution.py:474
  87.2 17.9 %collective-permute-start.21 = (bf16[512,512]{1,0:T(8,128)(2,1)S(1)}, bf16[512,512]{1,0:T(8,128)(2,1)S(1)}, u32[]{:S(2)}, u32[]{:S(2)}) collective-permute-start(bf16[512,512]{1,0:T(8,128)(2,1)S(1)} %get-tuple-element.74), channel_id=1, source_target_pairs={{0,2},{1,3},{2,0},{3,1},{4,6},{5,7},{6,4},{7,5},{8,10},{9,11},{10,... | collective-permute-start | bytes 1572872 | tf_op jit(solution)/shard_map/ppermute | solution.py:474
  88.8 16.3 %collective-permute-start.22 = (bf16[512,512]{1,0:T(8,128)(2,1)S(1)}, bf16[512,512]{1,0:T(8,128)(2,1)S(1)}, u32[]{:S(2)}, u32[]{:S(2)}) collective-permute-start(bf16[512,512]{1,0:T(8,128)(2,1)S(1)} %get-tuple-element.75), channel_id=1, source_target_pairs={{2,4},{3,5},{4,2},{5,3},{10,12},{11,13},{12,10},{13,11},{18,20},{1... | collective-permute-start | bytes 1572872 | tf_op jit(solution)/shard_map/ppermute | solution.py:474
  92.1 3.7 %copy-start.4 = (f32[1,512,1024]{2,1,0:T(8,128)S(1)}, f32[1,512,1024]{2,1,0:T(8,128)}, u32[]{:S(2)}) copy-start(f32[1,512,1024]{2,1,0:T(8,128)} %param.11) | copy-start | bytes 6291460
  92.1 3.7 %copy-start.5 = (f32[1,512,1024]{2,1,0:T(8,128)S(1)}, f32[1,512,1024]{2,1,0:T(8,128)}, u32[]{:S(2)}) copy-start(f32[1,512,1024]{2,1,0:T(8,128)} %param.12) | copy-start | bytes 6291460
  94.0 26.1 %collective-permute-start.12 = (bf16[384,1536]{1,0:T(8,128)(2,1)S(1)}, bf16[384,1536]{1,0:T(8,128)(2,1)S(1)}, u32[]{:S(2)}, u32[]{:S(2)}) collective-permute-start(bf16[384,1536]{1,0:T(8,128)(2,1)S(1)} %get-tuple-element.62), channel_id=1, source_target_pairs={{0,1},{1,0},{2,3},{3,2},{4,5},{5,4},{6,7},{7,6},{8,9},{9,8},{10,11... | collective-permute-start | bytes 3538952 | tf_op jit(solution)/shard_map/ppermute | solution.py:534
  98.6 11.5 %collective-permute-start.18 = (bf16[512,512]{1,0:T(8,128)(2,1)S(1)}, bf16[512,512]{1,0:T(8,128)(2,1)S(1)}, u32[]{:S(2)}, u32[]{:S(2)}) collective-permute-start(bf16[512,512]{1,0:T(8,128)(2,1)S(1)} %get-tuple-element.72.refs_0_), channel_id=1, source_target_pairs={{0,16},{8,24},{16,0},{24,8},{1,17},{9,25},{17,1},{25,9},{2,18},{10... | collective-permute-start | bytes 1572872 | tf_op jit(solution)/shard_map/ppermute | solution.py:449
  108.0 12.1 %collective-permute-start.24 = (bf16[512,512]{1,0:T(8,128)(2,1)S(1)}, bf16[512,512]{1,0:T(8,128)(2,1)S(1)}, u32[]{:S(2)}, u32[]{:S(2)}) collective-permute-start(bf16[512,512]{1,0:T(8,128)(2,1)S(1)} %get-tuple-element.79.refs_4_), channel_id=1, source_target_pairs={{0,16},{8,24},{16,0},{24,8},{1,17},{9,25},{17,1},{25,9},{2,18},{10... | collective-permute-start | bytes 1572872 | tf_op jit(solution)/shard_map/ppermute | solution.py:449
  109.5 12.3 %collective-permute-start.17 = (bf16[512,512]{1,0:T(8,128)(2,1)S(1)}, bf16[512,512]{1,0:T(8,128)(2,1)S(1)}, u32[]{:S(2)}, u32[]{:S(2)}) collective-permute-start(bf16[512,512]{1,0:T(8,128)(2,1)S(1)} %get-tuple-element.72.refs_0_), channel_id=1, source_target_pairs={{0,8},{8,0},{16,24},{24,16},{1,9},{9,1},{17,25},{25,17},{2,10},{10... | collective-permute-start | bytes 1572872 | tf_op jit(solution)/shard_map/ppermute | solution.py:451
  109.5 12.3 %collective-permute-start.23 = (bf16[512,512]{1,0:T(8,128)(2,1)S(1)}, bf16[512,512]{1,0:T(8,128)(2,1)S(1)}, u32[]{:S(2)}, u32[]{:S(2)}) collective-permute-start(bf16[512,512]{1,0:T(8,128)(2,1)S(1)} %get-tuple-element.79.refs_4_), channel_id=1, source_target_pairs={{0,8},{8,0},{16,24},{24,16},{1,9},{9,1},{17,25},{25,17},{2,10},{10... | collective-permute-start | bytes 1572872 | tf_op jit(solution)/shard_map/ppermute | solution.py:451
  110.0 11.8 %collective-permute-start.19 = (bf16[512,512]{1,0:T(8,128)(2,1)S(1)}, bf16[512,512]{1,0:T(8,128)(2,1)S(1)}, u32[]{:S(2)}, u32[]{:S(2)}) collective-permute-start(bf16[512,512]{1,0:T(8,128)(2,1)S(1)} %collective-permute-done.18.refs_2_), channel_id=1, source_target_pairs={{0,8},{8,0},{16,24},{24,16},{1,9},{9,1},{17,25},{25,17},{2,10},{10... | collective-permute-start | bytes 1572872 | tf_op jit(solution)/shard_map/ppermute | solution.py:451
  120.1 1.9 %collective-permute-start.25 = (bf16[512,512]{1,0:T(8,128)(2,1)S(1)}, bf16[512,512]{1,0:T(8,128)(2,1)S(1)}, u32[]{:S(2)}, u32[]{:S(2)}) collective-permute-start(bf16[512,512]{1,0:T(8,128)(2,1)S(1)} %collective-permute-done.24.refs_6_), channel_id=1, source_target_pairs={{0,8},{8,0},{16,24},{24,16},{1,9},{9,1},{17,25},{25,17},{2,10},{10... | collective-permute-start | bytes 1572872 | tf_op jit(solution)/shard_map/ppermute | solution.py:451
  120.1 1.9 %copy-start.6 = (s32[4]{0:T(128)S(1)}, s32[4]{0:T(128)}, u32[]{:S(2)}) copy-start(s32[4]{0:T(128)} %numerator_ref.1) | copy-start | bytes 52
  (2 other events, 3.8 us)
